TPU v7x, 32 devices: a whole 2x2x4 slice. The times are simulated.
32 devices in a mesh: rep: 8 (over y, x, core), shard: 4 (over z).
Axes of the slice: x: 2, y: 2, z: 4, core: 2. Of those that a mesh axis runs over, the one named last changes fastest.
Arguments:
- inputs: bfloat16 [16384, 1536], P(('rep', 'shard')), may hold values from -6 to 6
- query_key_value_weight: bfloat16 [1536, 2560], P('shard'), may hold values from -0.15625 to 0.15625
- output_weight: bfloat16 [1536, 1536], P('shard'), may hold values from -1.25 to 1.25
- attention_gain: bfloat16 [1536], P('shard'), may hold values from 0.25 to 1.75
- feed_gain: bfloat16 [1536], P('shard'), may hold values from 0.25 to 1.75
- router_weight: bfloat16 [1536, 16], P('shard'), may hold values from -0.078125 to 0.078125
- expert_weight: bfloat16 [16, 1536, 1536], P('shard'), may hold values from -3 to 3, as said below
- routes: int32 [16384, 8], P(('rep', 'shard')), may hold values from 0 to 15, all different within a row; in each aligned block of 512 rows (0 to 511, 512 to 1023, ...) at most 320 rows name the same one
- cotangent: bfloat16 [16384, 1536], P(('rep', 'shard')), may hold values from -6 to 6
Outputs:
- activations: bfloat16 [16384, 1536], P(('rep', 'shard'))
- input_grad: bfloat16 [16384, 1536], P(('rep', 'shard'))
- attend_grad: float32 [1536, 2560], P('shard')
- output_grad: float32 [1536, 1536], P('shard')
- attention_gain_grad: float32 [1536], P('shard')
- feed_gain_grad: float32 [1536], P('shard')
- router_grad: float32 [1536, 16], P('shard')
- expert_grad: float32 [16, 1536, 1536], P('shard')
Inputs may be any that keep to these rules, and one draw needn't show every extreme that they name: `routes`: each row names 8 different experts. Among the rows of one device no expert is named more than 320 times, and in some device's rows an expert is named exactly 320 times. `expert_weight`: columns 0 to 1023 of each expert's matrix are its gate then up projection, the last 512 columns its down projection transposed.
All inputs are finite; a program needn't handle non-finite values.
Results may differ from a plain program's by a relative error of at most 0.02.
Values may be sent and summed in bfloat16 or wider, within the bound.
No kernel may reach another device: no remote copies, remote signals or barrier semaphores. Data moves between devices by JAX's collectives and lax.ppermute only.
A program may use at most 576 MiB of HBM per device.

v0:
```python
import jax
import jax.numpy as jnp
from jax import lax
from jax.sharding import PartitionSpec as P

QUERY_HEADS = 24
KEY_VALUE_HEADS = 8
HEAD_WIDTH = 64
FF = 512
TOPK = 8
EXPERTS = 16
CAP = 320


EPSILON = 1e-06
MASKED = -1e30


def contract_rows(left, right):
    return lax.dot_general(
        left, right, (((0,), (0,)), ((), ())), preferred_element_type=jnp.float32
    )


def times_transposed(left, right):
    return lax.dot_general(
        left, right, (((1,), (1,)), ((), ())), preferred_element_type=jnp.float32
    )


def norm_rows(value_rows):
    inverse = lax.rsqrt(jnp.mean(value_rows * value_rows, axis=-1, keepdims=True) + EPSILON)
    return (value_rows * inverse, inverse)


def norm_back(scaled, inverse, upstream):
    return inverse * (upstream - scaled * jnp.mean(upstream * scaled, axis=-1, keepdims=True))


def rotary_tables(sequence_length, head_size):
    half_size = head_size // 2
    frequency = 10000.0 ** (-2.0 * jnp.arange(half_size, dtype=jnp.float32) / head_size)
    angles = jnp.arange(sequence_length, dtype=jnp.float32)[:, None] * frequency[None, :]
    return (jnp.cos(angles)[:, None, :], jnp.sin(angles)[:, None, :])


def apply_rotation(value_rows, cosine_table, sine_values):
    half_size = value_rows.shape[-1] // 2
    lower_half = value_rows[..., :half_size]
    upper_half = value_rows[..., half_size:]
    return jnp.concatenate(
        [
            lower_half * cosine_table - upper_half * sine_values,
            upper_half * cosine_table + lower_half * sine_values,
        ],
        axis=-1,
    )


def rotate_back(value_rows, cosine_table, sine_values):
    half_size = value_rows.shape[-1] // 2
    lower_half = value_rows[..., :half_size]
    upper_half = value_rows[..., half_size:]
    return jnp.concatenate(
        [
            lower_half * cosine_table + upper_half * sine_values,
            upper_half * cosine_table - lower_half * sine_values,
        ],
        axis=-1,
    )


def slot_tables(routes):
    sequence_length = routes.shape[0]
    listed = routes.reshape(-1)
    hits = (listed[:, None] == jnp.arange(EXPERTS, dtype=jnp.int32)[None, :]).astype(jnp.int32)
    earlier = jnp.cumsum(hits, axis=0) - hits
    places = jnp.sum(earlier * hits, axis=1)
    flat_slot = listed * CAP + places
    owners = jnp.arange(sequence_length * TOPK, dtype=jnp.int32) // TOPK
    slot_token = jnp.zeros((EXPERTS * CAP,), jnp.int32).at[flat_slot].set(owners)
    filled = jnp.zeros((EXPERTS * CAP,), jnp.int32).at[flat_slot].set(1) > 0
    return (slot_token, filled, flat_slot.reshape(sequence_length, TOPK))


def block_scores(query_rows, key_rows, offset, scale):
    scores = (
        jnp.einsum("qkgd,skd->kgqs", query_rows, key_rows, preferred_element_type=jnp.float32)
        * scale
    )
    key_place = jnp.arange(key_rows.shape[0], dtype=jnp.int32)
    allowed = (
        key_place[None, :] <= offset + jnp.arange(query_rows.shape[0], dtype=jnp.int32)[:, None]
    )
    return jnp.where(allowed, scores, MASKED)


def attention_forward(query_matrix, key_rows, value_rows):
    sequence_length, head_count, head_size = query_matrix.shape
    kv_count = key_rows.shape[1]
    rows_per_block = min(sequence_length, 512)
    query_block_count = query_matrix.reshape(
        sequence_length // rows_per_block,
        rows_per_block,
        kv_count,
        head_count // kv_count,
        head_size,
    )
    offsets = jnp.arange(sequence_length // rows_per_block, dtype=jnp.int32) * rows_per_block
    scale = head_size ** (-0.5)

    def attend_block(block_inputs):
        query_rows, offset = block_inputs
        scores = block_scores(query_rows, key_rows, offset, scale)
        maxima = jnp.max(scores, axis=-1, keepdims=True)
        powers = jnp.exp(scores - maxima)
        totals = jnp.sum(powers, axis=-1, keepdims=True)
        probability = (powers / totals).astype(jnp.bfloat16)
        mixed = jnp.einsum(
            "kgqs,skd->qkgd", probability, value_rows, preferred_element_type=jnp.float32
        )
        return (mixed, maxima, totals)

    mixed, maxima, totals = lax.map(attend_block, (query_block_count, offsets))
    return (mixed.reshape(sequence_length, head_count * head_size), maxima, totals)


def attention_backward(query_matrix, key_rows, value_rows, maxima, totals, upstream):
    sequence_length, head_count, head_size = query_matrix.shape
    kv_count = key_rows.shape[1]
    head_groups = head_count // kv_count
    rows_per_block = min(sequence_length, 512)
    blocks = sequence_length // rows_per_block
    query_block_count = query_matrix.reshape(
        blocks, rows_per_block, kv_count, head_groups, head_size
    )
    upstream_blocks = upstream.reshape(blocks, rows_per_block, kv_count, head_groups, head_size)
    offsets = jnp.arange(blocks, dtype=jnp.int32) * rows_per_block
    scale = head_size ** (-0.5)

    def backward_block(sums, block_inputs):
        query_rows, upstream_rows, block_max, block_total, offset = block_inputs
        scores = block_scores(query_rows, key_rows, offset, scale)
        probability = jnp.exp(scores - block_max) / block_total
        rounded = probability.astype(jnp.bfloat16)
        value_grad = jnp.einsum(
            "kgqs,qkgd->skd", rounded, upstream_rows, preferred_element_type=jnp.float32
        )
        prob_grad = jnp.einsum(
            "qkgd,skd->kgqs", upstream_rows, value_rows, preferred_element_type=jnp.float32
        )
        score_grad = probability * (
            prob_grad - jnp.sum(prob_grad * probability, axis=-1, keepdims=True)
        )
        score_grad = score_grad.astype(jnp.bfloat16)
        query_grad = (
            jnp.einsum("kgqs,skd->qkgd", score_grad, key_rows, preferred_element_type=jnp.float32)
            * scale
        )
        key_grad = (
            jnp.einsum("kgqs,qkgd->skd", score_grad, query_rows, preferred_element_type=jnp.float32)
            * scale
        )
        return ((sums[0] + key_grad, sums[1] + value_grad), query_grad)

    empty_keys = jnp.zeros(key_rows.shape, jnp.float32)
    (key_grads, value_grads), query_grads = lax.scan(
        backward_block,
        (empty_keys, empty_keys),
        (query_block_count, upstream_blocks, maxima, totals, offsets),
    )
    return (query_grads.reshape(sequence_length, head_count, head_size), key_grads, value_grads)


def expert_forward(slot_rows, weights):
    gate_up = jnp.einsum(
        "ecd,edf->ecf", slot_rows, weights[:, :, : 2 * FF], preferred_element_type=jnp.float32
    )
    hidden = (jax.nn.silu(gate_up[..., :FF]) * gate_up[..., FF:]).astype(jnp.bfloat16)
    return jnp.einsum(
        "ecf,edf->ecd", hidden, weights[:, :, 2 * FF :], preferred_element_type=jnp.float32
    ).astype(jnp.bfloat16)


def expert_backward(slot_rows, weights, upstream):
    gate_up = jnp.einsum(
        "ecd,edf->ecf", slot_rows, weights[:, :, : 2 * FF], preferred_element_type=jnp.float32
    )
    gate_part = gate_up[..., :FF]
    up_part = gate_up[..., FF:]
    sigma_gate = jax.nn.sigmoid(gate_part)
    activated = gate_part * sigma_gate
    hidden = (activated * up_part).astype(jnp.bfloat16)
    hidden_grad = jnp.einsum(
        "ecd,edf->ecf", upstream, weights[:, :, 2 * FF :], preferred_element_type=jnp.float32
    )
    gate_grad = hidden_grad * up_part * sigma_gate * (1.0 + gate_part * (1.0 - sigma_gate))
    up_grad = hidden_grad * activated
    pair_grad = jnp.concatenate([gate_grad, up_grad], axis=-1).astype(jnp.bfloat16)
    row_grad = jnp.einsum(
        "ecf,edf->ecd", pair_grad, weights[:, :, : 2 * FF], preferred_element_type=jnp.float32
    ).astype(jnp.bfloat16)
    return (pair_grad, hidden, row_grad)


def expert_terms(slot_rows, upstream, pair_grad, hidden):
    inner = jnp.einsum("ecd,ecf->edf", slot_rows, pair_grad, preferred_element_type=jnp.float32)
    outer = jnp.einsum("ecd,ecf->edf", upstream, hidden, preferred_element_type=jnp.float32)
    return jnp.concatenate([inner, outer], axis=-1)


def body(
    inputs,
    query_key_value_weight,
    output_weight,
    attention_gain,
    feed_gain,
    router_weight,
    expert_weight,
    routes,
    cotangent,
):
    sequence_length, features = inputs.shape
    query_total_width = QUERY_HEADS * HEAD_WIDTH
    key_total_width = KEY_VALUE_HEADS * HEAD_WIDTH
    attend_full, output_full, attention_full, feed_full, router_full = (
        lax.all_gather(query_key_value_weight, "shard", axis=0, tiled=True),
        lax.all_gather(output_weight, "shard", axis=0, tiled=True),
        lax.all_gather(attention_gain, "shard", axis=0, tiled=True),
        lax.all_gather(feed_gain, "shard", axis=0, tiled=True),
        lax.all_gather(router_weight, "shard", axis=0, tiled=True),
    )
    cosine_table, sine_values = rotary_tables(sequence_length, HEAD_WIDTH)
    residual = inputs.astype(jnp.float32)
    scaled_in, inverse_in = norm_rows(residual)
    attention_scale = attention_full.astype(jnp.float32)
    normed = (scaled_in * attention_scale).astype(jnp.bfloat16)
    projected_rows = jnp.dot(normed, attend_full, preferred_element_type=jnp.float32)
    query_matrix = apply_rotation(
        projected_rows[:, :query_total_width].reshape(sequence_length, QUERY_HEADS, HEAD_WIDTH),
        cosine_table,
        sine_values,
    ).astype(jnp.bfloat16)
    key_rows = apply_rotation(
        projected_rows[:, query_total_width : query_total_width + key_total_width].reshape(
            sequence_length, KEY_VALUE_HEADS, HEAD_WIDTH
        ),
        cosine_table,
        sine_values,
    ).astype(jnp.bfloat16)
    value_rows = (
        projected_rows[:, query_total_width + key_total_width :]
        .reshape(sequence_length, KEY_VALUE_HEADS, HEAD_WIDTH)
        .astype(jnp.bfloat16)
    )
    mixed_full, maxima, totals = attention_forward(query_matrix, key_rows, value_rows)
    mixed = mixed_full.astype(jnp.bfloat16)
    middle = residual + times_transposed(mixed, output_full)
    scaled_mid, inverse_mid = norm_rows(middle)
    feed_scale = feed_full.astype(jnp.float32)
    fed = (scaled_mid * feed_scale).astype(jnp.bfloat16)
    logits = jnp.dot(fed, router_full, preferred_element_type=jnp.float32)
    route_hits = routes[:, :, None] == jnp.arange(EXPERTS, dtype=jnp.int32)[None, None, :]
    chosen = jnp.sum(jnp.where(route_hits, logits[:, None, :], 0.0), axis=-1)
    gates = jax.nn.softmax(chosen, axis=-1)
    slot_token, filled, flat_slot = slot_tables(routes)
    dispatched = jnp.where(filled[:, None], fed[slot_token], jnp.zeros((), jnp.bfloat16)).reshape(
        EXPERTS, CAP, features
    )
    slot_rows = dispatched
    returned = expert_forward(slot_rows, lax.all_gather(expert_weight, "shard", axis=0, tiled=True))
    picked = returned.reshape(EXPERTS * CAP, features)[flat_slot].astype(jnp.float32)
    activations = (middle + jnp.sum(gates[:, :, None] * picked, axis=1)).astype(jnp.bfloat16)
    attend_back, output_back, router_back = (
        lax.all_gather(query_key_value_weight, "shard", axis=0, tiled=True),
        lax.all_gather(output_weight, "shard", axis=0, tiled=True),
        lax.all_gather(router_weight, "shard", axis=0, tiled=True),
    )
    upstream = cotangent.astype(jnp.float32)
    gate_grad = jnp.sum(upstream[:, None, :] * picked, axis=-1)
    slot_gate = (
        jnp.zeros((EXPERTS * CAP,), jnp.float32).at[flat_slot.reshape(-1)].set(gates.reshape(-1))
    )
    produced_grad = (
        (slot_gate[:, None] * upstream[slot_token])
        .astype(jnp.bfloat16)
        .reshape(EXPERTS, CAP, features)
    )
    slot_rows = dispatched
    results = expert_backward(
        slot_rows, lax.all_gather(expert_weight, "shard", axis=0, tiled=True), produced_grad
    )
    pair_grad, hidden, row_grads = tuple((fresh_rows for fresh_rows in results))
    expert_term = lax.psum_scatter(
        expert_terms(dispatched, produced_grad, pair_grad, hidden).astype(jnp.bfloat16),
        "shard",
        scatter_dimension=0,
        tiled=True,
    )
    chosen_grad = gates * (gate_grad - jnp.sum(gates * gate_grad, axis=-1, keepdims=True))
    logit_grad = jnp.sum(jnp.where(route_hits, chosen_grad[:, :, None], 0.0), axis=1).astype(
        jnp.bfloat16
    )
    router_term = contract_rows(fed, logit_grad)
    fed_grad = times_transposed(logit_grad, router_back) + jnp.sum(
        row_grads.reshape(EXPERTS * CAP, features)[flat_slot].astype(jnp.float32), axis=1
    )
    feed_term = jnp.sum(fed_grad * scaled_mid, axis=0)
    middle_grad = upstream + norm_back(scaled_mid, inverse_mid, fed_grad * feed_scale)
    branch_grad = middle_grad.astype(jnp.bfloat16)
    output_term = contract_rows(branch_grad, mixed)
    mixed_grad = jnp.dot(branch_grad, output_back, preferred_element_type=jnp.float32).astype(
        jnp.bfloat16
    )
    query_grad, key_grad, value_grad = attention_backward(
        query_matrix, key_rows, value_rows, maxima, totals, mixed_grad
    )
    projected_grad = jnp.concatenate(
        [
            rotate_back(query_grad, cosine_table, sine_values).reshape(
                sequence_length, query_total_width
            ),
            rotate_back(key_grad, cosine_table, sine_values).reshape(
                sequence_length, key_total_width
            ),
            value_grad.reshape(sequence_length, key_total_width),
        ],
        axis=1,
    ).astype(jnp.bfloat16)
    attend_term = contract_rows(normed, projected_grad)
    normed_grad = times_transposed(projected_grad, attend_back)
    attention_term = jnp.sum(normed_grad * scaled_in, axis=0)
    input_grad = (
        middle_grad + norm_back(scaled_in, inverse_in, normed_grad * attention_scale)
    ).astype(jnp.bfloat16)
    attend_part, output_part, attention_part, feed_part, router_part = (
        lax.psum_scatter(
            attend_term.astype(jnp.bfloat16), "shard", scatter_dimension=0, tiled=True
        ).astype(jnp.float32),
        lax.psum_scatter(
            output_term.astype(jnp.bfloat16), "shard", scatter_dimension=0, tiled=True
        ).astype(jnp.float32),
        lax.psum_scatter(
            attention_term.astype(jnp.bfloat16), "shard", scatter_dimension=0, tiled=True
        ).astype(jnp.float32),
        lax.psum_scatter(
            feed_term.astype(jnp.bfloat16), "shard", scatter_dimension=0, tiled=True
        ).astype(jnp.float32),
        lax.psum_scatter(
            router_term.astype(jnp.bfloat16), "shard", scatter_dimension=0, tiled=True
        ).astype(jnp.float32),
    )
    attention_sum, feed_sum, router_sum = lax.psum((attention_part, feed_part, router_part), "rep")
    expert_share, attend_share, output_share = (
        lax.psum_scatter(expert_term, "rep", scatter_dimension=1, tiled=True).astype(jnp.float32),
        lax.psum_scatter(
            attend_part.astype(jnp.bfloat16), "rep", scatter_dimension=1, tiled=True
        ).astype(jnp.float32),
        lax.psum_scatter(
            output_part.astype(jnp.bfloat16), "rep", scatter_dimension=1, tiled=True
        ).astype(jnp.float32),
    )
    expert_total, attend_total, output_total = (
        lax.all_gather(expert_share.astype(jnp.bfloat16), "rep", axis=1, tiled=True).astype(
            expert_share.dtype
        ),
        lax.all_gather(attend_share.astype(jnp.bfloat16), "rep", axis=1, tiled=True).astype(
            attend_share.dtype
        ),
        lax.all_gather(output_share.astype(jnp.bfloat16), "rep", axis=1, tiled=True).astype(
            output_share.dtype
        ),
    )
    return (
        activations,
        input_grad,
        attend_total,
        output_total,
        attention_sum,
        feed_sum,
        router_sum,
        expert_total,
    )


def solution(mesh):
    in_specs = (
        P(("rep", "shard"), None),
        P("shard", None),
        P("shard", None),
        P("shard"),
        P("shard"),
        P("shard", None),
        P("shard", None, None),
        P(("rep", "shard"), None),
        P(("rep", "shard"), None),
    )
    out_specs = (
        P(("rep", "shard"), None),
        P(("rep", "shard"), None),
        P("shard", None),
        P("shard", None),
        P("shard"),
        P("shard"),
        P("shard", None),
        P("shard", None, None),
    )
    return jax.shard_map(body, mesh=mesh, in_specs=in_specs, out_specs=out_specs, check_vma=False)
```

profile of v0, /device:TPU:0, one launch (start us, length us, event | category | flops | bytes accessed | tf_op | source)
XLA Modules:
  0.0 3712.8 jit_solution(2441235039145730856)
XLA Ops:
  9.9 13.5 all-gather.1
  23.5 13.8 all-gather
  37.4 4.6 reduce-window.6
  43.7 15.5 scatter_custom_fusion.1
  59.2 15.5 scatter_custom_fusion
  75.5 1.8 convert_element_type.148
  77.3 25.3 gather_fusion.2
  102.7 16.2 all_gather.35
  119.7 1.8 fusion.42
  122.4 31.8 all-gather.9.cloned.1.call-done
  154.2 7.3 fusion.61
  162.6 1.9 slice.86
  165.5 2.4 copy.92
  167.9 2.5 copy.91
  170.4 2.1 subtract_convert_fusion.3
  172.5 1.7 subtract_convert_fusion.1
  174.2 14.8 fusion.97
  189.1 11.8 fusion.45
  200.9 42.5 %all-gather.11.cloned.1.call-done = bf16[1536,1536]{1,0:T(8,128)(2,1)} async-done(((bf16[384,1536]{1,0:T(8,128)(2,1)}), bf16[1536,1536]{1,0:T(8,128)(2,1)}) %all-gather.11.cloned.1.call-update) | async-done | bytes 4718608 | tf_op jit(solution)/shard_map/all_gather | solution.py:228
  243.4 5.2 multiply_reduce_fusion.2
  248.7 1.6 copy-done.4
  250.7 23.8 gather_fusion
  276.0 16.1 scatter_custom_fusion.2
  292.2 1200.3 %all-gather.13.cloned.1.call-done = bf16[16,1536,1536]{2,1,0:T(8,128)(2,1)} async-done(((bf16[4,1536,1536]{2,1,0:T(8,128)(2,1)}), bf16[16,1536,1536]{2,1,0:T(8,128)(2,1)}) %all-gather.13.cloned.1.call-update) | async-done | bytes 75497488 | tf_op jit(solution)/shard_map/all_gather | solution.py:271
  1492.5 30.8 fusion.3
  1523.3 32.7 multiply_convert_fusion.2
  1556.0 20.2 fusion.15
  1576.2 32.9 gather_fusion.1
  1609.1 17.1 fusion.6
  1627.3 33.3 fusion.18
  1660.5 32.8 gather_fusion.3
  1693.4 10.7 convert_reduce_fusion
  1704.2 1.7 multiply_reduce_fusion
  1706.4 2.2 multiply_add_fusion
  1708.7 4.9 convolution_convert_fusion.3
  1713.5 6.0 convolution_convert_fusion.4
  1719.5 1.8 copy.101
  1721.4 17.9 fusion.7
  1739.3 21.8 fusion.9
  1761.1 8.7 fusion.52
  1770.9 6.9 convolution_multiply_fusion
  1778.5 14.1 fusion.53
  1792.6 8.4 convolution_convert_fusion.2
  1801.8 26.3 convolution_convert_fusion.1
  1828.1 37.1 convolution_convert_fusion
  1865.2 50.9 %pad_maximum_fusion = bf16[16,1536,1536]{1,2,0:T(8,128)(2,1)} fusion(bf16[16,1536,512]{1,2,0:T(8,128)(2,1)} %convolution_convert_fusion.1, bf16[16,1536,1024]{1,2,0:T(8,128)(2,1)} %convolution_convert_fusion), kind=kLoop, calls=%fused_computation.8 | loop fusion | flops 150994944 | bytes 150994944 | tf_op jit(solution)/shard_map/concatenate | solution.py:209
  1916.2 2.4 copy.121
  1918.6 25.2 reduce-scatter.13.cloned.1.call-done
  1943.9 3.9 copy.119
  1947.9 1228.8 %reduce-scatter.17.cloned.1.call-done = bf16[4,1536,1536]{1,2,0:T(8,128)(2,1)} async-done(((bf16[16,1536,1536]{1,2,0:T(8,128)(2,1)}), bf16[4,1536,1536]{1,2,0:T(8,128)(2,1)}) %reduce-scatter.17.cloned.1.call-update) | async-done | bytes 18874384 | tf_op jit(solution)/shard_map/reduce_scatter | solution.py:294
  3176.7 32.0 copy.107
  3211.4 7.3 reduce-scatter.21.cloned.1.call-done
  3218.8 44.2 %reduce-scatter.19.cloned.1.call-done = bf16[320,384]{1,0:T(8,128)(2,1)} async-done(((bf16[2560,384]{1,0:T(8,128)(2,1)}), bf16[320,384]{1,0:T(8,128)(2,1)}) %reduce-scatter.19.cloned.1.call-update) | async-done | bytes 245776
  3264.4 242.8 %all-reduce.7.cloned.1.call-done = bf16[4,1536,1536]{2,0,1:T(4,128)(2,1)} async-done(((bf16[4,1536,1536]{2,0,1:T(4,128)(2,1)}), bf16[4,1536,1536]{2,0,1:T(4,128)(2,1)}) %all-reduce.7.cloned.1.call-update) | async-done | bytes 18874384
  3507.2 3.9 constant_dynamic-slice_fusion
  3512.4 11.2 fusion.41
  3523.6 11.9 all-reduce.4
  3535.6 4.4 fusion.40
  3541.0 23.2 all-reduce.3
  3564.1 2.7 copy.109
  3566.9 17.1 all-gather.15.cloned.1.call-done
  3584.0 4.2 copy.108
  3588.1 96.6 %all-gather.19.cloned.1.call-done = bf16[4,1536,1536]{2,0,1:T(4,128)(2,1)} async-done(((bf16[4,192,1536]{2,0,1:T(4,128)(2,1)}), bf16[4,1536,1536]{2,0,1:T(4,128)(2,1)}) %all-gather.19.cloned.1.call-update) | async-done | bytes 18874384 | tf_op jit(solution)/shard_map/all_gather | solution.py:364
  3684.8 21.3 copy.110
  (212 shorter events, 20.3 us)
Async XLA Ops:
  7.2 147.0 %all-gather.9.cloned.1.call-start = ((), (), s32[]{:S(2)}) async-start(), calls=%async_computation.6 | async-start | bytes 9830400 | tf_op jit(solution)/shard_map/all_gather | solution.py:227
  7.9 235.5 %all-gather.11.cloned.1.call-start = ((), (), s32[]{:S(2)}) async-start(), calls=%async_computation.7 | async-start | bytes 5898240 | tf_op jit(solution)/shard_map/all_gather | solution.py:228
  8.7 1483.8 %all-gather.13.cloned.1.call-start = ((), (), s32[]{:S(2)}) async-start(), calls=%async_computation.8 | async-start | bytes 94371840 | tf_op jit(solution)/shard_map/all_gather | solution.py:271
  9.4 1906.8 %reduce-scatter.15.cloned.1.call-start = ((), (), s32[]{:S(2)}) async-start(), calls=%async_computation.11 | async-start | bytes 5898240 | tf_op jit(solution)/shard_map/reduce_scatter | solution.py:340
  23.5 225.1 %copy-start.39 = (f32[1536]{0:T(1024)}, f32[1536]{0:T(1024)S(1)}, u32[]{:S(2)}) copy-start(f32[1536]{0:T(1024)S(1)} %reshape.368) | copy-start | bytes 18436
  37.4 116.8 %copy-start.47 = (f32[1536]{0:T(1024)}, f32[1536]{0:T(1024)S(1)}, u32[]{:S(2)}) copy-start(f32[1536]{0:T(1024)S(1)} %reshape.367) | copy-start | bytes 18436
  43.6 15.6 copy-start.52
  77.3 25.4 copy-start
  77.3 25.3 copy-start.32
  77.3 25.3 copy-start.53
  121.5 40.1 %copy-start.54 = (f32[512]{0:T(512)}, f32[512]{0:T(512)S(1)}, u32[]{:S(2)}) copy-start(f32[512]{0:T(512)S(1)} %add_rsqrt_fusion.1) | copy-start | bytes 6148
  122.4 50.1 %copy-start.15 = (f32[512,32]{0,1:T(8,128)}, f32[512,32]{0,1:T(8,128)S(1)}, u32[]{:S(2)}) copy-start(f32[512,32]{0,1:T(8,128)S(1)} %get-tuple-element.125) | copy-start | bytes 196612
  122.4 50.1 %copy-start.17 = (f32[512,32]{0,1:T(8,128)}, f32[512,32]{0,1:T(8,128)S(1)}, u32[]{:S(2)}) copy-start(f32[512,32]{0,1:T(8,128)S(1)} %get-tuple-element.126) | copy-start | bytes 196612
  172.5 16.6 copy-start.21
  174.2 14.8 copy-start.26
  189.1 11.9 copy-start.41
  189.1 54.3 %copy-start.10 = (bf16[512,1536]{1,0:T(8,128)(2,1)S(1)}, bf16[512,1536]{1,0:T(8,128)(2,1)}, u32[]{:S(2)}) copy-start(bf16[512,1536]{1,0:T(8,128)(2,1)} %param.9) | copy-start | bytes 4718596
  243.4 7.2 copy-start.33
  250.6 23.8 copy-start.2
  250.7 23.8 copy-start.28
  250.7 24.3 copy-start.37
  250.7 1241.9 %copy-start.56 = (pred[16,320]{1,0:T(8,128)(4,1)S(1)}, pred[16,320]{1,0:T(8,128)(4,1)}, u32[]{:S(2)}) copy-start(pred[16,320]{1,0:T(8,128)(4,1)} %broadcast_in_dim.121) | copy-start | bytes 15364
  275.1 1248.3 %copy-start.24 = (f32[512,8]{0,1:T(8,128)}, f32[512,8]{0,1:T(8,128)S(1)}, u32[]{:S(2)}) copy-start(f32[512,8]{0,1:T(8,128)S(1)} %select_reduce_fusion.1) | copy-start | bytes 49156
  292.2 1231.1 %copy-start.30 = (f32[16,320]{1,0:T(8,128)}, f32[16,320]{1,0:T(8,128)S(1)}, u32[]{:S(2)}) copy-start(f32[16,320]{1,0:T(8,128)S(1)} %mul.482) | copy-start | bytes 61444
  1556.0 20.2 copy-start.6
  1576.2 32.9 copy-start.1
  1693.3 10.7 copy-start.25
  1693.3 10.8 copy-start.44
  1693.3 10.8 copy-start.50
  1693.3 10.8 copy-start.38
  1693.3 10.9 copy-start.5
  1693.3 10.9 copy-start.29
  1693.3 10.9 copy-start.40
  1693.3 10.9 copy-start.46
  1704.1 1.9 copy-start.9
  1704.1 2.4 copy-start.12
  1706.4 2.2 copy-start.60
  1708.7 4.9 copy-start.7
  1719.5 1.9 copy-start.42
  1721.3 18.0 copy-start.20
  1721.3 222.5 %reduce-scatter.13.cloned.1.call-start = ((), (), s32[]{:S(2)}) async-start(), calls=%async_computation.9 | async-start | bytes 9830400 | tf_op jit(solution)/shard_map/reduce_scatter | solution.py:337
  1739.3 21.8 copy-start.13
  1739.3 21.8 copy-start.14
  1761.1 8.7 copy-start.16
  1761.1 8.7 copy-start.18
  1761.1 9.8 copy-start.22
  1761.1 9.8 copy-start.23
  1778.5 14.1 copy-start.19
  1778.5 14.1 copy-start.11
  1778.5 14.1 copy-start.48
  1778.5 14.1 copy-start.55
  1801.1 27.0 copy-start.57
  1801.1 1375.6 %reduce-scatter.17.cloned.1.call-start = ((), (), s32[]{:S(2)}) async-start(), calls=%async_computation.13 | async-start | bytes 94371840 | tf_op jit(solution)/shard_map/reduce_scatter | solution.py:294
  1916.1 1302.7 %reduce-scatter.21.cloned.1.call-start = ((), (), s32[]{:S(2)}) async-start(), calls=%async_computation.16 | async-start | bytes 1327104
  1918.6 1344.5 %reduce-scatter.19.cloned.1.call-start = ((), (), s32[]{:S(2)}) async-start(), calls=%async_computation.15 | async-start | bytes 2211840
  1947.9 1559.4 %all-reduce.7.cloned.1.call-start = ((), (), s32[]{:S(2)}) async-start(), calls=%async_computation.18 | async-start | bytes 37748736
  3208.7 54.5 %copy-start.62 = (u32[32]{0:T(128)S(1)}, u32[32]{0:T(128)}, u32[]{:S(2)}) copy-start(u32[32]{0:T(128)} %constant.118) | copy-start | bytes 388
  3208.7 302.4 %copy-start.61 = (u32[32]{0:T(128)S(1)}, u32[32]{0:T(128)}, u32[]{:S(2)}) copy-start(u32[32]{0:T(128)} %constant.110) | copy-start | bytes 388
  3208.7 331.3 %reduce-scatter.23.cloned.1.call-start = ((), (), s32[]{:S(2)}) async-start(), calls=%async_computation.17 | async-start | bytes 491520
  3211.4 352.8 %all-gather.17.cloned.1.call-start = ((), (), s32[]{:S(2)}) async-start(), calls=%async_computation.12 | async-start | bytes 1327104 | tf_op jit(solution)/shard_map/all_gather | solution.py:370
  3218.8 365.2 %all-gather.15.cloned.1.call-start = ((), (), s32[]{:S(2)}) async-start(), calls=%async_computation.10 | async-start | bytes 2211840 | tf_op jit(solution)/shard_map/all_gather | solution.py:367
  3263.1 421.6 %all-gather.19.cloned.1.call-start = ((), (), s32[]{:S(2)}) async-start(), calls=%async_computation.14 | async-start | bytes 21233664 | tf_op jit(solution)/shard_map/all_gather | solution.py:364
  3512.4 11.2 copy-start.51
  3512.4 23.2 copy-start.8
  (12 other events, 15.3 us)
Sparse Core Ops, SparseCore 0:
  9.6 144.5 all-gather.8
  155.7 87.6 all-gather.10
  245.0 1247.4 all-gather.12
  1721.5 83.4 reduce-scatter.14
  1807.1 136.7 reduce-scatter.12
  1946.1 1230.5 reduce-scatter.16
  3180.9 37.8 reduce-scatter.20
  3222.7 40.2 reduce-scatter.18
  3267.8 239.3 all-reduce.6
  3509.4 20.7 reduce-scatter.22
  3532.2 22.3 all-gather.16
  3556.5 27.3 all-gather.14
  3586.0 98.7 all-gather.18
where the time goes:
time: 3720 us; the launch traced here: 3710 us
  waiting for transfers between devices  2940 us (79%)
  matrix products  300 us (8%)
  local copies, waits for them, and re-layouts  254 us (7%)
  other arithmetic  124 us (3%)
  blocking collectives  78.6 us (2%)
    reduce_scatter x1, waiting for transfers between devices, body(): lax.psum_scatter(expert_terms(dispatched, produced_grad, pair_grad, hidde...  1230 us
    all_gather x1, waiting for transfers between devices, body(): lax.all_gather(expert_weight, 'shard', axis=0, tiled=True)  1200 us
    unnamed x17, waiting for transfers between devices  297 us
    all_gather x1, waiting for transfers between devices, body(): lax.all_gather(expert_share.astype(jnp.bfloat16), 'rep', axis=1, tiled=True)  96.6 us
  transfers between devices with their start and end apart: 13, of which 10 were waited for; matrix products, arithmetic and copies ran while one was open for 11% of the time, Pallas kernels for 0%

commit v1 on v0

v1 whole, which is shorter than its diff:
```python
import functools

import jax
import jax.numpy as jnp
from jax import lax
from jax.experimental import pallas as pl
from jax.experimental.pallas import tpu as pltpu
from jax.sharding import PartitionSpec as P

QUERY_HEADS = 24
KEY_VALUE_HEADS = 8
HEAD_WIDTH = 64
FF = 512
EXPERTS = 16

EPSILON = 1e-06
MASKED = -1e30

GROUP = QUERY_HEADS // KEY_VALUE_HEADS
PAIRS = KEY_VALUE_HEADS // 2
PAIR_QUERY = 2 * GROUP * HEAD_WIDTH
PAIR_KEY = 2 * HEAD_WIDTH
PAIR_WIDTH = PAIR_QUERY + 2 * PAIR_KEY
BLOCK = 256
LANES = 128
VMEM = 60 * 2**20


def cost(flops, moved):
    return pl.CostEstimate(flops=int(flops), bytes_accessed=int(moved), transcendentals=0)

bf16 = jnp.bfloat16
f32 = jnp.float32


def dot(left, right):
    return jnp.dot(left, right, preferred_element_type=f32)


def contract_rows(left, right):
    return lax.dot_general(left, right, (((0,), (0,)), ((), ())), preferred_element_type=f32)


def times_transposed(left, right):
    return lax.dot_general(left, right, (((1,), (1,)), ((), ())), preferred_element_type=f32)


def norm_rows(value_rows):
    inverse = lax.rsqrt(jnp.mean(value_rows * value_rows, axis=-1, keepdims=True) + EPSILON)
    return (value_rows * inverse, inverse)


def norm_back(scaled, inverse, upstream):
    return inverse * (upstream - scaled * jnp.mean(upstream * scaled, axis=-1, keepdims=True))


def rotary_tables(length, width):
    half = HEAD_WIDTH // 2
    frequency = 10000.0 ** (-2.0 * jnp.arange(half, dtype=f32) / HEAD_WIDTH)
    angles = jnp.arange(length, dtype=f32)[:, None] * frequency[None, :]
    cosine, sine = jnp.cos(angles), jnp.sin(angles)
    heads = width // HEAD_WIDTH
    return (
        jnp.tile(jnp.concatenate([cosine, cosine], axis=1), (1, heads)),
        jnp.tile(jnp.concatenate([-sine, sine], axis=1), (1, heads)),
    )


def rotate(values, cosine, sine):
    width = values.shape[1]
    half = HEAD_WIDTH // 2
    lane = lax.broadcasted_iota(jnp.int32, values.shape, 1)
    swapped = jnp.where(
        lane % HEAD_WIDTH < half,
        pltpu.roll(values, width - half, 1),
        pltpu.roll(values, half, 1),
    )
    return values * cosine + swapped * sine


def causal_block():
    shape = (BLOCK, BLOCK)
    return lax.broadcasted_iota(jnp.int32, shape, 0) <= lax.broadcasted_iota(jnp.int32, shape, 1)


def stack_rows(parts):
    return parts[0] if len(parts) == 1 else jnp.concatenate(parts, axis=0)


def attend_forward_kernel(
    own_ref, other_ref, own_weight_ref, other_weight_ref, cosine_ref, sine_ref, mixed_ref, qkv_ref, lse_ref
):
    length = own_ref.shape[0]
    keep = causal_block()
    projected = dot(own_ref[...], own_weight_ref[...].reshape(-1, PAIR_WIDTH)) + dot(
        other_ref[...], other_weight_ref[...].reshape(-1, PAIR_WIDTH)
    )
    rotated = rotate(projected[:, : PAIR_QUERY + PAIR_KEY], cosine_ref[...], sine_ref[...])
    query = (rotated[:, :PAIR_QUERY] * HEAD_WIDTH**-0.5).astype(bf16)
    key = rotated[:, PAIR_QUERY:].astype(bf16)
    value = projected[:, PAIR_QUERY + PAIR_KEY :].astype(bf16)
    qkv_ref[:, :PAIR_QUERY] = query
    qkv_ref[:, PAIR_QUERY : PAIR_QUERY + PAIR_KEY] = key
    qkv_ref[:, PAIR_QUERY + PAIR_KEY :] = value
    value_columns = value.T
    outs = []
    for head in range(2 * GROUP):
        kv = (head // GROUP) * HEAD_WIDTH
        columns = []
        for block in range(length // BLOCK):
            start, stop = block * BLOCK, (block + 1) * BLOCK
            scores = times_transposed(
                key[:stop, kv : kv + HEAD_WIDTH],
                query[start:stop, head * HEAD_WIDTH : (head + 1) * HEAD_WIDTH],
            )
            parts = [scores[:start]] if block else []
            scores = stack_rows(parts + [jnp.where(keep, scores[start:], MASKED)])
            top = jnp.max(scores, axis=0, keepdims=True)
            powers = jnp.exp(scores - top)
            total = jnp.sum(powers, axis=0, keepdims=True)
            probability = (powers * (1.0 / total)).astype(bf16)
            columns.append(dot(value_columns[kv : kv + HEAD_WIDTH, :stop], probability))
            lse_ref[head, start:stop] = (top + jnp.log(total))[0]
        outs.append(jnp.concatenate(columns, axis=1))
    mixed_ref[...] = jnp.concatenate(outs, axis=0).T.astype(bf16)


def attend_forward(halves, weights, cosine, sine):
    length = halves[0].shape[0]
    return pl.pallas_call(
        attend_forward_kernel,
        out_shape=[
            jax.ShapeDtypeStruct((length, PAIR_QUERY), bf16),
            jax.ShapeDtypeStruct((length, PAIR_WIDTH), bf16),
            jax.ShapeDtypeStruct((8, length), f32),
        ],
        compiler_params=pltpu.CompilerParams(vmem_limit_bytes=VMEM),
        cost_estimate=cost(5e9, 5e6),
    )(*halves, *weights, cosine, sine)


def output_kernel(*refs):
    mixed, own, other = refs[:PAIRS], refs[PAIRS : 2 * PAIRS], refs[2 * PAIRS : 3 * PAIRS]
    for out_ref, weights in zip(refs[3 * PAIRS :], (own, other)):
        total = None
        for m in range(PAIRS):
            added = times_transposed(mixed[m][...], weights[m][...].reshape(-1, PAIR_QUERY))
            total = added if total is None else total + added
        out_ref[...] = total


def output_product(mixed, weights):
    length = mixed[0].shape[0]
    half = weights[0][0].shape[0] * weights[0][0].shape[1]
    return pl.pallas_call(
        output_kernel,
        out_shape=[jax.ShapeDtypeStruct((length, half), f32)] * 2,
        compiler_params=pltpu.CompilerParams(vmem_limit_bytes=VMEM),
        cost_estimate=cost(2.4e9, 1e7),
    )(*mixed, *[w[0] for w in weights], *[w[1] for w in weights])


def attend_backward_kernel(
    own_branch_ref,
    other_branch_ref,
    own_output_ref,
    other_output_ref,
    qkv_ref,
    lse_ref,
    mixed_ref,
    own_normed_ref,
    other_normed_ref,
    own_weight_ref,
    other_weight_ref,
    cosine_ref,
    sine_ref,
    own_total_ref,
    other_total_ref,
    own_term_ref,
    other_term_ref,
    own_grad_ref,
    other_grad_ref,
):
    length = own_branch_ref.shape[0]
    keep = causal_block()
    blocks = length // BLOCK
    mixed_grad = (
        dot(own_branch_ref[...], own_output_ref[...].reshape(-1, PAIR_QUERY))
        + dot(other_branch_ref[...], other_output_ref[...].reshape(-1, PAIR_QUERY))
    ).astype(bf16)
    query = qkv_ref[:, :PAIR_QUERY]
    key = qkv_ref[:, PAIR_QUERY : PAIR_QUERY + PAIR_KEY]
    value = qkv_ref[:, PAIR_QUERY + PAIR_KEY :]
    scaled_key = (key.astype(f32) * HEAD_WIDTH**-0.5).T.astype(bf16)
    query_grads, key_grads, value_grads = [], [], []
    for side in range(2):
        kv = side * HEAD_WIDTH
        key_part = key[:, kv : kv + HEAD_WIDTH]
        value_part = value[:, kv : kv + HEAD_WIDTH]
        key_grad, value_grad = [None] * blocks, [None] * blocks
        for head in range(side * GROUP, (side + 1) * GROUP):
            column = head * HEAD_WIDTH
            columns = []
            for block in range(blocks):
                start, stop = block * BLOCK, (block + 1) * BLOCK
                query_rows = query[start:stop, column : column + HEAD_WIDTH]
                upstream = mixed_grad[start:stop, column : column + HEAD_WIDTH]
                scores = times_transposed(key_part[:stop], query_rows)
                prob_grad = times_transposed(value_part[:stop], upstream)
                probability = jnp.exp(scores - lse_ref[head, start:stop][None, :])
                parts = [probability[:start]] if block else []
                probability = stack_rows(parts + [jnp.where(keep, probability[start:], 0.0)])
                shift = jnp.sum(probability * prob_grad, axis=0, keepdims=True)
                score_grad = (probability * (prob_grad - shift)).astype(bf16)
                value_add = dot(probability.astype(bf16), upstream)
                key_add = dot(score_grad, query_rows)
                for j in range(block + 1):
                    rows = slice(j * BLOCK, (j + 1) * BLOCK)
                    value_grad[j] = (
                        value_add[rows] if value_grad[j] is None else value_grad[j] + value_add[rows]
                    )
                    key_grad[j] = (
                        key_add[rows] if key_grad[j] is None else key_grad[j] + key_add[rows]
                    )
                columns.append(dot(scaled_key[kv : kv + HEAD_WIDTH, :stop], score_grad))
            query_grads.append(jnp.concatenate(columns, axis=1))
        key_grads.append(stack_rows(key_grad))
        value_grads.append(stack_rows(value_grad))
    turned = rotate(
        jnp.concatenate([jnp.concatenate(query_grads, axis=0).T] + key_grads, axis=1),
        cosine_ref[...],
        -sine_ref[...],
    )
    projected_grad = jnp.concatenate([turned] + value_grads, axis=1).astype(bf16)
    for normed_ref, branch_ref, term_ref in (
        (own_normed_ref, own_branch_ref, own_term_ref),
        (other_normed_ref, other_branch_ref, other_term_ref),
    ):
        term_ref[:, :PAIR_WIDTH] = contract_rows(normed_ref[...], projected_grad).astype(bf16)
        term_ref[:, PAIR_WIDTH:] = contract_rows(branch_ref[...], mixed_ref[...]).astype(bf16)
    for total_ref, weight_ref, grad_ref in (
        (own_total_ref, own_weight_ref, own_grad_ref),
        (other_total_ref, other_weight_ref, other_grad_ref),
    ):
        added = times_transposed(projected_grad, weight_ref[...].reshape(-1, PAIR_WIDTH))
        grad_ref[...] = total_ref[...] + added


def attend_backward(branch, output, saved, normed, weights, tables, totals):
    length, half = branch[0].shape
    term = jax.ShapeDtypeStruct((half, PAIR_WIDTH + PAIR_QUERY), bf16)
    return pl.pallas_call(
        attend_backward_kernel,
        out_shape=[term, term] + [jax.ShapeDtypeStruct((length, half), f32)] * 2,
        input_output_aliases={13: 2, 14: 3},
        compiler_params=pltpu.CompilerParams(vmem_limit_bytes=VMEM),
        cost_estimate=cost(9e9, 1.5e7),
    )(
        *branch,
        *output,
        *saved,
        *normed,
        *weights,
        *tables,
        *totals,
    )


def expert_kernel(
    first_ref,
    fed_ref,
    upstream_ref,
    chosen_ref,
    router_ref,
    weight_ref,
    row_ref,
    combined_ref,
    gate_grad_ref,
    pair_ref,
    gated_ref,
    gates_ref,
    row_total,
    combined_total,
):
    step, steps = pl.program_id(0), pl.num_programs(0)
    index = first_ref[0] + step
    lane = lax.broadcasted_iota(jnp.int32, gates_ref.shape, 1)

    @pl.when(step == 0)
    def _():
        logits = dot(fed_ref[...], router_ref[...])
        chosen = chosen_ref[0] > 0.0
        logits = jnp.where(chosen, logits, MASKED)
        powers = jnp.where(chosen, jnp.exp(logits - jnp.max(logits, axis=1, keepdims=True)), 0.0)
        gates_ref[...] = powers / jnp.sum(powers, axis=1, keepdims=True)
        gate_grad_ref[...] = jnp.zeros_like(gate_grad_ref)

    gate = jnp.sum(jnp.where(lane == index, gates_ref[...], 0.0), axis=1, keepdims=True)
    gate_grad = None
    width = FF // 2
    for start in range(0, FF, width):
        stop = start + width
        gate_part = dot(fed_ref[...], weight_ref[0, :, start:stop])
        up_part = dot(fed_ref[...], weight_ref[0, :, FF + start : FF + stop])
        raw_grad = dot(upstream_ref[0], weight_ref[0, :, 2 * FF + start : 2 * FF + stop])
        sigma = jax.nn.sigmoid(gate_part)
        activated = gate_part * sigma
        hidden = activated * up_part
        part = jnp.sum(hidden * raw_grad, axis=1, keepdims=True)
        gate_grad = part if gate_grad is None else gate_grad + part
        hidden_grad = gate * raw_grad
        slope = sigma * (1.0 + gate_part * (1.0 - sigma))
        pair_ref[0, :, start:stop] = (hidden_grad * up_part * slope).astype(bf16)
        pair_ref[0, :, FF + start : FF + stop] = (hidden_grad * activated).astype(bf16)
        gated_ref[0, :, start:stop] = (gate * hidden).astype(bf16)
    gate_grad_ref[...] += jnp.where(lane == index, gate_grad, 0.0)
    combined = times_transposed(gated_ref[0], weight_ref[0, :, 2 * FF :])
    row = times_transposed(pair_ref[0], weight_ref[0, :, : 2 * FF])

    @pl.when(step == 0)
    def _():
        combined_total[...] = combined
        row_total[...] = row

    @pl.when(step > 0)
    def _():
        combined_total[...] += combined
        row_total[...] += row

    @pl.when(step == steps - 1)
    def _():
        row_ref[...] = row_total[...].astype(bf16)
        combined_ref[...] = combined_total[...].astype(bf16)


def expert_slot(places, fed, upstream, chosen, router, weights):
    length, features = fed.shape
    count = weights.shape[0]
    full = lambda *shape: pl.BlockSpec(shape, lambda e, at: (0,) * len(shape))
    each = lambda *shape: pl.BlockSpec((1,) + shape, lambda e, at: (e,) + (0,) * len(shape))
    there = lambda *shape: pl.BlockSpec((1,) + shape, lambda e, at: (at[1],) + (0,) * len(shape))
    return pl.pallas_call(
        expert_kernel,
        grid_spec=pltpu.PrefetchScalarGridSpec(
            num_scalar_prefetch=1,
            grid=(count,),
            in_specs=[
                full(length, features),
                there(length, features),
                there(length, LANES),
                full(features, LANES),
                each(features, 3 * FF),
            ],
            out_specs=[
                full(length, features),
                full(length, features),
                full(length, LANES),
                each(length, 2 * FF),
                each(length, FF),
            ],
            scratch_shapes=[
                pltpu.VMEM((length, LANES), f32),
                pltpu.VMEM((length, features), f32),
                pltpu.VMEM((length, features), f32),
            ],
        ),
        out_shape=[
            jax.ShapeDtypeStruct((length, features), bf16),
            jax.ShapeDtypeStruct((length, features), bf16),
            jax.ShapeDtypeStruct((length, LANES), f32),
            jax.ShapeDtypeStruct((count, length, 2 * FF), bf16),
            jax.ShapeDtypeStruct((count, length, FF), bf16),
        ],
        compiler_params=pltpu.CompilerParams(vmem_limit_bytes=VMEM),
        cost_estimate=cost(12 * count * length * features * FF, 3.2e7),
    )(places, fed, upstream, chosen, router, weights)


def expert_grad_kernel(places_ref, *refs):
    slots = (len(refs) - 1) // 4
    fed, upstream, pair, gated = (refs[i * slots : (i + 1) * slots] for i in range(4))
    out_ref = refs[-1]
    inner = outer = None
    for k in range(slots):
        add_inner = contract_rows(fed[k][...], pair[k][0])
        add_outer = contract_rows(upstream[k][0], gated[k][0])
        inner = add_inner if inner is None else inner + add_inner
        outer = add_outer if outer is None else outer + add_outer
    out_ref[0, :, : 2 * FF] = inner.astype(out_ref.dtype)
    out_ref[0, :, 2 * FF :] = outer.astype(out_ref.dtype)


def expert_grads(places, fed, upstream, pairs, gated):
    length, features = fed[0].shape
    slots, count = len(pairs), pairs[0].shape[0]
    rows = features // 2
    column = pl.BlockSpec((length, rows), lambda e, i, at: (0, i))
    there = lambda k: pl.BlockSpec((1, length, rows), lambda e, i, at: (at[k], 0, i))
    each = lambda width: pl.BlockSpec((1, length, width), lambda e, i, at: (e, 0, 0))
    return pl.pallas_call(
        expert_grad_kernel,
        grid_spec=pltpu.PrefetchScalarGridSpec(
            num_scalar_prefetch=1,
            grid=(count, features // rows),
            in_specs=[column] * slots
            + [there(k) for k in range(slots)]
            + [each(2 * FF)] * slots
            + [each(FF)] * slots,
            out_specs=pl.BlockSpec((1, rows, 3 * FF), lambda e, i, at: (e, i, 0)),
        ),
        out_shape=jax.ShapeDtypeStruct((count, features, 3 * FF), bf16),
        compiler_params=pltpu.CompilerParams(vmem_limit_bytes=VMEM),
        cost_estimate=cost(6 * slots * count * length * features * FF, 8e7),
    )(places, *fed, *[upstream] * slots, *pairs, *gated)


def exchange(value, k):
    return lax.ppermute(value, "shard", [(i, i ^ k) for i in range(4)])


def inside(place):
    return (place == 1) | (place == 2)


def sources(place, count):
    if count != 4:
        return [place ^ k for k in range(count)]
    middle = inside(place)
    order = ((1, 3), (2, 1), (3, 2))
    return [place] + [place ^ jnp.where(middle, mid, out) for out, mid in order]


def after(value, *earlier):
    return lax.optimization_barrier((value, earlier))[0]


def line_gather(rows, place, count):
    if count != 4:
        everything = lax.all_gather(rows, "shard", axis=0)
        for source in sources(place, count):
            yield pick(everything, source)
            yield
        return
    middle = inside(place)
    near = exchange(rows, 1)
    across = lax.ppermute(rows, "shard", [(1, 2), (2, 1)])
    made = yield rows
    yield
    near_on, across_on = after((near, across), made)
    second_inside = lax.ppermute(near_on, "shard", [(1, 2), (2, 1)])
    second_outside = lax.ppermute(across_on, "shard", [(1, 0), (2, 3)])
    made = yield jnp.where(middle, across, near)
    yield
    third_outside = lax.ppermute(after(second_inside, made), "shard", [(1, 0), (2, 3)])
    yield jnp.where(middle, near, second_outside)
    yield
    yield jnp.where(middle, second_inside, third_outside)
    yield


def line_scatter(parts, place, count):
    if count != 4:
        stacked = jnp.stack(parts)
        ordered = jnp.stack([pick(stacked, place ^ d) for d in range(count)])
        return lax.psum_scatter(ordered, "shard", scatter_dimension=0, tiled=False), []
    return parts[0], [come for k in range(1, 4) for come in line_send(parts[k], k)]


def line_send(part, k):
    ways = {
        1: ([(0, 1), (3, 2)], [(1, 2), (2, 1)]),
        2: ([(0, 2), (3, 1)], [(1, 0), (2, 3)]),
        3: ([(0, 3), (3, 0)], [(1, 3), (2, 0)]),
    }
    return [lax.ppermute(part, "shard", way) for way in ways[k]]


def total_of(kept, arrived):
    total = kept.astype(f32)
    for part in arrived:
        total = total + part.astype(f32)
    return total


def hop(value, bit):
    return lax.ppermute(value, "rep", [(i, i ^ bit) for i in range(8)])


def pick(stacked, index, axis=0):
    return lax.dynamic_index_in_dim(stacked, index, axis, False)


def gather_near(local, core, spot):
    mine = local(spot, core)
    return jnp.stack([exchange(mine, k) for k in range(1, 4)])


def send_pairs(near):
    return [hop(near, 2 * m) for m in range(1, 4)]


def join_pair(local, part, m, core, spot):
    own = jnp.concatenate([local(spot ^ m, core)[None], part])
    return own, hop(own, 1)


def halve_columns(rows, places, base, core):
    length, features = rows.shape
    parts = rows.reshape(length, places, 2, -1).transpose(2, 1, 0, 3)
    parts = jnp.stack([pick(parts, base ^ k, 1) for k in range(places)], axis=1)
    return [
        pick(parts, side).transpose(1, 0, 2).reshape(length, features // 2)
        for side in (core, 1 - core)
    ]


def join_columns(halves, places, base, core):
    length, width = halves[0].shape
    parts = jnp.stack(halves).reshape(2, length, places, -1).transpose(2, 0, 1, 3)
    parts = jnp.stack([pick(parts, base ^ k) for k in range(places)])
    parts = jnp.stack([pick(parts, core, 1), pick(parts, 1 - core, 1)], axis=1)
    return parts.transpose(2, 0, 1, 3).reshape(length, 2 * width)


def join_chip(term, special):
    kept, given = term
    return (kept.astype(f32) + hop(given, 1).astype(f32)).astype(bf16) if special else kept


def reduce_plane(terms, core, spot):
    kept, given = pick(terms, core, 2), pick(terms, 1 - core, 2)
    chip = (kept.astype(f32) + hop(given, 1).astype(f32)).astype(terms.dtype)
    total = pick(chip, spot).astype(f32)
    for m in range(1, 4):
        total = total + hop(pick(chip, spot ^ m), 2 * m).astype(f32)
    return total.astype(terms.dtype)


def finish_pairs(plane, core, spot):
    piece = plane[0].astype(f32)
    for k in range(1, 4):
        piece = piece + exchange(plane[k], k).astype(f32)
    piece = piece.astype(plane.dtype)
    mine = jnp.stack([piece] + [hop(piece, 2 * m) for m in range(1, 4)])
    other = hop(mine, 1)
    both = jnp.stack(
        [jnp.where(core == 0, mine, other), jnp.where(core == 0, other, mine)], axis=1
    )
    return jnp.stack([pick(both, spot ^ p) for p in range(4)])


def reduce_terms(terms, place, core, spot, special):
    if not special:
        part = lax.psum_scatter(terms, "shard", scatter_dimension=1, tiled=False)
        return lax.psum(part, "rep")
    plane = reduce_plane(terms, core, spot)
    plane = jnp.stack([pick(plane, place ^ k) for k in range(4)])
    return finish_pairs(plane, core, spot)


def body(
    inputs,
    query_key_value_weight,
    output_weight,
    attention_gain,
    feed_gain,
    router_weight,
    expert_weight,
    routes,
    cotangent,
    *,
    places,
    ranks,
):
    length, features = inputs.shape
    own = query_key_value_weight.shape[0]
    local = expert_weight.shape[0]
    query_width = QUERY_HEADS * HEAD_WIDTH
    key_width = KEY_VALUE_HEADS * HEAD_WIDTH
    place, rank = lax.axis_index("shard"), lax.axis_index("rep")

    special = places == 4 and ranks == 8
    half = own // 2
    base, core, spot = (place, rank % 2, rank // 2) if special else (0, 0, 0)

    projection = query_key_value_weight

    def projection_share(pair, side):
        rows = lax.dynamic_slice_in_dim(projection, side * half, half, 0)
        return jnp.concatenate(
            [
                lax.dynamic_slice_in_dim(rows, pair * PAIR_QUERY, PAIR_QUERY, 1),
                lax.dynamic_slice_in_dim(rows, query_width + pair * PAIR_KEY, PAIR_KEY, 1),
                lax.dynamic_slice_in_dim(
                    rows, query_width + key_width + pair * PAIR_KEY, PAIR_KEY, 1
                ),
            ],
            axis=1,
        )

    def output_share(weight, pair, side):
        return lax.dynamic_slice(
            weight, (side * half, pair * PAIR_QUERY), (half, PAIR_QUERY)
        )

    chosen_own = jnp.sum(
        (routes[:, :, None] == jnp.arange(EXPERTS, dtype=jnp.int32)).astype(f32), axis=1
    )
    small = jnp.concatenate(
        [feed_gain.reshape(-1), router_weight.reshape(-1), chosen_own.astype(bf16).reshape(-1)]
    )
    if special:
        projection_near = gather_near(projection_share, core, spot)
        projection_sent = send_pairs(projection_near)
        held, _ = lax.optimization_barrier((output_weight, projection_near))
        output_near = gather_near(functools.partial(output_share, held), core, spot)
        output_sent = send_pairs(lax.optimization_barrier((output_near, projection_sent))[0])

        def attend_weights(m, outs):
            part = after(projection_sent[m - 1], outs[0]) if m else projection_near
            return join_pair(projection_share, part, m, core, spot)

        output_weights = [
            join_pair(functools.partial(output_share, output_weight), part, m, core, spot)
            for m, part in enumerate([output_near] + output_sent)
        ]
        cotangent_sent, _ = lax.optimization_barrier((cotangent, projection_near))
        gains = jnp.stack([attention_gain] + [exchange(attention_gain, k) for k in range(1, 4)])
        gains = jnp.stack([pick(gains, place ^ k) for k in range(4)])
        small_slots = jnp.stack([small] + [exchange(small, k) for k in range(1, 4)])
        small_all = jnp.stack([pick(small_slots, place ^ k) for k in range(4)])
    else:
        whole = lax.all_gather(projection, "shard", axis=0)
        whole_output = lax.all_gather(output_weight, "shard", axis=0)
        attend_weights, output_weights = [], []
        for p in range(PAIRS):
            columns = jnp.concatenate(
                [
                    whole[:, :, p * PAIR_QUERY : (p + 1) * PAIR_QUERY],
                    whole[:, :, query_width + p * PAIR_KEY : query_width + (p + 1) * PAIR_KEY],
                    whole[:, :, query_width + key_width + p * PAIR_KEY :][:, :, :PAIR_KEY],
                ],
                axis=2,
            )
            attend_weights.append((columns[:, :half], columns[:, half:]))
            columns = whole_output[:, :, p * PAIR_QUERY : (p + 1) * PAIR_QUERY]
            output_weights.append((columns[:, :half], columns[:, half:]))
        gains = lax.all_gather(attention_gain, "shard", axis=0)
        small_all = lax.all_gather(small, "shard", axis=0)
        cotangent_sent = cotangent

    upstream_all = lax.all_gather(cotangent_sent, "shard", axis=0)

    cosine, sine = rotary_tables(length, PAIR_QUERY + PAIR_KEY)
    residual = inputs.astype(f32)
    scaled_in, inverse_in = norm_rows(residual)
    attention_scale = gains.reshape(features).astype(f32)
    normed = (scaled_in * attention_scale).astype(bf16)
    pair_outs, joined = [], []
    normed_halves = halve_columns(normed, places, base, core)
    for m in range(PAIRS):
        weights = attend_weights(m, pair_outs) if special else attend_weights[m]
        pair_outs.append(attend_forward(normed_halves, weights, cosine, sine))
        joined.append(weights)
    attend_weights = joined
    branch = output_product([out[0] for out in pair_outs], output_weights)
    middle = residual + join_columns(branch, places, base, core)
    scaled_mid, inverse_mid = norm_rows(middle)
    feed_scale = small_all[:, :own].reshape(features).astype(f32)
    router_full = small_all[:, own : (1 + EXPERTS) * own].reshape(features, EXPERTS)
    chosen_all = small_all[:, (1 + EXPERTS) * own :].reshape(places, length, EXPERTS).astype(f32)
    fed = (scaled_mid * feed_scale).astype(bf16)

    router_wide = jnp.pad(router_full, ((0, 0), (0, LANES - EXPERTS)))
    chosen_wide = jnp.pad(chosen_all, ((0, 0), (0, 0), (0, LANES - EXPERTS)))
    rows, combined, gate_grads, pair_grads, gated = [], [], [], [], []
    order = sources(place, places)
    fed_slots, arriving = [], line_gather(fed, place, places)
    rows_come = []
    for k, source in enumerate(order):
        fed_k = next(arriving)
        if special and k == 3:
            fed_k = after(fed_k, rows_come)
        fed_slots.append(fed_k)
        at = jnp.stack([place * local, source]).astype(jnp.int32)
        slot = expert_slot(
            at, fed_slots[k], upstream_all, chosen_wide, router_wide, expert_weight
        )
        for held, value in zip((rows, combined, gate_grads, pair_grads, gated), slot):
            held.append(value)
        arriving.send(slot[0])
        if special and k:
            rows_come += line_send(slot[0], k)
    expert_term = expert_grads(
        jnp.stack(order).astype(jnp.int32),
        after(fed_slots, rows_come[2:4]),
        upstream_all,
        pair_grads,
        gated,
    )
    expert_total = lax.psum(expert_term, "rep").astype(f32)

    row_sum = total_of(rows[0], rows_come) if special else total_of(*line_scatter(rows, place, places))
    row_sum = after(row_sum, expert_term)
    gate_grad = total_of(
        *line_scatter([g[:, :EXPERTS].T for g in gate_grads], place, places)
    ).T
    upstream = cotangent.astype(f32)
    logits = dot(fed, router_full)
    gates = jax.nn.softmax(jnp.where(chosen_own > 0.0, logits, -jnp.inf), axis=-1)
    logit_grad = (
        gates * (gate_grad - jnp.sum(gates * gate_grad, axis=-1, keepdims=True))
    ).astype(bf16)
    router_term = contract_rows(fed, logit_grad)
    fed_grad = times_transposed(logit_grad, router_full) + row_sum
    feed_term = jnp.sum(fed_grad * scaled_mid, axis=0)
    middle_grad = upstream + norm_back(scaled_mid, inverse_mid, fed_grad * feed_scale)
    branch_grad = middle_grad.astype(bf16)

    branch_halves = halve_columns(branch_grad, places, base, core)
    combined_kept, combined_come = line_scatter(after(combined, row_sum), place, places)
    totals = [jnp.zeros((length, features // 2), f32)] * 2
    terms, chips = [None] * PAIRS, [None] * PAIRS
    waits = {1: combined_come[:2], 2: [], 0: combined_come[2:4]}
    sent = []
    for m in (3, 1, 2, 0):
        if m == 2:
            chips[3] = join_chip(terms[3], special)
            waits[2] = [chips[3]]
        if m == 0:
            chips[1] = join_chip(terms[1], special)
            waits[0] = waits[0] + [chips[1]]
        own_term, other_term, *totals = attend_backward(
            after(branch_halves, *waits.get(m, [])),
            output_weights[m],
            (pair_outs[m][1], pair_outs[m][2], pair_outs[m][0]),
            normed_halves,
            attend_weights[m],
            (cosine, sine),
            totals,
        )
        terms[m] = (own_term, other_term)
    if special:
        chips[2], chips[0] = join_chip(terms[2], special), join_chip(terms[0], special)
        plane = chips[0].astype(f32)
        for m in (3, 1, 2):
            plane = plane + hop(chips[m], 2 * m).astype(f32)
        plane = plane.astype(bf16).reshape(places, half, -1)
        weight_sums = finish_pairs(after(plane, *combined_come[4:]), core, spot)
    else:
        stacked = jnp.stack([jnp.stack(term) for term in terms])
        stacked = stacked.reshape(PAIRS, 2, places, half, -1).transpose(0, 2, 1, 3, 4)
        weight_sums = reduce_terms(stacked, place, core, spot, special)
    weight_sums = weight_sums.reshape(PAIRS, own, -1).transpose(1, 0, 2).astype(f32)
    attend_total = jnp.concatenate(
        [
            weight_sums[:, :, :PAIR_QUERY].reshape(own, query_width),
            weight_sums[:, :, PAIR_QUERY : PAIR_QUERY + PAIR_KEY].reshape(own, key_width),
            weight_sums[:, :, PAIR_QUERY + PAIR_KEY : PAIR_WIDTH].reshape(own, key_width),
        ],
        axis=1,
    )
    output_total = weight_sums[:, :, PAIR_WIDTH:].reshape(own, query_width)

    normed_grad = join_columns(totals, places, base, core)
    attention_term = jnp.sum(normed_grad * scaled_in, axis=0)
    input_grad = (
        middle_grad + norm_back(scaled_in, inverse_in, normed_grad * attention_scale)
    ).astype(bf16)

    small_terms = jnp.concatenate([attention_term[None], feed_term[None], router_term.T], axis=0)
    count = (EXPERTS + 2) * own
    tiles = -(-count // (2 * PAIRS * 8 * LANES)) * 8
    small_terms = small_terms.reshape(EXPERTS + 2, places, own).transpose(1, 0, 2)
    small_terms = jnp.pad(
        small_terms.reshape(places, count), ((0, 0), (0, 2 * PAIRS * tiles * LANES - count))
    )
    small_terms = small_terms.reshape(places, PAIRS, 2, tiles, LANES).transpose(1, 0, 2, 3, 4)
    small_sums = reduce_terms(small_terms, place, core, spot, special)
    small_sums = small_sums.reshape(-1)[:count].reshape(EXPERTS + 2, own)

    combined_sum = total_of(combined_kept, combined_come)
    activations = (middle + combined_sum).astype(bf16)
    return (
        activations,
        input_grad,
        attend_total,
        output_total,
        small_sums[0],
        small_sums[1],
        small_sums[2:].T,
        expert_total,
    )


def solution(mesh):
    in_specs = (
        P(("rep", "shard"), None),
        P("shard", None),
        P("shard", None),
        P("shard"),
        P("shard"),
        P("shard", None),
        P("shard", None, None),
        P(("rep", "shard"), None),
        P(("rep", "shard"), None),
    )
    out_specs = (
        P(("rep", "shard"), None),
        P(("rep", "shard"), None),
        P("shard", None),
        P("shard", None),
        P("shard"),
        P("shard"),
        P("shard", None),
        P("shard", None, None),
    )
    run = functools.partial(body, places=mesh.shape["shard"], ranks=mesh.shape["rep"])
    return jax.shard_map(run, mesh=mesh, in_specs=in_specs, out_specs=out_specs, check_vma=False)
```

time: 3720 us -> 908 us (0.24)
  waiting for transfers between devices: 2940 us -> 269 us
  matrix products: 300 us -> 5.39 us
  Pallas kernels: 0 us -> 277 us
  local copies, waits for them, and re-layouts: 254 us -> 95.3 us
  starting transfers between devices: 0.73 us -> 127 us
  blocking collectives: 78.6 us -> 0 us
    all_gather x6 -> x1, waiting for transfers between devices: 1390 us -> 8.91 us  [body(): upstream_all = lax.all_gather(cotangent_sent, 'shard', axis=0)]
    reduce_scatter x3 -> x0, waiting for transfers between devices: 1250 us -> none  [the longest x1 1230 us: body(): lax.psum_scatter(expert_terms(dispatched, produced_grad, pair_grad, hidde...]
    unnamed x17 -> x2, waiting for transfers between devices: 297 us -> 0.03 us
    pallas_call x0 -> x14, Pallas kernels: none -> 277 us  [the longest x4 122 us: expert_slot(): pl.pallas_call(expert_kernel, grid_spec=pltpu.PrefetchScalarGridSpec(num_...]
    dot_general x14 -> x1, matrix products: 253 us -> 2.06 us  [dot(): return jnp.dot(left, right, preferred_element_type=f32)]
    ppermute x0 -> x74, waiting for transfers between devices: none -> 212 us  [the longest x33 118 us: hop(): return lax.ppermute(value, 'rep', [(i, i ^ bit) for i in range(8)])]
    ppermute x0 -> x74, starting transfers between devices: none -> 126 us  [the longest x18 52.4 us: line_send(): return [lax.ppermute(part, 'shard', way) for way in ways[k]]]
    gather x4 -> x0, local copies, waits for them, and re-layouts: 115 us -> none  [the longest x1 32.9 us: body(): returned.reshape(EXPERTS * CAP, features)[flat_slot].astype(jnp.float32)]
  transfers between devices with their start and end apart: 13 -> 76, of which waited for: 10 -> 21; matrix products, arithmetic and copies ran while one was open for 11% -> 20% of each run, Pallas kernels for 0% -> 31%
where the time goes in v1:
time: 908 us; the launch traced here: 900 us
  Pallas kernels  277 us (31%)
  waiting for transfers between devices  269 us (30%)
  starting transfers between devices  127 us (14%)
  other arithmetic  111 us (12%)
  local copies, waits for them, and re-layouts  95.3 us (10%)
  between operations  15.6 us (2%)
    pallas_call x4, Pallas kernels, expert_slot(): pl.pallas_call(expert_kernel, grid_spec=pltpu.PrefetchScalarGridSpec(num_...  122 us
    ppermute x33, waiting for transfers between devices, hop(): return lax.ppermute(value, 'rep', [(i, i ^ bit) for i in range(8)])  118 us
    pallas_call x4, Pallas kernels, attend_backward(): pl.pallas_call(attend_backward_kernel, out_shape=[term, term] + [jax.Shap...  62.8 us
    ppermute x18, starting transfers between devices, line_send(): return [lax.ppermute(part, 'shard', way) for way in ways[k]]  52.4 us
    pallas_call x1, Pallas kernels, expert_grads(): pl.pallas_call(expert_grad_kernel, grid_spec=pltpu.PrefetchScalarGridSpec...  48.5 us
    psum x1, waiting for transfers between devices, body(): expert_total = lax.psum(expert_term, 'rep').astype(f32)  47.7 us
    ppermute x18, waiting for transfers between devices, line_send(): return [lax.ppermute(part, 'shard', way) for way in ways[k]]  41.5 us
    ppermute x19, starting transfers between devices, exchange(): return lax.ppermute(value, 'shard', [(i, i ^ k) for i in range(4)])  39.8 us
  transfers between devices with their start and end apart: 76, of which 21 were waited for; matrix products, arithmetic and copies ran while one was open for 20% of the time, Pallas kernels for 31%

profile of v1, /device:TPU:0, one launch (start us, length us, event | category | flops | bytes accessed | tf_op | source)
XLA Modules:
  0.0 900.0 jit_solution(9806153272200924245)
XLA Ops:
  7.2 5.1 collective-permute-start.2
  17.6 3.7 collective-permute-start.5
  47.9 4.7 collective-permute-done.3
  65.2 11.7 %collective-permute-done.7 = bf16[3,192,640]{2,1,0:T(8,128)(2,1)S(1)} collective-permute-done((bf16[3,192,640]{2,1,0:T(8,128)(2,1)}, bf16[3,192,640]{2,1,0:T(8,128)(2,1)S(1)}, u32[]{:S(2)}, u32[]{:S(2)}) %collective-permute-start.7) | collective-permute-done | bytes 737312 | tf_op jit(solution)/shard_map/ppermute | solution.py:486
  78.9 9.0 %shard_map.152 = (bf16[512,384]{1,0:T(8,128)(2,1)}, bf16[512,640]{1,0:T(8,128)(2,1)}, f32[8,512]{1,0:T(8,128)}) custom-call(bf16[512,768]{1,0:T(8,128)(2,1)} %copy.211.own_ref.own_normed_ref, bf16[512,768]{1,0:T(8,128)(2,1)} %copy.212.other_ref.other_normed_ref, bf16[4,192,640]{2,1,0:T(8,128)(2,1)} %copy-done.15, ...), custom_call_target="tpu_custom_call" | custom-call | flops 5000000000 | bytes 5000000 | tf_op jit(solution)/shard_map/pallas_call | solution.py:130
  89.4 3.9 collective-permute-done.14
  105.0 4.8 collective-permute-done.16
  111.7 6.6 collective-permute-done.17
  120.1 9.2 %shard_map.153 = (bf16[512,384]{1,0:T(8,128)(2,1)}, bf16[512,640]{1,0:T(8,128)(2,1)}, f32[8,512]{1,0:T(8,128)}) custom-call(bf16[512,768]{1,0:T(8,128)(2,1)} %copy.211.own_ref.own_normed_ref, bf16[512,768]{1,0:T(8,128)(2,1)} %copy.212.other_ref.other_normed_ref, bf16[4,192,640]{2,1,0:T(8,128)(2,1)} %copy-done.17, ...), custom_call_target="tpu_custom_call" | custom-call | flops 5000000000 | bytes 5000000 | tf_op jit(solution)/shard_map/pallas_call | solution.py:130
  129.8 9.1 %shard_map.154 = (bf16[512,384]{1,0:T(8,128)(2,1)}, bf16[512,640]{1,0:T(8,128)(2,1)}, f32[8,512]{1,0:T(8,128)}) custom-call(bf16[512,768]{1,0:T(8,128)(2,1)} %copy.211.own_ref.own_normed_ref, bf16[512,768]{1,0:T(8,128)(2,1)} %copy.212.other_ref.other_normed_ref, bf16[4,192,640]{2,1,0:T(8,128)(2,1)} %copy-done.16, ...), custom_call_target="tpu_custom_call" | custom-call | flops 5000000000 | bytes 5000000 | tf_op jit(solution)/shard_map/pallas_call | solution.py:130
  138.9 9.0 %shard_map.155 = (bf16[512,384]{1,0:T(8,128)(2,1)}, bf16[512,640]{1,0:T(8,128)(2,1)}, f32[8,512]{1,0:T(8,128)}) custom-call(bf16[512,768]{1,0:T(8,128)(2,1)} %copy.211.own_ref.own_normed_ref, bf16[512,768]{1,0:T(8,128)(2,1)} %copy.212.other_ref.other_normed_ref, bf16[4,192,640]{2,1,0:T(8,128)(2,1)} %copy-done.18, ...), custom_call_target="tpu_custom_call" | custom-call | flops 5000000000 | bytes 5000000 | tf_op jit(solution)/shard_map/pallas_call | solution.py:130
  148.7 7.8 shard_map.156
  164.1 2.8 multiply_reduce_fusion.2
  168.4 3.3 collective-permute-start.27
  173.5 8.9 all-gather.3.cloned.1.call-done
  182.4 30.6 %shard_map.157 = (bf16[512,1536]{1,0:T(8,128)(2,1)}, bf16[512,1536]{1,0:T(8,128)(2,1)}, f32[512,128]{1,0:T(8,128)}, bf16[4,512,1024]{2,1,0:T(8,128)(2,1)}, bf16[4,512,512]{2,1,0:T(8,128)(2,1)}) custom-call(s32[2]{0:T(128)} %get-tuple-element.283.first_ref, bf16[512,1536]{1,0:T(8,128)(2,1)} %multiply_convert_fusion.fed_ref.refs_0_, ...), custom_call_target="tpu_custom_call" | custom-call | flops 19327352832 | bytes 32000000 | tf_op jit(solution)/shard_map/pallas_call | solution.py:342
  217.2 34.4 %collective-permute-done.28 = bf16[512,1536]{1,0:T(8,128)(2,1)} collective-permute-done((bf16[512,1536]{1,0:T(8,128)(2,1)}, bf16[512,1536]{1,0:T(8,128)(2,1)}, u32[]{:S(2)}, u32[]{:S(2)}) %collective-permute-start.28) | collective-permute-done | bytes 1572896 | tf_op jit(solution)/shard_map/ppermute | solution.py:451
  251.6 3.8 broadcast_select_fusion.1
  255.4 30.4 %shard_map.158 = (bf16[512,1536]{1,0:T(8,128)(2,1)}, bf16[512,1536]{1,0:T(8,128)(2,1)}, f32[512,128]{1,0:T(8,128)}, bf16[4,512,1024]{2,1,0:T(8,128)(2,1)}, bf16[4,512,512]{2,1,0:T(8,128)(2,1)}) custom-call(s32[2]{0:T(128)} %get-tuple-element.285.first_ref, bf16[512,1536]{1,0:T(8,128)(2,1)} %get-tuple-element.113.fed_ref.refs_1_, ...), custom_call_target="tpu_custom_call" | custom-call | flops 19327352832 | bytes 32000000 | tf_op jit(solution)/shard_map/pallas_call | solution.py:342
  285.8 2.6 collective-permute-start.31
  292.0 30.5 %shard_map.159 = (bf16[512,1536]{1,0:T(8,128)(2,1)}, bf16[512,1536]{1,0:T(8,128)(2,1)}, f32[512,128]{1,0:T(8,128)}, bf16[4,512,1024]{2,1,0:T(8,128)(2,1)}, bf16[4,512,512]{2,1,0:T(8,128)(2,1)}) custom-call(s32[2]{0:T(128)} %get-tuple-element.286.first_ref, bf16[512,1536]{1,0:T(8,128)(2,1)} %get-tuple-element.114.fed_ref.refs_2_, ...), custom_call_target="tpu_custom_call" | custom-call | flops 19327352832 | bytes 32000000 | tf_op jit(solution)/shard_map/pallas_call | solution.py:342
  322.5 8.5 collective-permute-start.33
  337.3 2.7 broadcast_select_fusion.fed_ref.refs_3_
  340.0 5.8 collective-permute-start.45
  347.2 17.8 %collective-permute-done.33 = bf16[512,1536]{1,0:T(8,128)(2,1)} collective-permute-done((bf16[512,1536]{1,0:T(8,128)(2,1)}, bf16[512,1536]{1,0:T(8,128)(2,1)}, u32[]{:S(2)}, u32[]{:S(2)}) %collective-permute-start.33) | collective-permute-done | bytes 1572896 | tf_op jit(solution)/shard_map/ppermute | solution.py:475
  365.0 4.7 collective-permute-start.43
  370.5 30.4 %shard_map.160 = (bf16[512,1536]{1,0:T(8,128)(2,1)}, bf16[512,1536]{1,0:T(8,128)(2,1)}, f32[512,128]{1,0:T(8,128)}, bf16[4,512,1024]{2,1,0:T(8,128)(2,1)}, bf16[4,512,512]{2,1,0:T(8,128)(2,1)}) custom-call(s32[2]{0:T(128)} %get-tuple-element.284.first_ref, bf16[512,1536]{1,0:T(8,128)(2,1)} %broadcast_select_fusion.fed_ref.refs_3_, ...), custom_call_target="tpu_custom_call" | custom-call | flops 19327352832 | bytes 32000000 | tf_op jit(solution)/shard_map/pallas_call | solution.py:342
  403.9 4.1 collective-permute-start.35
  409.3 3.8 collective-permute-start.47
  413.1 48.5 %shard_map.161 = bf16[4,1536,1536]{2,1,0:T(8,128)(2,1)} custom-call(s32[4]{0:T(128)} %pad_add_fusion.4.places_ref, bf16[512,1536]{1,0:T(8,128)(2,1)} %multiply_convert_fusion.fed_ref.refs_0_, bf16[512,1536]{1,0:T(8,128)(2,1)} %get-tuple-element.113.fed_ref.refs_1_, bf16[512,1536]{1,0:T(8,128)(2,1)} %get-tuple-element.114.fed_ref.refs_2_, ...), custom_call_target="tpu_custom_call" | custom-call | flops 38654705664 | bytes 80000000 | tf_op jit(solution)/shard_map/pallas_call | solution.py:400
  461.7 18.6 %collective-permute-done.48 = f32[16,512]{0,1:T(8,128)} collective-permute-done((f32[16,512]{0,1:T(8,128)}, f32[16,512]{0,1:T(8,128)}, u32[]{:S(2)}, u32[]{:S(2)}) %collective-permute-start.48) | collective-permute-done | bytes 32800 | tf_op jit(solution)/shard_map/ppermute | solution.py:475
  482.0 5.2 convert_add_fusion.1
  487.2 2.7 collective-permute-start.37
  496.8 3.0 copy.234
  510.0 15.5 %shard_map.162 = (bf16[768,1024]{1,0:T(8,128)(2,1)}, bf16[768,1024]{1,0:T(8,128)(2,1)}, f32[512,768]{1,0:T(8,128)}, f32[512,768]{1,0:T(8,128)}) custom-call(bf16[512,768]{1,0:T(8,128)(2,1)} %copy.235.own_branch_ref, bf16[512,768]{1,0:T(8,128)(2,1)} %copy.236.other_branch_ref, ...), custom_call_target="tpu_custom_call", output_to_operand_aliasing={{2}: (13, {}), {3}: (14, {})} | custom-call | flops 8999999488 | bytes 15000000 | tf_op jit(solution)/shard_map/pallas_call | solution.py:252
  530.1 15.7 %shard_map.163 = (bf16[768,1024]{1,0:T(8,128)(2,1)}, bf16[768,1024]{1,0:T(8,128)(2,1)}, f32[512,768]{1,0:T(8,128)}, f32[512,768]{1,0:T(8,128)}) custom-call(bf16[512,768]{1,0:T(8,128)(2,1)} %copy.241.own_branch_ref, bf16[512,768]{1,0:T(8,128)(2,1)} %copy.242.other_branch_ref, ...), custom_call_target="tpu_custom_call", output_to_operand_aliasing={{2}: (13, {}), {3}: (14, {})} | custom-call | flops 8999999488 | bytes 15000000 | tf_op jit(solution)/shard_map/pallas_call | solution.py:252
  546.3 2.9 collective-permute-start.39
  552.6 3.8 add_convert_fusion.3
  556.4 2.6 collective-permute-start.52
  559.0 2.4 copy.247.own_branch_ref
  563.7 15.5 %shard_map.164 = (bf16[768,1024]{1,0:T(8,128)(2,1)}, bf16[768,1024]{1,0:T(8,128)(2,1)}, f32[512,768]{1,0:T(8,128)}, f32[512,768]{1,0:T(8,128)}) custom-call(bf16[512,768]{1,0:T(8,128)(2,1)} %copy.247.own_branch_ref, bf16[512,768]{1,0:T(8,128)(2,1)} %copy.248.other_branch_ref, ...), custom_call_target="tpu_custom_call", output_to_operand_aliasing={{2}: (13, {}), {3}: (14, {})} | custom-call | flops 8999999488 | bytes 15000000 | tf_op jit(solution)/shard_map/pallas_call | solution.py:252
  579.2 3.7 add_convert_fusion.4
  583.6 3.8 collective-permute-done.40
  592.0 16.1 %shard_map.165 = (bf16[768,1024]{1,0:T(8,128)(2,1)}, bf16[768,1024]{1,0:T(8,128)(2,1)}, f32[512,768]{1,0:T(8,128)}, f32[512,768]{1,0:T(8,128)}) custom-call(bf16[512,768]{1,0:T(8,128)(2,1)} %copy.253.own_branch_ref, bf16[512,768]{1,0:T(8,128)(2,1)} %copy.254.other_branch_ref, ...), custom_call_target="tpu_custom_call", output_to_operand_aliasing={{2}: (13, {}), {3}: (14, {})} | custom-call | flops 8999999488 | bytes 15000000 | tf_op jit(solution)/shard_map/pallas_call | solution.py:252
  608.0 3.0 copy.259
  611.1 3.0 copy.260
  614.1 2.7 fusion.19
  619.4 3.7 copy.261
  623.0 3.9 add_convert_fusion.1
  631.8 4.6 collective-permute-start.41
  636.4 61.3 %collective-permute-done.55 = bf16[768,1024]{1,0:T(8,128)(2,1)} collective-permute-done((bf16[768,1024]{1,0:T(8,128)(2,1)}, bf16[768,1024]{1,0:T(8,128)(2,1)}, u32[]{:S(2)}, u32[]{:S(2)}) %collective-permute-start.55) | collective-permute-done | bytes 1572896 | tf_op jit(solution)/shard_map/ppermute | solution.py:486
  697.7 5.3 add_convert_fusion
  716.8 2.7 collective-permute-done.64
  722.3 12.1 %collective-permute-start.67 = (f32[8,128]{1,0:T(8,128)S(1)}, f32[8,128]{1,0:T(8,128)S(1)}, u32[]{:S(2)}, u32[]{:S(2)}) collective-permute-start(f32[8,128]{1,0:T(8,128)S(1)} %get-tuple-element.270), channel_id=1, source_target_pairs={{0,1},{1,0},{2,3},{3,2},{4,5},{5,4},{6,7},{7,6},{8,9},{9,8},{10,11... | collective-permute-start | bytes 12296 | tf_op jit(solution)/shard_map/ppermute | solution.py:418
  734.4 7.4 collective-permute-done.57
  750.4 27.1 %collective-permute-done.72 = f32[8,128]{1,0:T(8,128)} collective-permute-done((f32[8,128]{1,0:T(8,128)}, f32[8,128]{1,0:T(8,128)}, u32[]{:S(2)}, u32[]{:S(2)}) %collective-permute-start.72) | collective-permute-done | bytes 4128 | tf_op jit(solution)/shard_map/ppermute | solution.py:486
  782.1 2.6 pad_maximum_fusion.8
  785.2 8.9 fusion.9
  799.9 2.6 copy-done.5
  804.1 4.3 fusion.72
  810.3 4.1 pad_maximum_fusion
  814.4 5.6 copy.270
  824.2 47.7 %all-reduce.5.cloned.1.call-done = bf16[4,1536,1536]{2,1,0:T(8,128)(2,1)} async-done(((bf16[4,1536,1536]{2,1,0:T(8,128)(2,1)}), bf16[4,1536,1536]{2,1,0:T(8,128)(2,1)}) %all-reduce.5.cloned.1.call-update) | async-done | bytes 18874384 | tf_op jit(solution)/shard_map/psum | solution.py:701
  871.9 21.0 %convert_element_type.243 = f32[4,1536,1536]{2,1,0:T(8,128)} convert(bf16[4,1536,1536]{2,1,0:T(8,128)(2,1)} %all-reduce.5.cloned.1.call-done) | non-fusion elementwise | flops 9437184 | bytes 56623104 | tf_op jit(solution)/shard_map/convert_element_type | solution.py:701
  (361 shorter events, 181.0 us)
Async XLA Ops:
  7.2 175.2 %all-gather.3.cloned.1.call-start = ((), (), s32[]{:S(2)}) async-start(), calls=%async_computation.1 | async-start | bytes 7864320 | tf_op jit(solution)/shard_map/all_gather | solution.py:652
  7.2 29.1 %collective-permute-start.2 = (bf16[384]{0:T(512)(128)(2,1)}, bf16[384]{0:T(512)(128)(2,1)}, u32[]{:S(2)}, u32[]{:S(2)}) collective-permute-start(bf16[384]{0:T(512)(128)(2,1)} %param.12), channel_id=1, source_target_pairs={{0,3},{1,2},{2,1},{3,0},{4,7},{5,6},{6,5},{7,4},{8,11},{9,10},{10,... | collective-permute-start | bytes 2312 | tf_op jit(solution)/shard_map/ppermute | solution.py:418
  12.3 26.1 %collective-permute-start.1 = (bf16[384]{0:T(512)(128)(2,1)}, bf16[384]{0:T(512)(128)(2,1)}, u32[]{:S(2)}, u32[]{:S(2)}) collective-permute-start(bf16[384]{0:T(512)(128)(2,1)} %param.12), channel_id=1, source_target_pairs={{0,2},{1,3},{2,0},{3,1},{4,6},{5,7},{6,4},{7,5},{8,10},{9,11},{10,... | collective-permute-start | bytes 2312 | tf_op jit(solution)/shard_map/ppermute | solution.py:418
  12.4 28.3 %collective-permute-start = (bf16[384]{0:T(512)(128)(2,1)}, bf16[384]{0:T(512)(128)(2,1)S(1)}, u32[]{:S(2)}, u32[]{:S(2)}) collective-permute-start(bf16[384]{0:T(512)(128)(2,1)} %param.12), channel_id=1, source_target_pairs={{0,1},{1,0},{2,3},{3,2},{4,5},{5,4},{6,7},{7,6},{8,9},{9,8},{10,11... | collective-permute-start | bytes 2312 | tf_op jit(solution)/shard_map/ppermute | solution.py:418
  17.6 30.3 %collective-permute-start.5 = (bf16[192,640]{1,0:T(8,128)(2,1)}, bf16[192,640]{1,0:T(8,128)(2,1)}, u32[]{:S(2)}, u32[]{:S(2)}) collective-permute-start(bf16[192,640]{1,0:T(8,128)(2,1)} %get-tuple-element.254), channel_id=1, source_target_pairs={{0,3},{1,2},{2,1},{3,0},{4,7},{5,6},{6,5},{7,4},{8,11},{9,10},{10,... | collective-permute-start | bytes 737288 | tf_op jit(solution)/shard_map/ppermute | solution.py:418
  21.3 26.6 %collective-permute-start.4 = (bf16[192,640]{1,0:T(8,128)(2,1)}, bf16[192,640]{1,0:T(8,128)(2,1)}, u32[]{:S(2)}, u32[]{:S(2)}) collective-permute-start(bf16[192,640]{1,0:T(8,128)(2,1)} %get-tuple-element.254), channel_id=1, source_target_pairs={{0,2},{1,3},{2,0},{3,1},{4,6},{5,7},{6,4},{7,5},{8,10},{9,11},{10,... | collective-permute-start | bytes 737288 | tf_op jit(solution)/shard_map/ppermute | solution.py:418
  54.6 817.3 %all-reduce.5.cloned.1.call-start = ((), (), s32[]{:S(2)}) async-start(), calls=%async_computation | async-start | bytes 37748736 | tf_op jit(solution)/shard_map/psum | solution.py:701
  56.6 22.3 %collective-permute-start.6 = (bf16[4,192,640]{2,1,0:T(8,128)(2,1)S(1)}, bf16[4,192,640]{2,1,0:T(8,128)(2,1)}, u32[]{:S(2)}, u32[]{:S(2)}) collective-permute-start(bf16[4,192,640]{2,1,0:T(8,128)(2,1)S(1)} %pad_maximum_fusion.9.own_weight_ref), channel_id=1, source_target_pairs={{0,4},{4,0},{8,12},{12,8},{16,20},{20,16},{24,28},{28,24},{1,5},{5... | collective-permute-start | bytes 2949128 | tf_op jit(solution)/shard_map/ppermute | solution.py:486
  57.4 19.6 %collective-permute-start.7 = (bf16[3,192,640]{2,1,0:T(8,128)(2,1)}, bf16[3,192,640]{2,1,0:T(8,128)(2,1)S(1)}, u32[]{:S(2)}, u32[]{:S(2)}) collective-permute-start(bf16[3,192,640]{2,1,0:T(8,128)(2,1)} %pad_maximum_fusion.13), channel_id=1, source_target_pairs={{0,8},{4,12},{8,0},{12,4},{16,24},{20,28},{24,16},{28,20},{1,9},{5... | collective-permute-start | bytes 2211848 | tf_op jit(solution)/shard_map/ppermute | solution.py:486
  59.7 36.7 %collective-permute-start.9 = (bf16[3,192,640]{2,1,0:T(8,128)(2,1)}, bf16[3,192,640]{2,1,0:T(8,128)(2,1)}, u32[]{:S(2)}, u32[]{:S(2)}) collective-permute-start(bf16[3,192,640]{2,1,0:T(8,128)(2,1)} %pad_maximum_fusion.13), channel_id=1, source_target_pairs={{0,16},{4,20},{8,24},{12,28},{16,0},{20,4},{24,8},{28,12},{1,17},{... | collective-permute-start | bytes 2211848 | tf_op jit(solution)/shard_map/ppermute | solution.py:486
  61.2 35.2 %collective-permute-start.11 = (bf16[3,192,640]{2,1,0:T(8,128)(2,1)}, bf16[3,192,640]{2,1,0:T(8,128)(2,1)}, u32[]{:S(2)}, u32[]{:S(2)}) collective-permute-start(bf16[3,192,640]{2,1,0:T(8,128)(2,1)} %pad_maximum_fusion.13), channel_id=1, source_target_pairs={{0,24},{4,28},{8,16},{12,20},{16,8},{20,12},{24,0},{28,4},{1,25},{... | collective-permute-start | bytes 2211848 | tf_op jit(solution)/shard_map/ppermute | solution.py:486
  63.7 25.6 %collective-permute-start.15 = (bf16[192,384]{1,0:T(8,128)(2,1)S(1)}, bf16[192,384]{1,0:T(8,128)(2,1)S(1)}, u32[]{:S(2)}, u32[]{:S(2)}) collective-permute-start(bf16[192,384]{1,0:T(8,128)(2,1)S(1)} %dynamic_slice.243), channel_id=1, source_target_pairs={{0,3},{1,2},{2,1},{3,0},{4,7},{5,6},{6,5},{7,4},{8,11},{9,10},{10,... | collective-permute-start | bytes 442376 | tf_op jit(solution)/shard_map/ppermute | solution.py:418
  76.9 16.3 %collective-permute-start.14 = (bf16[192,384]{1,0:T(8,128)(2,1)S(1)}, bf16[192,384]{1,0:T(8,128)(2,1)S(1)}, u32[]{:S(2)}, u32[]{:S(2)}) collective-permute-start(bf16[192,384]{1,0:T(8,128)(2,1)S(1)} %dynamic_slice.243), channel_id=1, source_target_pairs={{0,2},{1,3},{2,0},{3,1},{4,6},{5,7},{6,4},{7,5},{8,10},{9,11},{10,... | collective-permute-start | bytes 442376 | tf_op jit(solution)/shard_map/ppermute | solution.py:418
  78.9 16.7 %collective-permute-start.13 = (bf16[192,384]{1,0:T(8,128)(2,1)S(1)}, bf16[192,384]{1,0:T(8,128)(2,1)S(1)}, u32[]{:S(2)}, u32[]{:S(2)}) collective-permute-start(bf16[192,384]{1,0:T(8,128)(2,1)S(1)} %dynamic_slice.243), channel_id=1, source_target_pairs={{0,1},{1,0},{2,3},{3,2},{4,5},{5,4},{6,7},{7,6},{8,9},{9,8},{10,11... | collective-permute-start | bytes 442376 | tf_op jit(solution)/shard_map/ppermute | solution.py:418
  89.3 30.7 %collective-permute-start.8 = (bf16[4,192,640]{2,1,0:T(8,128)(2,1)S(1)}, bf16[4,192,640]{2,1,0:T(8,128)(2,1)}, u32[]{:S(2)}, u32[]{:S(2)}) collective-permute-start(bf16[4,192,640]{2,1,0:T(8,128)(2,1)S(1)} %pad_maximum_fusion.10.own_weight_ref), channel_id=1, source_target_pairs={{0,4},{4,0},{8,12},{12,8},{16,20},{20,16},{24,28},{28,24},{1,5},{5... | collective-permute-start | bytes 2949128 | tf_op jit(solution)/shard_map/ppermute | solution.py:486
  99.1 19.3 %collective-permute-start.17 = (bf16[3,192,384]{2,1,0:T(8,128)(2,1)}, bf16[3,192,384]{2,1,0:T(8,128)(2,1)S(1)}, u32[]{:S(2)}, u32[]{:S(2)}) collective-permute-start(bf16[3,192,384]{2,1,0:T(8,128)(2,1)} %pad_maximum_fusion.18), channel_id=1, source_target_pairs={{0,16},{4,20},{8,24},{12,28},{16,0},{20,4},{24,8},{28,12},{1,17},{... | collective-permute-start | bytes 1327112 | tf_op jit(solution)/shard_map/ppermute | solution.py:486
  101.5 17.0 %collective-permute-start.18 = (bf16[3,192,384]{2,1,0:T(8,128)(2,1)}, bf16[3,192,384]{2,1,0:T(8,128)(2,1)S(1)}, u32[]{:S(2)}, u32[]{:S(2)}) collective-permute-start(bf16[3,192,384]{2,1,0:T(8,128)(2,1)} %pad_maximum_fusion.18), channel_id=1, source_target_pairs={{0,24},{4,28},{8,16},{12,20},{16,8},{20,12},{24,0},{28,4},{1,25},{... | collective-permute-start | bytes 1327112 | tf_op jit(solution)/shard_map/ppermute | solution.py:486
  103.3 26.0 %collective-permute-start.10 = (bf16[4,192,640]{2,1,0:T(8,128)(2,1)S(1)}, bf16[4,192,640]{2,1,0:T(8,128)(2,1)}, u32[]{:S(2)}, u32[]{:S(2)}) collective-permute-start(bf16[4,192,640]{2,1,0:T(8,128)(2,1)S(1)} %pad_maximum_fusion.11.own_weight_ref), channel_id=1, source_target_pairs={{0,4},{4,0},{8,12},{12,8},{16,20},{20,16},{24,28},{28,24},{1,5},{5... | collective-permute-start | bytes 2949128 | tf_op jit(solution)/shard_map/ppermute | solution.py:486
  109.8 38.1 %collective-permute-start.19 = (bf16[4,192,384]{2,1,0:T(8,128)(2,1)}, bf16[4,192,384]{2,1,0:T(8,128)(2,1)}, u32[]{:S(2)}, u32[]{:S(2)}) collective-permute-start(bf16[4,192,384]{2,1,0:T(8,128)(2,1)} %pad_maximum_fusion.14.refs_4_.own_output_ref), channel_id=1, source_target_pairs={{0,4},{4,0},{8,12},{12,8},{16,20},{20,16},{24,28},{28,24},{1,5},{5... | collective-permute-start | bytes 1769480 | tf_op jit(solution)/shard_map/ppermute | solution.py:486
  118.4 20.5 %collective-permute-start.12 = (bf16[4,192,640]{2,1,0:T(8,128)(2,1)S(1)}, bf16[4,192,640]{2,1,0:T(8,128)(2,1)}, u32[]{:S(2)}, u32[]{:S(2)}) collective-permute-start(bf16[4,192,640]{2,1,0:T(8,128)(2,1)S(1)} %pad_maximum_fusion.12.own_weight_ref), channel_id=1, source_target_pairs={{0,4},{4,0},{8,12},{12,8},{16,20},{20,16},{24,28},{28,24},{1,5},{5... | collective-permute-start | bytes 2949128 | tf_op jit(solution)/shard_map/ppermute | solution.py:486
  118.5 29.4 %collective-permute-start.20 = (bf16[4,192,384]{2,1,0:T(8,128)(2,1)}, bf16[4,192,384]{2,1,0:T(8,128)(2,1)}, u32[]{:S(2)}, u32[]{:S(2)}) collective-permute-start(bf16[4,192,384]{2,1,0:T(8,128)(2,1)} %pad_maximum_fusion.15.refs_5_.own_output_ref), channel_id=1, source_target_pairs={{0,4},{4,0},{8,12},{12,8},{16,20},{20,16},{24,28},{28,24},{1,5},{5... | collective-permute-start | bytes 1769480 | tf_op jit(solution)/shard_map/ppermute | solution.py:486
  120.0 27.9 %collective-permute-start.21 = (bf16[4,192,384]{2,1,0:T(8,128)(2,1)S(1)}, bf16[4,192,384]{2,1,0:T(8,128)(2,1)}, u32[]{:S(2)}, u32[]{:S(2)}) collective-permute-start(bf16[4,192,384]{2,1,0:T(8,128)(2,1)S(1)} %pad_maximum_fusion.16.refs_6_.own_output_ref), channel_id=1, source_target_pairs={{0,4},{4,0},{8,12},{12,8},{16,20},{20,16},{24,28},{28,24},{1,5},{5... | collective-permute-start | bytes 1769480 | tf_op jit(solution)/shard_map/ppermute | solution.py:486
  129.3 18.6 %collective-permute-start.22 = (bf16[4,192,384]{2,1,0:T(8,128)(2,1)S(1)}, bf16[4,192,384]{2,1,0:T(8,128)(2,1)S(1)}, u32[]{:S(2)}, u32[]{:S(2)}) collective-permute-start(bf16[4,192,384]{2,1,0:T(8,128)(2,1)S(1)} %copy-done.27), channel_id=1, source_target_pairs={{0,4},{4,0},{8,12},{12,8},{16,20},{20,16},{24,28},{28,24},{1,5},{5... | collective-permute-start | bytes 1769480 | tf_op jit(solution)/shard_map/ppermute | solution.py:486
  168.4 44.5 %collective-permute-start.27 = (bf16[512,1536]{1,0:T(8,128)(2,1)}, bf16[512,1536]{1,0:T(8,128)(2,1)}, u32[]{:S(2)}, u32[]{:S(2)}) collective-permute-start(bf16[512,1536]{1,0:T(8,128)(2,1)} %multiply_convert_fusion.fed_ref.refs_0_), channel_id=1, source_target_pairs={{0,1},{1,0},{2,3},{3,2},{4,5},{5,4},{6,7},{7,6},{8,9},{9,8},{10,11... | collective-permute-start | bytes 4718600 | tf_op jit(solution)/shard_map/ppermute | solution.py:418
  171.7 41.3 %collective-permute-start.26 = (bf16[512,1536]{1,0:T(8,128)(2,1)}, bf16[512,1536]{1,0:T(8,128)(2,1)}, u32[]{:S(2)}, u32[]{:S(2)}) collective-permute-start(bf16[512,1536]{1,0:T(8,128)(2,1)} %multiply_convert_fusion.fed_ref.refs_0_), channel_id=1, source_target_pairs={{1,2},{2,1},{5,6},{6,5},{9,10},{10,9},{13,14},{14,13},{17,18},{18,... | collective-permute-start | bytes 4718600 | tf_op jit(solution)/shard_map/ppermute | solution.py:446
  213.0 38.6 %collective-permute-start.28 = (bf16[512,1536]{1,0:T(8,128)(2,1)}, bf16[512,1536]{1,0:T(8,128)(2,1)}, u32[]{:S(2)}, u32[]{:S(2)}) collective-permute-start(bf16[512,1536]{1,0:T(8,128)(2,1)} %collective-permute-done.26), channel_id=1, source_target_pairs={{1,0},{2,3},{5,4},{6,7},{9,8},{10,11},{13,12},{14,15},{17,16},{18,... | collective-permute-start | bytes 4718600 | tf_op jit(solution)/shard_map/ppermute | solution.py:451
  215.1 75.1 %collective-permute-start.29 = (bf16[512,1536]{1,0:T(8,128)(2,1)}, bf16[512,1536]{1,0:T(8,128)(2,1)}, u32[]{:S(2)}, u32[]{:S(2)}) collective-permute-start(bf16[512,1536]{1,0:T(8,128)(2,1)} %collective-permute-done.27), channel_id=1, source_target_pairs={{1,2},{2,1},{5,6},{6,5},{9,10},{10,9},{13,14},{14,13},{17,18},{18,... | collective-permute-start | bytes 4718600 | tf_op jit(solution)/shard_map/ppermute | solution.py:450
  285.8 54.3 %collective-permute-start.31 = (bf16[512,1536]{1,0:T(8,128)(2,1)}, bf16[512,1536]{1,0:T(8,128)(2,1)}, u32[]{:S(2)}, u32[]{:S(2)}) collective-permute-start(bf16[512,1536]{1,0:T(8,128)(2,1)} %get-tuple-element.106), channel_id=1, source_target_pairs={{0,1},{3,2},{4,5},{7,6},{8,9},{11,10},{12,13},{15,14},{16,17},{19,... | collective-permute-start | bytes 4718600 | tf_op jit(solution)/shard_map/ppermute | solution.py:475
  288.4 57.5 %collective-permute-start.32 = (bf16[512,1536]{1,0:T(8,128)(2,1)}, bf16[512,1536]{1,0:T(8,128)(2,1)}, u32[]{:S(2)}, u32[]{:S(2)}) collective-permute-start(bf16[512,1536]{1,0:T(8,128)(2,1)} %get-tuple-element.106), channel_id=1, source_target_pairs={{1,2},{2,1},{5,6},{6,5},{9,10},{10,9},{13,14},{14,13},{17,18},{18,... | collective-permute-start | bytes 4718600 | tf_op jit(solution)/shard_map/ppermute | solution.py:475
  290.2 45.8 %collective-permute-start.30 = (bf16[512,1536]{1,0:T(8,128)(2,1)}, bf16[512,1536]{1,0:T(8,128)(2,1)}, u32[]{:S(2)}, u32[]{:S(2)}) collective-permute-start(bf16[512,1536]{1,0:T(8,128)(2,1)} %collective-permute-done.29), channel_id=1, source_target_pairs={{1,0},{2,3},{5,4},{6,7},{9,8},{10,11},{13,12},{14,15},{17,16},{18,... | collective-permute-start | bytes 4718600 | tf_op jit(solution)/shard_map/ppermute | solution.py:454
  322.5 42.5 %collective-permute-start.33 = (bf16[512,1536]{1,0:T(8,128)(2,1)}, bf16[512,1536]{1,0:T(8,128)(2,1)}, u32[]{:S(2)}, u32[]{:S(2)}) collective-permute-start(bf16[512,1536]{1,0:T(8,128)(2,1)} %get-tuple-element.108), channel_id=1, source_target_pairs={{0,2},{3,1},{4,6},{7,5},{8,10},{11,9},{12,14},{15,13},{16,18},{19,... | collective-permute-start | bytes 4718600 | tf_op jit(solution)/shard_map/ppermute | solution.py:475
  331.0 39.5 %collective-permute-start.34 = (bf16[512,1536]{1,0:T(8,128)(2,1)}, bf16[512,1536]{1,0:T(8,128)(2,1)}, u32[]{:S(2)}, u32[]{:S(2)}) collective-permute-start(bf16[512,1536]{1,0:T(8,128)(2,1)} %get-tuple-element.108), channel_id=1, source_target_pairs={{1,0},{2,3},{5,4},{6,7},{9,8},{10,11},{13,12},{14,15},{17,16},{18,... | collective-permute-start | bytes 4718600 | tf_op jit(solution)/shard_map/ppermute | solution.py:475
  336.0 67.9 %collective-permute-start.46 = (f32[16,512]{0,1:T(8,128)S(1)}, f32[16,512]{0,1:T(8,128)S(1)}, u32[]{:S(2)}, u32[]{:S(2)}) collective-permute-start(f32[16,512]{0,1:T(8,128)S(1)} %slice_bitcast_fusion.4), channel_id=1, source_target_pairs={{1,0},{2,3},{5,4},{6,7},{9,8},{10,11},{13,12},{14,15},{17,16},{18,... | collective-permute-start | bytes 98312 | tf_op jit(solution)/shard_map/ppermute | solution.py:475
  340.0 68.0 %collective-permute-start.45 = (f32[16,512]{0,1:T(8,128)S(1)}, f32[16,512]{0,1:T(8,128)}, u32[]{:S(2)}, u32[]{:S(2)}) collective-permute-start(f32[16,512]{0,1:T(8,128)S(1)} %slice_bitcast_fusion.4), channel_id=1, source_target_pairs={{0,2},{3,1},{4,6},{7,5},{8,10},{11,9},{12,14},{15,13},{16,18},{19,... | collective-permute-start | bytes 98312 | tf_op jit(solution)/shard_map/ppermute | solution.py:475
  345.9 63.5 %collective-permute-start.44 = (f32[16,512]{0,1:T(8,128)}, f32[16,512]{0,1:T(8,128)}, u32[]{:S(2)}, u32[]{:S(2)}) collective-permute-start(f32[16,512]{0,1:T(8,128)} %slice_bitcast_fusion.5), channel_id=1, source_target_pairs={{1,2},{2,1},{5,6},{6,5},{9,10},{10,9},{13,14},{14,13},{17,18},{18,... | collective-permute-start | bytes 98312 | tf_op jit(solution)/shard_map/ppermute | solution.py:475
  365.0 96.6 %collective-permute-start.43 = (f32[16,512]{0,1:T(8,128)}, f32[16,512]{0,1:T(8,128)}, u32[]{:S(2)}, u32[]{:S(2)}) collective-permute-start(f32[16,512]{0,1:T(8,128)} %slice_bitcast_fusion.5), channel_id=1, source_target_pairs={{0,1},{3,2},{4,5},{7,6},{8,9},{11,10},{12,13},{15,14},{16,17},{19,... | collective-permute-start | bytes 98312 | tf_op jit(solution)/shard_map/ppermute | solution.py:475
  401.0 81.1 %collective-permute-start.36 = (bf16[512,1536]{1,0:T(8,128)(2,1)}, bf16[512,1536]{1,0:T(8,128)(2,1)}, u32[]{:S(2)}, u32[]{:S(2)}) collective-permute-start(bf16[512,1536]{1,0:T(8,128)(2,1)} %get-tuple-element.111), channel_id=1, source_target_pairs={{1,3},{2,0},{5,7},{6,4},{9,11},{10,8},{13,15},{14,12},{17,19},{18,... | collective-permute-start | bytes 4718600 | tf_op jit(solution)/shard_map/ppermute | solution.py:475
  403.9 78.1 %collective-permute-start.35 = (bf16[512,1536]{1,0:T(8,128)(2,1)}, bf16[512,1536]{1,0:T(8,128)(2,1)}, u32[]{:S(2)}, u32[]{:S(2)}) collective-permute-start(bf16[512,1536]{1,0:T(8,128)(2,1)} %get-tuple-element.111), channel_id=1, source_target_pairs={{0,3},{3,0},{4,7},{7,4},{8,11},{11,8},{12,15},{15,12},{16,19},{19,... | collective-permute-start | bytes 4718600 | tf_op jit(solution)/shard_map/ppermute | solution.py:475
  408.0 72.2 %collective-permute-start.48 = (f32[16,512]{0,1:T(8,128)}, f32[16,512]{0,1:T(8,128)}, u32[]{:S(2)}, u32[]{:S(2)}) collective-permute-start(f32[16,512]{0,1:T(8,128)} %slice_bitcast_fusion.3), channel_id=1, source_target_pairs={{1,3},{2,0},{5,7},{6,4},{9,11},{10,8},{13,15},{14,12},{17,19},{18,... | collective-permute-start | bytes 98312 | tf_op jit(solution)/shard_map/ppermute | solution.py:475
  409.3 70.9 %collective-permute-start.47 = (f32[16,512]{0,1:T(8,128)}, f32[16,512]{0,1:T(8,128)}, u32[]{:S(2)}, u32[]{:S(2)}) collective-permute-start(f32[16,512]{0,1:T(8,128)} %slice_bitcast_fusion.3), channel_id=1, source_target_pairs={{0,3},{3,0},{4,7},{7,4},{8,11},{11,8},{12,15},{15,12},{16,19},{19,... | collective-permute-start | bytes 98312 | tf_op jit(solution)/shard_map/ppermute | solution.py:475
  487.2 38.2 %collective-permute-start.37 = (bf16[512,1536]{1,0:T(8,128)(2,1)}, bf16[512,1536]{1,0:T(8,128)(2,1)}, u32[]{:S(2)}, u32[]{:S(2)}) collective-permute-start(bf16[512,1536]{1,0:T(8,128)(2,1)} %get-tuple-element.126), channel_id=1, source_target_pairs={{0,1},{3,2},{4,5},{7,6},{8,9},{11,10},{12,13},{15,14},{16,17},{19,... | collective-permute-start | bytes 4718600 | tf_op jit(solution)/shard_map/ppermute | solution.py:475
  489.9 35.6 %collective-permute-start.38 = (bf16[512,1536]{1,0:T(8,128)(2,1)}, bf16[512,1536]{1,0:T(8,128)(2,1)}, u32[]{:S(2)}, u32[]{:S(2)}) collective-permute-start(bf16[512,1536]{1,0:T(8,128)(2,1)} %get-tuple-element.126), channel_id=1, source_target_pairs={{1,2},{2,1},{5,6},{6,5},{9,10},{10,9},{13,14},{14,13},{17,18},{18,... | collective-permute-start | bytes 4718600 | tf_op jit(solution)/shard_map/ppermute | solution.py:475
  525.5 27.1 %collective-permute-start.50 = (bf16[768,1024]{1,0:T(8,128)(2,1)}, bf16[768,1024]{1,0:T(8,128)(2,1)}, u32[]{:S(2)}, u32[]{:S(2)}) collective-permute-start(bf16[768,1024]{1,0:T(8,128)(2,1)} %get-tuple-element.148), channel_id=1, source_target_pairs={{0,4},{4,0},{8,12},{12,8},{16,20},{20,16},{24,28},{28,24},{1,5},{5... | collective-permute-start | bytes 4718600 | tf_op jit(solution)/shard_map/ppermute | solution.py:486
  545.8 33.4 %collective-permute-start.49 = (bf16[768,1024]{1,0:T(8,128)(2,1)}, bf16[768,1024]{1,0:T(8,128)(2,1)}, u32[]{:S(2)}, u32[]{:S(2)}) collective-permute-start(bf16[768,1024]{1,0:T(8,128)(2,1)} %get-tuple-element.144), channel_id=1, source_target_pairs={{0,4},{4,0},{8,12},{12,8},{16,20},{20,16},{24,28},{28,24},{1,5},{5... | collective-permute-start | bytes 4718600 | tf_op jit(solution)/shard_map/ppermute | solution.py:486
  546.3 37.3 %collective-permute-start.39 = (bf16[512,1536]{1,0:T(8,128)(2,1)}, bf16[512,1536]{1,0:T(8,128)(2,1)}, u32[]{:S(2)}, u32[]{:S(2)}) collective-permute-start(bf16[512,1536]{1,0:T(8,128)(2,1)} %get-tuple-element.127), channel_id=1, source_target_pairs={{0,2},{3,1},{4,6},{7,5},{8,10},{11,9},{12,14},{15,13},{16,18},{19,... | collective-permute-start | bytes 4718600 | tf_op jit(solution)/shard_map/ppermute | solution.py:475
  549.2 38.2 %collective-permute-start.40 = (bf16[512,1536]{1,0:T(8,128)(2,1)}, bf16[512,1536]{1,0:T(8,128)(2,1)}, u32[]{:S(2)}, u32[]{:S(2)}) collective-permute-start(bf16[512,1536]{1,0:T(8,128)(2,1)} %get-tuple-element.127), channel_id=1, source_target_pairs={{1,0},{2,3},{5,4},{6,7},{9,8},{10,11},{13,12},{14,15},{17,16},{18,... | collective-permute-start | bytes 4718600 | tf_op jit(solution)/shard_map/ppermute | solution.py:475
  556.4 73.9 %collective-permute-start.52 = (bf16[768,1024]{1,0:T(8,128)(2,1)}, bf16[768,1024]{1,0:T(8,128)(2,1)}, u32[]{:S(2)}, u32[]{:S(2)}) collective-permute-start(bf16[768,1024]{1,0:T(8,128)(2,1)} %add_convert_fusion.3), channel_id=1, source_target_pairs={{0,24},{4,28},{8,16},{12,20},{16,8},{20,12},{24,0},{28,4},{1,25},{... | collective-permute-start | bytes 4718600 | tf_op jit(solution)/shard_map/ppermute | solution.py:486
  579.2 43.8 %collective-permute-start.54 = (bf16[768,1024]{1,0:T(8,128)(2,1)}, bf16[768,1024]{1,0:T(8,128)(2,1)}, u32[]{:S(2)}, u32[]{:S(2)}) collective-permute-start(bf16[768,1024]{1,0:T(8,128)(2,1)} %get-tuple-element.162), channel_id=1, source_target_pairs={{0,4},{4,0},{8,12},{12,8},{16,20},{20,16},{24,28},{28,24},{1,5},{5... | collective-permute-start | bytes 4718600 | tf_op jit(solution)/shard_map/ppermute | solution.py:486
  582.9 114.8 %collective-permute-start.53 = (bf16[768,1024]{1,0:T(8,128)(2,1)}, bf16[768,1024]{1,0:T(8,128)(2,1)}, u32[]{:S(2)}, u32[]{:S(2)}) collective-permute-start(bf16[768,1024]{1,0:T(8,128)(2,1)} %add_convert_fusion.4), channel_id=1, source_target_pairs={{0,8},{4,12},{8,0},{12,4},{16,24},{20,28},{24,16},{28,20},{1,9},{5... | collective-permute-start | bytes 4718600 | tf_op jit(solution)/shard_map/ppermute | solution.py:486
  627.0 70.8 %collective-permute-start.55 = (bf16[768,1024]{1,0:T(8,128)(2,1)}, bf16[768,1024]{1,0:T(8,128)(2,1)}, u32[]{:S(2)}, u32[]{:S(2)}) collective-permute-start(bf16[768,1024]{1,0:T(8,128)(2,1)} %add_convert_fusion.1), channel_id=1, source_target_pairs={{0,16},{4,20},{8,24},{12,28},{16,0},{20,4},{24,8},{28,12},{1,17},{... | collective-permute-start | bytes 4718600 | tf_op jit(solution)/shard_map/ppermute | solution.py:486
  628.1 69.6 %collective-permute-start.51 = (bf16[768,1024]{1,0:T(8,128)(2,1)}, bf16[768,1024]{1,0:T(8,128)(2,1)}, u32[]{:S(2)}, u32[]{:S(2)}) collective-permute-start(bf16[768,1024]{1,0:T(8,128)(2,1)} %get-tuple-element.160), channel_id=1, source_target_pairs={{0,4},{4,0},{8,12},{12,8},{16,20},{20,16},{24,28},{28,24},{1,5},{5... | collective-permute-start | bytes 4718600 | tf_op jit(solution)/shard_map/ppermute | solution.py:486
  630.3 73.1 %collective-permute-start.42 = (bf16[512,1536]{1,0:T(8,128)(2,1)}, bf16[512,1536]{1,0:T(8,128)(2,1)}, u32[]{:S(2)}, u32[]{:S(2)}) collective-permute-start(bf16[512,1536]{1,0:T(8,128)(2,1)} %get-tuple-element.128), channel_id=1, source_target_pairs={{1,3},{2,0},{5,7},{6,4},{9,11},{10,8},{13,15},{14,12},{17,19},{18,... | collective-permute-start | bytes 4718600 | tf_op jit(solution)/shard_map/ppermute | solution.py:475
  631.8 71.7 %collective-permute-start.41 = (bf16[512,1536]{1,0:T(8,128)(2,1)}, bf16[512,1536]{1,0:T(8,128)(2,1)}, u32[]{:S(2)}, u32[]{:S(2)}) collective-permute-start(bf16[512,1536]{1,0:T(8,128)(2,1)} %get-tuple-element.128), channel_id=1, source_target_pairs={{0,3},{3,0},{4,7},{7,4},{8,11},{11,8},{12,15},{15,12},{16,19},{19,... | collective-permute-start | bytes 4718600 | tf_op jit(solution)/shard_map/ppermute | solution.py:475
  705.2 17.2 %collective-permute-start.58 = (bf16[192,1024]{1,0:T(8,128)(2,1)}, bf16[192,1024]{1,0:T(8,128)(2,1)}, u32[]{:S(2)}, u32[]{:S(2)}) collective-permute-start(bf16[192,1024]{1,0:T(8,128)(2,1)} %get-tuple-element.233), channel_id=1, source_target_pairs={{0,3},{1,2},{2,1},{3,0},{4,7},{5,6},{6,5},{7,4},{8,11},{9,10},{10,... | collective-permute-start | bytes 1179656 | tf_op jit(solution)/shard_map/ppermute | solution.py:418
  707.1 34.7 %collective-permute-start.57 = (bf16[192,1024]{1,0:T(8,128)(2,1)}, bf16[192,1024]{1,0:T(8,128)(2,1)}, u32[]{:S(2)}, u32[]{:S(2)}) collective-permute-start(bf16[192,1024]{1,0:T(8,128)(2,1)} %get-tuple-element.234), channel_id=1, source_target_pairs={{0,2},{1,3},{2,0},{3,1},{4,6},{5,7},{6,4},{7,5},{8,10},{9,11},{10,... | collective-permute-start | bytes 1179656 | tf_op jit(solution)/shard_map/ppermute | solution.py:418
  708.1 33.6 %collective-permute-start.56 = (bf16[192,1024]{1,0:T(8,128)(2,1)S(1)}, bf16[192,1024]{1,0:T(8,128)(2,1)}, u32[]{:S(2)}, u32[]{:S(2)}) collective-permute-start(bf16[192,1024]{1,0:T(8,128)(2,1)S(1)} %get-tuple-element.232), channel_id=1, source_target_pairs={{0,1},{1,0},{2,3},{3,2},{4,5},{5,4},{6,7},{7,6},{8,9},{9,8},{10,11... | collective-permute-start | bytes 1179656 | tf_op jit(solution)/shard_map/ppermute | solution.py:418
  720.3 26.0 %collective-permute-start.69 = (f32[8,128]{1,0:T(8,128)S(1)}, f32[8,128]{1,0:T(8,128)S(1)}, u32[]{:S(2)}, u32[]{:S(2)}) collective-permute-start(f32[8,128]{1,0:T(8,128)S(1)} %get-tuple-element.271), channel_id=1, source_target_pairs={{0,3},{1,2},{2,1},{3,0},{4,7},{5,6},{6,5},{7,4},{8,11},{9,10},{10,... | collective-permute-start | bytes 12296 | tf_op jit(solution)/shard_map/ppermute | solution.py:418
  722.1 24.8 %collective-permute-start.68 = (f32[8,128]{1,0:T(8,128)S(1)}, f32[8,128]{1,0:T(8,128)S(1)}, u32[]{:S(2)}, u32[]{:S(2)}) collective-permute-start(f32[8,128]{1,0:T(8,128)S(1)} %get-tuple-element.272), channel_id=1, source_target_pairs={{0,2},{1,3},{2,0},{3,1},{4,6},{5,7},{6,4},{7,5},{8,10},{9,11},{10,... | collective-permute-start | bytes 12296 | tf_op jit(solution)/shard_map/ppermute | solution.py:418
  722.3 24.6 %collective-permute-start.67 = (f32[8,128]{1,0:T(8,128)S(1)}, f32[8,128]{1,0:T(8,128)S(1)}, u32[]{:S(2)}, u32[]{:S(2)}) collective-permute-start(f32[8,128]{1,0:T(8,128)S(1)} %get-tuple-element.270), channel_id=1, source_target_pairs={{0,1},{1,0},{2,3},{3,2},{4,5},{5,4},{6,7},{7,6},{8,9},{9,8},{10,11... | collective-permute-start | bytes 12296 | tf_op jit(solution)/shard_map/ppermute | solution.py:418
  743.4 38.7 %collective-permute-start.61 = (bf16[192,1024]{1,0:T(8,128)(2,1)S(1)}, bf16[192,1024]{1,0:T(8,128)(2,1)}, u32[]{:S(2)}, u32[]{:S(2)}) collective-permute-start(bf16[192,1024]{1,0:T(8,128)(2,1)S(1)} %fusion.34), channel_id=1, source_target_pairs={{0,24},{4,28},{8,16},{12,20},{16,8},{20,12},{24,0},{28,4},{1,25},{... | collective-permute-start | bytes 1179656 | tf_op jit(solution)/shard_map/ppermute | solution.py:486
  745.2 36.9 %collective-permute-start.60 = (bf16[192,1024]{1,0:T(8,128)(2,1)S(1)}, bf16[192,1024]{1,0:T(8,128)(2,1)}, u32[]{:S(2)}, u32[]{:S(2)}) collective-permute-start(bf16[192,1024]{1,0:T(8,128)(2,1)S(1)} %fusion.34), channel_id=1, source_target_pairs={{0,16},{4,20},{8,24},{12,28},{16,0},{20,4},{24,8},{28,12},{1,17},{... | collective-permute-start | bytes 1179656 | tf_op jit(solution)/shard_map/ppermute | solution.py:486
  746.3 35.9 %collective-permute-start.59 = (bf16[192,1024]{1,0:T(8,128)(2,1)S(1)}, bf16[192,1024]{1,0:T(8,128)(2,1)}, u32[]{:S(2)}, u32[]{:S(2)}) collective-permute-start(bf16[192,1024]{1,0:T(8,128)(2,1)S(1)} %fusion.34), channel_id=1, source_target_pairs={{0,8},{4,12},{8,0},{12,4},{16,24},{20,28},{24,16},{28,20},{1,9},{5... | collective-permute-start | bytes 1179656 | tf_op jit(solution)/shard_map/ppermute | solution.py:486
  747.5 30.0 %collective-permute-start.72 = (f32[8,128]{1,0:T(8,128)}, f32[8,128]{1,0:T(8,128)}, u32[]{:S(2)}, u32[]{:S(2)}) collective-permute-start(f32[8,128]{1,0:T(8,128)} %fusion.62), channel_id=1, source_target_pairs={{0,24},{4,28},{8,16},{12,20},{16,8},{20,12},{24,0},{28,4},{1,25},{... | collective-permute-start | bytes 12296 | tf_op jit(solution)/shard_map/ppermute | solution.py:486
  749.3 30.6 %collective-permute-start.71 = (f32[8,128]{1,0:T(8,128)}, f32[8,128]{1,0:T(8,128)S(1)}, u32[]{:S(2)}, u32[]{:S(2)}) collective-permute-start(f32[8,128]{1,0:T(8,128)} %fusion.62), channel_id=1, source_target_pairs={{0,16},{4,20},{8,24},{12,28},{16,0},{20,4},{24,8},{28,12},{1,17},{... | collective-permute-start | bytes 12296 | tf_op jit(solution)/shard_map/ppermute | solution.py:486
  (61 other events, 1146.0 us)
Sparse Core Ops, SparseCore 0:
  54.7 127.6 all-gather.2
  552.7 319.1 all-reduce.4

commit v2 on v1

v2 whole, which is shorter than its diff:
```python
import functools

import jax
import jax.numpy as jnp
from jax import lax
from jax.experimental import pallas as pl
from jax.experimental.pallas import tpu as pltpu
from jax.sharding import PartitionSpec as P

QUERY_HEADS = 24
KEY_VALUE_HEADS = 8
HEAD_WIDTH = 64
FF = 512
EXPERTS = 16

EPSILON = 1e-06
MASKED = -1e30

GROUP = QUERY_HEADS // KEY_VALUE_HEADS
PAIRS = KEY_VALUE_HEADS // 2
PAIR_QUERY = 2 * GROUP * HEAD_WIDTH
PAIR_KEY = 2 * HEAD_WIDTH
PAIR_WIDTH = PAIR_QUERY + 2 * PAIR_KEY
BLOCK = 256
LANES = 128
VMEM = 60 * 2**20


def cost(flops, moved):
    return pl.CostEstimate(flops=int(flops), bytes_accessed=int(moved), transcendentals=0)

bf16 = jnp.bfloat16
f32 = jnp.float32


def dot(left, right):
    return jnp.dot(left, right, preferred_element_type=f32)


def contract_rows(left, right):
    return lax.dot_general(left, right, (((0,), (0,)), ((), ())), preferred_element_type=f32)


def times_transposed(left, right):
    return lax.dot_general(left, right, (((1,), (1,)), ((), ())), preferred_element_type=f32)


def norm_rows(value_rows):
    inverse = lax.rsqrt(jnp.mean(value_rows * value_rows, axis=-1, keepdims=True) + EPSILON)
    return (value_rows * inverse, inverse)


def norm_back(scaled, inverse, upstream):
    return inverse * (upstream - scaled * jnp.mean(upstream * scaled, axis=-1, keepdims=True))


def rotary_tables(length, width):
    half = HEAD_WIDTH // 2
    frequency = 10000.0 ** (-2.0 * jnp.arange(half, dtype=f32) / HEAD_WIDTH)
    angles = jnp.arange(length, dtype=f32)[:, None] * frequency[None, :]
    cosine, sine = jnp.cos(angles), jnp.sin(angles)
    heads = width // HEAD_WIDTH
    return (
        jnp.tile(jnp.concatenate([cosine, cosine], axis=1), (1, heads)),
        jnp.tile(jnp.concatenate([-sine, sine], axis=1), (1, heads)),
    )


def rotate(values, cosine, sine):
    width = values.shape[1]
    half = HEAD_WIDTH // 2
    lane = lax.broadcasted_iota(jnp.int32, values.shape, 1)
    swapped = jnp.where(
        lane % HEAD_WIDTH < half,
        pltpu.roll(values, width - half, 1),
        pltpu.roll(values, half, 1),
    )
    return values * cosine + swapped * sine


def causal_block():
    shape = (BLOCK, BLOCK)
    return lax.broadcasted_iota(jnp.int32, shape, 0) <= lax.broadcasted_iota(jnp.int32, shape, 1)


def stack_rows(parts):
    return parts[0] if len(parts) == 1 else jnp.concatenate(parts, axis=0)


def natural(at_ref, own_ref, other_ref, held_ref):
    shards, half = own_ref.shape[1:3]
    for k in range(shards):
        for side, ref in enumerate((own_ref, other_ref)):
            start = (at_ref[0] ^ k) * (2 * half) + (at_ref[1] ^ side) * half
            held_ref[pl.ds(pl.multiple_of(start, half), half), :] = ref[0, k]


def attend_forward_kernel(
    at_ref, normed_ref, own_ref, other_ref, cosine_ref, sine_ref, mixed_ref, qkv_ref, lse_ref, weight_ref
):
    length = normed_ref.shape[0]
    natural(at_ref, own_ref, other_ref, weight_ref)
    keep = causal_block()
    projected = dot(normed_ref[...], weight_ref[...])
    rotated = rotate(projected[:, : PAIR_QUERY + PAIR_KEY], cosine_ref[...], sine_ref[...])
    query = (rotated[:, :PAIR_QUERY] * HEAD_WIDTH**-0.5).astype(bf16)
    key = rotated[:, PAIR_QUERY:].astype(bf16)
    value = projected[:, PAIR_QUERY + PAIR_KEY :].astype(bf16)
    qkv_ref[0, :, :PAIR_QUERY] = query
    qkv_ref[0, :, PAIR_QUERY : PAIR_QUERY + PAIR_KEY] = key
    qkv_ref[0, :, PAIR_QUERY + PAIR_KEY :] = value
    value_columns = value.T
    outs = []
    for head in range(2 * GROUP):
        kv = (head // GROUP) * HEAD_WIDTH
        columns = []
        for block in range(length // BLOCK):
            start, stop = block * BLOCK, (block + 1) * BLOCK
            scores = times_transposed(
                key[:stop, kv : kv + HEAD_WIDTH],
                query[start:stop, head * HEAD_WIDTH : (head + 1) * HEAD_WIDTH],
            )
            parts = [scores[:start]] if block else []
            scores = stack_rows(parts + [jnp.where(keep, scores[start:], MASKED)])
            top = jnp.max(scores, axis=0, keepdims=True)
            powers = jnp.exp(scores - top)
            total = jnp.sum(powers, axis=0, keepdims=True)
            probability = (powers * (1.0 / total)).astype(bf16)
            columns.append(dot(value_columns[kv : kv + HEAD_WIDTH, :stop], probability))
            lse_ref[0, head, start:stop] = (top + jnp.log(total))[0]
        outs.append(jnp.concatenate(columns, axis=1))
    mixed_ref[0] = jnp.concatenate(outs, axis=0).T.astype(bf16)


def whole(array):
    return pl.BlockSpec(array.shape, lambda *_: (0,) * array.ndim)


def entry(array, index=None):
    rest = (0,) * (array.ndim - 1)
    return pl.BlockSpec(
        (1,) + array.shape[1:], lambda p, at: ((p if index is None else index),) + rest
    )


def attend_forward(at, normed, weights, tables):
    length, features = normed.shape
    shapes = [
        jax.ShapeDtypeStruct((PAIRS, length, PAIR_QUERY), bf16),
        jax.ShapeDtypeStruct((PAIRS, length, PAIR_WIDTH), bf16),
        jax.ShapeDtypeStruct((PAIRS, 8, length), f32),
    ]
    return pl.pallas_call(
        attend_forward_kernel,
        grid_spec=pltpu.PrefetchScalarGridSpec(
            num_scalar_prefetch=1,
            grid=(PAIRS,),
            in_specs=[whole(normed)] + [entry(w) for w in weights] + [whole(t) for t in tables],
            out_specs=[entry(shape) for shape in shapes],
            scratch_shapes=[pltpu.VMEM((features, PAIR_WIDTH), bf16)],
        ),
        out_shape=shapes,
        compiler_params=pltpu.CompilerParams(vmem_limit_bytes=VMEM),
        cost_estimate=cost(2e10, 2e7),
    )(at, normed, *weights, *tables)


def middle_kernel(
    at_ref, mixed_ref, own_ref, other_ref, input_ref, gain_ref, middle_ref, fed_ref, weight_ref
):
    step = pl.program_id(0)
    natural(at_ref, own_ref, other_ref, weight_ref)
    added = times_transposed(mixed_ref[0], weight_ref[...])

    @pl.when(step == 0)
    def _():
        middle_ref[...] = input_ref[...].astype(f32) + added

    @pl.when(step > 0)
    def _():
        middle_ref[...] += added

    @pl.when(step == pl.num_programs(0) - 1)
    def _():
        fed_ref[...] = (norm_rows(middle_ref[...])[0] * gain_ref[...]).astype(bf16)


def middle_rows(at, mixed, weights, inputs, gain):
    length, features = inputs.shape
    shapes = [jax.ShapeDtypeStruct((length, features), kind) for kind in (f32, bf16)]
    return pl.pallas_call(
        middle_kernel,
        grid_spec=pltpu.PrefetchScalarGridSpec(
            num_scalar_prefetch=1,
            grid=(PAIRS,),
            in_specs=[entry(mixed)] + [entry(w) for w in weights] + [whole(inputs), whole(gain)],
            out_specs=[whole(shape) for shape in shapes],
            scratch_shapes=[pltpu.VMEM((features, PAIR_QUERY), bf16)],
        ),
        out_shape=shapes,
        compiler_params=pltpu.CompilerParams(vmem_limit_bytes=VMEM),
        cost_estimate=cost(2.4e9, 1e7),
    )(at, mixed, *weights, inputs, gain)


def attend_backward_kernel(
    at_ref,
    branch_ref,
    own_output_ref,
    other_output_ref,
    mixed_ref,
    qkv_ref,
    lse_ref,
    normed_ref,
    own_weight_ref,
    other_weight_ref,
    cosine_ref,
    sine_ref,
    total_ref,
    own_term_ref,
    other_term_ref,
    grad_ref,
    output_ref,
    weight_ref,
    term_ref,
):
    length = branch_ref.shape[0]
    natural(at_ref, own_output_ref, other_output_ref, output_ref)
    natural(at_ref, own_weight_ref, other_weight_ref, weight_ref)
    keep = causal_block()
    blocks = length // BLOCK
    mixed_grad = dot(branch_ref[...], output_ref[...]).astype(bf16)
    query = qkv_ref[0, :, :PAIR_QUERY]
    key = qkv_ref[0, :, PAIR_QUERY : PAIR_QUERY + PAIR_KEY]
    value = qkv_ref[0, :, PAIR_QUERY + PAIR_KEY :]
    scaled_key = (key.astype(f32) * HEAD_WIDTH**-0.5).T.astype(bf16)
    query_grads, key_grads, value_grads = [], [], []
    for side in range(2):
        kv = side * HEAD_WIDTH
        key_part = key[:, kv : kv + HEAD_WIDTH]
        value_part = value[:, kv : kv + HEAD_WIDTH]
        key_grad, value_grad = [None] * blocks, [None] * blocks
        for head in range(side * GROUP, (side + 1) * GROUP):
            column = head * HEAD_WIDTH
            columns = []
            for block in range(blocks):
                start, stop = block * BLOCK, (block + 1) * BLOCK
                query_rows = query[start:stop, column : column + HEAD_WIDTH]
                upstream = mixed_grad[start:stop, column : column + HEAD_WIDTH]
                scores = times_transposed(key_part[:stop], query_rows)
                prob_grad = times_transposed(value_part[:stop], upstream)
                probability = jnp.exp(scores - lse_ref[0, head, start:stop][None, :])
                parts = [probability[:start]] if block else []
                probability = stack_rows(parts + [jnp.where(keep, probability[start:], 0.0)])
                shift = jnp.sum(probability * prob_grad, axis=0, keepdims=True)
                score_grad = (probability * (prob_grad - shift)).astype(bf16)
                value_add = dot(probability.astype(bf16), upstream)
                key_add = dot(score_grad, query_rows)
                for j in range(block + 1):
                    rows = slice(j * BLOCK, (j + 1) * BLOCK)
                    value_grad[j] = (
                        value_add[rows] if value_grad[j] is None else value_grad[j] + value_add[rows]
                    )
                    key_grad[j] = (
                        key_add[rows] if key_grad[j] is None else key_grad[j] + key_add[rows]
                    )
                columns.append(dot(scaled_key[kv : kv + HEAD_WIDTH, :stop], score_grad))
            query_grads.append(jnp.concatenate(columns, axis=1))
        key_grads.append(stack_rows(key_grad))
        value_grads.append(stack_rows(value_grad))
    turned = rotate(
        jnp.concatenate([jnp.concatenate(query_grads, axis=0).T] + key_grads, axis=1),
        cosine_ref[...],
        -sine_ref[...],
    )
    projected_grad = jnp.concatenate([turned] + value_grads, axis=1).astype(bf16)
    term_ref[:, :PAIR_WIDTH] = contract_rows(normed_ref[...], projected_grad).astype(bf16)
    term_ref[:, PAIR_WIDTH:] = contract_rows(branch_ref[...], mixed_ref[0]).astype(bf16)
    shards, half = own_weight_ref.shape[1:3]
    for k in range(shards):
        for side, ref in enumerate((own_term_ref, other_term_ref)):
            start = (at_ref[0] ^ k) * (2 * half) + (at_ref[1] ^ side) * half
            ref[k] = term_ref[pl.ds(pl.multiple_of(start, half), half), :]
    grad_ref[...] = total_ref[...] + times_transposed(projected_grad, weight_ref[...])


def attend_backward(at, m, branch_grad, output, saved, normed, weights, tables, total):
    length, features = branch_grad.shape
    shards, half = weights[0].shape[1:3]
    width = PAIR_WIDTH + PAIR_QUERY
    term = jax.ShapeDtypeStruct((shards, half, width), bf16)
    shapes = [term, term, jax.ShapeDtypeStruct((length, features), f32)]
    ones = [*output, *saved]
    operands = [branch_grad, *ones, normed, *weights, *tables, total]
    specs = [whole(branch_grad)] + [entry(one, m) for one in ones] + [whole(normed)]
    specs += [entry(w, m) for w in weights] + [whole(t) for t in tables] + [whole(total)]
    return pl.pallas_call(
        attend_backward_kernel,
        grid_spec=pltpu.PrefetchScalarGridSpec(
            num_scalar_prefetch=1,
            grid=(1,),
            in_specs=specs,
            out_specs=[whole(shape) for shape in shapes],
            scratch_shapes=[
                pltpu.VMEM((features, PAIR_QUERY), bf16),
                pltpu.VMEM((features, PAIR_WIDTH), bf16),
                pltpu.VMEM((features, width), bf16),
            ],
        ),
        out_shape=shapes,
        input_output_aliases={len(operands): 2},
        compiler_params=pltpu.CompilerParams(vmem_limit_bytes=VMEM),
        cost_estimate=cost(9e9, 1.5e7),
    )(at, *operands)


def expert_kernel(
    first_ref,
    inner_ref,
    outer_ref,
    upstream_ref,
    chosen_ref,
    router_ref,
    weight_ref,
    _,
    fed_ref,
    row_ref,
    combined_ref,
    pair_ref,
    gated_ref,
    gates_ref,
    gate_grad_ref,
    row_total,
    combined_total,
):
    step, steps = pl.program_id(0), pl.num_programs(0)
    index = first_ref[0] + step
    lane = lax.broadcasted_iota(jnp.int32, gates_ref.shape, 1)

    @pl.when(step == 0)
    def _():
        @pl.when(first_ref[3] > 0)
        def _():
            fed_ref[...] = inner_ref[...]

        @pl.when(first_ref[3] == 0)
        def _():
            fed_ref[...] = outer_ref[...]

        logits = dot(fed_ref[...], router_ref[...])
        chosen = chosen_ref[0] > 0.0
        logits = jnp.where(chosen, logits, MASKED)
        powers = jnp.where(chosen, jnp.exp(logits - jnp.max(logits, axis=1, keepdims=True)), 0.0)
        gates_ref[...] = powers / jnp.sum(powers, axis=1, keepdims=True)
        gate_grad_ref[...] = jnp.zeros_like(gate_grad_ref)

    gate = jnp.sum(jnp.where(lane == index, gates_ref[...], 0.0), axis=1, keepdims=True)
    gate_grad = None
    width = FF // 2
    for start in range(0, FF, width):
        stop = start + width
        gate_part = dot(fed_ref[...], weight_ref[0, :, start:stop])
        up_part = dot(fed_ref[...], weight_ref[0, :, FF + start : FF + stop])
        raw_grad = dot(upstream_ref[0], weight_ref[0, :, 2 * FF + start : 2 * FF + stop])
        sigma = jax.nn.sigmoid(gate_part)
        activated = gate_part * sigma
        hidden = activated * up_part
        part = jnp.sum(hidden * raw_grad, axis=1, keepdims=True)
        gate_grad = part if gate_grad is None else gate_grad + part
        hidden_grad = gate * raw_grad
        slope = sigma * (1.0 + gate_part * (1.0 - sigma))
        pair_ref[0, :, start:stop] = (hidden_grad * up_part * slope).astype(bf16)
        pair_ref[0, :, FF + start : FF + stop] = (hidden_grad * activated).astype(bf16)
        gated_ref[0, :, start:stop] = (gate * hidden).astype(bf16)
    gate_grad_ref[...] += jnp.where(lane == index, gate_grad, 0.0)
    combined = times_transposed(gated_ref[0], weight_ref[0, :, 2 * FF :])
    row = times_transposed(pair_ref[0], weight_ref[0, :, : 2 * FF])

    @pl.when(step == 0)
    def _():
        combined_total[...] = combined
        row_total[...] = row

    @pl.when(step > 0)
    def _():
        combined_total[...] += combined
        row_total[...] += row

    @pl.when(step == steps - 1)
    def _():
        features = row_total.shape[1]
        row_ref[:, :features] = row_total[...].astype(bf16)
        high = gate_grad_ref[...].astype(bf16)
        low = gate_grad_ref[...] - high.astype(f32)
        row_ref[:, features:] = (high.astype(f32) + pltpu.roll(low, LANES // 2, 1)).astype(bf16)
        combined_ref[0] = combined_total[...].astype(bf16)


def expert_slot(at, choices, upstream, chosen, router, weights, combined):
    length, features = choices[0].shape
    count = weights.shape[0]
    full = lambda *shape: pl.BlockSpec(shape, lambda e, at: (0,) * len(shape))
    each = lambda *shape: pl.BlockSpec((1,) + shape, lambda e, at: (e,) + (0,) * len(shape))
    there = lambda i, *shape: pl.BlockSpec(
        (1,) + shape, lambda e, at: (at[i],) + (0,) * len(shape)
    )
    return pl.pallas_call(
        expert_kernel,
        grid_spec=pltpu.PrefetchScalarGridSpec(
            num_scalar_prefetch=1,
            grid=(count,),
            in_specs=[
                full(length, features),
                full(length, features),
                there(1, length, features),
                there(2, length, LANES),
                full(features, LANES),
                each(features, 3 * FF),
                pl.BlockSpec(memory_space=pl.ANY),
            ],
            out_specs=[
                full(length, features),
                full(length, features + LANES),
                there(2, length, features),
                each(length, 2 * FF),
                each(length, FF),
            ],
            scratch_shapes=[
                pltpu.VMEM((length, LANES), f32),
                pltpu.VMEM((length, LANES), f32),
                pltpu.VMEM((length, features), f32),
                pltpu.VMEM((length, features), f32),
            ],
        ),
        out_shape=[
            jax.ShapeDtypeStruct((length, features), bf16),
            jax.ShapeDtypeStruct((length, features + LANES), bf16),
            jax.ShapeDtypeStruct(combined.shape, bf16),
            jax.ShapeDtypeStruct((count, length, 2 * FF), bf16),
            jax.ShapeDtypeStruct((count, length, FF), bf16),
        ],
        input_output_aliases={7: 2},
        compiler_params=pltpu.CompilerParams(vmem_limit_bytes=VMEM),
        cost_estimate=cost(12 * count * length * features * FF, 3.2e7),
    )(at, *choices, upstream, chosen, router, weights, combined)


def fed_grad_kernel(*refs):
    arrived = refs[:-10]
    (
        fed_ref,
        middle_ref,
        upstream_ref,
        chosen_ref,
        router_ref,
        gain_ref,
        middle_grad_ref,
        branch_ref,
        router_grad_ref,
        gain_grad_ref,
    ) = refs[-10:]
    step = pl.program_id(0)
    total = arrived[0][...].astype(f32)
    for ref in arrived[1:]:
        total = total + ref[...].astype(f32)
    features = fed_ref.shape[1]
    parts = total[:, features:]
    gate_grad = parts + pltpu.roll(parts, LANES // 2, 1)
    chosen = chosen_ref[...] > 0.0
    logits = jnp.where(chosen, dot(fed_ref[...], router_ref[...]), MASKED)
    powers = jnp.where(chosen, jnp.exp(logits - jnp.max(logits, axis=1, keepdims=True)), 0.0)
    gates = powers / jnp.sum(powers, axis=1, keepdims=True)
    gate_grad = jnp.where(chosen, gate_grad, 0.0)
    mean = jnp.sum(gates * gate_grad, axis=1, keepdims=True)
    logit_grad = (gates * (gate_grad - mean)).astype(bf16)
    fed_grad = times_transposed(logit_grad, router_ref[...]) + total[:, :features]
    scaled, inverse = norm_rows(middle_ref[...])
    back = norm_back(scaled, inverse, fed_grad * gain_ref[...])
    middle_grad = upstream_ref[...].astype(f32) + back
    middle_grad_ref[...] = middle_grad
    branch_ref[...] = middle_grad.astype(bf16)
    router_grad = contract_rows(logit_grad, fed_ref[...])
    gain_grad = jnp.sum(fed_grad * scaled, axis=0, keepdims=True)

    @pl.when(step == 0)
    def _():
        router_grad_ref[...] = router_grad
        gain_grad_ref[...] = gain_grad

    @pl.when(step > 0)
    def _():
        router_grad_ref[...] += router_grad
        gain_grad_ref[...] += gain_grad


def fed_grads(arrived, fed, middle, upstream, chosen, router, gain):
    length, features = fed.shape
    rows = length // 4
    split = lambda array: pl.BlockSpec((rows, array.shape[1]), lambda i: (i, 0))
    shapes = [
        jax.ShapeDtypeStruct((length, features), f32),
        jax.ShapeDtypeStruct((length, features), bf16),
        jax.ShapeDtypeStruct((LANES, features), f32),
        jax.ShapeDtypeStruct((1, features), f32),
    ]
    operands = [*arrived, fed, middle, upstream, chosen, router, gain]
    return pl.pallas_call(
        fed_grad_kernel,
        grid=(4,),
        in_specs=[split(a) for a in operands[:-2]] + [whole(router), whole(gain)],
        out_specs=[split(shapes[0]), split(shapes[1]), whole(shapes[2]), whole(shapes[3])],
        out_shape=shapes,
        compiler_params=pltpu.CompilerParams(vmem_limit_bytes=VMEM),
        cost_estimate=cost(1e8, 2e7),
    )(*operands)


def expert_grad_kernel(places_ref, *refs):
    slots = (len(refs) - 1) // 4
    fed, upstream, pair, gated = (refs[i * slots : (i + 1) * slots] for i in range(4))
    out_ref = refs[-1]
    inner = outer = None
    for k in range(slots):
        add_inner = contract_rows(fed[k][...], pair[k][0])
        add_outer = contract_rows(upstream[k][0], gated[k][0])
        inner = add_inner if inner is None else inner + add_inner
        outer = add_outer if outer is None else outer + add_outer
    out_ref[0, :, : 2 * FF] = inner.astype(out_ref.dtype)
    out_ref[0, :, 2 * FF :] = outer.astype(out_ref.dtype)


def expert_grads(places, fed, upstream, pairs, gated):
    length, features = fed[0].shape
    slots, count = len(pairs), pairs[0].shape[0]
    rows = features // 2
    column = pl.BlockSpec((length, rows), lambda e, i, at: (0, i))
    there = lambda k: pl.BlockSpec((1, length, rows), lambda e, i, at: (at[k], 0, i))
    each = lambda width: pl.BlockSpec((1, length, width), lambda e, i, at: (e, 0, 0))
    return pl.pallas_call(
        expert_grad_kernel,
        grid_spec=pltpu.PrefetchScalarGridSpec(
            num_scalar_prefetch=1,
            grid=(count, features // rows),
            in_specs=[column] * slots
            + [there(k) for k in range(slots)]
            + [each(2 * FF)] * slots
            + [each(FF)] * slots,
            out_specs=pl.BlockSpec((1, rows, 3 * FF), lambda e, i, at: (e, i, 0)),
        ),
        out_shape=jax.ShapeDtypeStruct((count, features, 3 * FF), bf16),
        compiler_params=pltpu.CompilerParams(vmem_limit_bytes=VMEM),
        cost_estimate=cost(6 * slots * count * length * features * FF, 8e7),
    )(places, *fed, *[upstream] * slots, *pairs, *gated)


def exchange(value, k):
    return lax.ppermute(value, "shard", [(i, i ^ k) for i in range(4)])


def inside(place):
    return (place == 1) | (place == 2)


def sources(place, count):
    if count != 4:
        return [place ^ k for k in range(count)]
    middle = inside(place)
    order = ((1, 3), (2, 1), (3, 2))
    return [place] + [place ^ jnp.where(middle, mid, out) for out, mid in order]


def after(value, *earlier):
    return lax.optimization_barrier((value, earlier))[0]


def line_gather(rows, place, count):
    if count != 4:
        everything = lax.all_gather(rows, "shard", axis=0)
        for source in sources(place, count):
            yield (pick(everything, source),) * 2
            yield
        return
    middle = inside(place)
    near = exchange(rows, 1)
    across = lax.ppermute(rows, "shard", [(1, 2), (2, 1)])
    made = yield rows, rows
    yield
    near_on, across_on = after((near, across), made)
    second_inside = lax.ppermute(near_on, "shard", [(1, 2), (2, 1)])
    second_outside = lax.ppermute(across_on, "shard", [(1, 0), (2, 3)])
    yield across, near
    yield
    third_outside = lax.ppermute(second_inside, "shard", [(1, 0), (2, 3)])
    yield near, second_outside
    yield
    yield second_inside, third_outside
    yield


def scatter_all(parts, place, count):
    stacked = jnp.stack(parts)
    ordered = jnp.stack([pick(stacked, place ^ d) for d in range(count)])
    return lax.psum_scatter(ordered, "shard", scatter_dimension=0, tiled=False)


def line_send(part, k):
    ways = {
        1: ([(0, 1), (3, 2)], [(1, 2), (2, 1)]),
        2: ([(0, 2), (3, 1)], [(1, 0), (2, 3)]),
        3: ([(0, 3), (3, 0)], [(1, 3), (2, 0)]),
    }
    return [lax.ppermute(part, "shard", way) for way in ways[k]]


def total_of(kept, arrived):
    total = kept.astype(f32)
    for part in arrived:
        total = total + part.astype(f32)
    return total


def hop(value, bit):
    return lax.ppermute(value, "rep", [(i, i ^ bit) for i in range(8)])


def pick(stacked, index, axis=0):
    return lax.dynamic_index_in_dim(stacked, index, axis, False)


def gather_near(mine):
    return jnp.stack([exchange(mine, k) for k in range(1, 4)])


def send_pairs(near):
    return [hop(near, 2 * m) for m in range(1, 4)]


def join_pairs(local, parts, core, spot):
    own = jnp.stack(
        [
            jnp.concatenate([local(spot ^ m, core)[None], part])
            for m, part in enumerate(parts)
        ]
    )
    return own, hop(own, 1)


def join_chip(term, special):
    kept, given = term
    return (kept.astype(f32) + hop(given, 1).astype(f32)).astype(bf16) if special else kept


def place_kernel(at_ref, own_ref, other_ref, attend_ref, output_ref):
    half = own_ref.shape[1]
    query, key = QUERY_HEADS * HEAD_WIDTH, KEY_VALUE_HEADS * HEAD_WIDTH
    for m in range(PAIRS):
        pair = at_ref[0] ^ m
        for side, ref in enumerate((own_ref, other_ref)):
            rows = pl.ds(pl.multiple_of((at_ref[1] ^ side) * half, half), half)
            start = 0
            for out_ref, base, width in (
                (attend_ref, 0, PAIR_QUERY),
                (attend_ref, query, PAIR_KEY),
                (attend_ref, query + key, PAIR_KEY),
                (output_ref, 0, PAIR_QUERY),
            ):
                columns = pl.ds(pl.multiple_of(base + pair * width, LANES), width)
                out_ref[rows, columns] = ref[m, :, start : start + width].astype(f32)
                start += width


def finish_pairs(plane, core, spot):
    piece = plane[0].astype(f32)
    for k in range(1, 4):
        piece = piece + exchange(plane[k], k).astype(f32)
    piece = piece.astype(plane.dtype)
    mine = jnp.stack([piece] + [hop(piece, 2 * m) for m in range(1, 4)])
    other = hop(mine, 1)
    rows = 2 * piece.shape[0]
    return pl.pallas_call(
        place_kernel,
        grid_spec=pltpu.PrefetchScalarGridSpec(
            num_scalar_prefetch=1,
            grid=(1,),
            in_specs=[whole(mine), whole(other)],
            out_specs=[
                pl.BlockSpec((rows, PAIRS * PAIR_WIDTH), lambda i, at: (0, 0)),
                pl.BlockSpec((rows, PAIRS * PAIR_QUERY), lambda i, at: (0, 0)),
            ],
        ),
        out_shape=[
            jax.ShapeDtypeStruct((rows, PAIRS * PAIR_WIDTH), f32),
            jax.ShapeDtypeStruct((rows, PAIRS * PAIR_QUERY), f32),
        ],
        compiler_params=pltpu.CompilerParams(vmem_limit_bytes=VMEM),
        cost_estimate=cost(1e6, 1e7),
    )(jnp.stack([spot, core]).astype(jnp.int32), mine, other)


def reduce_terms(terms):
    part = lax.psum_scatter(terms, "shard", scatter_dimension=1, tiled=False)
    return lax.psum(part, "rep")


def body(
    inputs,
    query_key_value_weight,
    output_weight,
    attention_gain,
    feed_gain,
    router_weight,
    expert_weight,
    routes,
    cotangent,
    *,
    places,
    ranks,
):
    length, features = inputs.shape
    own = query_key_value_weight.shape[0]
    local = expert_weight.shape[0]
    query_width = QUERY_HEADS * HEAD_WIDTH
    key_width = KEY_VALUE_HEADS * HEAD_WIDTH
    place, rank = lax.axis_index("shard"), lax.axis_index("rep")

    special = places == 4 and ranks == 8
    half = own // 2
    base, core, spot = (place, rank % 2, rank // 2) if special else (0, 0, 0)

    projection = query_key_value_weight

    def projection_share(pair, side):
        rows = lax.dynamic_slice_in_dim(projection, side * half, half, 0)
        return jnp.concatenate(
            [
                lax.dynamic_slice_in_dim(rows, pair * PAIR_QUERY, PAIR_QUERY, 1),
                lax.dynamic_slice_in_dim(rows, query_width + pair * PAIR_KEY, PAIR_KEY, 1),
                lax.dynamic_slice_in_dim(
                    rows, query_width + key_width + pair * PAIR_KEY, PAIR_KEY, 1
                ),
            ],
            axis=1,
        )

    def output_share(pair, side):
        return lax.dynamic_slice(
            output_weight, (side * half, pair * PAIR_QUERY), (half, PAIR_QUERY)
        )

    chosen_own = jnp.sum(
        (routes[:, :, None] == jnp.arange(EXPERTS, dtype=jnp.int32)).astype(f32), axis=1
    )
    small = jnp.concatenate(
        [
            attention_gain.reshape(-1),
            feed_gain.reshape(-1),
            router_weight.reshape(-1),
            chosen_own.astype(bf16).reshape(-1),
        ]
    )
    if special:
        extra = -(-small.size // (16 * PAIR_WIDTH)) * 16
        below = jnp.pad(small, (0, extra * PAIR_WIDTH - small.size)).reshape(extra, PAIR_WIDTH)
        near = gather_near(jnp.concatenate([projection_share(spot, core), below]))
        projection_near = near[:, :half]
        small_slots = jnp.concatenate(
            [small[None], near[:, half:].reshape(3, -1)[:, : small.size]]
        )
        small_all = jnp.stack([pick(small_slots, place ^ k) for k in range(4)])
        projection_sent = send_pairs(projection_near)
        output_near = gather_near(after(output_share(spot, core), near))
        output_sent = send_pairs(after(output_near, projection_sent))
        attend_weights = join_pairs(
            projection_share, [projection_near] + projection_sent, core, spot
        )
        output_weights = join_pairs(output_share, [output_near] + output_sent, core, spot)
        cotangent_sent = after(cotangent, near)
    else:
        gathered = lax.all_gather(projection, "shard", axis=0)
        gathered_output = lax.all_gather(output_weight, "shard", axis=0)
        columns = jnp.concatenate(
            [
                gathered[:, :, :query_width].reshape(places, own, PAIRS, PAIR_QUERY),
                gathered[:, :, query_width : query_width + key_width].reshape(
                    places, own, PAIRS, PAIR_KEY
                ),
                gathered[:, :, query_width + key_width :].reshape(places, own, PAIRS, PAIR_KEY),
            ],
            axis=3,
        ).transpose(2, 0, 1, 3)
        attend_weights = (columns[:, :, :half], columns[:, :, half:])
        columns = gathered_output.reshape(places, own, PAIRS, PAIR_QUERY).transpose(2, 0, 1, 3)
        output_weights = (columns[:, :, :half], columns[:, :, half:])
        small_all = lax.all_gather(small, "shard", axis=0)
        cotangent_sent = cotangent

    upstream_all = lax.all_gather(cotangent_sent, "shard", axis=0)

    tables = rotary_tables(length, PAIR_QUERY + PAIR_KEY)
    residual = inputs.astype(f32)
    scaled_in, inverse_in = norm_rows(residual)
    attention_scale = small_all[:, :own].reshape(features).astype(f32)
    feed_scale = small_all[:, own : 2 * own].reshape(features).astype(f32)
    router_full = small_all[:, 2 * own : (2 + EXPERTS) * own].reshape(features, EXPERTS)
    chosen_all = small_all[:, (2 + EXPERTS) * own :].reshape(places, length, EXPERTS).astype(f32)
    normed = (scaled_in * attention_scale).astype(bf16)
    where = jnp.stack([base, core]).astype(jnp.int32)
    mixed, qkv, lse = attend_forward(where, normed, attend_weights, tables)
    middle, fed = middle_rows(where, mixed, output_weights, inputs, feed_scale[None])
    router_wide = jnp.pad(router_full, ((0, 0), (0, LANES - EXPERTS)))
    chosen_wide = jnp.pad(chosen_all, ((0, 0), (0, 0), (0, LANES - EXPERTS)))
    rows, pair_grads, gated = [], [], []
    combined = jnp.zeros((places, length, features), bf16)
    order = sources(place, places)
    middle_place = inside(place).astype(jnp.int32)
    fed_slots, rows_come, arriving = [], [], line_gather(fed, place, places)
    for k, source in enumerate(order):
        index = jnp.zeros_like(source) if k == 0 else source
        at = jnp.stack([place * local, index, source, middle_place]).astype(jnp.int32)
        rows_up = cotangent[None] if k == 0 else upstream_all
        fed_k, row, combined, *kept = expert_slot(
            at, next(arriving), rows_up, chosen_wide, router_wide, expert_weight, combined
        )
        for held, value in zip((fed_slots, rows, pair_grads, gated), (fed_k, row, *kept)):
            held.append(value)
        arriving.send((row, upstream_all))
        if special and k:
            rows_come += line_send(row, k)
    expert_term = expert_grads(
        jnp.stack(order).astype(jnp.int32),
        fed_slots,
        upstream_all,
        pair_grads,
        gated,
    )
    expert_total = lax.psum(expert_term, "rep").astype(f32)

    if special:
        arrived = [rows[0], *rows_come]
    else:
        arrived = [scatter_all(rows, place, places)]
    arrived = after(arrived, expert_term)

    combined = lax.all_to_all(after(combined, arrived), "shard", 0, 0)

    def rest():
        chosen = jnp.pad(chosen_own, ((0, 0), (0, LANES - EXPERTS)))
        middle_grad, branch_grad, router_term, feed_term = fed_grads(
            arrived, fed, middle, cotangent, chosen, router_wide, feed_scale[None]
        )
        normed_grad = jnp.zeros((length, features), f32)
        terms, chips = [None] * PAIRS, [None] * PAIRS
        steps = (3, 1, 2, 0)
        for i, m in enumerate(steps):
            ready = [chips[steps[i - 2]]] if i >= 2 else []
            own_term, other_term, normed_grad = attend_backward(
                where,
                m,
                after(branch_grad, *ready),
                output_weights,
                (mixed, qkv, lse),
                normed,
                attend_weights,
                tables,
                normed_grad,
            )
            terms[m] = (own_term, other_term)
            if i >= 1:
                chips[steps[i - 1]] = join_chip(terms[steps[i - 1]], special)
        if special:
            chips[0] = join_chip(terms[0], special)
            plane = chips[0].astype(f32)
            for m in (3, 1, 2):
                plane = plane + hop(chips[m], 2 * m).astype(f32)
            attend_total, output_total = finish_pairs(plane.astype(bf16), core, spot)
        else:
            stacked = jnp.stack([jnp.stack(term) for term in terms])
            weight_sums = reduce_terms(stacked.transpose(0, 2, 1, 3, 4))
            weight_sums = weight_sums.reshape(PAIRS, own, -1).transpose(1, 0, 2).astype(f32)
            attend_total = jnp.concatenate(
                [
                    weight_sums[:, :, :PAIR_QUERY].reshape(own, query_width),
                    weight_sums[:, :, PAIR_QUERY : PAIR_QUERY + PAIR_KEY].reshape(own, key_width),
                    weight_sums[:, :, PAIR_QUERY + PAIR_KEY : PAIR_WIDTH].reshape(own, key_width),
                ],
                axis=1,
            )
            output_total = weight_sums[:, :, PAIR_WIDTH:].reshape(own, query_width)

        attention_term = jnp.sum(normed_grad * scaled_in, axis=0)
        input_grad = (
            middle_grad + norm_back(scaled_in, inverse_in, normed_grad * attention_scale)
        ).astype(bf16)

        small_terms = jnp.concatenate(
            [attention_term[None], feed_term, router_term[:EXPERTS]], axis=0
        )
        if special:
            for axis, bit in (("rep", 1), ("rep", 2), ("rep", 4), ("shard", 1), ("shard", 2)):
                size = 8 if axis == "rep" else 4
                pairs = [(i, i ^ bit) for i in range(size)]
                small_terms = small_terms + lax.ppermute(small_terms, axis, pairs)
        else:
            small_terms = lax.psum(small_terms, ("rep", "shard"))
        small_sums = lax.dynamic_slice_in_dim(small_terms, place * own, own, 1)
        return (
            input_grad,
            attend_total,
            output_total,
            small_sums[0],
            small_sums[1],
            small_sums[2:].T,
        )

    shapes = (
        ((length, features), bf16),
        (query_key_value_weight.shape, f32),
        (output_weight.shape, f32),
        ((own,), f32),
        ((own,), f32),
        ((own, EXPERTS), f32),
    )
    empty = lambda: tuple(jnp.zeros(*shape) for shape in shapes)
    grads = lax.cond(routes[0, 0] >= 0, rest, empty)
    activations = (middle + jnp.sum(combined.astype(f32), axis=0)).astype(bf16)
    return (activations, *grads, expert_total)


def solution(mesh):
    in_specs = (
        P(("rep", "shard"), None),
        P("shard", None),
        P("shard", None),
        P("shard"),
        P("shard"),
        P("shard", None),
        P("shard", None, None),
        P(("rep", "shard"), None),
        P(("rep", "shard"), None),
    )
    out_specs = (
        P(("rep", "shard"), None),
        P(("rep", "shard"), None),
        P("shard", None),
        P("shard", None),
        P("shard"),
        P("shard"),
        P("shard", None),
        P("shard", None, None),
    )
    run = functools.partial(body, places=mesh.shape["shard"], ranks=mesh.shape["rep"])
    return jax.shard_map(run, mesh=mesh, in_specs=in_specs, out_specs=out_specs, check_vma=False)
```

time: 908 us -> 766 us (0.84)
  local copies, waits for them, and re-layouts: 95.3 us -> 35.5 us
  starting transfers between devices: 127 us -> 70.3 us
  other arithmetic: 111 us -> 76.1 us
  Pallas kernels: 277 us -> 301 us
  waiting for transfers between devices: 269 us -> 258 us
    ppermute x1 -> x6, waiting for transfers between devices: 0.01 us -> 50.1 us  [the longest x5 50.1 us: rest(): small_terms = small_terms + lax.ppermute(small_terms, axis, pairs)]
    ppermute x19 -> x10, waiting for transfers between devices: 18.3 us -> 56.6 us  [exchange(): return lax.ppermute(value, 'shard', [(i, i ^ k) for i in range(4)])]
    ppermute x1, waiting for transfers between devices: 34.4 us -> 0.01 us  [line_gather(): second_outside = lax.ppermute(across_on, 'shard', [(1, 0), (2, 3)])]
    psum x1, waiting for transfers between devices: 47.7 us -> 16 us  [body(): expert_total = lax.psum(expert_term, 'rep').astype(f32)]
    ppermute x18 -> x6, starting transfers between devices: 52.4 us -> 23 us  [line_send(): return [lax.ppermute(part, 'shard', way) for way in ways[k]]]
    ppermute x19 -> x10, starting transfers between devices: 39.8 us -> 17.4 us  [exchange(): return lax.ppermute(value, 'shard', [(i, i ^ k) for i in range(4)])]
    optimization_barrier x8 -> x0, local copies, waits for them, and re-layouts: 18.6 us -> none  [after(): return lax.optimization_barrier((value, earlier))[0]]
    pallas_call x9 -> x8, Pallas kernels: 107 us -> 124 us  [the longest x4 68.7 us: attend_backward(): pl.pallas_call(attend_backward_kernel, grid_spec=pltpu.PrefetchScalarGrid...]
  transfers between devices with their start and end apart: 76 -> 47, of which waited for: 21 -> 19; matrix products, arithmetic and copies ran while one was open for 20% -> 10% of each run, Pallas kernels for 31% -> 40%
where the time goes in v2:
time: 766 us; the launch traced here: 758 us
  Pallas kernels  301 us (39%)
  waiting for transfers between devices  258 us (34%)
  other arithmetic  76.1 us (10%)
  starting transfers between devices  70.3 us (9%)
  local copies, waits for them, and re-layouts  35.5 us (5%)
  between operations  16 us (2%)
    pallas_call x4, Pallas kernels, expert_slot(): pl.pallas_call(expert_kernel, grid_spec=pltpu.PrefetchScalarGridSpec(num_...  128 us
    ppermute x19, waiting for transfers between devices, hop(): return lax.ppermute(value, 'rep', [(i, i ^ bit) for i in range(8)])  110 us
    pallas_call x4, Pallas kernels, attend_backward(): pl.pallas_call(attend_backward_kernel, grid_spec=pltpu.PrefetchScalarGrid...  68.7 us
    ppermute x10, waiting for transfers between devices, exchange(): return lax.ppermute(value, 'shard', [(i, i ^ k) for i in range(4)])  56.6 us
    ppermute x5, waiting for transfers between devices, rest(): small_terms = small_terms + lax.ppermute(small_terms, axis, pairs)  50.1 us
    pallas_call x1, Pallas kernels, expert_grads(): pl.pallas_call(expert_grad_kernel, grid_spec=pltpu.PrefetchScalarGridSpec...  48.7 us
    pallas_call x1, Pallas kernels, attend_forward(): pl.pallas_call(attend_forward_kernel, grid_spec=pltpu.PrefetchScalarGridS...  27.2 us
    ppermute x6, waiting for transfers between devices, line_send(): return [lax.ppermute(part, 'shard', way) for way in ways[k]]  24.6 us
  transfers between devices with their start and end apart: 47, of which 19 were waited for; matrix products, arithmetic and copies ran while one was open for 10% of the time, Pallas kernels for 40%

profile of v2, /device:TPU:0, one launch (start us, length us, event | category | flops | bytes accessed | tf_op | source)
XLA Modules:
  0.0 757.6 jit_solution(4815780699181194597)
XLA Ops:
  12.6 2.3 fusion.12
  14.9 2.1 fusion.13
  17.8 5.0 collective-permute-start.21
  29.7 1.9 dynamic-slice_bitcast_fusion.2
  33.2 14.3 %collective-permute-done.20 = bf16[224,640]{1,0:T(8,128)(2,1)} collective-permute-done((bf16[224,640]{1,0:T(8,128)(2,1)}, bf16[224,640]{1,0:T(8,128)(2,1)}, u32[]{:S(2)}, u32[]{:S(2)}) %collective-permute-start.20) | collective-permute-done | bytes 286752 | tf_op jit(solution)/shard_map/ppermute | solution.py:557
  48.8 2.5 collective-permute-start.28
  51.4 2.5 collective-permute-start.24
  56.4 15.5 %collective-permute-done.24 = bf16[3,192,640]{2,1,0:T(8,128)(2,1)} collective-permute-done((bf16[3,192,640]{2,1,0:T(8,128)(2,1)S(1)}, bf16[3,192,640]{2,1,0:T(8,128)(2,1)}, u32[]{:S(2)}, u32[]{:S(2)}) %collective-permute-start.24) | collective-permute-done | bytes 737312 | tf_op jit(solution)/shard_map/ppermute | solution.py:623
  72.0 1.9 collective-permute-start.26
  75.1 10.2 %collective-permute-done.23 = bf16[3,192,640]{2,1,0:T(8,128)(2,1)} collective-permute-done((bf16[3,192,640]{2,1,0:T(8,128)(2,1)S(1)}, bf16[3,192,640]{2,1,0:T(8,128)(2,1)}, u32[]{:S(2)}, u32[]{:S(2)}) %collective-permute-start.23) | collective-permute-done | bytes 737312 | tf_op jit(solution)/shard_map/ppermute | solution.py:623
  86.7 2.2 pad_maximum_fusion.2.own_ref
  90.3 2.5 collective-permute-start.31
  98.9 5.6 collective-permute-done.31
  104.5 7.9 %collective-permute-done.30 = bf16[3,192,384]{2,1,0:T(8,128)(2,1)} collective-permute-done((bf16[3,192,384]{2,1,0:T(8,128)(2,1)S(1)}, bf16[3,192,384]{2,1,0:T(8,128)(2,1)}, u32[]{:S(2)}, u32[]{:S(2)}) %collective-permute-start.30) | collective-permute-done | bytes 442400 | tf_op jit(solution)/shard_map/ppermute | solution.py:623
  116.2 2.6 convert_multiply_fusion
  118.8 27.2 %shard_map.152 = (bf16[4,512,384]{2,1,0:T(8,128)(2,1)S(1)}, bf16[4,512,640]{2,1,0:T(8,128)(2,1)}, f32[4,8,512]{2,1,0:T(8,128)}) custom-call(s32[2]{0:T(128)S(1)} %pad_add_fusion.1.at_ref, bf16[512,1536]{1,0:T(8,128)(2,1)} %get-tuple-element.300.normed_ref, bf16[4,4,192,640]{3,2,1,0:T(8,128)(2,1)} %pad_maximum_fusion.2.own_ref, ...), custom_call_target="tpu_custom_call" | custom-call | flops 20000000000 | bytes 20000000 | tf_op jit(solution)/shard_map/pallas_call | solution.py:153
  146.0 10.5 %shard_map.153 = (f32[512,1536]{1,0:T(8,128)}, bf16[512,1536]{1,0:T(8,128)(2,1)}) custom-call(s32[2]{0:T(128)S(1)} %pad_add_fusion.1.at_ref, bf16[4,512,384]{2,1,0:T(8,128)(2,1)S(1)} %get-tuple-element.174.mixed_ref, bf16[4,4,192,384]{3,2,1,0:T(8,128)(2,1)S(1)} %pad_maximum_fusion.3.own_ref, bf16[4,4,192,384]{3,2,1,0:T(8,128)(2,1)} %collective-permute-done.32.other_ref, ...), custom_call_target="tpu_custom_call" | custom-call | flops 2400000000 | bytes 10000000 | tf_op jit(solution)/shard_map/pallas_call | solution.py:191
  156.5 1.8 collective-permute-start.34
  158.4 3.4 collective-permute-start.33
  161.8 3.1 broadcast_in_dim.56._
  164.8 32.6 %shard_map.154 = (bf16[512,1536]{1,0:T(8,128)(2,1)}, bf16[512,1664]{1,0:T(8,128)(2,1)}, bf16[4,512,1536]{2,1,0:T(8,128)(2,1)}, bf16[4,512,1024]{2,1,0:T(8,128)(2,1)}, bf16[4,512,512]{2,1,0:T(8,128)(2,1)}) custom-call(s32[4]{0:T(128)} %add_add_fusion.1.first_ref, ...), custom_call_target="tpu_custom_call", output_to_operand_aliasing={{2}: (7, {})} | custom-call | flops 19327352832 | bytes 32000000 | tf_op jit(solution)/shard_map/pallas_call | solution.py:407
  197.4 7.9 %collective-permute-done.33.outer_ref.inner_ref = bf16[512,1536]{1,0:T(8,128)(2,1)} collective-permute-done((bf16[512,1536]{1,0:T(8,128)(2,1)}, bf16[512,1536]{1,0:T(8,128)(2,1)}, u32[]{:S(2)}, u32[]{:S(2)}) %collective-permute-start.33) | collective-permute-done | bytes 1572896 | tf_op jit(solution)/shard_map/ppermute | solution.py:557
  205.4 1.9 collective-permute-start.35
  208.5 32.0 %shard_map.155 = (bf16[512,1536]{1,0:T(8,128)(2,1)}, bf16[512,1664]{1,0:T(8,128)(2,1)}, bf16[4,512,1536]{2,1,0:T(8,128)(2,1)}, bf16[4,512,1024]{2,1,0:T(8,128)(2,1)}, bf16[4,512,512]{2,1,0:T(8,128)(2,1)}) custom-call(s32[4]{0:T(128)} %add_add_fusion.3.first_ref, ...), custom_call_target="tpu_custom_call", output_to_operand_aliasing={{2}: (7, {})} | custom-call | flops 19327352832 | bytes 32000000 | tf_op jit(solution)/shard_map/pallas_call | solution.py:407
  240.5 1.9 collective-permute-start.39
  242.4 7.4 collective-permute-start.38
  251.0 31.7 %shard_map.156 = (bf16[512,1536]{1,0:T(8,128)(2,1)}, bf16[512,1664]{1,0:T(8,128)(2,1)}, bf16[4,512,1536]{2,1,0:T(8,128)(2,1)}, bf16[4,512,1024]{2,1,0:T(8,128)(2,1)}, bf16[4,512,512]{2,1,0:T(8,128)(2,1)}) custom-call(s32[4]{0:T(128)} %add_add_fusion.2.first_ref, ...), custom_call_target="tpu_custom_call", output_to_operand_aliasing={{2}: (7, {})} | custom-call | flops 19327352832 | bytes 32000000 | tf_op jit(solution)/shard_map/pallas_call | solution.py:407
  284.1 7.8 %collective-permute-start.40 = (bf16[512,1664]{1,0:T(8,128)(2,1)}, bf16[512,1664]{1,0:T(8,128)(2,1)}, u32[]{:S(2)}, u32[]{:S(2)}) collective-permute-start(bf16[512,1664]{1,0:T(8,128)(2,1)} %get-tuple-element.188), channel_id=1, source_target_pairs={{0,2},{3,1},{4,6},{7,5},{8,10},{11,9},{12,14},{15,13},{16,18},{19,... | collective-permute-start | bytes 5111816 | tf_op jit(solution)/shard_map/ppermute | solution.py:612
  291.9 31.6 %shard_map.157 = (bf16[512,1536]{1,0:T(8,128)(2,1)}, bf16[512,1664]{1,0:T(8,128)(2,1)}, bf16[4,512,1536]{2,1,0:T(8,128)(2,1)}, bf16[4,512,1024]{2,1,0:T(8,128)(2,1)}, bf16[4,512,512]{2,1,0:T(8,128)(2,1)}) custom-call(s32[4]{0:T(128)} %add_add_fusion.first_ref, bf16[512,1536]{1,0:T(8,128)(2,1)} %collective-permute-done.35.inner_ref, ...), custom_call_target="tpu_custom_call", output_to_operand_aliasing={{2}: (7, {})} | custom-call | flops 19327352832 | bytes 32000000 | tf_op jit(solution)/shard_map/pallas_call | solution.py:407
  324.8 3.5 collective-permute-start.42
  328.2 48.7 %shard_map.158 = bf16[4,1536,1536]{2,1,0:T(8,128)(2,1)} custom-call(s32[4]{0:T(128)} %pad_add_fusion.2.places_ref, bf16[512,1536]{1,0:T(8,128)(2,1)} %get-tuple-element.190.refs_0_, bf16[512,1536]{1,0:T(8,128)(2,1)} %get-tuple-element.191.refs_1_, bf16[512,1536]{1,0:T(8,128)(2,1)} %get-tuple-element.192.refs_2_, ...), custom_call_target="tpu_custom_call" | custom-call | flops 38654705664 | bytes 80000000 | tf_op jit(solution)/shard_map/pallas_call | solution.py:539
  376.9 24.6 %collective-permute-done.43 = bf16[512,1664]{1,0:T(8,128)(2,1)} collective-permute-done((bf16[512,1664]{1,0:T(8,128)(2,1)}, bf16[512,1664]{1,0:T(8,128)(2,1)}, u32[]{:S(2)}, u32[]{:S(2)}) %collective-permute-start.43) | collective-permute-done | bytes 1703968 | tf_op jit(solution)/shard_map/ppermute | solution.py:612
  401.6 5.2 all-to-all-start
  409.8 297.5 %conditional.1 = (bf16[512,1536]{1,0:T(8,128)(2,1)}, f32[384,2560]{1,0:T(8,128)}, f32[384,1536]{1,0:T(8,128)}, f32[384]{0:T(512)}, f32[384]{0:T(512)}, /*index=5*/f32[384,16]{0,1:T(8,128)}) conditional(s32[]{:T(128)} %bitcast.45, () %tuple.30, (f32[512,16]{0,1:T(8,128)}, bf16[4,384]{1,0:T(4,128)(2,1)}, bf16[512,1664]{1,0:T(8,128)(2,1)}, ...), branch_computations={%region_3.4_spmd, %region_4.7_spmd} | conditional | flops 36132687872 | bytes 241758896 | solution.py:924
  411.6 1.6 copy.36
  413.2 1.7 pad.13.refs_10_
  414.9 12.0 %branch_1_fun.6 = (f32[512,1536]{1,0:T(8,128)}, bf16[512,1536]{1,0:T(8,128)(2,1)}, f32[128,1536]{1,0:T(8,128)}, f32[1,1536]{1,0:T(1,128)}) custom-call(bf16[512,1664]{1,0:T(8,128)(2,1)} %get-tuple-element.72.refs_0_, bf16[512,1664]{1,0:T(8,128)(2,1)} %get-tuple-element.73.refs_1_, bf16[512,1664]{1,0:T(8,128)(2,1)} %get-tuple-element.74.refs_2_, ...), custom_call_target="tpu_custom_call" | custom-call | flops 100000000 | bytes 20000000 | tf_op jit(solution)/shard_map/cond/branch_1_fun/pallas_call | solution.py:507
  426.9 2.6 copy.38.sine_ref
  429.5 2.6 copy.37.cosine_ref
  432.1 2.1 broadcast_14_total_ref.0.total_ref
  434.2 17.1 %branch_1_fun.7 = (bf16[4,192,1024]{2,1,0:T(8,128)(2,1)}, bf16[4,192,1024]{2,1,0:T(8,128)(2,1)}, f32[512,1536]{1,0:T(8,128)}) custom-call(s32[2]{0:T(128)S(1)} %copy-done.25, bf16[512,1536]{1,0:T(8,128)(2,1)} %get-tuple-element.105.branch_ref, bf16[4,4,192,384]{3,2,1,0:T(8,128)(2,1)} %get-tuple-element.89.own_output_ref, ...), custom_call_target="tpu_custom_call", output_to_operand_aliasing={{2}: (12, {})} | custom-call | flops 8999999488 | bytes 15000000 | tf_op jit(solution)/shard_map/cond/branch_1_fun/pallas_call | solution.py:297
  451.3 17.3 %branch_1_fun.8 = (bf16[4,192,1024]{2,1,0:T(8,128)(2,1)}, bf16[4,192,1024]{2,1,0:T(8,128)(2,1)}, f32[512,1536]{1,0:T(8,128)}) custom-call(s32[2]{0:T(128)S(1)} %copy-done.25, bf16[512,1536]{1,0:T(8,128)(2,1)} %get-tuple-element.105.branch_ref, bf16[4,4,192,384]{3,2,1,0:T(8,128)(2,1)} %get-tuple-element.89.own_output_ref, ...), custom_call_target="tpu_custom_call", output_to_operand_aliasing={{2}: (12, {})} | custom-call | flops 8999999488 | bytes 15000000 | tf_op jit(solution)/shard_map/cond/branch_1_fun/pallas_call | solution.py:297
  469.1 3.8 add_convert_fusion.4
  472.9 17.4 %branch_1_fun.9 = (bf16[4,192,1024]{2,1,0:T(8,128)(2,1)}, bf16[4,192,1024]{2,1,0:T(8,128)(2,1)}, f32[512,1536]{1,0:T(8,128)}) custom-call(s32[2]{0:T(128)S(1)} %copy-done.25, bf16[512,1536]{1,0:T(8,128)(2,1)} %get-tuple-element.105.branch_ref, bf16[4,4,192,384]{3,2,1,0:T(8,128)(2,1)} %get-tuple-element.89.own_output_ref, ...), custom_call_target="tpu_custom_call", output_to_operand_aliasing={{2}: (12, {})} | custom-call | flops 8999999488 | bytes 15000000 | tf_op jit(solution)/shard_map/cond/branch_1_fun/pallas_call | solution.py:297
  490.3 2.6 collective-permute-start.3
  493.0 4.0 add_convert_fusion.5
  497.3 17.0 %branch_1_fun.10 = (bf16[4,192,1024]{2,1,0:T(8,128)(2,1)}, bf16[4,192,1024]{2,1,0:T(8,128)(2,1)}, f32[512,1536]{1,0:T(8,128)}) custom-call(s32[2]{0:T(128)S(1)} %copy-done.25, bf16[512,1536]{1,0:T(8,128)(2,1)} %get-tuple-element.105.branch_ref, bf16[4,4,192,384]{3,2,1,0:T(8,128)(2,1)} %get-tuple-element.89.own_output_ref, ...), custom_call_target="tpu_custom_call", output_to_operand_aliasing={{2}: (12, {})} | custom-call | flops 8999999488 | bytes 15000000 | tf_op jit(solution)/shard_map/cond/branch_1_fun/pallas_call | solution.py:297
  514.3 3.7 add_convert_fusion.1
  519.3 12.1 %collective-permute-done.3 = bf16[4,192,1024]{2,1,0:T(8,128)(2,1)} collective-permute-done((bf16[4,192,1024]{2,1,0:T(8,128)(2,1)}, bf16[4,192,1024]{2,1,0:T(8,128)(2,1)}, u32[]{:S(2)}, u32[]{:S(2)}) %collective-permute-start.3) | collective-permute-done | bytes 1572896 | tf_op jit(solution)/shard_map/cond/branch_1_fun/ppermute | solution.py:623
  531.4 58.0 %collective-permute-done.4 = bf16[4,192,1024]{2,1,0:T(8,128)(2,1)} collective-permute-done((bf16[4,192,1024]{2,1,0:T(8,128)(2,1)}, bf16[4,192,1024]{2,1,0:T(8,128)(2,1)}, u32[]{:S(2)}, u32[]{:S(2)}) %collective-permute-start.4) | collective-permute-done | bytes 1572896 | tf_op jit(solution)/shard_map/cond/branch_1_fun/ppermute | solution.py:623
  590.3 5.3 add_convert_fusion
  597.2 2.4 collective-permute-start.9
  600.7 6.2 collective-permute-done.7
  606.9 11.2 %collective-permute-done.9 = bf16[192,1024]{1,0:T(8,128)(2,1)S(1)} collective-permute-done((bf16[192,1024]{1,0:T(8,128)(2,1)S(1)}, bf16[192,1024]{1,0:T(8,128)(2,1)S(1)}, u32[]{:S(2)}, u32[]{:S(2)}) %collective-permute-start.9) | collective-permute-done | bytes 393248 | tf_op jit(solution)/shard_map/cond/branch_1_fun/ppermute | solution.py:557
  618.1 15.9 %collective-permute-done.8 = bf16[192,1024]{1,0:T(8,128)(2,1)S(1)} collective-permute-done((bf16[192,1024]{1,0:T(8,128)(2,1)S(1)}, bf16[192,1024]{1,0:T(8,128)(2,1)S(1)}, u32[]{:S(2)}, u32[]{:S(2)}) %collective-permute-start.8) | collective-permute-done | bytes 393248 | tf_op jit(solution)/shard_map/cond/branch_1_fun/ppermute | solution.py:557
  639.7 37.7 %collective-permute-done.15 = f32[18,1536]{1,0:T(8,128)} collective-permute-done((f32[18,1536]{1,0:T(8,128)}, f32[18,1536]{1,0:T(8,128)}, u32[]{:S(2)}, u32[]{:S(2)}) %collective-permute-start.15) | collective-permute-done | bytes 110624 | tf_op jit(solution)/shard_map/cond/branch_1_fun/ppermute | solution.py:902
  682.3 5.1 collective-permute-done.16
  687.5 5.1 collective-permute-done.17
  693.7 3.9 add_convert_fusion.3
  697.6 2.2 collective-permute-done.18
  701.0 6.0 branch_1_fun.11
  707.3 4.3 convert_reduce_fusion
  713.2 16.0 %all-reduce.6.cloned.1.call-done = bf16[4,1536,1536]{2,1,0:T(8,128)(2,1)} async-done(((bf16[4,1536,1536]{2,1,0:T(8,128)(2,1)}), bf16[4,1536,1536]{2,1,0:T(8,128)(2,1)}) %all-reduce.6.cloned.1.call-update) | async-done | bytes 18874384 | tf_op jit(solution)/shard_map/psum | solution.py:836
  729.2 21.0 %convert_element_type.170 = f32[4,1536,1536]{2,1,0:T(8,128)} convert(bf16[4,1536,1536]{2,1,0:T(8,128)(2,1)} %all-reduce.6.cloned.1.call-done) | non-fusion elementwise | flops 9437184 | bytes 56623104 | tf_op jit(solution)/shard_map/convert_element_type | solution.py:836
  (200 shorter events, 61.5 us)
Async XLA Ops:
  7.2 18.9 %copy-start.6 = (bf16[512,1536]{1,0:T(8,128)(2,1)S(1)}, bf16[512,1536]{1,0:T(8,128)(2,1)}, u32[]{:S(2)}) copy-start(bf16[512,1536]{1,0:T(8,128)(2,1)} %input_ref.1) | copy-start | bytes 4718596
  7.2 198.2 %all-gather.3.cloned.1.call-start = ((), (), s32[]{:S(2)}) async-start(), calls=%async_computation.2 | async-start | bytes 7864320 | tf_op jit(solution)/shard_map/all_gather | solution.py:797
  17.8 15.5 %collective-permute-start.21 = (bf16[224,640]{1,0:T(8,128)(2,1)}, bf16[224,640]{1,0:T(8,128)(2,1)}, u32[]{:S(2)}, u32[]{:S(2)}) collective-permute-start(bf16[224,640]{1,0:T(8,128)(2,1)} %pad_maximum_fusion.6), channel_id=1, source_target_pairs={{0,3},{1,2},{2,1},{3,0},{4,7},{5,6},{6,5},{7,4},{8,11},{9,10},{10,... | collective-permute-start | bytes 860168 | tf_op jit(solution)/shard_map/ppermute | solution.py:557
  22.8 24.7 %collective-permute-start.20 = (bf16[224,640]{1,0:T(8,128)(2,1)}, bf16[224,640]{1,0:T(8,128)(2,1)}, u32[]{:S(2)}, u32[]{:S(2)}) collective-permute-start(bf16[224,640]{1,0:T(8,128)(2,1)} %pad_maximum_fusion.6), channel_id=1, source_target_pairs={{0,2},{1,3},{2,0},{3,1},{4,6},{5,7},{6,4},{7,5},{8,10},{9,11},{10,... | collective-permute-start | bytes 860168 | tf_op jit(solution)/shard_map/ppermute | solution.py:557
  22.8 24.7 %collective-permute-start.19 = (bf16[224,640]{1,0:T(8,128)(2,1)}, bf16[224,640]{1,0:T(8,128)(2,1)}, u32[]{:S(2)}, u32[]{:S(2)}) collective-permute-start(bf16[224,640]{1,0:T(8,128)(2,1)} %pad_maximum_fusion.6), channel_id=1, source_target_pairs={{0,1},{1,0},{2,3},{3,2},{4,5},{5,4},{6,7},{7,6},{8,9},{9,8},{10,11... | collective-permute-start | bytes 860168 | tf_op jit(solution)/shard_map/ppermute | solution.py:557
  26.4 6.8 copy-start.21
  28.4 4.3 copy-start.5
  48.8 40.4 %collective-permute-start.28 = (bf16[192,384]{1,0:T(8,128)(2,1)}, bf16[192,384]{1,0:T(8,128)(2,1)S(1)}, u32[]{:S(2)}, u32[]{:S(2)}) collective-permute-start(bf16[192,384]{1,0:T(8,128)(2,1)} %get-tuple-element.175), channel_id=1, source_target_pairs={{0,3},{1,2},{2,1},{3,0},{4,7},{5,6},{6,5},{7,4},{8,11},{9,10},{10,... | collective-permute-start | bytes 442376 | tf_op jit(solution)/shard_map/ppermute | solution.py:557
  51.3 37.9 %collective-permute-start.27 = (bf16[192,384]{1,0:T(8,128)(2,1)}, bf16[192,384]{1,0:T(8,128)(2,1)S(1)}, u32[]{:S(2)}, u32[]{:S(2)}) collective-permute-start(bf16[192,384]{1,0:T(8,128)(2,1)} %get-tuple-element.175), channel_id=1, source_target_pairs={{0,2},{1,3},{2,0},{3,1},{4,6},{5,7},{6,4},{7,5},{8,10},{9,11},{10,... | collective-permute-start | bytes 442376 | tf_op jit(solution)/shard_map/ppermute | solution.py:557
  51.4 20.5 %collective-permute-start.24 = (bf16[3,192,640]{2,1,0:T(8,128)(2,1)S(1)}, bf16[3,192,640]{2,1,0:T(8,128)(2,1)}, u32[]{:S(2)}, u32[]{:S(2)}) collective-permute-start(bf16[3,192,640]{2,1,0:T(8,128)(2,1)S(1)} %slice.65), channel_id=1, source_target_pairs={{0,24},{4,28},{8,16},{12,20},{16,8},{20,12},{24,0},{28,4},{1,25},{... | collective-permute-start | bytes 2211848 | tf_op jit(solution)/shard_map/ppermute | solution.py:623
  53.9 31.4 %collective-permute-start.23 = (bf16[3,192,640]{2,1,0:T(8,128)(2,1)S(1)}, bf16[3,192,640]{2,1,0:T(8,128)(2,1)}, u32[]{:S(2)}, u32[]{:S(2)}) collective-permute-start(bf16[3,192,640]{2,1,0:T(8,128)(2,1)S(1)} %slice.65), channel_id=1, source_target_pairs={{0,16},{4,20},{8,24},{12,28},{16,0},{20,4},{24,8},{28,12},{1,17},{... | collective-permute-start | bytes 2211848 | tf_op jit(solution)/shard_map/ppermute | solution.py:623
  54.4 32.1 %collective-permute-start.22 = (bf16[3,192,640]{2,1,0:T(8,128)(2,1)S(1)}, bf16[3,192,640]{2,1,0:T(8,128)(2,1)S(1)}, u32[]{:S(2)}, u32[]{:S(2)}) collective-permute-start(bf16[3,192,640]{2,1,0:T(8,128)(2,1)S(1)} %slice.65), channel_id=1, source_target_pairs={{0,8},{4,12},{8,0},{12,4},{16,24},{20,28},{24,16},{28,20},{1,9},{5... | collective-permute-start | bytes 2211848 | tf_op jit(solution)/shard_map/ppermute | solution.py:623
  72.0 18.3 %collective-permute-start.26 = (bf16[192,384]{1,0:T(8,128)(2,1)}, bf16[192,384]{1,0:T(8,128)(2,1)S(1)}, u32[]{:S(2)}, u32[]{:S(2)}) collective-permute-start(bf16[192,384]{1,0:T(8,128)(2,1)} %get-tuple-element.175), channel_id=1, source_target_pairs={{0,1},{1,0},{2,3},{3,2},{4,5},{5,4},{6,7},{7,6},{8,9},{9,8},{10,11... | collective-permute-start | bytes 442376 | tf_op jit(solution)/shard_map/ppermute | solution.py:557
  88.9 29.9 %collective-permute-start.25 = (bf16[4,4,192,640]{3,2,1,0:T(8,128)(2,1)}, bf16[4,4,192,640]{3,2,1,0:T(8,128)(2,1)}, u32[]{:S(2)}, u32[]{:S(2)}) collective-permute-start(bf16[4,4,192,640]{3,2,1,0:T(8,128)(2,1)} %pad_maximum_fusion.2.own_ref), channel_id=1, source_target_pairs={{0,4},{4,0},{8,12},{12,8},{16,20},{20,16},{24,28},{28,24},{1,5},{5... | collective-permute-start | bytes 11796488 | tf_op jit(solution)/shard_map/ppermute | solution.py:623
  90.3 14.1 %collective-permute-start.31 = (bf16[3,192,384]{2,1,0:T(8,128)(2,1)S(1)}, bf16[3,192,384]{2,1,0:T(8,128)(2,1)S(1)}, u32[]{:S(2)}, u32[]{:S(2)}) collective-permute-start(bf16[3,192,384]{2,1,0:T(8,128)(2,1)S(1)} %pad_maximum_fusion.5), channel_id=1, source_target_pairs={{0,24},{4,28},{8,16},{12,20},{16,8},{20,12},{24,0},{28,4},{1,25},{... | collective-permute-start | bytes 1327112 | tf_op jit(solution)/shard_map/ppermute | solution.py:623
  92.9 11.5 %copy-start.16 = (bf16[1,192,384]{2,1,0:T(8,128)(2,1)S(1)}, bf16[1,192,384]{2,1,0:T(8,128)(2,1)}, u32[]{:S(2)}) copy-start(bf16[1,192,384]{2,1,0:T(8,128)(2,1)} %get-tuple-element.303) | copy-start | bytes 442372
  93.3 19.1 %collective-permute-start.30 = (bf16[3,192,384]{2,1,0:T(8,128)(2,1)S(1)}, bf16[3,192,384]{2,1,0:T(8,128)(2,1)}, u32[]{:S(2)}, u32[]{:S(2)}) collective-permute-start(bf16[3,192,384]{2,1,0:T(8,128)(2,1)S(1)} %pad_maximum_fusion.5), channel_id=1, source_target_pairs={{0,16},{4,20},{8,24},{12,28},{16,0},{20,4},{24,8},{28,12},{1,17},{... | collective-permute-start | bytes 1327112 | tf_op jit(solution)/shard_map/ppermute | solution.py:623
  95.0 18.6 %collective-permute-start.29 = (bf16[3,192,384]{2,1,0:T(8,128)(2,1)S(1)}, bf16[3,192,384]{2,1,0:T(8,128)(2,1)}, u32[]{:S(2)}, u32[]{:S(2)}) collective-permute-start(bf16[3,192,384]{2,1,0:T(8,128)(2,1)S(1)} %pad_maximum_fusion.5), channel_id=1, source_target_pairs={{0,8},{4,12},{8,0},{12,4},{16,24},{20,28},{24,16},{28,20},{1,9},{5... | collective-permute-start | bytes 1327112 | tf_op jit(solution)/shard_map/ppermute | solution.py:623
  96.1 17.4 %copy-start.18 = (bf16[4,384]{1,0:T(4,128)(2,1)}, bf16[4,384]{1,0:T(4,128)(2,1)S(1)}, u32[]{:S(2)}) copy-start(bf16[4,384]{1,0:T(4,128)(2,1)S(1)} %get-tuple-element.305) | copy-start | bytes 9220
  115.0 31.0 %copy-start.10 = (bf16[4,4,192,384]{3,2,1,0:T(8,128)(2,1)}, bf16[4,4,192,384]{3,2,1,0:T(8,128)(2,1)S(1)}, u32[]{:S(2)}) copy-start(bf16[4,4,192,384]{3,2,1,0:T(8,128)(2,1)S(1)} %pad_maximum_fusion.3.own_ref) | copy-start | bytes 7077892
  115.0 31.0 %collective-permute-start.32 = (bf16[4,4,192,384]{3,2,1,0:T(8,128)(2,1)S(1)}, bf16[4,4,192,384]{3,2,1,0:T(8,128)(2,1)}, u32[]{:S(2)}, u32[]{:S(2)}) collective-permute-start(bf16[4,4,192,384]{3,2,1,0:T(8,128)(2,1)S(1)} %pad_maximum_fusion.3.own_ref), channel_id=1, source_target_pairs={{0,4},{4,0},{8,12},{12,8},{16,20},{20,16},{24,28},{28,24},{1,5},{5... | collective-permute-start | bytes 7077896 | tf_op jit(solution)/shard_map/ppermute | solution.py:623
  146.0 10.5 %copy-start.26 = (bf16[4,512,384]{2,1,0:T(8,128)(2,1)}, bf16[4,512,384]{2,1,0:T(8,128)(2,1)S(1)}, u32[]{:S(2)}) copy-start(bf16[4,512,384]{2,1,0:T(8,128)(2,1)S(1)} %get-tuple-element.174.mixed_ref) | copy-start | bytes 4718596
  156.5 40.9 %collective-permute-start.34 = (bf16[512,1536]{1,0:T(8,128)(2,1)}, bf16[512,1536]{1,0:T(8,128)(2,1)}, u32[]{:S(2)}, u32[]{:S(2)}) collective-permute-start(bf16[512,1536]{1,0:T(8,128)(2,1)} %get-tuple-element.178.inner_ref.outer_ref), channel_id=1, source_target_pairs={{1,2},{2,1},{5,6},{6,5},{9,10},{10,9},{13,14},{14,13},{17,18},{18,... | collective-permute-start | bytes 4718600 | tf_op jit(solution)/shard_map/ppermute | solution.py:585
  158.4 47.0 %collective-permute-start.33 = (bf16[512,1536]{1,0:T(8,128)(2,1)}, bf16[512,1536]{1,0:T(8,128)(2,1)}, u32[]{:S(2)}, u32[]{:S(2)}) collective-permute-start(bf16[512,1536]{1,0:T(8,128)(2,1)} %get-tuple-element.178.inner_ref.outer_ref), channel_id=1, source_target_pairs={{0,1},{1,0},{2,3},{3,2},{4,5},{5,4},{6,7},{7,6},{8,9},{9,8},{10,11... | collective-permute-start | bytes 4718600 | tf_op jit(solution)/shard_map/ppermute | solution.py:557
  205.4 44.4 %collective-permute-start.35 = (bf16[512,1536]{1,0:T(8,128)(2,1)}, bf16[512,1536]{1,0:T(8,128)(2,1)}, u32[]{:S(2)}, u32[]{:S(2)}) collective-permute-start(bf16[512,1536]{1,0:T(8,128)(2,1)} %collective-permute-done.33.outer_ref.inner_ref), channel_id=1, source_target_pairs={{1,2},{2,1},{5,6},{6,5},{9,10},{10,9},{13,14},{14,13},{17,18},{18,... | collective-permute-start | bytes 4718600 | tf_op jit(solution)/shard_map/ppermute | solution.py:589
  207.2 43.8 %collective-permute-start.37 = (bf16[512,1536]{1,0:T(8,128)(2,1)}, bf16[512,1536]{1,0:T(8,128)(2,1)}, u32[]{:S(2)}, u32[]{:S(2)}) collective-permute-start(bf16[512,1536]{1,0:T(8,128)(2,1)} %collective-permute-done.34.inner_ref), channel_id=1, source_target_pairs={{1,0},{2,3},{5,4},{6,7},{9,8},{10,11},{13,12},{14,15},{17,16},{18,... | collective-permute-start | bytes 4718600 | tf_op jit(solution)/shard_map/ppermute | solution.py:590
  240.5 84.3 %collective-permute-start.39 = (bf16[512,1664]{1,0:T(8,128)(2,1)}, bf16[512,1664]{1,0:T(8,128)(2,1)}, u32[]{:S(2)}, u32[]{:S(2)}) collective-permute-start(bf16[512,1664]{1,0:T(8,128)(2,1)} %get-tuple-element.187), channel_id=1, source_target_pairs={{1,2},{2,1},{5,6},{6,5},{9,10},{10,9},{13,14},{14,13},{17,18},{18,... | collective-permute-start | bytes 5111816 | tf_op jit(solution)/shard_map/ppermute | solution.py:612
  242.4 134.5 %collective-permute-start.38 = (bf16[512,1664]{1,0:T(8,128)(2,1)}, bf16[512,1664]{1,0:T(8,128)(2,1)S(1)}, u32[]{:S(2)}, u32[]{:S(2)}) collective-permute-start(bf16[512,1664]{1,0:T(8,128)(2,1)} %get-tuple-element.187), channel_id=1, source_target_pairs={{0,1},{3,2},{4,5},{7,6},{8,9},{11,10},{12,13},{15,14},{16,17},{19,... | collective-permute-start | bytes 5111816 | tf_op jit(solution)/shard_map/ppermute | solution.py:612
  249.7 42.2 %collective-permute-start.36 = (bf16[512,1536]{1,0:T(8,128)(2,1)}, bf16[512,1536]{1,0:T(8,128)(2,1)}, u32[]{:S(2)}, u32[]{:S(2)}) collective-permute-start(bf16[512,1536]{1,0:T(8,128)(2,1)} %collective-permute-done.35.inner_ref), channel_id=1, source_target_pairs={{1,0},{2,3},{5,4},{6,7},{9,8},{10,11},{13,12},{14,15},{17,16},{18,... | collective-permute-start | bytes 4718600 | tf_op jit(solution)/shard_map/ppermute | solution.py:593
  251.0 40.8 %copy-start.14 = (bf16[1536,128]{1,0:T(8,128)(2,1)S(1)}, bf16[1536,128]{1,0:T(8,128)(2,1)}, u32[]{:S(2)}) copy-start(bf16[1536,128]{1,0:T(8,128)(2,1)} %pad.21.router_ref) | copy-start | bytes 1179652
  282.8 94.1 %collective-permute-start.41 = (bf16[512,1664]{1,0:T(8,128)(2,1)}, bf16[512,1664]{1,0:T(8,128)(2,1)S(1)}, u32[]{:S(2)}, u32[]{:S(2)}) collective-permute-start(bf16[512,1664]{1,0:T(8,128)(2,1)} %get-tuple-element.188), channel_id=1, source_target_pairs={{1,0},{2,3},{5,4},{6,7},{9,8},{10,11},{13,12},{14,15},{17,16},{18,... | collective-permute-start | bytes 5111816 | tf_op jit(solution)/shard_map/ppermute | solution.py:612
  284.1 92.9 %collective-permute-start.40 = (bf16[512,1664]{1,0:T(8,128)(2,1)}, bf16[512,1664]{1,0:T(8,128)(2,1)}, u32[]{:S(2)}, u32[]{:S(2)}) collective-permute-start(bf16[512,1664]{1,0:T(8,128)(2,1)} %get-tuple-element.188), channel_id=1, source_target_pairs={{0,2},{3,1},{4,6},{7,5},{8,10},{11,9},{12,14},{15,13},{16,18},{19,... | collective-permute-start | bytes 5111816 | tf_op jit(solution)/shard_map/ppermute | solution.py:612
  323.5 78.1 %collective-permute-start.43 = (bf16[512,1664]{1,0:T(8,128)(2,1)}, bf16[512,1664]{1,0:T(8,128)(2,1)}, u32[]{:S(2)}, u32[]{:S(2)}) collective-permute-start(bf16[512,1664]{1,0:T(8,128)(2,1)} %get-tuple-element.189), channel_id=1, source_target_pairs={{1,3},{2,0},{5,7},{6,4},{9,11},{10,8},{13,15},{14,12},{17,19},{18,... | collective-permute-start | bytes 5111816 | tf_op jit(solution)/shard_map/ppermute | solution.py:612
  324.8 76.8 %collective-permute-start.42 = (bf16[512,1664]{1,0:T(8,128)(2,1)}, bf16[512,1664]{1,0:T(8,128)(2,1)}, u32[]{:S(2)}, u32[]{:S(2)}) collective-permute-start(bf16[512,1664]{1,0:T(8,128)(2,1)} %get-tuple-element.189), channel_id=1, source_target_pairs={{0,3},{3,0},{4,7},{7,4},{8,11},{11,8},{12,15},{15,12},{16,19},{19,... | collective-permute-start | bytes 5111816 | tf_op jit(solution)/shard_map/ppermute | solution.py:612
  376.9 24.7 %copy-start.11 = (bf16[512,1664]{1,0:T(8,128)(2,1)}, bf16[512,1664]{1,0:T(8,128)(2,1)S(1)}, u32[]{:S(2)}) copy-start(bf16[512,1664]{1,0:T(8,128)(2,1)S(1)} %collective-permute-done.38) | copy-start | bytes 5111812
  376.9 24.7 %copy-start.12 = (bf16[512,1664]{1,0:T(8,128)(2,1)}, bf16[512,1664]{1,0:T(8,128)(2,1)S(1)}, u32[]{:S(2)}) copy-start(bf16[512,1664]{1,0:T(8,128)(2,1)S(1)} %collective-permute-done.41) | copy-start | bytes 5111812
  401.6 305.7 %all-to-all-start = ((bf16[4,512,1536]{2,1,0:T(8,128)(2,1)}), bf16[4,512,1536]{2,1,0:T(8,128)(2,1)}, u32[]{:S(2)}, u32[]{:S(2)}) async-start(bf16[4,512,1536]{2,1,0:T(8,128)(2,1)} %get-tuple-element.209), calls=%async_computation | async-start | bytes 12582912 | tf_op jit(solution)/shard_map/all_to_all | solution.py:844
  406.9 322.3 %all-reduce.6.cloned.1.call-start = ((), (), s32[]{:S(2)}) async-start(), calls=%async_computation.1 | async-start | bytes 37748736 | tf_op jit(solution)/shard_map/psum | solution.py:836
  429.5 4.7 copy-start.25
  429.5 4.7 copy-start.27
  451.3 17.8 %collective-permute-start.1 = (bf16[4,192,1024]{2,1,0:T(8,128)(2,1)}, bf16[4,192,1024]{2,1,0:T(8,128)(2,1)}, u32[]{:S(2)}, u32[]{:S(2)}) collective-permute-start(bf16[4,192,1024]{2,1,0:T(8,128)(2,1)} %get-tuple-element.104), channel_id=1, source_target_pairs={{0,4},{4,0},{8,12},{12,8},{16,20},{20,16},{24,28},{28,24},{1,5},{5... | collective-permute-start | bytes 4718600 | tf_op jit(solution)/shard_map/cond/branch_1_fun/ppermute | solution.py:623
  468.6 24.4 %collective-permute-start = (bf16[4,192,1024]{2,1,0:T(8,128)(2,1)}, bf16[4,192,1024]{2,1,0:T(8,128)(2,1)}, u32[]{:S(2)}, u32[]{:S(2)}) collective-permute-start(bf16[4,192,1024]{2,1,0:T(8,128)(2,1)} %get-tuple-element.101), channel_id=1, source_target_pairs={{0,4},{4,0},{8,12},{12,8},{16,20},{20,16},{24,28},{28,24},{1,5},{5... | collective-permute-start | bytes 4718600 | tf_op jit(solution)/shard_map/cond/branch_1_fun/ppermute | solution.py:623
  490.3 24.1 %collective-permute-start.5 = (bf16[4,192,1024]{2,1,0:T(8,128)(2,1)}, bf16[4,192,1024]{2,1,0:T(8,128)(2,1)}, u32[]{:S(2)}, u32[]{:S(2)}) collective-permute-start(bf16[4,192,1024]{2,1,0:T(8,128)(2,1)} %get-tuple-element.116), channel_id=1, source_target_pairs={{0,4},{4,0},{8,12},{12,8},{16,20},{20,16},{24,28},{28,24},{1,5},{5... | collective-permute-start | bytes 4718600 | tf_op jit(solution)/shard_map/cond/branch_1_fun/ppermute | solution.py:623
  490.3 41.1 %collective-permute-start.3 = (bf16[4,192,1024]{2,1,0:T(8,128)(2,1)}, bf16[4,192,1024]{2,1,0:T(8,128)(2,1)}, u32[]{:S(2)}, u32[]{:S(2)}) collective-permute-start(bf16[4,192,1024]{2,1,0:T(8,128)(2,1)} %add_convert_fusion.4), channel_id=1, source_target_pairs={{0,24},{4,28},{8,16},{12,20},{16,8},{20,12},{24,0},{28,4},{1,25},{... | collective-permute-start | bytes 4718600 | tf_op jit(solution)/shard_map/cond/branch_1_fun/ppermute | solution.py:623
  496.9 92.5 %collective-permute-start.4 = (bf16[4,192,1024]{2,1,0:T(8,128)(2,1)}, bf16[4,192,1024]{2,1,0:T(8,128)(2,1)}, u32[]{:S(2)}, u32[]{:S(2)}) collective-permute-start(bf16[4,192,1024]{2,1,0:T(8,128)(2,1)} %add_convert_fusion.5), channel_id=1, source_target_pairs={{0,8},{4,12},{8,0},{12,4},{16,24},{20,28},{24,16},{28,20},{1,9},{5... | collective-permute-start | bytes 4718600 | tf_op jit(solution)/shard_map/cond/branch_1_fun/ppermute | solution.py:623
  514.3 75.1 %collective-permute-start.2 = (bf16[4,192,1024]{2,1,0:T(8,128)(2,1)}, bf16[4,192,1024]{2,1,0:T(8,128)(2,1)}, u32[]{:S(2)}, u32[]{:S(2)}) collective-permute-start(bf16[4,192,1024]{2,1,0:T(8,128)(2,1)} %get-tuple-element.114), channel_id=1, source_target_pairs={{0,4},{4,0},{8,12},{12,8},{16,20},{20,16},{24,28},{28,24},{1,5},{5... | collective-permute-start | bytes 4718600 | tf_op jit(solution)/shard_map/cond/branch_1_fun/ppermute | solution.py:623
  518.0 72.3 %collective-permute-start.6 = (bf16[4,192,1024]{2,1,0:T(8,128)(2,1)}, bf16[4,192,1024]{2,1,0:T(8,128)(2,1)}, u32[]{:S(2)}, u32[]{:S(2)}) collective-permute-start(bf16[4,192,1024]{2,1,0:T(8,128)(2,1)} %add_convert_fusion.1), channel_id=1, source_target_pairs={{0,16},{4,20},{8,24},{12,28},{16,0},{20,4},{24,8},{28,12},{1,17},{... | collective-permute-start | bytes 4718600 | tf_op jit(solution)/shard_map/cond/branch_1_fun/ppermute | solution.py:623
  590.3 9.3 %copy-start.1 = (f32[512,1536]{1,0:T(8,128)S(1)}, f32[512,1536]{1,0:T(8,128)}, u32[]{:S(2)}) copy-start(f32[512,1536]{1,0:T(8,128)} %get-tuple-element.108) | copy-start | bytes 9437188 | tf_op jit(solution)/shard_map/cond
  595.7 11.2 %collective-permute-start.7 = (bf16[192,1024]{1,0:T(8,128)(2,1)S(1)}, bf16[192,1024]{1,0:T(8,128)(2,1)S(1)}, u32[]{:S(2)}, u32[]{:S(2)}) collective-permute-start(bf16[192,1024]{1,0:T(8,128)(2,1)S(1)} %get-tuple-element.284), channel_id=1, source_target_pairs={{0,1},{1,0},{2,3},{3,2},{4,5},{5,4},{6,7},{7,6},{8,9},{9,8},{10,11... | collective-permute-start | bytes 1179656 | tf_op jit(solution)/shard_map/cond/branch_1_fun/ppermute | solution.py:557
  597.2 20.9 %collective-permute-start.9 = (bf16[192,1024]{1,0:T(8,128)(2,1)S(1)}, bf16[192,1024]{1,0:T(8,128)(2,1)S(1)}, u32[]{:S(2)}, u32[]{:S(2)}) collective-permute-start(bf16[192,1024]{1,0:T(8,128)(2,1)S(1)} %get-tuple-element.285), channel_id=1, source_target_pairs={{0,3},{1,2},{2,1},{3,0},{4,7},{5,6},{6,5},{7,4},{8,11},{9,10},{10,... | collective-permute-start | bytes 1179656 | tf_op jit(solution)/shard_map/cond/branch_1_fun/ppermute | solution.py:557
  599.6 34.4 %collective-permute-start.8 = (bf16[192,1024]{1,0:T(8,128)(2,1)S(1)}, bf16[192,1024]{1,0:T(8,128)(2,1)S(1)}, u32[]{:S(2)}, u32[]{:S(2)}) collective-permute-start(bf16[192,1024]{1,0:T(8,128)(2,1)S(1)} %get-tuple-element.286), channel_id=1, source_target_pairs={{0,2},{1,3},{2,0},{3,1},{4,6},{5,7},{6,4},{7,5},{8,10},{9,11},{10,... | collective-permute-start | bytes 1179656 | tf_op jit(solution)/shard_map/cond/branch_1_fun/ppermute | solution.py:557
  600.6 37.2 %collective-permute-start.14 = (f32[18,1536]{1,0:T(8,128)S(1)}, f32[18,1536]{1,0:T(8,128)S(1)}, u32[]{:S(2)}, u32[]{:S(2)}) collective-permute-start(f32[18,1536]{1,0:T(8,128)S(1)} %pad_maximum_fusion.1), channel_id=1, source_target_pairs={{0,4},{4,0},{8,12},{12,8},{16,20},{20,16},{24,28},{28,24},{1,5},{5... | collective-permute-start | bytes 331784 | tf_op jit(solution)/shard_map/cond/branch_1_fun/ppermute | solution.py:902
  634.3 45.7 %collective-permute-start.12 = (bf16[192,1024]{1,0:T(8,128)(2,1)S(1)}, bf16[192,1024]{1,0:T(8,128)(2,1)}, u32[]{:S(2)}, u32[]{:S(2)}) collective-permute-start(bf16[192,1024]{1,0:T(8,128)(2,1)S(1)} %fusion.2), channel_id=1, source_target_pairs={{0,24},{4,28},{8,16},{12,20},{16,8},{20,12},{24,0},{28,4},{1,25},{... | collective-permute-start | bytes 1179656 | tf_op jit(solution)/shard_map/cond/branch_1_fun/ppermute | solution.py:623
  634.9 45.1 %collective-permute-start.11 = (bf16[192,1024]{1,0:T(8,128)(2,1)S(1)}, bf16[192,1024]{1,0:T(8,128)(2,1)}, u32[]{:S(2)}, u32[]{:S(2)}) collective-permute-start(bf16[192,1024]{1,0:T(8,128)(2,1)S(1)} %fusion.2), channel_id=1, source_target_pairs={{0,16},{4,20},{8,24},{12,28},{16,0},{20,4},{24,8},{28,12},{1,17},{... | collective-permute-start | bytes 1179656 | tf_op jit(solution)/shard_map/cond/branch_1_fun/ppermute | solution.py:623
  636.4 43.6 %collective-permute-start.10 = (bf16[192,1024]{1,0:T(8,128)(2,1)S(1)}, bf16[192,1024]{1,0:T(8,128)(2,1)}, u32[]{:S(2)}, u32[]{:S(2)}) collective-permute-start(bf16[192,1024]{1,0:T(8,128)(2,1)S(1)} %fusion.2), channel_id=1, source_target_pairs={{0,8},{4,12},{8,0},{12,4},{16,24},{20,28},{24,16},{28,20},{1,9},{5... | collective-permute-start | bytes 1179656 | tf_op jit(solution)/shard_map/cond/branch_1_fun/ppermute | solution.py:623
  638.5 38.9 %collective-permute-start.15 = (f32[18,1536]{1,0:T(8,128)}, f32[18,1536]{1,0:T(8,128)}, u32[]{:S(2)}, u32[]{:S(2)}) collective-permute-start(f32[18,1536]{1,0:T(8,128)} %fusion.3), channel_id=1, source_target_pairs={{0,8},{4,12},{8,0},{12,4},{16,24},{20,28},{24,16},{28,20},{1,9},{5... | collective-permute-start | bytes 331784 | tf_op jit(solution)/shard_map/cond/branch_1_fun/ppermute | solution.py:902
  639.7 54.0 %copy-start.23 = (f32[512]{0:T(512)S(1)}, f32[512]{0:T(512)}, u32[]{:S(2)}) copy-start(f32[512]{0:T(512)} %add_rsqrt_fusion) | copy-start | bytes 6148 | tf_op jit(solution)/shard_map/cond
  639.7 54.0 %copy-start.2 = (f32[512,1536]{1,0:T(8,128)S(1)}, f32[512,1536]{1,0:T(8,128)}, u32[]{:S(2)}) copy-start(f32[512,1536]{1,0:T(8,128)} %get-tuple-element.108) | copy-start | bytes 9437188 | tf_op jit(solution)/shard_map/cond
  678.4 9.0 %collective-permute-start.16 = (f32[18,1536]{1,0:T(8,128)S(1)}, f32[18,1536]{1,0:T(8,128)S(1)}, u32[]{:S(2)}, u32[]{:S(2)}) collective-permute-start(f32[18,1536]{1,0:T(8,128)S(1)} %add.185), channel_id=1, source_target_pairs={{0,16},{4,20},{8,24},{12,28},{16,0},{20,4},{24,8},{28,12},{1,17},{... | collective-permute-start | bytes 331784 | tf_op jit(solution)/shard_map/cond/branch_1_fun/ppermute | solution.py:902
  681.4 16.1 %copy-start.8 = (bf16[4,192,1024]{2,1,0:T(8,128)(2,1)}, bf16[4,192,1024]{2,1,0:T(8,128)(2,1)S(1)}, u32[]{:S(2)}) copy-start(bf16[4,192,1024]{2,1,0:T(8,128)(2,1)S(1)} %pad_maximum_fusion.own_ref) | copy-start | bytes 4718596 | tf_op jit(solution)/shard_map/cond
  681.4 19.5 %collective-permute-start.13 = (bf16[4,192,1024]{2,1,0:T(8,128)(2,1)S(1)}, bf16[4,192,1024]{2,1,0:T(8,128)(2,1)}, u32[]{:S(2)}, u32[]{:S(2)}) collective-permute-start(bf16[4,192,1024]{2,1,0:T(8,128)(2,1)S(1)} %pad_maximum_fusion.own_ref), channel_id=1, source_target_pairs={{0,4},{4,0},{8,12},{12,8},{16,20},{20,16},{24,28},{28,24},{1,5},{5... | collective-permute-start | bytes 4718600 | tf_op jit(solution)/shard_map/cond/branch_1_fun/ppermute | solution.py:623
  687.4 5.2 collective-permute-start.17
  692.6 7.1 collective-permute-start.18
  707.3 4.4 copy-start.3
  (11 other events, 24.2 us)
Sparse Core Ops, SparseCore 0:
  55.1 122.4 all-gather.2
  412.0 317.1 all-reduce.5

commit v3 on v2

--- a/solution.py
+++ b/solution.py
@@ -322,17 +322,19 @@
     chosen_ref,
     router_ref,
     weight_ref,
-    _,
-    fed_ref,
-    row_ref,
-    combined_ref,
-    pair_ref,
-    gated_ref,
-    gates_ref,
-    gate_grad_ref,
-    row_total,
-    combined_total,
+    *refs,
 ):
+    (
+        fed_ref,
+        row_ref,
+        combined_ref,
+        pair_ref,
+        gated_ref,
+        gates_ref,
+        gate_grad_ref,
+        row_total,
+        combined_total,
+    ) = refs[-9:]
     step, steps = pl.program_id(0), pl.num_programs(0)
     index = first_ref[0] + step
     lane = lax.broadcasted_iota(jnp.int32, gates_ref.shape, 1)
@@ -399,6 +401,8 @@
 def expert_slot(at, choices, upstream, chosen, router, weights, combined):
     length, features = choices[0].shape
     count = weights.shape[0]
+    held = [] if isinstance(combined, int) else [combined]
+    sequences = combined if isinstance(combined, int) else combined.shape[0]
     full = lambda *shape: pl.BlockSpec(shape, lambda e, at: (0,) * len(shape))
     each = lambda *shape: pl.BlockSpec((1,) + shape, lambda e, at: (e,) + (0,) * len(shape))
     there = lambda i, *shape: pl.BlockSpec(
@@ -416,8 +420,8 @@
                 there(2, length, LANES),
                 full(features, LANES),
                 each(features, 3 * FF),
-                pl.BlockSpec(memory_space=pl.ANY),
-            ],
+            ]
+            + [pl.BlockSpec(memory_space=pl.ANY)] * len(held),
             out_specs=[
                 full(length, features),
                 full(length, features + LANES),
@@ -435,14 +439,14 @@
         out_shape=[
             jax.ShapeDtypeStruct((length, features), bf16),
             jax.ShapeDtypeStruct((length, features + LANES), bf16),
-            jax.ShapeDtypeStruct(combined.shape, bf16),
+            jax.ShapeDtypeStruct((sequences, length, features), bf16),
             jax.ShapeDtypeStruct((count, length, 2 * FF), bf16),
             jax.ShapeDtypeStruct((count, length, FF), bf16),
         ],
-        input_output_aliases={7: 2},
+        input_output_aliases={7: 2} if held else {},
         compiler_params=pltpu.CompilerParams(vmem_limit_bytes=VMEM),
         cost_estimate=cost(12 * count * length * features * FF, 3.2e7),
-    )(at, *choices, upstream, chosen, router, weights, combined)
+    )(at, *choices, upstream, chosen, router, weights, *held)
 
 
 def fed_grad_kernel(*refs):
@@ -635,13 +639,14 @@
     return [hop(near, 2 * m) for m in range(1, 4)]
 
 
-def join_pairs(local, parts, core, spot):
+def join_pairs(local, parts, core, spot, earlier=()):
     own = jnp.stack(
         [
             jnp.concatenate([local(spot ^ m, core)[None], part])
             for m, part in enumerate(parts)
         ]
     )
+    own = after(own, *earlier)
     return own, hop(own, 1)
 
 
@@ -768,13 +773,8 @@
         )
         small_all = jnp.stack([pick(small_slots, place ^ k) for k in range(4)])
         projection_sent = send_pairs(projection_near)
-        output_near = gather_near(after(output_share(spot, core), near))
-        output_sent = send_pairs(after(output_near, projection_sent))
-        attend_weights = join_pairs(
-            projection_share, [projection_near] + projection_sent, core, spot
-        )
-        output_weights = join_pairs(output_share, [output_near] + output_sent, core, spot)
-        cotangent_sent = after(cotangent, near)
+        output_near = gather_near(after(output_share(spot, core), projection_near))
+        cotangent_sent = after(cotangent, projection_near)
     else:
         gathered = lax.all_gather(projection, "shard", axis=0)
         gathered_output = lax.all_gather(output_weight, "shard", axis=0)
@@ -788,9 +788,9 @@
             ],
             axis=3,
         ).transpose(2, 0, 1, 3)
-        attend_weights = (columns[:, :, :half], columns[:, :, half:])
+        attend_columns = (columns[:, :, :half], columns[:, :, half:])
         columns = gathered_output.reshape(places, own, PAIRS, PAIR_QUERY).transpose(2, 0, 1, 3)
-        output_weights = (columns[:, :, :half], columns[:, :, half:])
+        output_columns = (columns[:, :, :half], columns[:, :, half:])
         small_all = lax.all_gather(small, "shard", axis=0)
         cotangent_sent = cotangent
 
@@ -805,12 +805,49 @@
     chosen_all = small_all[:, (2 + EXPERTS) * own :].reshape(places, length, EXPERTS).astype(f32)
     normed = (scaled_in * attention_scale).astype(bf16)
     where = jnp.stack([base, core]).astype(jnp.int32)
-    mixed, qkv, lse = attend_forward(where, normed, attend_weights, tables)
-    middle, fed = middle_rows(where, mixed, output_weights, inputs, feed_scale[None])
+
+    def attention():
+        if special:
+            attend_weights = join_pairs(
+                projection_share, [projection_near] + projection_sent, core, spot
+            )
+            output_sent = send_pairs(after(output_near, attend_weights))
+        else:
+            attend_weights = attend_columns
+        kept = attend_forward(where, normed, attend_weights, tables)
+        if special:
+            output_weights = join_pairs(
+                output_share, [output_near] + output_sent, core, spot, [kept[0]]
+            )
+        else:
+            output_weights = output_columns
+        rows = middle_rows(where, kept[0], output_weights, inputs, feed_scale[None])
+        return (*attend_weights, *output_weights, *kept, *rows)
+
+    always = routes[0, 0] >= 0
+
+    def apart(function, shapes):
+        empty = lambda: tuple(jnp.zeros(*shape) for shape in shapes)
+        return lax.cond(always, function, empty)
+
+    share = (PAIRS, places, half)
+    own_a, other_a, own_o, other_o, mixed, qkv, lse, middle, fed = apart(
+        attention,
+        [((*share, PAIR_WIDTH), bf16)] * 2
+        + [((*share, PAIR_QUERY), bf16)] * 2
+        + [
+            ((PAIRS, length, PAIR_QUERY), bf16),
+            ((PAIRS, length, PAIR_WIDTH), bf16),
+            ((PAIRS, 8, length), f32),
+            ((length, features), f32),
+            ((length, features), bf16),
+        ],
+    )
+    attend_weights, output_weights = (own_a, other_a), (own_o, other_o)
     router_wide = jnp.pad(router_full, ((0, 0), (0, LANES - EXPERTS)))
     chosen_wide = jnp.pad(chosen_all, ((0, 0), (0, 0), (0, LANES - EXPERTS)))
     rows, pair_grads, gated = [], [], []
-    combined = jnp.zeros((places, length, features), bf16)
+    combined = places
     order = sources(place, places)
     middle_place = inside(place).astype(jnp.int32)
     fed_slots, rows_come, arriving = [], [], line_gather(fed, place, places)
@@ -869,9 +906,20 @@
                 chips[steps[i - 1]] = join_chip(terms[steps[i - 1]], special)
         if special:
             chips[0] = join_chip(terms[0], special)
-            plane = chips[0].astype(f32)
-            for m in (3, 1, 2):
-                plane = plane + hop(chips[m], 2 * m).astype(f32)
+            part = half // 2
+            upper, lower = (lambda c: c[:, :part]), (lambda c: c[:, part:])
+            add = lambda a, b: a.astype(f32) + b.astype(f32)
+            over_x = hop(jnp.stack([upper(chips[1]), upper(chips[3])]), 2)
+            over_y = hop(jnp.stack([lower(chips[2]), lower(chips[3])]), 4)
+            upper_y = hop(add(upper(chips[2]), over_x[1]).astype(bf16), 4)
+            lower_x = hop(add(lower(chips[1]), over_y[1]).astype(bf16), 2)
+            plane = jnp.concatenate(
+                [
+                    add(upper(chips[0]), over_x[0]) + upper_y.astype(f32),
+                    add(lower(chips[0]), over_y[0]) + lower_x.astype(f32),
+                ],
+                axis=1,
+            )
             attend_total, output_total = finish_pairs(plane.astype(bf16), core, spot)
         else:
             stacked = jnp.stack([jnp.stack(term) for term in terms])
@@ -920,8 +968,7 @@
         ((own,), f32),
         ((own, EXPERTS), f32),
     )
-    empty = lambda: tuple(jnp.zeros(*shape) for shape in shapes)
-    grads = lax.cond(routes[0, 0] >= 0, rest, empty)
+    grads = apart(rest, shapes)
     activations = (middle + jnp.sum(combined.astype(f32), axis=0)).astype(bf16)
     return (activations, *grads, expert_total)
 

time: 766 us -> 751 us (0.980)
  waiting for transfers between devices: 258 us -> 235 us
    ppermute x19 -> x20, waiting for transfers between devices: 110 us -> 90.5 us  [hop(): return lax.ppermute(value, 'rep', [(i, i ^ bit) for i in range(8)])]
    ppermute x10, waiting for transfers between devices: 56.6 us -> 72.6 us  [exchange(): return lax.ppermute(value, 'shard', [(i, i ^ k) for i in range(4)])]
    psum x1, waiting for transfers between devices: 16 us -> 0.01 us  [body(): expert_total = lax.psum(expert_term, 'rep').astype(f32)]
    ppermute x19 -> x20, starting transfers between devices: 14.9 us -> 17.2 us  [hop(): return lax.ppermute(value, 'rep', [(i, i ^ bit) for i in range(8)])]
  transfers between devices with their start and end apart: 47 -> 48, of which waited for: 19 -> 20; matrix products, arithmetic and copies ran while one was open for 10% -> 11% of each run, Pallas kernels for 40% -> 41%
where the time goes in v3:
time: 751 us; the launch traced here: 743 us
  Pallas kernels  302 us (40%)
  waiting for transfers between devices  235 us (31%)
  other arithmetic  77.8 us (10%)
  starting transfers between devices  73.2 us (10%)
  local copies, waits for them, and re-layouts  38.3 us (5%)
  between operations  15.9 us (2%)
    pallas_call x4, Pallas kernels, expert_slot(): pl.pallas_call(expert_kernel, grid_spec=pltpu.PrefetchScalarGridSpec(num_...  127 us
    ppermute x20, waiting for transfers between devices, hop(): return lax.ppermute(value, 'rep', [(i, i ^ bit) for i in range(8)])  90.5 us
    ppermute x10, waiting for transfers between devices, exchange(): return lax.ppermute(value, 'shard', [(i, i ^ k) for i in range(4)])  72.6 us
    pallas_call x4, Pallas kernels, attend_backward(): pl.pallas_call(attend_backward_kernel, grid_spec=pltpu.PrefetchScalarGrid...  70.2 us
    pallas_call x1, Pallas kernels, expert_grads(): pl.pallas_call(expert_grad_kernel, grid_spec=pltpu.PrefetchScalarGridSpec...  48.5 us
    ppermute x5, waiting for transfers between devices, rest(): small_terms = small_terms + lax.ppermute(small_terms, axis, pairs)  46.8 us
    pallas_call x1, Pallas kernels, attend_forward(): pl.pallas_call(attend_forward_kernel, grid_spec=pltpu.PrefetchScalarGridS...  27 us
    ppermute x6, waiting for transfers between devices, line_send(): return [lax.ppermute(part, 'shard', way) for way in ways[k]]  24.3 us
  transfers between devices with their start and end apart: 48, of which 20 were waited for; matrix products, arithmetic and copies ran while one was open for 11% of the time, Pallas kernels for 41%

profile of v3, /device:TPU:0, one launch (start us, length us, event | category | flops | bytes accessed | tf_op | source)
XLA Modules:
  0.0 743.2 jit_solution(13723751023610572968)
XLA Ops:
  14.6 5.1 collective-permute-start.27
  20.4 7.2 collective-permute-done.27
  27.5 16.6 %collective-permute-done.26 = bf16[224,640]{1,0:T(8,128)(2,1)S(1)} collective-permute-done((bf16[224,640]{1,0:T(8,128)(2,1)S(1)}, bf16[224,640]{1,0:T(8,128)(2,1)S(1)}, u32[]{:S(2)}, u32[]{:S(2)}) %collective-permute-start.26) | collective-permute-done | bytes 286752 | tf_op jit(solution)/shard_map/ppermute | solution.py:561
  52.7 2.5 collective-permute-start.33
  56.9 1.9 collective-permute-start.31
  58.8 2.4 collective-permute-start.30
  61.8 2.6 collective-permute-done.33
  65.9 2.6 convert_multiply_fusion
  71.1 8.3 %collective-permute-done.32 = bf16[192,384]{1,0:T(8,128)(2,1)S(1)} collective-permute-done((bf16[192,384]{1,0:T(8,128)(2,1)}, bf16[192,384]{1,0:T(8,128)(2,1)S(1)}, u32[]{:S(2)}, u32[]{:S(2)}) %collective-permute-start.32) | collective-permute-done | bytes 147488 | tf_op jit(solution)/shard_map/ppermute | solution.py:561
  81.2 11.1 %collective-permute-done.29 = bf16[3,192,640]{2,1,0:T(8,128)(2,1)} collective-permute-done((bf16[3,192,640]{2,1,0:T(8,128)(2,1)S(1)}, bf16[3,192,640]{2,1,0:T(8,128)(2,1)}, u32[]{:S(2)}, u32[]{:S(2)}) %collective-permute-start.29) | collective-permute-done | bytes 737312 | tf_op jit(solution)/shard_map/ppermute | solution.py:627
  93.9 65.7 %conditional.2 = (bf16[4,4,192,640]{3,2,1,0:T(8,128)(2,1)}, bf16[4,4,192,640]{3,2,1,0:T(8,128)(2,1)}, bf16[4,4,192,384]{3,2,1,0:T(8,128)(2,1)}, bf16[4,4,192,384...) conditional(s32[]{:T(128)} %bitcast.40, () %tuple.33, ...), branch_computations={%region_2.3_spmd, %region_3.4_spmd} | conditional | flops 22415532032 | bytes 107542768 | solution.py:831
  100.4 2.2 pad_maximum_fusion.own_ref
  106.7 3.1 collective-permute-done.20.other_ref
  113.3 27.0 %branch_1_fun.8 = (bf16[4,512,384]{2,1,0:T(8,128)(2,1)}, bf16[4,512,640]{2,1,0:T(8,128)(2,1)}, f32[4,8,512]{2,1,0:T(8,128)S(1)}) custom-call(s32[2]{0:T(128)S(1)} %get-tuple-element.110.at_ref, bf16[512,1536]{1,0:T(8,128)(2,1)S(1)} %copy-done.15, bf16[4,4,192,640]{3,2,1,0:T(8,128)(2,1)} %pad_maximum_fusion.own_ref, ...), custom_call_target="tpu_custom_call" | custom-call | flops 20000000000 | bytes 20000000 | tf_op jit(solution)/shard_map/cond/branch_1_fun/pallas_call | solution.py:153
  144.9 4.3 collective-permute-done.24.other_ref
  149.1 10.4 %branch_1_fun.9 = (f32[512,1536]{1,0:T(8,128)}, bf16[512,1536]{1,0:T(8,128)(2,1)}) custom-call(s32[2]{0:T(128)S(1)} %get-tuple-element.110.at_ref, bf16[4,512,384]{2,1,0:T(8,128)(2,1)} %get-tuple-element.423.mixed_ref, bf16[4,4,192,384]{3,2,1,0:T(8,128)(2,1)} %pad_maximum_fusion.1.own_ref, bf16[4,4,192,384]{3,2,1,0:T(8,128)(2,1)} %collective-permute-done.24.other_ref, ...), custom_call_target="tpu_custom_call" | custom-call | flops 2400000000 | bytes 10000000 | tf_op jit(solution)/shard_map/cond/branch_1_fun/pallas_call | solution.py:191
  159.6 2.0 collective-permute-start.35
  161.6 1.8 collective-permute-start.34
  163.4 33.0 %shard_map.152 = (bf16[512,1536]{1,0:T(8,128)(2,1)}, bf16[512,1664]{1,0:T(8,128)(2,1)}, bf16[4,512,1536]{2,1,0:T(8,128)(2,1)}, bf16[4,512,1024]{2,1,0:T(8,128)(2,1)}, bf16[4,512,512]{2,1,0:T(8,128)(2,1)}) custom-call(s32[4]{0:T(128)} %add_add_fusion.1.first_ref, bf16[512,1536]{1,0:T(8,128)(2,1)} %get-tuple-element.229.inner_ref.outer_ref, ...), custom_call_target="tpu_custom_call" | custom-call | flops 19327352832 | bytes 32000000 | tf_op jit(solution)/shard_map/pallas_call | solution.py:411
  196.5 5.8 collective-permute-done.34.outer_ref.inner_ref
  202.2 1.8 collective-permute-start.36
  204.0 1.7 collective-permute-start.38
  205.8 31.4 %shard_map.153 = (bf16[512,1536]{1,0:T(8,128)(2,1)}, bf16[512,1664]{1,0:T(8,128)(2,1)}, bf16[4,512,1536]{2,1,0:T(8,128)(2,1)}, bf16[4,512,1024]{2,1,0:T(8,128)(2,1)}, bf16[4,512,512]{2,1,0:T(8,128)(2,1)}) custom-call(s32[4]{0:T(128)} %add_add_fusion.3.first_ref, ...), custom_call_target="tpu_custom_call", output_to_operand_aliasing={{2}: (7, {})} | custom-call | flops 19327352832 | bytes 32000000 | tf_op jit(solution)/shard_map/pallas_call | solution.py:411
  237.2 1.8 collective-permute-start.40
  239.1 6.3 collective-permute-start.39
  246.8 31.6 %shard_map.154 = (bf16[512,1536]{1,0:T(8,128)(2,1)}, bf16[512,1664]{1,0:T(8,128)(2,1)}, bf16[4,512,1536]{2,1,0:T(8,128)(2,1)}, bf16[4,512,1024]{2,1,0:T(8,128)(2,1)}, bf16[4,512,512]{2,1,0:T(8,128)(2,1)}) custom-call(s32[4]{0:T(128)} %add_add_fusion.2.first_ref, ...), custom_call_target="tpu_custom_call", output_to_operand_aliasing={{2}: (7, {})} | custom-call | flops 19327352832 | bytes 32000000 | tf_op jit(solution)/shard_map/pallas_call | solution.py:411
  279.7 8.2 %collective-permute-start.41 = (bf16[512,1664]{1,0:T(8,128)(2,1)}, bf16[512,1664]{1,0:T(8,128)(2,1)}, u32[]{:S(2)}, u32[]{:S(2)}) collective-permute-start(bf16[512,1664]{1,0:T(8,128)(2,1)} %get-tuple-element.239), channel_id=1, source_target_pairs={{0,2},{3,1},{4,6},{7,5},{8,10},{11,9},{12,14},{15,13},{16,18},{19,... | collective-permute-start | bytes 5111816 | tf_op jit(solution)/shard_map/ppermute | solution.py:616
  288.0 31.4 %shard_map.155 = (bf16[512,1536]{1,0:T(8,128)(2,1)}, bf16[512,1664]{1,0:T(8,128)(2,1)}, bf16[4,512,1536]{2,1,0:T(8,128)(2,1)}, bf16[4,512,1024]{2,1,0:T(8,128)(2,1)}, bf16[4,512,512]{2,1,0:T(8,128)(2,1)}) custom-call(s32[4]{0:T(128)} %add_add_fusion.first_ref, bf16[512,1536]{1,0:T(8,128)(2,1)} %collective-permute-done.36.inner_ref, ...), custom_call_target="tpu_custom_call", output_to_operand_aliasing={{2}: (7, {})} | custom-call | flops 19327352832 | bytes 32000000 | tf_op jit(solution)/shard_map/pallas_call | solution.py:411
  320.7 3.4 collective-permute-start.43
  324.1 48.5 %shard_map.156 = bf16[4,1536,1536]{2,1,0:T(8,128)(2,1)} custom-call(s32[4]{0:T(128)} %pad_add_fusion.2.places_ref, bf16[512,1536]{1,0:T(8,128)(2,1)} %get-tuple-element.241.refs_0_, bf16[512,1536]{1,0:T(8,128)(2,1)} %get-tuple-element.242.refs_1_, bf16[512,1536]{1,0:T(8,128)(2,1)} %get-tuple-element.243.refs_2_, ...), custom_call_target="tpu_custom_call" | custom-call | flops 38654705664 | bytes 80000000 | tf_op jit(solution)/shard_map/pallas_call | solution.py:543
  372.7 24.3 %collective-permute-done.44 = bf16[512,1664]{1,0:T(8,128)(2,1)} collective-permute-done((bf16[512,1664]{1,0:T(8,128)(2,1)}, bf16[512,1664]{1,0:T(8,128)(2,1)}, u32[]{:S(2)}, u32[]{:S(2)}) %collective-permute-start.44) | collective-permute-done | bytes 1703968 | tf_op jit(solution)/shard_map/ppermute | solution.py:616
  397.0 5.3 all-to-all-start
  404.2 304.8 %conditional.3 = (bf16[512,1536]{1,0:T(8,128)(2,1)}, f32[384,2560]{1,0:T(8,128)}, f32[384,1536]{1,0:T(8,128)}, f32[384]{0:T(512)}, f32[384]{0:T(512)}, /*index=5*/f32[384,16]{0,1:T(8,128)}) conditional(s32[]{:T(128)} %bitcast.40, () %tuple.40, (f32[512,16]{0,1:T(8,128)}, f32[1536]{0:T(1024)S(1)}, bf16[512,1664]{1,0:T(8,128)(2,1)}, ...), branch_computations={%region_5.6_spmd, %region_6.9_spmd} | conditional | flops 36138979328 | bytes 293654208 | solution.py:831
  408.1 12.9 %branch_1_fun.10 = (f32[512,1536]{1,0:T(8,128)}, bf16[512,1536]{1,0:T(8,128)(2,1)}, f32[128,1536]{1,0:T(8,128)}, f32[1,1536]{1,0:T(1,128)}) custom-call(bf16[512,1664]{1,0:T(8,128)(2,1)} %get-tuple-element.122.refs_0_, bf16[512,1664]{1,0:T(8,128)(2,1)} %get-tuple-element.123.refs_1_, bf16[512,1664]{1,0:T(8,128)(2,1)} %get-tuple-element.124.refs_2_, ...), custom_call_target="tpu_custom_call" | custom-call | flops 100000000 | bytes 20000000 | tf_op jit(solution)/shard_map/cond/branch_1_fun/pallas_call | solution.py:511
  421.0 2.5 copy.37.sine_ref
  423.5 2.6 copy.36.cosine_ref
  426.1 2.1 broadcast_28_total_ref.0.total_ref
  428.2 17.1 %branch_1_fun.11 = (bf16[4,192,1024]{2,1,0:T(8,128)(2,1)}, bf16[4,192,1024]{2,1,0:T(8,128)(2,1)}, f32[512,1536]{1,0:T(8,128)}) custom-call(s32[2]{0:T(128)S(1)} %copy-done.34, bf16[512,1536]{1,0:T(8,128)(2,1)} %get-tuple-element.155.branch_ref, bf16[4,4,192,384]{3,2,1,0:T(8,128)(2,1)} %get-tuple-element.139.own_output_ref, ...), custom_call_target="tpu_custom_call", output_to_operand_aliasing={{2}: (12, {})} | custom-call | flops 8999999488 | bytes 15000000 | tf_op jit(solution)/shard_map/cond/branch_1_fun/pallas_call | solution.py:297
  445.3 17.3 %branch_1_fun.12 = (bf16[4,192,1024]{2,1,0:T(8,128)(2,1)}, bf16[4,192,1024]{2,1,0:T(8,128)(2,1)}, f32[512,1536]{1,0:T(8,128)}) custom-call(s32[2]{0:T(128)S(1)} %copy-done.34, bf16[512,1536]{1,0:T(8,128)(2,1)} %get-tuple-element.155.branch_ref, bf16[4,4,192,384]{3,2,1,0:T(8,128)(2,1)} %get-tuple-element.139.own_output_ref, ...), custom_call_target="tpu_custom_call", output_to_operand_aliasing={{2}: (12, {})} | custom-call | flops 8999999488 | bytes 15000000 | tf_op jit(solution)/shard_map/cond/branch_1_fun/pallas_call | solution.py:297
  463.2 4.1 add_convert_fusion.3
  467.3 17.8 %branch_1_fun.13 = (bf16[4,192,1024]{2,1,0:T(8,128)(2,1)}, bf16[4,192,1024]{2,1,0:T(8,128)(2,1)}, f32[512,1536]{1,0:T(8,128)}) custom-call(s32[2]{0:T(128)S(1)} %copy-done.34, bf16[512,1536]{1,0:T(8,128)(2,1)} %get-tuple-element.155.branch_ref, bf16[4,4,192,384]{3,2,1,0:T(8,128)(2,1)} %get-tuple-element.139.own_output_ref, ...), custom_call_target="tpu_custom_call", output_to_operand_aliasing={{2}: (12, {})} | custom-call | flops 8999999488 | bytes 15000000 | tf_op jit(solution)/shard_map/cond/branch_1_fun/pallas_call | solution.py:297
  485.1 2.5 add_convert_fusion.4
  487.7 1.9 copy-done.9
  496.1 17.9 %branch_1_fun.14 = (bf16[4,192,1024]{2,1,0:T(8,128)(2,1)}, bf16[4,192,1024]{2,1,0:T(8,128)(2,1)}, f32[512,1536]{1,0:T(8,128)}) custom-call(s32[2]{0:T(128)S(1)} %copy-done.34, bf16[512,1536]{1,0:T(8,128)(2,1)} %get-tuple-element.155.branch_ref, bf16[4,4,192,384]{3,2,1,0:T(8,128)(2,1)} %get-tuple-element.139.own_output_ref, ...), custom_call_target="tpu_custom_call", output_to_operand_aliasing={{2}: (12, {})} | custom-call | flops 8999999488 | bytes 15000000 | tf_op jit(solution)/shard_map/cond/branch_1_fun/pallas_call | solution.py:297
  514.1 39.5 %collective-permute-done.3 = bf16[2,4,96,1024]{3,2,1,0:T(8,128)(2,1)} collective-permute-done((bf16[2,4,96,1024]{3,2,1,0:T(8,128)(2,1)}, bf16[2,4,96,1024]{3,2,1,0:T(8,128)(2,1)}, u32[]{:S(2)}, u32[]{:S(2)}) %collective-permute-start.3) | collective-permute-done | bytes 1572896 | tf_op jit(solution)/shard_map/cond/branch_1_fun/ppermute | solution.py:627
  553.6 2.6 fusion.3
  557.8 2.4 fusion
  562.0 2.7 add_convert_fusion.1
  564.7 25.8 %collective-permute-done.5 = bf16[4,96,1024]{2,1,0:T(8,128)(2,1)} collective-permute-done((bf16[4,96,1024]{2,1,0:T(8,128)(2,1)}, bf16[4,96,1024]{2,1,0:T(8,128)(2,1)}, u32[]{:S(2)}, u32[]{:S(2)}) %collective-permute-start.5) | collective-permute-done | bytes 786464 | tf_op jit(solution)/shard_map/cond/branch_1_fun/ppermute | solution.py:627
  590.5 6.5 collective-permute-done.7
  597.0 3.0 fusion.5
  600.2 1.8 collective-permute-start.8
  602.0 2.4 collective-permute-start.10
  605.2 6.3 collective-permute-done.8
  611.6 11.4 %collective-permute-done.10 = bf16[192,1024]{1,0:T(8,128)(2,1)S(1)} collective-permute-done((bf16[192,1024]{1,0:T(8,128)(2,1)S(1)}, bf16[192,1024]{1,0:T(8,128)(2,1)S(1)}, u32[]{:S(2)}, u32[]{:S(2)}) %collective-permute-start.10) | collective-permute-done | bytes 393248 | tf_op jit(solution)/shard_map/cond/branch_1_fun/ppermute | solution.py:561
  622.9 14.4 %collective-permute-done.9 = bf16[192,1024]{1,0:T(8,128)(2,1)S(1)} collective-permute-done((bf16[192,1024]{1,0:T(8,128)(2,1)S(1)}, bf16[192,1024]{1,0:T(8,128)(2,1)S(1)}, u32[]{:S(2)}, u32[]{:S(2)}) %collective-permute-start.9) | collective-permute-done | bytes 393248 | tf_op jit(solution)/shard_map/cond/branch_1_fun/ppermute | solution.py:561
  643.2 36.1 %collective-permute-done.16 = f32[18,1536]{1,0:T(8,128)} collective-permute-done((f32[18,1536]{1,0:T(8,128)}, f32[18,1536]{1,0:T(8,128)}, u32[]{:S(2)}, u32[]{:S(2)}) %collective-permute-start.16) | collective-permute-done | bytes 110624 | tf_op jit(solution)/shard_map/cond/branch_1_fun/ppermute | solution.py:950
  680.3 2.5 collective-permute-start.17
  685.4 3.8 collective-permute-done.17
  689.3 5.7 collective-permute-done.18
  696.8 3.8 add_convert_fusion.2
  703.0 5.8 branch_1_fun.15
  709.1 4.2 convert_reduce_fusion
  714.9 21.0 %convert_element_type.187 = f32[4,1536,1536]{2,1,0:T(8,128)} convert(bf16[4,1536,1536]{2,1,0:T(8,128)(2,1)} %all-reduce.6.cloned.1.call-done) | non-fusion elementwise | flops 9437184 | bytes 56623104 | tf_op jit(solution)/shard_map/convert_element_type | solution.py:873
  (227 shorter events, 80.0 us)
Async XLA Ops:
  7.2 195.1 %all-gather.3.cloned.1.call-start = ((), (), s32[]{:S(2)}) async-start(), calls=%async_computation.2 | async-start | bytes 7864320 | tf_op jit(solution)/shard_map/all_gather | solution.py:797
  14.6 12.9 %collective-permute-start.27 = (bf16[224,640]{1,0:T(8,128)(2,1)S(1)}, bf16[224,640]{1,0:T(8,128)(2,1)S(1)}, u32[]{:S(2)}, u32[]{:S(2)}) collective-permute-start(bf16[224,640]{1,0:T(8,128)(2,1)S(1)} %pad_maximum_fusion.9), channel_id=1, source_target_pairs={{0,3},{1,2},{2,1},{3,0},{4,7},{5,6},{6,5},{7,4},{8,11},{9,10},{10,... | collective-permute-start | bytes 860168 | tf_op jit(solution)/shard_map/ppermute | solution.py:561
  19.7 24.4 %collective-permute-start.26 = (bf16[224,640]{1,0:T(8,128)(2,1)S(1)}, bf16[224,640]{1,0:T(8,128)(2,1)S(1)}, u32[]{:S(2)}, u32[]{:S(2)}) collective-permute-start(bf16[224,640]{1,0:T(8,128)(2,1)S(1)} %pad_maximum_fusion.9), channel_id=1, source_target_pairs={{0,2},{1,3},{2,0},{3,1},{4,6},{5,7},{6,4},{7,5},{8,10},{9,11},{10,... | collective-permute-start | bytes 860168 | tf_op jit(solution)/shard_map/ppermute | solution.py:561
  19.7 24.4 %collective-permute-start.25 = (bf16[224,640]{1,0:T(8,128)(2,1)S(1)}, bf16[224,640]{1,0:T(8,128)(2,1)S(1)}, u32[]{:S(2)}, u32[]{:S(2)}) collective-permute-start(bf16[224,640]{1,0:T(8,128)(2,1)S(1)} %pad_maximum_fusion.9), channel_id=1, source_target_pairs={{0,1},{1,0},{2,3},{3,2},{4,5},{5,4},{6,7},{7,6},{8,9},{9,8},{10,11... | collective-permute-start | bytes 860168 | tf_op jit(solution)/shard_map/ppermute | solution.py:561
  44.3 7.8 %copy-start.6 = (bf16[512,1536]{1,0:T(8,128)(2,1)S(1)}, bf16[512,1536]{1,0:T(8,128)(2,1)}, u32[]{:S(2)}) copy-start(bf16[512,1536]{1,0:T(8,128)(2,1)} %param.13) | copy-start | bytes 4718596
  51.2 41.5 %copy-start.33 = (s32[2]{0:T(128)}, s32[2]{0:T(128)S(1)}, u32[]{:S(2)}) copy-start(s32[2]{0:T(128)S(1)} %pad_add_fusion.1) | copy-start | bytes 28
  52.5 9.3 %copy-start.30 = (f32[512]{0:T(512)}, f32[512]{0:T(512)S(1)}, u32[]{:S(2)}) copy-start(f32[512]{0:T(512)S(1)} %fusion.17) | copy-start | bytes 6148
  52.7 11.8 %collective-permute-start.33 = (bf16[192,384]{1,0:T(8,128)(2,1)}, bf16[192,384]{1,0:T(8,128)(2,1)S(1)}, u32[]{:S(2)}, u32[]{:S(2)}) collective-permute-start(bf16[192,384]{1,0:T(8,128)(2,1)} %dynamic_slice.84), channel_id=1, source_target_pairs={{0,3},{1,2},{2,1},{3,0},{4,7},{5,6},{6,5},{7,4},{8,11},{9,10},{10,... | collective-permute-start | bytes 442376 | tf_op jit(solution)/shard_map/ppermute | solution.py:561
  56.8 22.6 %collective-permute-start.32 = (bf16[192,384]{1,0:T(8,128)(2,1)}, bf16[192,384]{1,0:T(8,128)(2,1)S(1)}, u32[]{:S(2)}, u32[]{:S(2)}) collective-permute-start(bf16[192,384]{1,0:T(8,128)(2,1)} %dynamic_slice.84), channel_id=1, source_target_pairs={{0,2},{1,3},{2,0},{3,1},{4,6},{5,7},{6,4},{7,5},{8,10},{9,11},{10,... | collective-permute-start | bytes 442376 | tf_op jit(solution)/shard_map/ppermute | solution.py:561
  56.9 22.5 %collective-permute-start.31 = (bf16[192,384]{1,0:T(8,128)(2,1)}, bf16[192,384]{1,0:T(8,128)(2,1)}, u32[]{:S(2)}, u32[]{:S(2)}) collective-permute-start(bf16[192,384]{1,0:T(8,128)(2,1)} %dynamic_slice.84), channel_id=1, source_target_pairs={{0,1},{1,0},{2,3},{3,2},{4,5},{5,4},{6,7},{7,6},{8,9},{9,8},{10,11... | collective-permute-start | bytes 442376 | tf_op jit(solution)/shard_map/ppermute | solution.py:561
  58.8 22.4 %collective-permute-start.30 = (bf16[3,192,640]{2,1,0:T(8,128)(2,1)S(1)}, bf16[3,192,640]{2,1,0:T(8,128)(2,1)}, u32[]{:S(2)}, u32[]{:S(2)}) collective-permute-start(bf16[3,192,640]{2,1,0:T(8,128)(2,1)S(1)} %slice.113), channel_id=1, source_target_pairs={{0,24},{4,28},{8,16},{12,20},{16,8},{20,12},{24,0},{28,4},{1,25},{... | collective-permute-start | bytes 2211848 | tf_op jit(solution)/shard_map/ppermute | solution.py:627
  61.2 31.1 %collective-permute-start.29 = (bf16[3,192,640]{2,1,0:T(8,128)(2,1)S(1)}, bf16[3,192,640]{2,1,0:T(8,128)(2,1)}, u32[]{:S(2)}, u32[]{:S(2)}) collective-permute-start(bf16[3,192,640]{2,1,0:T(8,128)(2,1)S(1)} %slice.113), channel_id=1, source_target_pairs={{0,16},{4,20},{8,24},{12,28},{16,0},{20,4},{24,8},{28,12},{1,17},{... | collective-permute-start | bytes 2211848 | tf_op jit(solution)/shard_map/ppermute | solution.py:627
  61.8 6.7 copy-start.27
  64.4 28.0 %collective-permute-start.28 = (bf16[3,192,640]{2,1,0:T(8,128)(2,1)S(1)}, bf16[3,192,640]{2,1,0:T(8,128)(2,1)}, u32[]{:S(2)}, u32[]{:S(2)}) collective-permute-start(bf16[3,192,640]{2,1,0:T(8,128)(2,1)S(1)} %slice.113), channel_id=1, source_target_pairs={{0,8},{4,12},{8,0},{12,4},{16,24},{20,28},{24,16},{28,20},{1,9},{5... | collective-permute-start | bytes 2211848 | tf_op jit(solution)/shard_map/ppermute | solution.py:627
  68.6 11.5 %copy-start.23 = (bf16[192,384]{1,0:T(8,128)(2,1)S(1)}, bf16[192,384]{1,0:T(8,128)(2,1)}, u32[]{:S(2)}) copy-start(bf16[192,384]{1,0:T(8,128)(2,1)} %copy-done.22) | copy-start | bytes 442372
  102.6 7.1 collective-permute-start.20
  105.2 8.0 %copy-start.15 = (bf16[512,1536]{1,0:T(8,128)(2,1)S(1)}, bf16[512,1536]{1,0:T(8,128)(2,1)}, u32[]{:S(2)}) copy-start(bf16[512,1536]{1,0:T(8,128)(2,1)} %get-tuple-element.111.normed_ref) | copy-start | bytes 4718596 | tf_op jit(solution)/shard_map/cond
  109.8 30.5 %collective-permute-start.23 = (bf16[3,192,384]{2,1,0:T(8,128)(2,1)S(1)}, bf16[3,192,384]{2,1,0:T(8,128)(2,1)}, u32[]{:S(2)}, u32[]{:S(2)}) collective-permute-start(bf16[3,192,384]{2,1,0:T(8,128)(2,1)S(1)} %get-tuple-element.109), channel_id=1, source_target_pairs={{0,24},{4,28},{8,16},{12,20},{16,8},{20,12},{24,0},{28,4},{1,25},{... | collective-permute-start | bytes 1327112 | tf_op jit(solution)/shard_map/cond/branch_1_fun/ppermute | solution.py:627
  111.4 29.9 %collective-permute-start.22 = (bf16[3,192,384]{2,1,0:T(8,128)(2,1)S(1)}, bf16[3,192,384]{2,1,0:T(8,128)(2,1)}, u32[]{:S(2)}, u32[]{:S(2)}) collective-permute-start(bf16[3,192,384]{2,1,0:T(8,128)(2,1)S(1)} %get-tuple-element.109), channel_id=1, source_target_pairs={{0,16},{4,20},{8,24},{12,28},{16,0},{20,4},{24,8},{28,12},{1,17},{... | collective-permute-start | bytes 1327112 | tf_op jit(solution)/shard_map/cond/branch_1_fun/ppermute | solution.py:627
  112.7 29.7 %collective-permute-start.21 = (bf16[3,192,384]{2,1,0:T(8,128)(2,1)S(1)}, bf16[3,192,384]{2,1,0:T(8,128)(2,1)S(1)}, u32[]{:S(2)}, u32[]{:S(2)}) collective-permute-start(bf16[3,192,384]{2,1,0:T(8,128)(2,1)S(1)} %get-tuple-element.109), channel_id=1, source_target_pairs={{0,8},{4,12},{8,0},{12,4},{16,24},{20,28},{24,16},{28,20},{1,9},{5... | collective-permute-start | bytes 1327112 | tf_op jit(solution)/shard_map/cond/branch_1_fun/ppermute | solution.py:627
  144.2 4.9 collective-permute-start.24
  159.6 36.9 %copy-start.25 = (f32[4,8,512]{2,1,0:T(8,128)}, f32[4,8,512]{2,1,0:T(8,128)S(1)}, u32[]{:S(2)}) copy-start(f32[4,8,512]{2,1,0:T(8,128)S(1)} %get-tuple-element.265) | copy-start | bytes 196612
  159.6 36.9 %collective-permute-start.35 = (bf16[512,1536]{1,0:T(8,128)(2,1)}, bf16[512,1536]{1,0:T(8,128)(2,1)}, u32[]{:S(2)}, u32[]{:S(2)}) collective-permute-start(bf16[512,1536]{1,0:T(8,128)(2,1)} %get-tuple-element.229.inner_ref.outer_ref), channel_id=1, source_target_pairs={{1,2},{2,1},{5,6},{6,5},{9,10},{10,9},{13,14},{14,13},{17,18},{18,... | collective-permute-start | bytes 4718600 | tf_op jit(solution)/shard_map/ppermute | solution.py:589
  161.6 40.6 %collective-permute-start.34 = (bf16[512,1536]{1,0:T(8,128)(2,1)}, bf16[512,1536]{1,0:T(8,128)(2,1)}, u32[]{:S(2)}, u32[]{:S(2)}) collective-permute-start(bf16[512,1536]{1,0:T(8,128)(2,1)} %get-tuple-element.229.inner_ref.outer_ref), channel_id=1, source_target_pairs={{0,1},{1,0},{2,3},{3,2},{4,5},{5,4},{6,7},{7,6},{8,9},{9,8},{10,11... | collective-permute-start | bytes 4718600 | tf_op jit(solution)/shard_map/ppermute | solution.py:561
  163.4 42.3 %copy-start.17 = (bf16[1536,128]{1,0:T(8,128)(2,1)S(1)}, bf16[1536,128]{1,0:T(8,128)(2,1)}, u32[]{:S(2)}) copy-start(bf16[1536,128]{1,0:T(8,128)(2,1)} %pad.21.router_ref) | copy-start | bytes 1179652
  202.2 43.1 %collective-permute-start.36 = (bf16[512,1536]{1,0:T(8,128)(2,1)}, bf16[512,1536]{1,0:T(8,128)(2,1)}, u32[]{:S(2)}, u32[]{:S(2)}) collective-permute-start(bf16[512,1536]{1,0:T(8,128)(2,1)} %collective-permute-done.34.outer_ref.inner_ref), channel_id=1, source_target_pairs={{1,2},{2,1},{5,6},{6,5},{9,10},{10,9},{13,14},{14,13},{17,18},{18,... | collective-permute-start | bytes 4718600 | tf_op jit(solution)/shard_map/ppermute | solution.py:593
  204.0 42.8 %collective-permute-start.38 = (bf16[512,1536]{1,0:T(8,128)(2,1)}, bf16[512,1536]{1,0:T(8,128)(2,1)}, u32[]{:S(2)}, u32[]{:S(2)}) collective-permute-start(bf16[512,1536]{1,0:T(8,128)(2,1)} %collective-permute-done.35.inner_ref), channel_id=1, source_target_pairs={{1,0},{2,3},{5,4},{6,7},{9,8},{10,11},{13,12},{14,15},{17,16},{18,... | collective-permute-start | bytes 4718600 | tf_op jit(solution)/shard_map/ppermute | solution.py:594
  237.2 83.4 %collective-permute-start.40 = (bf16[512,1664]{1,0:T(8,128)(2,1)}, bf16[512,1664]{1,0:T(8,128)(2,1)}, u32[]{:S(2)}, u32[]{:S(2)}) collective-permute-start(bf16[512,1664]{1,0:T(8,128)(2,1)} %get-tuple-element.238), channel_id=1, source_target_pairs={{1,2},{2,1},{5,6},{6,5},{9,10},{10,9},{13,14},{14,13},{17,18},{18,... | collective-permute-start | bytes 5111816 | tf_op jit(solution)/shard_map/ppermute | solution.py:616
  239.1 133.6 %collective-permute-start.39 = (bf16[512,1664]{1,0:T(8,128)(2,1)}, bf16[512,1664]{1,0:T(8,128)(2,1)S(1)}, u32[]{:S(2)}, u32[]{:S(2)}) collective-permute-start(bf16[512,1664]{1,0:T(8,128)(2,1)} %get-tuple-element.238), channel_id=1, source_target_pairs={{0,1},{3,2},{4,5},{7,6},{8,9},{11,10},{12,13},{15,14},{16,17},{19,... | collective-permute-start | bytes 5111816 | tf_op jit(solution)/shard_map/ppermute | solution.py:616
  245.4 42.6 %collective-permute-start.37 = (bf16[512,1536]{1,0:T(8,128)(2,1)}, bf16[512,1536]{1,0:T(8,128)(2,1)}, u32[]{:S(2)}, u32[]{:S(2)}) collective-permute-start(bf16[512,1536]{1,0:T(8,128)(2,1)} %collective-permute-done.36.inner_ref), channel_id=1, source_target_pairs={{1,0},{2,3},{5,4},{6,7},{9,8},{10,11},{13,12},{14,15},{17,16},{18,... | collective-permute-start | bytes 4718600 | tf_op jit(solution)/shard_map/ppermute | solution.py:597
  246.8 41.1 %copy-start.18 = (bf16[1536,128]{1,0:T(8,128)(2,1)S(1)}, bf16[1536,128]{1,0:T(8,128)(2,1)}, u32[]{:S(2)}) copy-start(bf16[1536,128]{1,0:T(8,128)(2,1)} %pad.21.router_ref) | copy-start | bytes 1179652
  278.4 94.2 %collective-permute-start.42 = (bf16[512,1664]{1,0:T(8,128)(2,1)}, bf16[512,1664]{1,0:T(8,128)(2,1)S(1)}, u32[]{:S(2)}, u32[]{:S(2)}) collective-permute-start(bf16[512,1664]{1,0:T(8,128)(2,1)} %get-tuple-element.239), channel_id=1, source_target_pairs={{1,0},{2,3},{5,4},{6,7},{9,8},{10,11},{13,12},{14,15},{17,16},{18,... | collective-permute-start | bytes 5111816 | tf_op jit(solution)/shard_map/ppermute | solution.py:616
  279.7 93.0 %collective-permute-start.41 = (bf16[512,1664]{1,0:T(8,128)(2,1)}, bf16[512,1664]{1,0:T(8,128)(2,1)}, u32[]{:S(2)}, u32[]{:S(2)}) collective-permute-start(bf16[512,1664]{1,0:T(8,128)(2,1)} %get-tuple-element.239), channel_id=1, source_target_pairs={{0,2},{3,1},{4,6},{7,5},{8,10},{11,9},{12,14},{15,13},{16,18},{19,... | collective-permute-start | bytes 5111816 | tf_op jit(solution)/shard_map/ppermute | solution.py:616
  319.4 77.6 %collective-permute-start.44 = (bf16[512,1664]{1,0:T(8,128)(2,1)}, bf16[512,1664]{1,0:T(8,128)(2,1)}, u32[]{:S(2)}, u32[]{:S(2)}) collective-permute-start(bf16[512,1664]{1,0:T(8,128)(2,1)} %get-tuple-element.240), channel_id=1, source_target_pairs={{1,3},{2,0},{5,7},{6,4},{9,11},{10,8},{13,15},{14,12},{17,19},{18,... | collective-permute-start | bytes 5111816 | tf_op jit(solution)/shard_map/ppermute | solution.py:616
  320.7 76.3 %collective-permute-start.43 = (bf16[512,1664]{1,0:T(8,128)(2,1)}, bf16[512,1664]{1,0:T(8,128)(2,1)}, u32[]{:S(2)}, u32[]{:S(2)}) collective-permute-start(bf16[512,1664]{1,0:T(8,128)(2,1)} %get-tuple-element.240), channel_id=1, source_target_pairs={{0,3},{3,0},{4,7},{7,4},{8,11},{11,8},{12,15},{15,12},{16,19},{19,... | collective-permute-start | bytes 5111816 | tf_op jit(solution)/shard_map/ppermute | solution.py:616
  372.7 24.3 %copy-start.13 = (bf16[512,1664]{1,0:T(8,128)(2,1)}, bf16[512,1664]{1,0:T(8,128)(2,1)S(1)}, u32[]{:S(2)}) copy-start(bf16[512,1664]{1,0:T(8,128)(2,1)S(1)} %collective-permute-done.39) | copy-start | bytes 5111812
  372.7 24.3 %copy-start.14 = (bf16[512,1664]{1,0:T(8,128)(2,1)}, bf16[512,1664]{1,0:T(8,128)(2,1)S(1)}, u32[]{:S(2)}) copy-start(bf16[512,1664]{1,0:T(8,128)(2,1)S(1)} %collective-permute-done.42) | copy-start | bytes 5111812
  397.0 312.0 %all-to-all-start = ((bf16[4,512,1536]{2,1,0:T(8,128)(2,1)}), bf16[4,512,1536]{2,1,0:T(8,128)(2,1)}, u32[]{:S(2)}, u32[]{:S(2)}) async-start(bf16[4,512,1536]{2,1,0:T(8,128)(2,1)} %get-tuple-element.260), calls=%async_computation | async-start | bytes 12582912 | tf_op jit(solution)/shard_map/all_to_all | solution.py:881
  402.3 312.5 %all-reduce.6.cloned.1.call-start = ((), (), s32[]{:S(2)}) async-start(), calls=%async_computation.1 | async-start | bytes 37748736 | tf_op jit(solution)/shard_map/psum | solution.py:873
  445.3 17.9 %collective-permute-start.1 = (bf16[4,192,1024]{2,1,0:T(8,128)(2,1)}, bf16[4,192,1024]{2,1,0:T(8,128)(2,1)}, u32[]{:S(2)}, u32[]{:S(2)}) collective-permute-start(bf16[4,192,1024]{2,1,0:T(8,128)(2,1)} %get-tuple-element.154), channel_id=1, source_target_pairs={{0,4},{4,0},{8,12},{12,8},{16,20},{20,16},{24,28},{28,24},{1,5},{5... | collective-permute-start | bytes 4718600 | tf_op jit(solution)/shard_map/cond/branch_1_fun/ppermute | solution.py:627
  462.6 22.5 %collective-permute-start = (bf16[4,192,1024]{2,1,0:T(8,128)(2,1)}, bf16[4,192,1024]{2,1,0:T(8,128)(2,1)}, u32[]{:S(2)}, u32[]{:S(2)}) collective-permute-start(bf16[4,192,1024]{2,1,0:T(8,128)(2,1)} %get-tuple-element.151), channel_id=1, source_target_pairs={{0,4},{4,0},{8,12},{12,8},{16,20},{20,16},{24,28},{28,24},{1,5},{5... | collective-permute-start | bytes 4718600 | tf_op jit(solution)/shard_map/cond/branch_1_fun/ppermute | solution.py:627
  485.1 7.7 %collective-permute-start.4 = (bf16[4,192,1024]{2,1,0:T(8,128)(2,1)}, bf16[4,192,1024]{2,1,0:T(8,128)(2,1)S(1)}, u32[]{:S(2)}, u32[]{:S(2)}) collective-permute-start(bf16[4,192,1024]{2,1,0:T(8,128)(2,1)} %get-tuple-element.166), channel_id=1, source_target_pairs={{0,4},{4,0},{8,12},{12,8},{16,20},{20,16},{24,28},{28,24},{1,5},{5... | collective-permute-start | bytes 4718600 | tf_op jit(solution)/shard_map/cond/branch_1_fun/ppermute | solution.py:627
  491.1 62.5 %collective-permute-start.3 = (bf16[2,4,96,1024]{3,2,1,0:T(8,128)(2,1)}, bf16[2,4,96,1024]{3,2,1,0:T(8,128)(2,1)}, u32[]{:S(2)}, u32[]{:S(2)}) collective-permute-start(bf16[2,4,96,1024]{3,2,1,0:T(8,128)(2,1)} %pad_maximum_fusion.2), channel_id=1, source_target_pairs={{0,8},{4,12},{8,0},{12,4},{16,24},{20,28},{24,16},{28,20},{1,9},{5... | collective-permute-start | bytes 4718600 | tf_op jit(solution)/shard_map/cond/branch_1_fun/ppermute | solution.py:627
  495.2 62.6 %collective-permute-start.6 = (bf16[2,4,96,1024]{3,2,1,0:T(8,128)(2,1)}, bf16[2,4,96,1024]{3,2,1,0:T(8,128)(2,1)}, u32[]{:S(2)}, u32[]{:S(2)}) collective-permute-start(bf16[2,4,96,1024]{3,2,1,0:T(8,128)(2,1)} %pad_maximum_fusion.3), channel_id=1, source_target_pairs={{0,16},{4,20},{8,24},{12,28},{16,0},{20,4},{24,8},{28,12},{1,17},{... | collective-permute-start | bytes 4718600 | tf_op jit(solution)/shard_map/cond/branch_1_fun/ppermute | solution.py:627
  514.0 43.8 %copy-start.11 = (bf16[4,192,1024]{2,1,0:T(8,128)(2,1)S(1)}, bf16[4,192,1024]{2,1,0:T(8,128)(2,1)}, u32[]{:S(2)}) copy-start(bf16[4,192,1024]{2,1,0:T(8,128)(2,1)} %copy-done.10) | copy-start | bytes 4718596 | tf_op jit(solution)/shard_map/cond
  514.0 48.0 %collective-permute-start.2 = (bf16[4,192,1024]{2,1,0:T(8,128)(2,1)}, bf16[4,192,1024]{2,1,0:T(8,128)(2,1)}, u32[]{:S(2)}, u32[]{:S(2)}) collective-permute-start(bf16[4,192,1024]{2,1,0:T(8,128)(2,1)} %get-tuple-element.164), channel_id=1, source_target_pairs={{0,4},{4,0},{8,12},{12,8},{16,20},{20,16},{24,28},{28,24},{1,5},{5... | collective-permute-start | bytes 4718600 | tf_op jit(solution)/shard_map/cond/branch_1_fun/ppermute | solution.py:627
  556.1 34.4 %collective-permute-start.5 = (bf16[4,96,1024]{2,1,0:T(8,128)(2,1)}, bf16[4,96,1024]{2,1,0:T(8,128)(2,1)}, u32[]{:S(2)}, u32[]{:S(2)}) collective-permute-start(bf16[4,96,1024]{2,1,0:T(8,128)(2,1)} %fusion.3), channel_id=1, source_target_pairs={{0,16},{4,20},{8,24},{12,28},{16,0},{20,4},{24,8},{28,12},{1,17},{... | collective-permute-start | bytes 2359304 | tf_op jit(solution)/shard_map/cond/branch_1_fun/ppermute | solution.py:627
  560.2 36.8 %collective-permute-start.7 = (bf16[4,96,1024]{2,1,0:T(8,128)(2,1)}, bf16[4,96,1024]{2,1,0:T(8,128)(2,1)}, u32[]{:S(2)}, u32[]{:S(2)}) collective-permute-start(bf16[4,96,1024]{2,1,0:T(8,128)(2,1)} %fusion), channel_id=1, source_target_pairs={{0,8},{4,12},{8,0},{12,4},{16,24},{20,28},{24,16},{28,20},{1,9},{5... | collective-permute-start | bytes 2359304 | tf_op jit(solution)/shard_map/cond/branch_1_fun/ppermute | solution.py:627
  597.0 7.4 copy-start.1
  600.2 11.4 %collective-permute-start.8 = (bf16[192,1024]{1,0:T(8,128)(2,1)S(1)}, bf16[192,1024]{1,0:T(8,128)(2,1)S(1)}, u32[]{:S(2)}, u32[]{:S(2)}) collective-permute-start(bf16[192,1024]{1,0:T(8,128)(2,1)S(1)} %get-tuple-element.388), channel_id=1, source_target_pairs={{0,1},{1,0},{2,3},{3,2},{4,5},{5,4},{6,7},{7,6},{8,9},{9,8},{10,11... | collective-permute-start | bytes 1179656 | tf_op jit(solution)/shard_map/cond/branch_1_fun/ppermute | solution.py:561
  602.0 20.9 %collective-permute-start.10 = (bf16[192,1024]{1,0:T(8,128)(2,1)S(1)}, bf16[192,1024]{1,0:T(8,128)(2,1)S(1)}, u32[]{:S(2)}, u32[]{:S(2)}) collective-permute-start(bf16[192,1024]{1,0:T(8,128)(2,1)S(1)} %get-tuple-element.389), channel_id=1, source_target_pairs={{0,3},{1,2},{2,1},{3,0},{4,7},{5,6},{6,5},{7,4},{8,11},{9,10},{10,... | collective-permute-start | bytes 1179656 | tf_op jit(solution)/shard_map/cond/branch_1_fun/ppermute | solution.py:561
  604.4 33.0 %collective-permute-start.9 = (bf16[192,1024]{1,0:T(8,128)(2,1)S(1)}, bf16[192,1024]{1,0:T(8,128)(2,1)S(1)}, u32[]{:S(2)}, u32[]{:S(2)}) collective-permute-start(bf16[192,1024]{1,0:T(8,128)(2,1)S(1)} %get-tuple-element.390), channel_id=1, source_target_pairs={{0,2},{1,3},{2,0},{3,1},{4,6},{5,7},{6,4},{7,5},{8,10},{9,11},{10,... | collective-permute-start | bytes 1179656 | tf_op jit(solution)/shard_map/cond/branch_1_fun/ppermute | solution.py:561
  605.2 36.0 %collective-permute-start.15 = (f32[18,1536]{1,0:T(8,128)S(1)}, f32[18,1536]{1,0:T(8,128)S(1)}, u32[]{:S(2)}, u32[]{:S(2)}) collective-permute-start(f32[18,1536]{1,0:T(8,128)S(1)} %pad_maximum_fusion.6), channel_id=1, source_target_pairs={{0,4},{4,0},{8,12},{12,8},{16,20},{20,16},{24,28},{28,24},{1,5},{5... | collective-permute-start | bytes 331784 | tf_op jit(solution)/shard_map/cond/branch_1_fun/ppermute | solution.py:950
  637.6 45.2 %collective-permute-start.13 = (bf16[192,1024]{1,0:T(8,128)(2,1)S(1)}, bf16[192,1024]{1,0:T(8,128)(2,1)}, u32[]{:S(2)}, u32[]{:S(2)}) collective-permute-start(bf16[192,1024]{1,0:T(8,128)(2,1)S(1)} %fusion.8), channel_id=1, source_target_pairs={{0,24},{4,28},{8,16},{12,20},{16,8},{20,12},{24,0},{28,4},{1,25},{... | collective-permute-start | bytes 1179656 | tf_op jit(solution)/shard_map/cond/branch_1_fun/ppermute | solution.py:627
  639.2 43.6 %collective-permute-start.12 = (bf16[192,1024]{1,0:T(8,128)(2,1)S(1)}, bf16[192,1024]{1,0:T(8,128)(2,1)}, u32[]{:S(2)}, u32[]{:S(2)}) collective-permute-start(bf16[192,1024]{1,0:T(8,128)(2,1)S(1)} %fusion.8), channel_id=1, source_target_pairs={{0,16},{4,20},{8,24},{12,28},{16,0},{20,4},{24,8},{28,12},{1,17},{... | collective-permute-start | bytes 1179656 | tf_op jit(solution)/shard_map/cond/branch_1_fun/ppermute | solution.py:627
  639.9 42.9 %collective-permute-start.11 = (bf16[192,1024]{1,0:T(8,128)(2,1)S(1)}, bf16[192,1024]{1,0:T(8,128)(2,1)}, u32[]{:S(2)}, u32[]{:S(2)}) collective-permute-start(bf16[192,1024]{1,0:T(8,128)(2,1)S(1)} %fusion.8), channel_id=1, source_target_pairs={{0,8},{4,12},{8,0},{12,4},{16,24},{20,28},{24,16},{28,20},{1,9},{5... | collective-permute-start | bytes 1179656 | tf_op jit(solution)/shard_map/cond/branch_1_fun/ppermute | solution.py:627
  641.9 37.4 %collective-permute-start.16 = (f32[18,1536]{1,0:T(8,128)}, f32[18,1536]{1,0:T(8,128)}, u32[]{:S(2)}, u32[]{:S(2)}) collective-permute-start(f32[18,1536]{1,0:T(8,128)} %fusion.16), channel_id=1, source_target_pairs={{0,8},{4,12},{8,0},{12,4},{16,24},{20,28},{24,16},{28,20},{1,9},{5... | collective-permute-start | bytes 331784 | tf_op jit(solution)/shard_map/cond/branch_1_fun/ppermute | solution.py:950
  680.3 8.9 %collective-permute-start.17 = (f32[18,1536]{1,0:T(8,128)S(1)}, f32[18,1536]{1,0:T(8,128)S(1)}, u32[]{:S(2)}, u32[]{:S(2)}) collective-permute-start(f32[18,1536]{1,0:T(8,128)S(1)} %add.236), channel_id=1, source_target_pairs={{0,16},{4,20},{8,24},{12,28},{16,0},{20,4},{24,8},{28,12},{1,17},{... | collective-permute-start | bytes 331784 | tf_op jit(solution)/shard_map/cond/branch_1_fun/ppermute | solution.py:950
  682.8 14.0 %copy-start.2 = (f32[512,1536]{1,0:T(8,128)S(1)}, f32[512,1536]{1,0:T(8,128)}, u32[]{:S(2)}) copy-start(f32[512,1536]{1,0:T(8,128)} %get-tuple-element.158) | copy-start | bytes 9437188 | tf_op jit(solution)/shard_map/cond
  682.8 13.9 %copy-start.32 = (f32[512]{0:T(512)S(1)}, f32[512]{0:T(512)}, u32[]{:S(2)}) copy-start(f32[512]{0:T(512)} %add_rsqrt_fusion) | copy-start | bytes 6148 | tf_op jit(solution)/shard_map/cond
  684.6 16.0 %copy-start.8 = (bf16[4,192,1024]{2,1,0:T(8,128)(2,1)}, bf16[4,192,1024]{2,1,0:T(8,128)(2,1)S(1)}, u32[]{:S(2)}) copy-start(bf16[4,192,1024]{2,1,0:T(8,128)(2,1)S(1)} %pad_maximum_fusion.4.own_ref) | copy-start | bytes 4718596 | tf_op jit(solution)/shard_map/cond
  684.6 18.4 %collective-permute-start.14 = (bf16[4,192,1024]{2,1,0:T(8,128)(2,1)S(1)}, bf16[4,192,1024]{2,1,0:T(8,128)(2,1)}, u32[]{:S(2)}, u32[]{:S(2)}) collective-permute-start(bf16[4,192,1024]{2,1,0:T(8,128)(2,1)S(1)} %pad_maximum_fusion.4.own_ref), channel_id=1, source_target_pairs={{0,4},{4,0},{8,12},{12,8},{16,20},{20,16},{24,28},{28,24},{1,5},{5... | collective-permute-start | bytes 4718600 | tf_op jit(solution)/shard_map/cond/branch_1_fun/ppermute | solution.py:627
  689.2 5.8 collective-permute-start.18
  695.1 6.7 collective-permute-start.19
  (19 other events, 43.0 us)
Sparse Core Ops, SparseCore 0:
  44.5 127.9 all-gather.2
  407.5 302.9 all-reduce.5

commit v4 on v3

--- a/solution.py
+++ b/solution.py
@@ -315,7 +315,8 @@
 
 
 def expert_kernel(
-    first_ref,
+    sequences,
+    table_ref,
     inner_ref,
     outer_ref,
     upstream_ref,
@@ -336,16 +337,16 @@
         combined_total,
     ) = refs[-9:]
     step, steps = pl.program_id(0), pl.num_programs(0)
-    index = first_ref[0] + step
+    index = table_ref[sequences + 1] + step
     lane = lax.broadcasted_iota(jnp.int32, gates_ref.shape, 1)
 
     @pl.when(step == 0)
     def _():
-        @pl.when(first_ref[3] > 0)
+        @pl.when(table_ref[sequences + 2] > 0)
         def _():
             fed_ref[...] = inner_ref[...]
 
-        @pl.when(first_ref[3] == 0)
+        @pl.when(table_ref[sequences + 2] == 0)
         def _():
             fed_ref[...] = outer_ref[...]
 
@@ -398,7 +399,7 @@
         combined_ref[0] = combined_total[...].astype(bf16)
 
 
-def expert_slot(at, choices, upstream, chosen, router, weights, combined):
+def expert_slot(at, k, choices, upstream, chosen, router, weights, combined):
     length, features = choices[0].shape
     count = weights.shape[0]
     held = [] if isinstance(combined, int) else [combined]
@@ -409,15 +410,15 @@
         (1,) + shape, lambda e, at: (at[i],) + (0,) * len(shape)
     )
     return pl.pallas_call(
-        expert_kernel,
+        functools.partial(expert_kernel, sequences),
         grid_spec=pltpu.PrefetchScalarGridSpec(
             num_scalar_prefetch=1,
             grid=(count,),
             in_specs=[
                 full(length, features),
                 full(length, features),
-                there(1, length, features),
-                there(2, length, LANES),
+                there(sequences + 3 + k, length, features),
+                there(k, length, LANES),
                 full(features, LANES),
                 each(features, 3 * FF),
             ]
@@ -425,7 +426,7 @@
             out_specs=[
                 full(length, features),
                 full(length, features + LANES),
-                there(2, length, features),
+                there(k, length, features),
                 each(length, 2 * FF),
                 each(length, FF),
             ],
@@ -639,13 +640,8 @@
     return [hop(near, 2 * m) for m in range(1, 4)]
 
 
-def join_pairs(local, parts, core, spot, earlier=()):
-    own = jnp.stack(
-        [
-            jnp.concatenate([local(spot ^ m, core)[None], part])
-            for m, part in enumerate(parts)
-        ]
-    )
+def join_pairs(own, parts, earlier=()):
+    own = jnp.concatenate([own[:, None], jnp.stack(parts)], axis=1)
     own = after(own, *earlier)
     return own, hop(own, 1)
 
@@ -764,16 +760,22 @@
         ]
     )
     if special:
-        extra = -(-small.size // (16 * PAIR_WIDTH)) * 16
-        below = jnp.pad(small, (0, extra * PAIR_WIDTH - small.size)).reshape(extra, PAIR_WIDTH)
-        near = gather_near(jnp.concatenate([projection_share(spot, core), below]))
-        projection_near = near[:, :half]
+        projection_own = jnp.stack([projection_share(spot ^ m, core) for m in range(PAIRS)])
+        output_own = jnp.stack([output_share(spot ^ m, core) for m in range(PAIRS)])
+        projection_near = gather_near(projection_own[0])
+        projection_near, projection_own, output_own = after(
+            (projection_near, projection_own, output_own)
+        )
+        projection_sent = send_pairs(projection_near)
+        extra = -(-small.size // (16 * PAIR_QUERY)) * 16
+        below = jnp.pad(small, (0, extra * PAIR_QUERY - small.size)).reshape(extra, PAIR_QUERY)
+        near = jnp.concatenate([output_own[0], below])
+        near = gather_near(after(near, projection_near))
+        output_near = near[:, :half]
         small_slots = jnp.concatenate(
             [small[None], near[:, half:].reshape(3, -1)[:, : small.size]]
         )
         small_all = jnp.stack([pick(small_slots, place ^ k) for k in range(4)])
-        projection_sent = send_pairs(projection_near)
-        output_near = gather_near(after(output_share(spot, core), projection_near))
         cotangent_sent = after(cotangent, projection_near)
     else:
         gathered = lax.all_gather(projection, "shard", axis=0)
@@ -801,24 +803,18 @@
     scaled_in, inverse_in = norm_rows(residual)
     attention_scale = small_all[:, :own].reshape(features).astype(f32)
     feed_scale = small_all[:, own : 2 * own].reshape(features).astype(f32)
-    router_full = small_all[:, 2 * own : (2 + EXPERTS) * own].reshape(features, EXPERTS)
-    chosen_all = small_all[:, (2 + EXPERTS) * own :].reshape(places, length, EXPERTS).astype(f32)
     normed = (scaled_in * attention_scale).astype(bf16)
     where = jnp.stack([base, core]).astype(jnp.int32)
 
     def attention():
         if special:
-            attend_weights = join_pairs(
-                projection_share, [projection_near] + projection_sent, core, spot
-            )
+            attend_weights = join_pairs(projection_own, [projection_near] + projection_sent)
             output_sent = send_pairs(after(output_near, attend_weights))
         else:
             attend_weights = attend_columns
         kept = attend_forward(where, normed, attend_weights, tables)
         if special:
-            output_weights = join_pairs(
-                output_share, [output_near] + output_sent, core, spot, [kept[0]]
-            )
+            output_weights = join_pairs(output_own, [output_near] + output_sent, [kept[0]])
         else:
             output_weights = output_columns
         rows = middle_rows(where, kept[0], output_weights, inputs, feed_scale[None])
@@ -844,19 +840,21 @@
         ],
     )
     attend_weights, output_weights = (own_a, other_a), (own_o, other_o)
+    small_late = after(small_all, fed)
+    router_full = small_late[:, 2 * own : (2 + EXPERTS) * own].reshape(features, EXPERTS)
+    chosen_all = small_late[:, (2 + EXPERTS) * own :].reshape(places, length, EXPERTS).astype(f32)
     router_wide = jnp.pad(router_full, ((0, 0), (0, LANES - EXPERTS)))
     chosen_wide = jnp.pad(chosen_all, ((0, 0), (0, 0), (0, LANES - EXPERTS)))
     rows, pair_grads, gated = [], [], []
     combined = places
     order = sources(place, places)
-    middle_place = inside(place).astype(jnp.int32)
+    entries = [*order, core, place * local, inside(place), 0, *order[1:]]
+    table = jnp.stack([jnp.asarray(e, jnp.int32) for e in entries])
     fed_slots, rows_come, arriving = [], [], line_gather(fed, place, places)
     for k, source in enumerate(order):
-        index = jnp.zeros_like(source) if k == 0 else source
-        at = jnp.stack([place * local, index, source, middle_place]).astype(jnp.int32)
         rows_up = cotangent[None] if k == 0 else upstream_all
         fed_k, row, combined, *kept = expert_slot(
-            at, next(arriving), rows_up, chosen_wide, router_wide, expert_weight, combined
+            table, k, next(arriving), rows_up, chosen_wide, router_wide, expert_weight, combined
         )
         for held, value in zip((fed_slots, rows, pair_grads, gated), (fed_k, row, *kept)):
             held.append(value)
@@ -864,7 +862,7 @@
         if special and k:
             rows_come += line_send(row, k)
     expert_term = expert_grads(
-        jnp.stack(order).astype(jnp.int32),
+        table,
         fed_slots,
         upstream_all,
         pair_grads,

time: 751 us -> 746 us (level)
    ppermute x10, waiting for transfers between devices: 72.6 us -> 84.9 us  [exchange(): return lax.ppermute(value, 'shard', [(i, i ^ k) for i in range(4)])]
    another operation x14 -> x6, other arithmetic: 15.2 us -> 4.22 us  [the longest x8 9.16 us: join_pairs(): jnp.stack([jnp.concatenate([local(spot ^ m, core)[None], part]) for m, pa...]
    ppermute x20, waiting for transfers between devices: 90.5 us -> 82.2 us  [hop(): return lax.ppermute(value, 'rep', [(i, i ^ bit) for i in range(8)])]
  transfers between devices with their start and end apart: 48 -> 48, of which waited for: 20 -> 20; matrix products, arithmetic and copies ran while one was open for 11% -> 10% of each run, Pallas kernels for 41% -> 41%
where the time goes in v4:
time: 746 us; the launch traced here: 738 us
  Pallas kernels  302 us (40%)
  waiting for transfers between devices  240 us (32%)
  starting transfers between devices  74.3 us (10%)
  other arithmetic  73.4 us (10%)
  local copies, waits for them, and re-layouts  31.8 us (4%)
  between operations  16 us (2%)
    pallas_call x4, Pallas kernels, expert_slot(): pl.pallas_call(functools.partial(expert_kernel, sequences), grid_spec=plt...  127 us
    ppermute x10, waiting for transfers between devices, exchange(): return lax.ppermute(value, 'shard', [(i, i ^ k) for i in range(4)])  84.9 us
    ppermute x20, waiting for transfers between devices, hop(): return lax.ppermute(value, 'rep', [(i, i ^ bit) for i in range(8)])  82.2 us
    pallas_call x4, Pallas kernels, attend_backward(): pl.pallas_call(attend_backward_kernel, grid_spec=pltpu.PrefetchScalarGrid...  70.1 us
    pallas_call x1, Pallas kernels, expert_grads(): pl.pallas_call(expert_grad_kernel, grid_spec=pltpu.PrefetchScalarGridSpec...  48.5 us
    ppermute x5, waiting for transfers between devices, rest(): small_terms = small_terms + lax.ppermute(small_terms, axis, pairs)  47.7 us
    pallas_call x1, Pallas kernels, attend_forward(): pl.pallas_call(attend_forward_kernel, grid_spec=pltpu.PrefetchScalarGridS...  27.5 us
    ppermute x6, waiting for transfers between devices, line_send(): return [lax.ppermute(part, 'shard', way) for way in ways[k]]  24.5 us
  transfers between devices with their start and end apart: 48, of which 20 were waited for; matrix products, arithmetic and copies ran while one was open for 10% of the time, Pallas kernels for 41%

profile of v4, /device:TPU:0, one launch (start us, length us, event | category | flops | bytes accessed | tf_op | source)
XLA Modules:
  0.0 738.2 jit_solution(13558194741141742156)
XLA Ops:
  10.7 5.1 collective-permute-start.27
  17.7 5.1 collective-permute-done.27
  22.9 13.9 %collective-permute-done.26 = bf16[192,640]{1,0:T(8,128)(2,1)} collective-permute-done((bf16[192,640]{1,0:T(8,128)(2,1)S(1)}, bf16[192,640]{1,0:T(8,128)(2,1)}, u32[]{:S(2)}, u32[]{:S(2)}) %collective-permute-start.26) | collective-permute-done | bytes 245792 | tf_op jit(solution)/shard_map/ppermute | solution.py:562
  36.8 2.2 pad_maximum_fusion.6
  45.2 2.5 collective-permute-start.33
  47.8 1.9 collective-permute-start.31
  49.7 2.4 collective-permute-start.30
  52.6 4.0 collective-permute-done.33
  58.3 17.5 %collective-permute-done.32 = bf16[240,384]{1,0:T(8,128)(2,1)S(1)} collective-permute-done((bf16[240,384]{1,0:T(8,128)(2,1)S(1)}, bf16[240,384]{1,0:T(8,128)(2,1)S(1)}, u32[]{:S(2)}, u32[]{:S(2)}) %collective-permute-start.32) | collective-permute-done | bytes 184352 | tf_op jit(solution)/shard_map/ppermute | solution.py:562
  78.9 2.6 convert_multiply_fusion
  81.5 1.9 collective-permute-done.29
  85.0 60.4 %conditional.2 = (bf16[4,4,192,640]{3,2,1,0:T(8,128)(2,1)}, bf16[4,4,192,640]{3,2,1,0:T(8,128)(2,1)}, bf16[4,4,192,384]{3,2,1,0:T(8,128)(2,1)}, bf16[4,4,192,384...) conditional(s32[]{:T(128)} %bitcast.34, () %tuple.35, ...), branch_computations={%region_2.3_spmd, %region_3.4_spmd} | conditional | flops 22412582912 | bytes 91223296 | solution.py:827
  85.2 3.4 maximum_maximum_fusion.own_ref
  91.3 4.4 collective-permute-done.other_ref
  99.2 27.5 %branch_1_fun.8 = (bf16[4,512,384]{2,1,0:T(8,128)(2,1)}, bf16[4,512,640]{2,1,0:T(8,128)(2,1)}, f32[4,8,512]{2,1,0:T(8,128)}) custom-call(s32[2]{0:T(128)S(1)} %get-tuple-element.105.at_ref, bf16[512,1536]{1,0:T(8,128)(2,1)} %get-tuple-element.106.normed_ref, bf16[4,4,192,640]{3,2,1,0:T(8,128)(2,1)} %maximum_maximum_fusion.own_ref, ...), custom_call_target="tpu_custom_call" | custom-call | flops 20000000000 | bytes 20000000 | tf_op jit(solution)/shard_map/cond/branch_1_fun/pallas_call | solution.py:153
  127.5 2.6 maximum_maximum_fusion.1.own_ref
  130.7 4.3 collective-permute-done.4.other_ref
  135.0 10.4 %branch_1_fun.9 = (f32[512,1536]{1,0:T(8,128)}, bf16[512,1536]{1,0:T(8,128)(2,1)}) custom-call(s32[2]{0:T(128)S(1)} %get-tuple-element.105.at_ref, bf16[4,512,384]{2,1,0:T(8,128)(2,1)} %get-tuple-element.423.mixed_ref, bf16[4,4,192,384]{3,2,1,0:T(8,128)(2,1)} %maximum_maximum_fusion.1.own_ref, bf16[4,4,192,384]{3,2,1,0:T(8,128)(2,1)} %collective-permute-done.4.other_ref, ...), custom_call_target="tpu_custom_call" | custom-call | flops 2400000000 | bytes 10000000 | tf_op jit(solution)/shard_map/cond/branch_1_fun/pallas_call | solution.py:191
  145.5 2.2 collective-permute-start.35
  147.6 1.8 collective-permute-start.34
  151.3 32.4 %shard_map.152 = (bf16[512,1536]{1,0:T(8,128)(2,1)}, bf16[512,1664]{1,0:T(8,128)(2,1)}, bf16[4,512,1536]{2,1,0:T(8,128)(2,1)}, bf16[4,512,1024]{2,1,0:T(8,128)(2,1)}, bf16[4,512,512]{2,1,0:T(8,128)(2,1)}) custom-call(s32[11]{0:T(128)} %stack.196.table_ref.places_ref, bf16[512,1536]{1,0:T(8,128)(2,1)} %get-tuple-element.231.inner_ref.outer_ref, ...), custom_call_target="tpu_custom_call" | custom-call | flops 19327352832 | bytes 32000000 | tf_op jit(solution)/shard_map/pallas_call | solution.py:412
  183.7 12.0 %collective-permute-done.34.outer_ref.inner_ref = bf16[512,1536]{1,0:T(8,128)(2,1)} collective-permute-done((bf16[512,1536]{1,0:T(8,128)(2,1)}, bf16[512,1536]{1,0:T(8,128)(2,1)}, u32[]{:S(2)}, u32[]{:S(2)}) %collective-permute-start.34) | collective-permute-done | bytes 1572896 | tf_op jit(solution)/shard_map/ppermute | solution.py:562
  199.3 31.5 %shard_map.153 = (bf16[512,1536]{1,0:T(8,128)(2,1)}, bf16[512,1664]{1,0:T(8,128)(2,1)}, bf16[4,512,1536]{2,1,0:T(8,128)(2,1)}, bf16[4,512,1024]{2,1,0:T(8,128)(2,1)}, bf16[4,512,512]{2,1,0:T(8,128)(2,1)}) custom-call(s32[11]{0:T(128)} %stack.196.table_ref.places_ref, ...), custom_call_target="tpu_custom_call", output_to_operand_aliasing={{2}: (7, {})} | custom-call | flops 19327352832 | bytes 32000000 | tf_op jit(solution)/shard_map/pallas_call | solution.py:412
  230.8 1.8 collective-permute-start.40
  232.6 7.2 collective-permute-start.39
  241.3 31.5 %shard_map.154 = (bf16[512,1536]{1,0:T(8,128)(2,1)}, bf16[512,1664]{1,0:T(8,128)(2,1)}, bf16[4,512,1536]{2,1,0:T(8,128)(2,1)}, bf16[4,512,1024]{2,1,0:T(8,128)(2,1)}, bf16[4,512,512]{2,1,0:T(8,128)(2,1)}) custom-call(s32[11]{0:T(128)} %stack.196.table_ref.places_ref, ...), custom_call_target="tpu_custom_call", output_to_operand_aliasing={{2}: (7, {})} | custom-call | flops 19327352832 | bytes 32000000 | tf_op jit(solution)/shard_map/pallas_call | solution.py:412
  274.1 7.4 %collective-permute-start.41 = (bf16[512,1664]{1,0:T(8,128)(2,1)}, bf16[512,1664]{1,0:T(8,128)(2,1)}, u32[]{:S(2)}, u32[]{:S(2)}) collective-permute-start(bf16[512,1664]{1,0:T(8,128)(2,1)} %get-tuple-element.242), channel_id=1, source_target_pairs={{0,2},{3,1},{4,6},{7,5},{8,10},{11,9},{12,14},{15,13},{16,18},{19,... | collective-permute-start | bytes 5111816 | tf_op jit(solution)/shard_map/ppermute | solution.py:617
  281.6 31.5 %shard_map.155 = (bf16[512,1536]{1,0:T(8,128)(2,1)}, bf16[512,1664]{1,0:T(8,128)(2,1)}, bf16[4,512,1536]{2,1,0:T(8,128)(2,1)}, bf16[4,512,1024]{2,1,0:T(8,128)(2,1)}, bf16[4,512,512]{2,1,0:T(8,128)(2,1)}) custom-call(s32[11]{0:T(128)} %stack.196.table_ref.places_ref, ...), custom_call_target="tpu_custom_call", output_to_operand_aliasing={{2}: (7, {})} | custom-call | flops 19327352832 | bytes 32000000 | tf_op jit(solution)/shard_map/pallas_call | solution.py:412
  314.4 4.1 collective-permute-start.43
  318.5 48.5 %shard_map.156 = bf16[4,1536,1536]{2,1,0:T(8,128)(2,1)} custom-call(s32[11]{0:T(128)} %stack.196.table_ref.places_ref, bf16[512,1536]{1,0:T(8,128)(2,1)} %get-tuple-element.244.refs_0_, bf16[512,1536]{1,0:T(8,128)(2,1)} %get-tuple-element.245.refs_1_, bf16[512,1536]{1,0:T(8,128)(2,1)} %get-tuple-element.246.refs_2_, ...), custom_call_target="tpu_custom_call" | custom-call | flops 38654705664 | bytes 80000000 | tf_op jit(solution)/shard_map/pallas_call | solution.py:544
  367.1 24.5 %collective-permute-done.44 = bf16[512,1664]{1,0:T(8,128)(2,1)} collective-permute-done((bf16[512,1664]{1,0:T(8,128)(2,1)}, bf16[512,1664]{1,0:T(8,128)(2,1)}, u32[]{:S(2)}, u32[]{:S(2)}) %collective-permute-start.44) | collective-permute-done | bytes 1703968 | tf_op jit(solution)/shard_map/ppermute | solution.py:617
  391.5 5.3 all-to-all-start
  398.8 305.2 %conditional.3 = (bf16[512,1536]{1,0:T(8,128)(2,1)}, f32[384,2560]{1,0:T(8,128)}, f32[384,1536]{1,0:T(8,128)}, f32[384]{0:T(512)}, f32[384]{0:T(512)}, /*index=5*/f32[384,16]{0,1:T(8,128)}) conditional(s32[]{:T(128)} %bitcast.34, () %tuple.44, (f32[512,16]{0,1:T(8,128)}, f32[1536]{0:T(1024)S(1)}, bf16[512,1664]{1,0:T(8,128)(2,1)}, ...), branch_computations={%region_5.6_spmd, %region_6.9_spmd} | conditional | flops 36138979328 | bytes 293654208 | solution.py:827
  402.6 12.9 %branch_1_fun.10 = (f32[512,1536]{1,0:T(8,128)}, bf16[512,1536]{1,0:T(8,128)(2,1)}, f32[128,1536]{1,0:T(8,128)}, f32[1,1536]{1,0:T(1,128)}) custom-call(bf16[512,1664]{1,0:T(8,128)(2,1)} %get-tuple-element.117.refs_0_, bf16[512,1664]{1,0:T(8,128)(2,1)} %get-tuple-element.118.refs_1_, bf16[512,1664]{1,0:T(8,128)(2,1)} %get-tuple-element.119.refs_2_, ...), custom_call_target="tpu_custom_call" | custom-call | flops 100000000 | bytes 20000000 | tf_op jit(solution)/shard_map/cond/branch_1_fun/pallas_call | solution.py:512
  415.5 2.5 copy.37.sine_ref
  418.1 2.5 copy.36.cosine_ref
  420.6 2.0 broadcast_28_total_ref.0.total_ref
  422.7 17.1 %branch_1_fun.11 = (bf16[4,192,1024]{2,1,0:T(8,128)(2,1)}, bf16[4,192,1024]{2,1,0:T(8,128)(2,1)}, f32[512,1536]{1,0:T(8,128)}) custom-call(s32[2]{0:T(128)S(1)} %copy-done.37, bf16[512,1536]{1,0:T(8,128)(2,1)} %get-tuple-element.150.branch_ref, bf16[4,4,192,384]{3,2,1,0:T(8,128)(2,1)} %get-tuple-element.134.own_output_ref, ...), custom_call_target="tpu_custom_call", output_to_operand_aliasing={{2}: (12, {})} | custom-call | flops 8999999488 | bytes 15000000 | tf_op jit(solution)/shard_map/cond/branch_1_fun/pallas_call | solution.py:297
  439.8 17.3 %branch_1_fun.12 = (bf16[4,192,1024]{2,1,0:T(8,128)(2,1)}, bf16[4,192,1024]{2,1,0:T(8,128)(2,1)}, f32[512,1536]{1,0:T(8,128)}) custom-call(s32[2]{0:T(128)S(1)} %copy-done.37, bf16[512,1536]{1,0:T(8,128)(2,1)} %get-tuple-element.150.branch_ref, bf16[4,4,192,384]{3,2,1,0:T(8,128)(2,1)} %get-tuple-element.134.own_output_ref, ...), custom_call_target="tpu_custom_call", output_to_operand_aliasing={{2}: (12, {})} | custom-call | flops 8999999488 | bytes 15000000 | tf_op jit(solution)/shard_map/cond/branch_1_fun/pallas_call | solution.py:297
  457.7 4.0 add_convert_fusion.3
  461.7 17.8 %branch_1_fun.13 = (bf16[4,192,1024]{2,1,0:T(8,128)(2,1)}, bf16[4,192,1024]{2,1,0:T(8,128)(2,1)}, f32[512,1536]{1,0:T(8,128)}) custom-call(s32[2]{0:T(128)S(1)} %copy-done.37, bf16[512,1536]{1,0:T(8,128)(2,1)} %get-tuple-element.150.branch_ref, bf16[4,4,192,384]{3,2,1,0:T(8,128)(2,1)} %get-tuple-element.134.own_output_ref, ...), custom_call_target="tpu_custom_call", output_to_operand_aliasing={{2}: (12, {})} | custom-call | flops 8999999488 | bytes 15000000 | tf_op jit(solution)/shard_map/cond/branch_1_fun/pallas_call | solution.py:297
  479.5 2.5 add_convert_fusion.4
  482.2 1.9 copy-done.9
  490.5 17.9 %branch_1_fun.14 = (bf16[4,192,1024]{2,1,0:T(8,128)(2,1)}, bf16[4,192,1024]{2,1,0:T(8,128)(2,1)}, f32[512,1536]{1,0:T(8,128)}) custom-call(s32[2]{0:T(128)S(1)} %copy-done.37, bf16[512,1536]{1,0:T(8,128)(2,1)} %get-tuple-element.150.branch_ref, bf16[4,4,192,384]{3,2,1,0:T(8,128)(2,1)} %get-tuple-element.134.own_output_ref, ...), custom_call_target="tpu_custom_call", output_to_operand_aliasing={{2}: (12, {})} | custom-call | flops 8999999488 | bytes 15000000 | tf_op jit(solution)/shard_map/cond/branch_1_fun/pallas_call | solution.py:297
  508.5 39.5 %collective-permute-done.8 = bf16[2,4,96,1024]{3,2,1,0:T(8,128)(2,1)} collective-permute-done((bf16[2,4,96,1024]{3,2,1,0:T(8,128)(2,1)}, bf16[2,4,96,1024]{3,2,1,0:T(8,128)(2,1)}, u32[]{:S(2)}, u32[]{:S(2)}) %collective-permute-start.8) | collective-permute-done | bytes 1572896 | tf_op jit(solution)/shard_map/cond/branch_1_fun/ppermute | solution.py:628
  547.9 2.6 fusion.3
  552.2 2.4 fusion
  556.4 2.7 add_convert_fusion.1
  559.2 25.5 %collective-permute-done.10 = bf16[4,96,1024]{2,1,0:T(8,128)(2,1)} collective-permute-done((bf16[4,96,1024]{2,1,0:T(8,128)(2,1)}, bf16[4,96,1024]{2,1,0:T(8,128)(2,1)}, u32[]{:S(2)}, u32[]{:S(2)}) %collective-permute-start.10) | collective-permute-done | bytes 786464 | tf_op jit(solution)/shard_map/cond/branch_1_fun/ppermute | solution.py:628
  584.7 6.5 collective-permute-done.12
  591.2 3.0 fusion.5
  594.3 2.1 collective-permute-start.13
  596.5 2.4 collective-permute-start.15
  599.7 6.4 collective-permute-done.13
  606.0 11.4 %collective-permute-done.15 = bf16[192,1024]{1,0:T(8,128)(2,1)S(1)} collective-permute-done((bf16[192,1024]{1,0:T(8,128)(2,1)S(1)}, bf16[192,1024]{1,0:T(8,128)(2,1)S(1)}, u32[]{:S(2)}, u32[]{:S(2)}) %collective-permute-start.15) | collective-permute-done | bytes 393248 | tf_op jit(solution)/shard_map/cond/branch_1_fun/ppermute | solution.py:562
  617.4 14.6 %collective-permute-done.14 = bf16[192,1024]{1,0:T(8,128)(2,1)S(1)} collective-permute-done((bf16[192,1024]{1,0:T(8,128)(2,1)S(1)}, bf16[192,1024]{1,0:T(8,128)(2,1)S(1)}, u32[]{:S(2)}, u32[]{:S(2)}) %collective-permute-start.14) | collective-permute-done | bytes 393248 | tf_op jit(solution)/shard_map/cond/branch_1_fun/ppermute | solution.py:562
  637.7 36.2 %collective-permute-done.21 = f32[18,1536]{1,0:T(8,128)} collective-permute-done((f32[18,1536]{1,0:T(8,128)}, f32[18,1536]{1,0:T(8,128)}, u32[]{:S(2)}, u32[]{:S(2)}) %collective-permute-start.21) | collective-permute-done | bytes 110624 | tf_op jit(solution)/shard_map/cond/branch_1_fun/ppermute | solution.py:948
  674.9 2.6 collective-permute-start.22
  680.1 3.9 collective-permute-done.22
  684.2 5.8 collective-permute-done.23
  691.2 3.8 add_convert_fusion.2
  698.0 5.8 branch_1_fun.15
  704.0 4.2 convert_reduce_fusion
  709.8 21.0 %convert_element_type.187 = f32[4,1536,1536]{2,1,0:T(8,128)} convert(bf16[4,1536,1536]{2,1,0:T(8,128)(2,1)} %all-reduce.6.cloned.1.call-done) | non-fusion elementwise | flops 9437184 | bytes 56623104 | tf_op jit(solution)/shard_map/convert_element_type | solution.py:871
  (222 shorter events, 66.9 us)
Async XLA Ops:
  7.2 9.3 %copy-start.25 = (bf16[384,1536]{1,0:T(8,128)(2,1)S(1)}, bf16[384,1536]{1,0:T(8,128)(2,1)}, u32[]{:S(2)}) copy-start(bf16[384,1536]{1,0:T(8,128)(2,1)} %param.15) | copy-start | bytes 3538948
  7.2 188.5 %all-gather.3.cloned.1.call-start = ((), (), s32[]{:S(2)}) async-start(), calls=%async_computation.2 | async-start | bytes 7864320 | tf_op jit(solution)/shard_map/all_gather | solution.py:799
  10.7 12.2 %collective-permute-start.27 = (bf16[192,640]{1,0:T(8,128)(2,1)S(1)}, bf16[192,640]{1,0:T(8,128)(2,1)}, u32[]{:S(2)}, u32[]{:S(2)}) collective-permute-start(bf16[192,640]{1,0:T(8,128)(2,1)S(1)} %get-tuple-element.395), channel_id=1, source_target_pairs={{0,3},{1,2},{2,1},{3,0},{4,7},{5,6},{6,5},{7,4},{8,11},{9,10},{10,... | collective-permute-start | bytes 737288 | tf_op jit(solution)/shard_map/ppermute | solution.py:562
  15.8 21.0 %collective-permute-start.26 = (bf16[192,640]{1,0:T(8,128)(2,1)S(1)}, bf16[192,640]{1,0:T(8,128)(2,1)}, u32[]{:S(2)}, u32[]{:S(2)}) collective-permute-start(bf16[192,640]{1,0:T(8,128)(2,1)S(1)} %get-tuple-element.395), channel_id=1, source_target_pairs={{0,2},{1,3},{2,0},{3,1},{4,6},{5,7},{6,4},{7,5},{8,10},{9,11},{10,... | collective-permute-start | bytes 737288 | tf_op jit(solution)/shard_map/ppermute | solution.py:562
  15.8 21.0 %collective-permute-start.25 = (bf16[192,640]{1,0:T(8,128)(2,1)S(1)}, bf16[192,640]{1,0:T(8,128)(2,1)}, u32[]{:S(2)}, u32[]{:S(2)}) collective-permute-start(bf16[192,640]{1,0:T(8,128)(2,1)S(1)} %get-tuple-element.395), channel_id=1, source_target_pairs={{0,1},{1,0},{2,3},{3,2},{4,5},{5,4},{6,7},{7,6},{8,9},{9,8},{10,11... | collective-permute-start | bytes 737288 | tf_op jit(solution)/shard_map/ppermute | solution.py:562
  17.7 21.4 %copy-start.30 = (s32[512,8]{0,1:T(8,128)S(1)}, s32[512,8]{0,1:T(8,128)}, u32[]{:S(2)}) copy-start(s32[512,8]{0,1:T(8,128)} %param.20) | copy-start | bytes 49156
  17.7 23.2 %copy-start.31 = (bf16[384,16]{0,1:T(8,128)(2,1)S(1)}, bf16[384,16]{0,1:T(8,128)(2,1)}, u32[]{:S(2)}) copy-start(bf16[384,16]{0,1:T(8,128)(2,1)} %param.18) | copy-start | bytes 36868
  43.5 40.3 %copy-start.36 = (s32[2]{0:T(128)}, s32[2]{0:T(128)S(1)}, u32[]{:S(2)}) copy-start(s32[2]{0:T(128)S(1)} %pad_add_fusion.1) | copy-start | bytes 28
  44.3 31.5 %copy-start.28 = (f32[512]{0:T(512)}, f32[512]{0:T(512)S(1)}, u32[]{:S(2)}) copy-start(f32[512]{0:T(512)S(1)} %fusion.17) | copy-start | bytes 6148
  45.2 11.4 %collective-permute-start.33 = (bf16[240,384]{1,0:T(8,128)(2,1)S(1)}, bf16[240,384]{1,0:T(8,128)(2,1)S(1)}, u32[]{:S(2)}, u32[]{:S(2)}) collective-permute-start(bf16[240,384]{1,0:T(8,128)(2,1)S(1)} %pad_maximum_fusion.10), channel_id=1, source_target_pairs={{0,3},{1,2},{2,1},{3,0},{4,7},{5,6},{6,5},{7,4},{8,11},{9,10},{10,... | collective-permute-start | bytes 552968 | tf_op jit(solution)/shard_map/ppermute | solution.py:562
  47.8 28.0 %collective-permute-start.32 = (bf16[240,384]{1,0:T(8,128)(2,1)S(1)}, bf16[240,384]{1,0:T(8,128)(2,1)S(1)}, u32[]{:S(2)}, u32[]{:S(2)}) collective-permute-start(bf16[240,384]{1,0:T(8,128)(2,1)S(1)} %pad_maximum_fusion.10), channel_id=1, source_target_pairs={{0,2},{1,3},{2,0},{3,1},{4,6},{5,7},{6,4},{7,5},{8,10},{9,11},{10,... | collective-permute-start | bytes 552968 | tf_op jit(solution)/shard_map/ppermute | solution.py:562
  47.8 28.0 %collective-permute-start.31 = (bf16[240,384]{1,0:T(8,128)(2,1)S(1)}, bf16[240,384]{1,0:T(8,128)(2,1)S(1)}, u32[]{:S(2)}, u32[]{:S(2)}) collective-permute-start(bf16[240,384]{1,0:T(8,128)(2,1)S(1)} %pad_maximum_fusion.10), channel_id=1, source_target_pairs={{0,1},{1,0},{2,3},{3,2},{4,5},{5,4},{6,7},{7,6},{8,9},{9,8},{10,11... | collective-permute-start | bytes 552968 | tf_op jit(solution)/shard_map/ppermute | solution.py:562
  49.7 31.8 %collective-permute-start.30 = (bf16[3,192,640]{2,1,0:T(8,128)(2,1)}, bf16[3,192,640]{2,1,0:T(8,128)(2,1)}, u32[]{:S(2)}, u32[]{:S(2)}) collective-permute-start(bf16[3,192,640]{2,1,0:T(8,128)(2,1)} %pad_maximum_fusion.6), channel_id=1, source_target_pairs={{0,24},{4,28},{8,16},{12,20},{16,8},{20,12},{24,0},{28,4},{1,25},{... | collective-permute-start | bytes 2211848 | tf_op jit(solution)/shard_map/ppermute | solution.py:628
  52.1 31.3 %collective-permute-start.29 = (bf16[3,192,640]{2,1,0:T(8,128)(2,1)}, bf16[3,192,640]{2,1,0:T(8,128)(2,1)}, u32[]{:S(2)}, u32[]{:S(2)}) collective-permute-start(bf16[3,192,640]{2,1,0:T(8,128)(2,1)} %pad_maximum_fusion.6), channel_id=1, source_target_pairs={{0,16},{4,20},{8,24},{12,28},{16,0},{20,4},{24,8},{28,12},{1,17},{... | collective-permute-start | bytes 2211848 | tf_op jit(solution)/shard_map/ppermute | solution.py:628
  56.7 26.8 %collective-permute-start.28 = (bf16[3,192,640]{2,1,0:T(8,128)(2,1)}, bf16[3,192,640]{2,1,0:T(8,128)(2,1)}, u32[]{:S(2)}, u32[]{:S(2)}) collective-permute-start(bf16[3,192,640]{2,1,0:T(8,128)(2,1)} %pad_maximum_fusion.6), channel_id=1, source_target_pairs={{0,8},{4,12},{8,0},{12,4},{16,24},{20,28},{24,16},{28,20},{1,9},{5... | collective-permute-start | bytes 2211848 | tf_op jit(solution)/shard_map/ppermute | solution.py:628
  88.6 7.1 collective-permute-start
  95.7 31.0 %collective-permute-start.3 = (bf16[3,192,384]{2,1,0:T(8,128)(2,1)S(1)}, bf16[3,192,384]{2,1,0:T(8,128)(2,1)S(1)}, u32[]{:S(2)}, u32[]{:S(2)}) collective-permute-start(bf16[3,192,384]{2,1,0:T(8,128)(2,1)S(1)} %get-tuple-element.104), channel_id=1, source_target_pairs={{0,24},{4,28},{8,16},{12,20},{16,8},{20,12},{24,0},{28,4},{1,25},{... | collective-permute-start | bytes 1327112 | tf_op jit(solution)/shard_map/cond/branch_1_fun/ppermute | solution.py:628
  97.4 29.3 %collective-permute-start.2 = (bf16[3,192,384]{2,1,0:T(8,128)(2,1)S(1)}, bf16[3,192,384]{2,1,0:T(8,128)(2,1)S(1)}, u32[]{:S(2)}, u32[]{:S(2)}) collective-permute-start(bf16[3,192,384]{2,1,0:T(8,128)(2,1)S(1)} %get-tuple-element.104), channel_id=1, source_target_pairs={{0,16},{4,20},{8,24},{12,28},{16,0},{20,4},{24,8},{28,12},{1,17},{... | collective-permute-start | bytes 1327112 | tf_op jit(solution)/shard_map/cond/branch_1_fun/ppermute | solution.py:628
  98.7 28.0 %collective-permute-start.1 = (bf16[3,192,384]{2,1,0:T(8,128)(2,1)S(1)}, bf16[3,192,384]{2,1,0:T(8,128)(2,1)S(1)}, u32[]{:S(2)}, u32[]{:S(2)}) collective-permute-start(bf16[3,192,384]{2,1,0:T(8,128)(2,1)S(1)} %get-tuple-element.104), channel_id=1, source_target_pairs={{0,8},{4,12},{8,0},{12,4},{16,24},{20,28},{24,16},{28,20},{1,9},{5... | collective-permute-start | bytes 1327112 | tf_op jit(solution)/shard_map/cond/branch_1_fun/ppermute | solution.py:628
  99.2 28.3 %copy-start.14 = (bf16[4,192,384]{2,1,0:T(8,128)(2,1)S(1)}, bf16[4,192,384]{2,1,0:T(8,128)(2,1)}, u32[]{:S(2)}) copy-start(bf16[4,192,384]{2,1,0:T(8,128)(2,1)} %get-tuple-element.102) | copy-start | bytes 1769476 | tf_op jit(solution)/shard_map/cond
  127.5 7.5 %copy-start.7 = (bf16[512,1536]{1,0:T(8,128)(2,1)S(1)}, bf16[512,1536]{1,0:T(8,128)(2,1)}, u32[]{:S(2)}) copy-start(bf16[512,1536]{1,0:T(8,128)(2,1)} %get-tuple-element.113.input_ref) | copy-start | bytes 4718596 | tf_op jit(solution)/shard_map/cond
  130.1 4.9 collective-permute-start.4
  145.4 5.8 copy-start.13
  145.5 38.2 %collective-permute-start.35 = (bf16[512,1536]{1,0:T(8,128)(2,1)}, bf16[512,1536]{1,0:T(8,128)(2,1)}, u32[]{:S(2)}, u32[]{:S(2)}) collective-permute-start(bf16[512,1536]{1,0:T(8,128)(2,1)} %get-tuple-element.231.inner_ref.outer_ref), channel_id=1, source_target_pairs={{1,2},{2,1},{5,6},{6,5},{9,10},{10,9},{13,14},{14,13},{17,18},{18,... | collective-permute-start | bytes 4718600 | tf_op jit(solution)/shard_map/ppermute | solution.py:590
  147.6 48.1 %collective-permute-start.34 = (bf16[512,1536]{1,0:T(8,128)(2,1)}, bf16[512,1536]{1,0:T(8,128)(2,1)}, u32[]{:S(2)}, u32[]{:S(2)}) collective-permute-start(bf16[512,1536]{1,0:T(8,128)(2,1)} %get-tuple-element.231.inner_ref.outer_ref), channel_id=1, source_target_pairs={{0,1},{1,0},{2,3},{3,2},{4,5},{5,4},{6,7},{7,6},{8,9},{9,8},{10,11... | collective-permute-start | bytes 4718600 | tf_op jit(solution)/shard_map/ppermute | solution.py:562
  149.8 91.5 %copy-start.21 = (bf16[1536,128]{1,0:T(8,128)(2,1)}, bf16[1536,128]{1,0:T(8,128)(2,1)S(1)}, u32[]{:S(2)}) copy-start(bf16[1536,128]{1,0:T(8,128)(2,1)S(1)} %pad.21.router_ref) | copy-start | bytes 1179652
  195.7 44.1 %collective-permute-start.36 = (bf16[512,1536]{1,0:T(8,128)(2,1)}, bf16[512,1536]{1,0:T(8,128)(2,1)}, u32[]{:S(2)}, u32[]{:S(2)}) collective-permute-start(bf16[512,1536]{1,0:T(8,128)(2,1)} %collective-permute-done.34.outer_ref.inner_ref), channel_id=1, source_target_pairs={{1,2},{2,1},{5,6},{6,5},{9,10},{10,9},{13,14},{14,13},{17,18},{18,... | collective-permute-start | bytes 4718600 | tf_op jit(solution)/shard_map/ppermute | solution.py:594
  197.5 43.8 %collective-permute-start.38 = (bf16[512,1536]{1,0:T(8,128)(2,1)}, bf16[512,1536]{1,0:T(8,128)(2,1)}, u32[]{:S(2)}, u32[]{:S(2)}) collective-permute-start(bf16[512,1536]{1,0:T(8,128)(2,1)} %collective-permute-done.35.inner_ref), channel_id=1, source_target_pairs={{1,0},{2,3},{5,4},{6,7},{9,8},{10,11},{13,12},{14,15},{17,16},{18,... | collective-permute-start | bytes 4718600 | tf_op jit(solution)/shard_map/ppermute | solution.py:595
  230.8 83.6 %collective-permute-start.40 = (bf16[512,1664]{1,0:T(8,128)(2,1)}, bf16[512,1664]{1,0:T(8,128)(2,1)}, u32[]{:S(2)}, u32[]{:S(2)}) collective-permute-start(bf16[512,1664]{1,0:T(8,128)(2,1)} %get-tuple-element.241), channel_id=1, source_target_pairs={{1,2},{2,1},{5,6},{6,5},{9,10},{10,9},{13,14},{14,13},{17,18},{18,... | collective-permute-start | bytes 5111816 | tf_op jit(solution)/shard_map/ppermute | solution.py:617
  232.6 134.4 %collective-permute-start.39 = (bf16[512,1664]{1,0:T(8,128)(2,1)}, bf16[512,1664]{1,0:T(8,128)(2,1)S(1)}, u32[]{:S(2)}, u32[]{:S(2)}) collective-permute-start(bf16[512,1664]{1,0:T(8,128)(2,1)} %get-tuple-element.241), channel_id=1, source_target_pairs={{0,1},{3,2},{4,5},{7,6},{8,9},{11,10},{12,13},{15,14},{16,17},{19,... | collective-permute-start | bytes 5111816 | tf_op jit(solution)/shard_map/ppermute | solution.py:617
  239.8 41.7 %collective-permute-start.37 = (bf16[512,1536]{1,0:T(8,128)(2,1)}, bf16[512,1536]{1,0:T(8,128)(2,1)}, u32[]{:S(2)}, u32[]{:S(2)}) collective-permute-start(bf16[512,1536]{1,0:T(8,128)(2,1)} %collective-permute-done.36.inner_ref), channel_id=1, source_target_pairs={{1,0},{2,3},{5,4},{6,7},{9,8},{10,11},{13,12},{14,15},{17,16},{18,... | collective-permute-start | bytes 4718600 | tf_op jit(solution)/shard_map/ppermute | solution.py:598
  272.8 94.2 %collective-permute-start.42 = (bf16[512,1664]{1,0:T(8,128)(2,1)}, bf16[512,1664]{1,0:T(8,128)(2,1)S(1)}, u32[]{:S(2)}, u32[]{:S(2)}) collective-permute-start(bf16[512,1664]{1,0:T(8,128)(2,1)} %get-tuple-element.242), channel_id=1, source_target_pairs={{1,0},{2,3},{5,4},{6,7},{9,8},{10,11},{13,12},{14,15},{17,16},{18,... | collective-permute-start | bytes 5111816 | tf_op jit(solution)/shard_map/ppermute | solution.py:617
  274.1 92.9 %collective-permute-start.41 = (bf16[512,1664]{1,0:T(8,128)(2,1)}, bf16[512,1664]{1,0:T(8,128)(2,1)}, u32[]{:S(2)}, u32[]{:S(2)}) collective-permute-start(bf16[512,1664]{1,0:T(8,128)(2,1)} %get-tuple-element.242), channel_id=1, source_target_pairs={{0,2},{3,1},{4,6},{7,5},{8,10},{11,9},{12,14},{15,13},{16,18},{19,... | collective-permute-start | bytes 5111816 | tf_op jit(solution)/shard_map/ppermute | solution.py:617
  313.1 78.5 %collective-permute-start.44 = (bf16[512,1664]{1,0:T(8,128)(2,1)}, bf16[512,1664]{1,0:T(8,128)(2,1)}, u32[]{:S(2)}, u32[]{:S(2)}) collective-permute-start(bf16[512,1664]{1,0:T(8,128)(2,1)} %get-tuple-element.243), channel_id=1, source_target_pairs={{1,3},{2,0},{5,7},{6,4},{9,11},{10,8},{13,15},{14,12},{17,19},{18,... | collective-permute-start | bytes 5111816 | tf_op jit(solution)/shard_map/ppermute | solution.py:617
  314.4 77.2 %collective-permute-start.43 = (bf16[512,1664]{1,0:T(8,128)(2,1)}, bf16[512,1664]{1,0:T(8,128)(2,1)}, u32[]{:S(2)}, u32[]{:S(2)}) collective-permute-start(bf16[512,1664]{1,0:T(8,128)(2,1)} %get-tuple-element.243), channel_id=1, source_target_pairs={{0,3},{3,0},{4,7},{7,4},{8,11},{11,8},{12,15},{15,12},{16,19},{19,... | collective-permute-start | bytes 5111816 | tf_op jit(solution)/shard_map/ppermute | solution.py:617
  367.0 24.5 %copy-start.18 = (bf16[512,1664]{1,0:T(8,128)(2,1)}, bf16[512,1664]{1,0:T(8,128)(2,1)S(1)}, u32[]{:S(2)}) copy-start(bf16[512,1664]{1,0:T(8,128)(2,1)S(1)} %collective-permute-done.39) | copy-start | bytes 5111812
  367.0 24.5 %copy-start.19 = (bf16[512,1664]{1,0:T(8,128)(2,1)}, bf16[512,1664]{1,0:T(8,128)(2,1)S(1)}, u32[]{:S(2)}) copy-start(bf16[512,1664]{1,0:T(8,128)(2,1)S(1)} %collective-permute-done.42) | copy-start | bytes 5111812
  391.5 312.5 %all-to-all-start = ((bf16[4,512,1536]{2,1,0:T(8,128)(2,1)}), bf16[4,512,1536]{2,1,0:T(8,128)(2,1)}, u32[]{:S(2)}, u32[]{:S(2)}) async-start(bf16[4,512,1536]{2,1,0:T(8,128)(2,1)} %get-tuple-element.263), calls=%async_computation | async-start | bytes 12582912 | tf_op jit(solution)/shard_map/all_to_all | solution.py:879
  396.9 312.9 %all-reduce.6.cloned.1.call-start = ((), (), s32[]{:S(2)}) async-start(), calls=%async_computation.1 | async-start | bytes 37748736 | tf_op jit(solution)/shard_map/psum | solution.py:871
  439.8 17.9 %collective-permute-start.6 = (bf16[4,192,1024]{2,1,0:T(8,128)(2,1)}, bf16[4,192,1024]{2,1,0:T(8,128)(2,1)}, u32[]{:S(2)}, u32[]{:S(2)}) collective-permute-start(bf16[4,192,1024]{2,1,0:T(8,128)(2,1)} %get-tuple-element.149), channel_id=1, source_target_pairs={{0,4},{4,0},{8,12},{12,8},{16,20},{20,16},{24,28},{28,24},{1,5},{5... | collective-permute-start | bytes 4718600 | tf_op jit(solution)/shard_map/cond/branch_1_fun/ppermute | solution.py:628
  457.1 22.4 %collective-permute-start.5 = (bf16[4,192,1024]{2,1,0:T(8,128)(2,1)}, bf16[4,192,1024]{2,1,0:T(8,128)(2,1)}, u32[]{:S(2)}, u32[]{:S(2)}) collective-permute-start(bf16[4,192,1024]{2,1,0:T(8,128)(2,1)} %get-tuple-element.146), channel_id=1, source_target_pairs={{0,4},{4,0},{8,12},{12,8},{16,20},{20,16},{24,28},{28,24},{1,5},{5... | collective-permute-start | bytes 4718600 | tf_op jit(solution)/shard_map/cond/branch_1_fun/ppermute | solution.py:628
  479.5 7.6 %collective-permute-start.9 = (bf16[4,192,1024]{2,1,0:T(8,128)(2,1)}, bf16[4,192,1024]{2,1,0:T(8,128)(2,1)S(1)}, u32[]{:S(2)}, u32[]{:S(2)}) collective-permute-start(bf16[4,192,1024]{2,1,0:T(8,128)(2,1)} %get-tuple-element.161), channel_id=1, source_target_pairs={{0,4},{4,0},{8,12},{12,8},{16,20},{20,16},{24,28},{28,24},{1,5},{5... | collective-permute-start | bytes 4718600 | tf_op jit(solution)/shard_map/cond/branch_1_fun/ppermute | solution.py:628
  485.5 62.4 %collective-permute-start.8 = (bf16[2,4,96,1024]{3,2,1,0:T(8,128)(2,1)}, bf16[2,4,96,1024]{3,2,1,0:T(8,128)(2,1)}, u32[]{:S(2)}, u32[]{:S(2)}) collective-permute-start(bf16[2,4,96,1024]{3,2,1,0:T(8,128)(2,1)} %pad_maximum_fusion), channel_id=1, source_target_pairs={{0,8},{4,12},{8,0},{12,4},{16,24},{20,28},{24,16},{28,20},{1,9},{5... | collective-permute-start | bytes 4718600 | tf_op jit(solution)/shard_map/cond/branch_1_fun/ppermute | solution.py:628
  489.5 62.7 %collective-permute-start.11 = (bf16[2,4,96,1024]{3,2,1,0:T(8,128)(2,1)}, bf16[2,4,96,1024]{3,2,1,0:T(8,128)(2,1)}, u32[]{:S(2)}, u32[]{:S(2)}) collective-permute-start(bf16[2,4,96,1024]{3,2,1,0:T(8,128)(2,1)} %pad_maximum_fusion.1), channel_id=1, source_target_pairs={{0,16},{4,20},{8,24},{12,28},{16,0},{20,4},{24,8},{28,12},{1,17},{... | collective-permute-start | bytes 4718600 | tf_op jit(solution)/shard_map/cond/branch_1_fun/ppermute | solution.py:628
  508.4 43.7 %copy-start.11 = (bf16[4,192,1024]{2,1,0:T(8,128)(2,1)S(1)}, bf16[4,192,1024]{2,1,0:T(8,128)(2,1)}, u32[]{:S(2)}) copy-start(bf16[4,192,1024]{2,1,0:T(8,128)(2,1)} %copy-done.10) | copy-start | bytes 4718596 | tf_op jit(solution)/shard_map/cond
  508.5 48.0 %collective-permute-start.7 = (bf16[4,192,1024]{2,1,0:T(8,128)(2,1)}, bf16[4,192,1024]{2,1,0:T(8,128)(2,1)}, u32[]{:S(2)}, u32[]{:S(2)}) collective-permute-start(bf16[4,192,1024]{2,1,0:T(8,128)(2,1)} %get-tuple-element.159), channel_id=1, source_target_pairs={{0,4},{4,0},{8,12},{12,8},{16,20},{20,16},{24,28},{28,24},{1,5},{5... | collective-permute-start | bytes 4718600 | tf_op jit(solution)/shard_map/cond/branch_1_fun/ppermute | solution.py:628
  550.5 34.2 %collective-permute-start.10 = (bf16[4,96,1024]{2,1,0:T(8,128)(2,1)}, bf16[4,96,1024]{2,1,0:T(8,128)(2,1)}, u32[]{:S(2)}, u32[]{:S(2)}) collective-permute-start(bf16[4,96,1024]{2,1,0:T(8,128)(2,1)} %fusion.3), channel_id=1, source_target_pairs={{0,16},{4,20},{8,24},{12,28},{16,0},{20,4},{24,8},{28,12},{1,17},{... | collective-permute-start | bytes 2359304 | tf_op jit(solution)/shard_map/cond/branch_1_fun/ppermute | solution.py:628
  554.5 36.6 %collective-permute-start.12 = (bf16[4,96,1024]{2,1,0:T(8,128)(2,1)}, bf16[4,96,1024]{2,1,0:T(8,128)(2,1)}, u32[]{:S(2)}, u32[]{:S(2)}) collective-permute-start(bf16[4,96,1024]{2,1,0:T(8,128)(2,1)} %fusion), channel_id=1, source_target_pairs={{0,8},{4,12},{8,0},{12,4},{16,24},{20,28},{24,16},{28,20},{1,9},{5... | collective-permute-start | bytes 2359304 | tf_op jit(solution)/shard_map/cond/branch_1_fun/ppermute | solution.py:628
  591.2 7.7 %copy-start.1 = (f32[512,1536]{1,0:T(8,128)S(1)}, f32[512,1536]{1,0:T(8,128)}, u32[]{:S(2)}) copy-start(f32[512,1536]{1,0:T(8,128)} %get-tuple-element.153) | copy-start | bytes 9437188 | tf_op jit(solution)/shard_map/cond
  594.3 11.7 %collective-permute-start.13 = (bf16[192,1024]{1,0:T(8,128)(2,1)S(1)}, bf16[192,1024]{1,0:T(8,128)(2,1)S(1)}, u32[]{:S(2)}, u32[]{:S(2)}) collective-permute-start(bf16[192,1024]{1,0:T(8,128)(2,1)S(1)} %get-tuple-element.369), channel_id=1, source_target_pairs={{0,1},{1,0},{2,3},{3,2},{4,5},{5,4},{6,7},{7,6},{8,9},{9,8},{10,11... | collective-permute-start | bytes 1179656 | tf_op jit(solution)/shard_map/cond/branch_1_fun/ppermute | solution.py:562
  596.5 20.9 %collective-permute-start.15 = (bf16[192,1024]{1,0:T(8,128)(2,1)S(1)}, bf16[192,1024]{1,0:T(8,128)(2,1)S(1)}, u32[]{:S(2)}, u32[]{:S(2)}) collective-permute-start(bf16[192,1024]{1,0:T(8,128)(2,1)S(1)} %get-tuple-element.370), channel_id=1, source_target_pairs={{0,3},{1,2},{2,1},{3,0},{4,7},{5,6},{6,5},{7,4},{8,11},{9,10},{10,... | collective-permute-start | bytes 1179656 | tf_op jit(solution)/shard_map/cond/branch_1_fun/ppermute | solution.py:562
  598.8 33.2 %collective-permute-start.14 = (bf16[192,1024]{1,0:T(8,128)(2,1)S(1)}, bf16[192,1024]{1,0:T(8,128)(2,1)S(1)}, u32[]{:S(2)}, u32[]{:S(2)}) collective-permute-start(bf16[192,1024]{1,0:T(8,128)(2,1)S(1)} %get-tuple-element.371), channel_id=1, source_target_pairs={{0,2},{1,3},{2,0},{3,1},{4,6},{5,7},{6,4},{7,5},{8,10},{9,11},{10,... | collective-permute-start | bytes 1179656 | tf_op jit(solution)/shard_map/cond/branch_1_fun/ppermute | solution.py:562
  599.6 36.2 %collective-permute-start.20 = (f32[18,1536]{1,0:T(8,128)S(1)}, f32[18,1536]{1,0:T(8,128)S(1)}, u32[]{:S(2)}, u32[]{:S(2)}) collective-permute-start(f32[18,1536]{1,0:T(8,128)S(1)} %pad_maximum_fusion.4), channel_id=1, source_target_pairs={{0,4},{4,0},{8,12},{12,8},{16,20},{20,16},{24,28},{28,24},{1,5},{5... | collective-permute-start | bytes 331784 | tf_op jit(solution)/shard_map/cond/branch_1_fun/ppermute | solution.py:948
  632.2 45.3 %collective-permute-start.18 = (bf16[192,1024]{1,0:T(8,128)(2,1)S(1)}, bf16[192,1024]{1,0:T(8,128)(2,1)}, u32[]{:S(2)}, u32[]{:S(2)}) collective-permute-start(bf16[192,1024]{1,0:T(8,128)(2,1)S(1)} %fusion.8), channel_id=1, source_target_pairs={{0,24},{4,28},{8,16},{12,20},{16,8},{20,12},{24,0},{28,4},{1,25},{... | collective-permute-start | bytes 1179656 | tf_op jit(solution)/shard_map/cond/branch_1_fun/ppermute | solution.py:628
  633.7 43.8 %collective-permute-start.17 = (bf16[192,1024]{1,0:T(8,128)(2,1)S(1)}, bf16[192,1024]{1,0:T(8,128)(2,1)}, u32[]{:S(2)}, u32[]{:S(2)}) collective-permute-start(bf16[192,1024]{1,0:T(8,128)(2,1)S(1)} %fusion.8), channel_id=1, source_target_pairs={{0,16},{4,20},{8,24},{12,28},{16,0},{20,4},{24,8},{28,12},{1,17},{... | collective-permute-start | bytes 1179656 | tf_op jit(solution)/shard_map/cond/branch_1_fun/ppermute | solution.py:628
  634.3 43.2 %collective-permute-start.16 = (bf16[192,1024]{1,0:T(8,128)(2,1)S(1)}, bf16[192,1024]{1,0:T(8,128)(2,1)}, u32[]{:S(2)}, u32[]{:S(2)}) collective-permute-start(bf16[192,1024]{1,0:T(8,128)(2,1)S(1)} %fusion.8), channel_id=1, source_target_pairs={{0,8},{4,12},{8,0},{12,4},{16,24},{20,28},{24,16},{28,20},{1,9},{5... | collective-permute-start | bytes 1179656 | tf_op jit(solution)/shard_map/cond/branch_1_fun/ppermute | solution.py:628
  636.5 37.4 %collective-permute-start.21 = (f32[18,1536]{1,0:T(8,128)}, f32[18,1536]{1,0:T(8,128)}, u32[]{:S(2)}, u32[]{:S(2)}) collective-permute-start(f32[18,1536]{1,0:T(8,128)} %fusion.16), channel_id=1, source_target_pairs={{0,8},{4,12},{8,0},{12,4},{16,24},{20,28},{24,16},{28,20},{1,9},{5... | collective-permute-start | bytes 331784 | tf_op jit(solution)/shard_map/cond/branch_1_fun/ppermute | solution.py:948
  674.9 9.1 %collective-permute-start.22 = (f32[18,1536]{1,0:T(8,128)S(1)}, f32[18,1536]{1,0:T(8,128)S(1)}, u32[]{:S(2)}, u32[]{:S(2)}) collective-permute-start(f32[18,1536]{1,0:T(8,128)S(1)} %add.186), channel_id=1, source_target_pairs={{0,16},{4,20},{8,24},{12,28},{16,0},{20,4},{24,8},{28,12},{1,17},{... | collective-permute-start | bytes 331784 | tf_op jit(solution)/shard_map/cond/branch_1_fun/ppermute | solution.py:948
  677.5 13.7 %copy-start.2 = (f32[512,1536]{1,0:T(8,128)S(1)}, f32[512,1536]{1,0:T(8,128)}, u32[]{:S(2)}) copy-start(f32[512,1536]{1,0:T(8,128)} %get-tuple-element.153) | copy-start | bytes 9437188 | tf_op jit(solution)/shard_map/cond
  677.5 13.7 %copy-start.33 = (f32[512]{0:T(512)S(1)}, f32[512]{0:T(512)}, u32[]{:S(2)}) copy-start(f32[512]{0:T(512)} %add_rsqrt_fusion) | copy-start | bytes 6148 | tf_op jit(solution)/shard_map/cond
  679.3 15.8 %copy-start.8 = (bf16[4,192,1024]{2,1,0:T(8,128)(2,1)}, bf16[4,192,1024]{2,1,0:T(8,128)(2,1)S(1)}, u32[]{:S(2)}) copy-start(bf16[4,192,1024]{2,1,0:T(8,128)(2,1)S(1)} %pad_maximum_fusion.2.own_ref) | copy-start | bytes 4718596 | tf_op jit(solution)/shard_map/cond
  679.3 18.7 %collective-permute-start.19 = (bf16[4,192,1024]{2,1,0:T(8,128)(2,1)S(1)}, bf16[4,192,1024]{2,1,0:T(8,128)(2,1)}, u32[]{:S(2)}, u32[]{:S(2)}) collective-permute-start(bf16[4,192,1024]{2,1,0:T(8,128)(2,1)S(1)} %pad_maximum_fusion.2.own_ref), channel_id=1, source_target_pairs={{0,4},{4,0},{8,12},{12,8},{16,20},{20,16},{24,28},{28,24},{1,5},{5... | collective-permute-start | bytes 4718600 | tf_op jit(solution)/shard_map/cond/branch_1_fun/ppermute | solution.py:628
  684.1 5.9 collective-permute-start.23
  690.0 6.7 collective-permute-start.24
  (22 other events, 49.0 us)
Sparse Core Ops, SparseCore 0:
  39.1 132.9 all-gather.2
  402.0 302.9 all-reduce.5

commit v5 on v4

--- a/solution.py
+++ b/solution.py
@@ -316,6 +316,7 @@
 
 def expert_kernel(
     sequences,
+    whole_slot,
     table_ref,
     inner_ref,
     outer_ref,
@@ -325,17 +326,11 @@
     weight_ref,
     *refs,
 ):
-    (
-        fed_ref,
-        row_ref,
-        combined_ref,
-        pair_ref,
-        gated_ref,
-        gates_ref,
-        gate_grad_ref,
-        row_total,
-        combined_total,
-    ) = refs[-9:]
+    (fed_ref, row_ref, pair_ref, gated_ref, back_ref, *refs) = refs[-10 if whole_slot else -8 :]
+    if whole_slot:
+        combined_ref, gates_ref, gate_grad_ref, row_total, combined_total = refs
+    else:
+        gates_ref, gate_grad_ref, row_total = refs
     step, steps = pl.program_id(0), pl.num_programs(0)
     index = table_ref[sequences + 1] + step
     lane = lax.broadcasted_iota(jnp.int32, gates_ref.shape, 1)
@@ -376,41 +371,59 @@
         pair_ref[0, :, FF + start : FF + stop] = (hidden_grad * activated).astype(bf16)
         gated_ref[0, :, start:stop] = (gate * hidden).astype(bf16)
     gate_grad_ref[...] += jnp.where(lane == index, gate_grad, 0.0)
-    combined = times_transposed(gated_ref[0], weight_ref[0, :, 2 * FF :])
-    row = times_transposed(pair_ref[0], weight_ref[0, :, : 2 * FF])
+    sums = [(row_total, times_transposed(pair_ref[0], weight_ref[0, :, : 2 * FF]))]
+    if whole_slot:
+        sums.append((combined_total, times_transposed(gated_ref[0], weight_ref[0, :, 2 * FF :])))
 
     @pl.when(step == 0)
     def _():
-        combined_total[...] = combined
-        row_total[...] = row
+        for total, added in sums:
+            total[...] = added
 
     @pl.when(step > 0)
     def _():
-        combined_total[...] += combined
-        row_total[...] += row
+        for total, added in sums:
+            total[...] += added
 
     @pl.when(step == steps - 1)
     def _():
-        features = row_total.shape[1]
-        row_ref[:, :features] = row_total[...].astype(bf16)
-        high = gate_grad_ref[...].astype(bf16)
-        low = gate_grad_ref[...] - high.astype(f32)
-        row_ref[:, features:] = (high.astype(f32) + pltpu.roll(low, LANES // 2, 1)).astype(bf16)
-        combined_ref[0] = combined_total[...].astype(bf16)
-
-
-def expert_slot(at, k, choices, upstream, chosen, router, weights, combined):
+        row_ref[...] = row_total[...].astype(bf16)
+        back_ref[0] = gate_grad_ref[...].T[:EXPERTS]
+        if whole_slot:
+            combined_ref[0] = combined_total[...].astype(bf16)
+
+
+def expert_slot(at, k, choices, upstream, chosen, router, weights, gate_grads, combined, sequences):
     length, features = choices[0].shape
     count = weights.shape[0]
-    held = [] if isinstance(combined, int) else [combined]
-    sequences = combined if isinstance(combined, int) else combined.shape[0]
+    whole_slot = k < sequences - 1
+    held = [] if gate_grads is None else [gate_grads, combined][: 1 + whole_slot]
     full = lambda *shape: pl.BlockSpec(shape, lambda e, at: (0,) * len(shape))
     each = lambda *shape: pl.BlockSpec((1,) + shape, lambda e, at: (e,) + (0,) * len(shape))
     there = lambda i, *shape: pl.BlockSpec(
         (1,) + shape, lambda e, at: (at[i],) + (0,) * len(shape)
     )
+    rows = pltpu.VMEM((length, features), f32)
+    gates = pltpu.VMEM((length, LANES), f32)
+    out_specs = [
+        full(length, features),
+        full(length, features),
+        each(length, 2 * FF),
+        each(length, FF),
+        there(k, EXPERTS, length),
+    ]
+    out_shape = [
+        jax.ShapeDtypeStruct((length, features), bf16),
+        jax.ShapeDtypeStruct((length, features), bf16),
+        jax.ShapeDtypeStruct((count, length, 2 * FF), bf16),
+        jax.ShapeDtypeStruct((count, length, FF), bf16),
+        jax.ShapeDtypeStruct((sequences, EXPERTS, length), f32),
+    ]
+    if whole_slot:
+        out_specs.append(there(k, length, features))
+        out_shape.append(jax.ShapeDtypeStruct((sequences, length, features), bf16))
     return pl.pallas_call(
-        functools.partial(expert_kernel, sequences),
+        functools.partial(expert_kernel, sequences, whole_slot),
         grid_spec=pltpu.PrefetchScalarGridSpec(
             num_scalar_prefetch=1,
             grid=(count,),
@@ -423,36 +436,60 @@
                 each(features, 3 * FF),
             ]
             + [pl.BlockSpec(memory_space=pl.ANY)] * len(held),
-            out_specs=[
-                full(length, features),
-                full(length, features + LANES),
-                there(k, length, features),
-                each(length, 2 * FF),
-                each(length, FF),
-            ],
-            scratch_shapes=[
-                pltpu.VMEM((length, LANES), f32),
-                pltpu.VMEM((length, LANES), f32),
-                pltpu.VMEM((length, features), f32),
-                pltpu.VMEM((length, features), f32),
-            ],
+            out_specs=out_specs,
+            scratch_shapes=[gates, gates, rows] + [rows] * whole_slot,
         ),
-        out_shape=[
-            jax.ShapeDtypeStruct((length, features), bf16),
-            jax.ShapeDtypeStruct((length, features + LANES), bf16),
-            jax.ShapeDtypeStruct((sequences, length, features), bf16),
-            jax.ShapeDtypeStruct((count, length, 2 * FF), bf16),
-            jax.ShapeDtypeStruct((count, length, FF), bf16),
-        ],
-        input_output_aliases={7: 2} if held else {},
+        out_shape=out_shape,
+        input_output_aliases={7 + i: 4 + i for i in range(len(held))},
         compiler_params=pltpu.CompilerParams(vmem_limit_bytes=VMEM),
         cost_estimate=cost(12 * count * length * features * FF, 3.2e7),
     )(at, *choices, upstream, chosen, router, weights, *held)
 
 
+def combine_kernel(table_ref, gated_ref, weight_ref, _, combined_ref, total_ref):
+    step = pl.program_id(0)
+    added = times_transposed(gated_ref[0], weight_ref[0])
+
+    @pl.when(step == 0)
+    def _():
+        total_ref[...] = added
+
+    @pl.when(step > 0)
+    def _():
+        total_ref[...] += added
+
+    @pl.when(step == pl.num_programs(0) - 1)
+    def _():
+        combined_ref[0] = total_ref[...].astype(bf16)
+
+
+def combine_slot(at, k, gated, weights, combined):
+    count, length, _ = gated.shape
+    features = weights.shape[1]
+    return pl.pallas_call(
+        combine_kernel,
+        grid_spec=pltpu.PrefetchScalarGridSpec(
+            num_scalar_prefetch=1,
+            grid=(count,),
+            in_specs=[
+                pl.BlockSpec((1, length, FF), lambda e, at: (e, 0, 0)),
+                pl.BlockSpec((1, features, FF), lambda e, at: (e, 0, 2)),
+                pl.BlockSpec(memory_space=pl.ANY),
+            ],
+            out_specs=pl.BlockSpec((1, length, features), lambda e, at: (at[k], 0, 0)),
+            scratch_shapes=[pltpu.VMEM((length, features), f32)],
+        ),
+        out_shape=jax.ShapeDtypeStruct(combined.shape, bf16),
+        input_output_aliases={3: 0},
+        compiler_params=pltpu.CompilerParams(vmem_limit_bytes=VMEM),
+        cost_estimate=cost(2 * count * length * features * FF, 1e7),
+    )(at, gated, weights, combined)
+
+
 def fed_grad_kernel(*refs):
-    arrived = refs[:-10]
+    arrived = refs[:-11]
     (
+        back_ref,
         fed_ref,
         middle_ref,
         upstream_ref,
@@ -463,14 +500,16 @@
         branch_ref,
         router_grad_ref,
         gain_grad_ref,
-    ) = refs[-10:]
+    ) = refs[-11:]
     step = pl.program_id(0)
     total = arrived[0][...].astype(f32)
     for ref in arrived[1:]:
         total = total + ref[...].astype(f32)
-    features = fed_ref.shape[1]
-    parts = total[:, features:]
-    gate_grad = parts + pltpu.roll(parts, LANES // 2, 1)
+    columns = back_ref[0]
+    for i in range(1, back_ref.shape[0]):
+        columns = columns + back_ref[i]
+    empty = jnp.zeros((LANES - EXPERTS, columns.shape[1]), f32)
+    gate_grad = jnp.concatenate([columns, empty], axis=0).T
     chosen = chosen_ref[...] > 0.0
     logits = jnp.where(chosen, dot(fed_ref[...], router_ref[...]), MASKED)
     powers = jnp.where(chosen, jnp.exp(logits - jnp.max(logits, axis=1, keepdims=True)), 0.0)
@@ -478,7 +517,7 @@
     gate_grad = jnp.where(chosen, gate_grad, 0.0)
     mean = jnp.sum(gates * gate_grad, axis=1, keepdims=True)
     logit_grad = (gates * (gate_grad - mean)).astype(bf16)
-    fed_grad = times_transposed(logit_grad, router_ref[...]) + total[:, :features]
+    fed_grad = times_transposed(logit_grad, router_ref[...]) + total
     scaled, inverse = norm_rows(middle_ref[...])
     back = norm_back(scaled, inverse, fed_grad * gain_ref[...])
     middle_grad = upstream_ref[...].astype(f32) + back
@@ -498,7 +537,7 @@
         gain_grad_ref[...] += gain_grad
 
 
-def fed_grads(arrived, fed, middle, upstream, chosen, router, gain):
+def fed_grads(arrived, gate_grads, fed, middle, upstream, chosen, router, gain):
     length, features = fed.shape
     rows = length // 4
     split = lambda array: pl.BlockSpec((rows, array.shape[1]), lambda i: (i, 0))
@@ -508,11 +547,13 @@
         jax.ShapeDtypeStruct((LANES, features), f32),
         jax.ShapeDtypeStruct((1, features), f32),
     ]
-    operands = [*arrived, fed, middle, upstream, chosen, router, gain]
+    operands = [*arrived, gate_grads, fed, middle, upstream, chosen, router, gain]
+    columns = pl.BlockSpec((*gate_grads.shape[:2], rows), lambda i: (0, 0, i))
+    specs = [split(a) for a in arrived] + [columns] + [split(a) for a in operands[-6:-2]]
     return pl.pallas_call(
         fed_grad_kernel,
         grid=(4,),
-        in_specs=[split(a) for a in operands[:-2]] + [whole(router), whole(gain)],
+        in_specs=specs + [whole(router), whole(gain)],
         out_specs=[split(shapes[0]), split(shapes[1]), whole(shapes[2]), whole(shapes[3])],
         out_shape=shapes,
         compiler_params=pltpu.CompilerParams(vmem_limit_bytes=VMEM),
@@ -846,17 +887,27 @@
     router_wide = jnp.pad(router_full, ((0, 0), (0, LANES - EXPERTS)))
     chosen_wide = jnp.pad(chosen_all, ((0, 0), (0, 0), (0, LANES - EXPERTS)))
     rows, pair_grads, gated = [], [], []
-    combined = places
+    combined = gate_grads = None
     order = sources(place, places)
     entries = [*order, core, place * local, inside(place), 0, *order[1:]]
     table = jnp.stack([jnp.asarray(e, jnp.int32) for e in entries])
     fed_slots, rows_come, arriving = [], [], line_gather(fed, place, places)
     for k, source in enumerate(order):
         rows_up = cotangent[None] if k == 0 else upstream_all
-        fed_k, row, combined, *kept = expert_slot(
-            table, k, next(arriving), rows_up, chosen_wide, router_wide, expert_weight, combined
+        fed_k, row, pair_k, gated_k, gate_grads, *buffer = expert_slot(
+            table,
+            k,
+            next(arriving),
+            rows_up,
+            chosen_wide,
+            router_wide,
+            expert_weight,
+            gate_grads,
+            combined,
+            places,
         )
-        for held, value in zip((fed_slots, rows, pair_grads, gated), (fed_k, row, *kept)):
+        combined = buffer[0] if buffer else combined
+        for held, value in zip((fed_slots, rows, pair_grads, gated), (fed_k, row, pair_k, gated_k)):
             held.append(value)
         arriving.send((row, upstream_all))
         if special and k:
@@ -876,12 +927,16 @@
         arrived = [scatter_all(rows, place, places)]
     arrived = after(arrived, expert_term)
 
+    combined = combine_slot(
+        table, places - 1, after(gated[-1], expert_term), expert_weight, combined
+    )
+    gate_grads = lax.all_to_all(gate_grads, "shard", 0, 0)
     combined = lax.all_to_all(after(combined, arrived), "shard", 0, 0)
 
     def rest():
         chosen = jnp.pad(chosen_own, ((0, 0), (0, LANES - EXPERTS)))
         middle_grad, branch_grad, router_term, feed_term = fed_grads(
-            arrived, fed, middle, cotangent, chosen, router_wide, feed_scale[None]
+            arrived, gate_grads, fed, middle, cotangent, chosen, router_wide, feed_scale[None]
         )
         normed_grad = jnp.zeros((length, features), f32)
         terms, chips = [None] * PAIRS, [None] * PAIRS

time: 746 us -> 738 us (0.989)
  waiting for transfers between devices: 240 us -> 224 us
    ppermute x6, waiting for transfers between devices: 24.5 us -> 10.1 us  [line_send(): return [lax.ppermute(part, 'shard', way) for way in ways[k]]]
    pallas_call x5 -> x6, Pallas kernels: 140 us -> 143 us  [the longest x4 121 us: expert_slot(): pl.pallas_call(functools.partial(expert_kernel, sequences, whole_slot), g...]
  transfers between devices with their start and end apart: 48 -> 49, of which waited for: 20 -> 19; matrix products, arithmetic and copies ran while one was open for 10% -> 10% of each run, Pallas kernels for 41% -> 42%
where the time goes in v5:
time: 738 us; the launch traced here: 730 us
  Pallas kernels  305 us (41%)
  waiting for transfers between devices  224 us (30%)
  starting transfers between devices  77.7 us (11%)
  other arithmetic  73 us (10%)
  local copies, waits for them, and re-layouts  32.9 us (4%)
  between operations  15.9 us (2%)
    pallas_call x4, Pallas kernels, expert_slot(): pl.pallas_call(functools.partial(expert_kernel, sequences, whole_slot), g...  121 us
    ppermute x10, waiting for transfers between devices, exchange(): return lax.ppermute(value, 'shard', [(i, i ^ k) for i in range(4)])  84.1 us
    ppermute x20, waiting for transfers between devices, hop(): return lax.ppermute(value, 'rep', [(i, i ^ bit) for i in range(8)])  80.4 us
    pallas_call x4, Pallas kernels, attend_backward(): pl.pallas_call(attend_backward_kernel, grid_spec=pltpu.PrefetchScalarGrid...  69.9 us
    pallas_call x1, Pallas kernels, expert_grads(): pl.pallas_call(expert_grad_kernel, grid_spec=pltpu.PrefetchScalarGridSpec...  48.7 us
    ppermute x5, waiting for transfers between devices, rest(): small_terms = small_terms + lax.ppermute(small_terms, axis, pairs)  48.7 us
    pallas_call x1, Pallas kernels, attend_forward(): pl.pallas_call(attend_forward_kernel, grid_spec=pltpu.PrefetchScalarGridS...  27.5 us
    convert_element_type x1, other arithmetic, body(): expert_total = lax.psum(expert_term, 'rep').astype(f32)  21 us
  transfers between devices with their start and end apart: 49, of which 19 were waited for; matrix products, arithmetic and copies ran while one was open for 10% of the time, Pallas kernels for 42%

profile of v5, /device:TPU:0, one launch (start us, length us, event | category | flops | bytes accessed | tf_op | source)
XLA Modules:
  0.0 729.7 jit_solution(6263388422189037238)
XLA Ops:
  10.7 5.1 collective-permute-start.27
  17.7 5.1 collective-permute-done.27
  22.9 13.9 %collective-permute-done.26 = bf16[192,640]{1,0:T(8,128)(2,1)} collective-permute-done((bf16[192,640]{1,0:T(8,128)(2,1)S(1)}, bf16[192,640]{1,0:T(8,128)(2,1)}, u32[]{:S(2)}, u32[]{:S(2)}) %collective-permute-start.26) | collective-permute-done | bytes 245792 | tf_op jit(solution)/shard_map/ppermute | solution.py:603
  36.8 2.2 pad_maximum_fusion.6
  45.2 2.5 collective-permute-start.33
  47.7 1.9 collective-permute-start.31
  52.7 4.0 collective-permute-done.33
  56.7 2.6 collective-permute-start.30
  59.2 16.5 %collective-permute-done.32 = bf16[240,384]{1,0:T(8,128)(2,1)S(1)} collective-permute-done((bf16[240,384]{1,0:T(8,128)(2,1)S(1)}, bf16[240,384]{1,0:T(8,128)(2,1)S(1)}, u32[]{:S(2)}, u32[]{:S(2)}) %collective-permute-start.32) | collective-permute-done | bytes 184352 | tf_op jit(solution)/shard_map/ppermute | solution.py:603
  78.9 2.6 convert_multiply_fusion
  81.5 2.2 collective-permute-done.29
  85.2 60.4 %conditional.2 = (bf16[4,4,192,640]{3,2,1,0:T(8,128)(2,1)}, bf16[4,4,192,640]{3,2,1,0:T(8,128)(2,1)}, bf16[4,4,192,384]{3,2,1,0:T(8,128)(2,1)}, bf16[4,4,192,384...) conditional(s32[]{:T(128)} %bitcast.34, () %tuple.36, ...), branch_computations={%region_2.3_spmd, %region_3.4_spmd} | conditional | flops 22412582912 | bytes 91223296 | solution.py:868
  85.4 3.4 maximum_maximum_fusion.own_ref
  91.5 4.4 collective-permute-done.other_ref
  99.5 27.5 %branch_1_fun.8 = (bf16[4,512,384]{2,1,0:T(8,128)(2,1)}, bf16[4,512,640]{2,1,0:T(8,128)(2,1)}, f32[4,8,512]{2,1,0:T(8,128)}) custom-call(s32[2]{0:T(128)S(1)} %get-tuple-element.107.at_ref, bf16[512,1536]{1,0:T(8,128)(2,1)} %get-tuple-element.108.normed_ref, bf16[4,4,192,640]{3,2,1,0:T(8,128)(2,1)} %maximum_maximum_fusion.own_ref, ...), custom_call_target="tpu_custom_call" | custom-call | flops 20000000000 | bytes 20000000 | tf_op jit(solution)/shard_map/cond/branch_1_fun/pallas_call | solution.py:153
  127.8 2.7 maximum_maximum_fusion.1.own_ref
  131.0 4.3 collective-permute-done.4.other_ref
  135.3 10.3 %branch_1_fun.9 = (f32[512,1536]{1,0:T(8,128)}, bf16[512,1536]{1,0:T(8,128)(2,1)}) custom-call(s32[2]{0:T(128)S(1)} %get-tuple-element.107.at_ref, bf16[4,512,384]{2,1,0:T(8,128)(2,1)} %get-tuple-element.436.mixed_ref, bf16[4,4,192,384]{3,2,1,0:T(8,128)(2,1)} %maximum_maximum_fusion.1.own_ref, bf16[4,4,192,384]{3,2,1,0:T(8,128)(2,1)} %collective-permute-done.4.other_ref, ...), custom_call_target="tpu_custom_call" | custom-call | flops 2400000000 | bytes 10000000 | tf_op jit(solution)/shard_map/cond/branch_1_fun/pallas_call | solution.py:191
  145.9 2.1 collective-permute-start.35
  149.8 32.3 %shard_map.152 = (bf16[512,1536]{1,0:T(8,128)(2,1)}, bf16[512,1536]{1,0:T(8,128)(2,1)}, bf16[4,512,1024]{2,1,0:T(8,128)(2,1)}, bf16[4,512,512]{2,1,0:T(8,128)(2,...) custom-call(s32[11]{0:T(128)} %stack.196.table_ref.places_ref, ...), custom_call_target="tpu_custom_call" | custom-call | flops 19327352832 | bytes 32000000 | tf_op jit(solution)/shard_map/pallas_call | solution.py:425
  182.2 13.5 %collective-permute-done.34.outer_ref.inner_ref = bf16[512,1536]{1,0:T(8,128)(2,1)} collective-permute-done((bf16[512,1536]{1,0:T(8,128)(2,1)}, bf16[512,1536]{1,0:T(8,128)(2,1)}, u32[]{:S(2)}, u32[]{:S(2)}) %collective-permute-start.34) | collective-permute-done | bytes 1572896 | tf_op jit(solution)/shard_map/ppermute | solution.py:603
  195.7 1.8 collective-permute-start.36
  199.3 31.3 %shard_map.153 = (bf16[512,1536]{1,0:T(8,128)(2,1)}, bf16[512,1536]{1,0:T(8,128)(2,1)}, bf16[4,512,1024]{2,1,0:T(8,128)(2,1)}, bf16[4,512,512]{2,1,0:T(8,128)(2,...) custom-call(s32[11]{0:T(128)} %stack.196.table_ref.places_ref, ...), custom_call_target="tpu_custom_call", output_to_operand_aliasing={{4}: (7, {}), {5}: (8, {})} | custom-call | flops 19327352832 | bytes 32000000 | tf_op jit(solution)/shard_map/pallas_call | solution.py:425
  230.6 5.9 collective-permute-start.39
  239.7 31.3 %shard_map.154 = (bf16[512,1536]{1,0:T(8,128)(2,1)}, bf16[512,1536]{1,0:T(8,128)(2,1)}, bf16[4,512,1024]{2,1,0:T(8,128)(2,1)}, bf16[4,512,512]{2,1,0:T(8,128)(2,...) custom-call(s32[11]{0:T(128)} %stack.196.table_ref.places_ref, ...), custom_call_target="tpu_custom_call", output_to_operand_aliasing={{4}: (7, {}), {5}: (8, {})} | custom-call | flops 19327352832 | bytes 32000000 | tf_op jit(solution)/shard_map/pallas_call | solution.py:425
  271.0 6.5 collective-permute-start.41
  279.0 26.3 %shard_map.155 = (bf16[512,1536]{1,0:T(8,128)(2,1)}, bf16[512,1536]{1,0:T(8,128)(2,1)}, bf16[4,512,1024]{2,1,0:T(8,128)(2,1)}, bf16[4,512,512]{2,1,0:T(8,128)(2,1)}, f32[4,16,512]{2,1,0:T(8,128)}) custom-call(s32[11]{0:T(128)} %stack.196.table_ref.places_ref, bf16[512,1536]{1,0:T(8,128)(2,1)} %collective-permute-done.36.inner_ref, ...), custom_call_target="tpu_custom_call", output_to_operand_aliasing={{4}: (7, {})} | custom-call | flops 19327352832 | bytes 32000000 | tf_op jit(solution)/shard_map/pallas_call | solution.py:425
  305.3 3.6 collective-permute-start.43
  310.2 48.7 %shard_map.156 = bf16[4,1536,1536]{2,1,0:T(8,128)(2,1)} custom-call(s32[11]{0:T(128)} %stack.196.table_ref.places_ref, bf16[512,1536]{1,0:T(8,128)(2,1)} %get-tuple-element.250.refs_0_, bf16[512,1536]{1,0:T(8,128)(2,1)} %get-tuple-element.251.refs_1_, bf16[512,1536]{1,0:T(8,128)(2,1)} %get-tuple-element.252.refs_2_, ...), custom_call_target="tpu_custom_call" | custom-call | flops 38654705664 | bytes 80000000 | tf_op jit(solution)/shard_map/pallas_call | solution.py:585
  359.0 5.9 all-to-all-start.1
  364.9 9.0 %shard_map.157 = bf16[4,512,1536]{2,1,0:T(8,128)(2,1)} custom-call(s32[11]{0:T(128)} %stack.196.table_ref.places_ref, bf16[4,512,512]{2,1,0:T(8,128)(2,1)} %get-tuple-element.261.refs_15_.gated_ref, bf16[4,1536,1536]{2,1,0:T(8,128)(2,1)} %weight_ref.9, bf16[4,512,1536]{2,1,0:T(8,128)(2,1)} %get-tuple-element.262._), custom_call_target="tpu_custom_call", output_to_operand_aliasing={{}: (3, {})} | custom-call | flops 3221225472 | bytes 10000000 | tf_op jit(solution)/shard_map/pallas_call | solution.py:469
  373.9 10.1 %collective-permute-done.42 = bf16[512,1536]{1,0:T(8,128)(2,1)} collective-permute-done((bf16[512,1536]{1,0:T(8,128)(2,1)}, bf16[512,1536]{1,0:T(8,128)(2,1)}, u32[]{:S(2)}, u32[]{:S(2)}) %collective-permute-start.42) | collective-permute-done | bytes 1572896 | tf_op jit(solution)/shard_map/ppermute | solution.py:658
  384.4 5.2 all-to-all-start
  391.5 304.0 %conditional.3 = (bf16[512,1536]{1,0:T(8,128)(2,1)}, f32[384,2560]{1,0:T(8,128)}, f32[384,1536]{1,0:T(8,128)}, f32[384]{0:T(512)}, f32[384]{0:T(512)}, /*index=5*/f32[384,16]{0,1:T(8,128)}) conditional(s32[]{:T(128)} %bitcast.34, () %tuple.46, (f32[512,16]{0,1:T(8,128)}, f32[1536]{0:T(1024)S(1)}, bf16[512,1536]{1,0:T(8,128)(2,1)}, ...), branch_computations={%region_5.6_spmd, %region_6.9_spmd} | conditional | flops 36138979328 | bytes 293654208 | solution.py:868
  395.4 12.5 %branch_1_fun.10 = (f32[512,1536]{1,0:T(8,128)}, bf16[512,1536]{1,0:T(8,128)(2,1)}, f32[128,1536]{1,0:T(8,128)}, f32[1,1536]{1,0:T(1,128)}) custom-call(bf16[512,1536]{1,0:T(8,128)(2,1)} %get-tuple-element.119.refs_0_, bf16[512,1536]{1,0:T(8,128)(2,1)} %get-tuple-element.120.refs_1_, bf16[512,1536]{1,0:T(8,128)(2,1)} %get-tuple-element.121.refs_2_, ...), custom_call_target="tpu_custom_call" | custom-call | flops 100000000 | bytes 20000000 | tf_op jit(solution)/shard_map/cond/branch_1_fun/pallas_call | solution.py:553
  407.9 2.6 copy.39.cosine_ref
  410.4 2.5 copy.40.sine_ref
  413.0 2.0 broadcast_28_total_ref.0.total_ref
  415.0 17.1 %branch_1_fun.11 = (bf16[4,192,1024]{2,1,0:T(8,128)(2,1)}, bf16[4,192,1024]{2,1,0:T(8,128)(2,1)}, f32[512,1536]{1,0:T(8,128)}) custom-call(s32[2]{0:T(128)S(1)} %copy-done.36, bf16[512,1536]{1,0:T(8,128)(2,1)} %get-tuple-element.153.branch_ref, bf16[4,4,192,384]{3,2,1,0:T(8,128)(2,1)} %get-tuple-element.137.own_output_ref, ...), custom_call_target="tpu_custom_call", output_to_operand_aliasing={{2}: (12, {})} | custom-call | flops 8999999488 | bytes 15000000 | tf_op jit(solution)/shard_map/cond/branch_1_fun/pallas_call | solution.py:297
  432.1 17.1 %branch_1_fun.12 = (bf16[4,192,1024]{2,1,0:T(8,128)(2,1)}, bf16[4,192,1024]{2,1,0:T(8,128)(2,1)}, f32[512,1536]{1,0:T(8,128)}) custom-call(s32[2]{0:T(128)S(1)} %copy-done.36, bf16[512,1536]{1,0:T(8,128)(2,1)} %get-tuple-element.153.branch_ref, bf16[4,4,192,384]{3,2,1,0:T(8,128)(2,1)} %get-tuple-element.137.own_output_ref, ...), custom_call_target="tpu_custom_call", output_to_operand_aliasing={{2}: (12, {})} | custom-call | flops 8999999488 | bytes 15000000 | tf_op jit(solution)/shard_map/cond/branch_1_fun/pallas_call | solution.py:297
  449.9 3.8 add_convert_fusion.3
  453.6 17.8 %branch_1_fun.13 = (bf16[4,192,1024]{2,1,0:T(8,128)(2,1)}, bf16[4,192,1024]{2,1,0:T(8,128)(2,1)}, f32[512,1536]{1,0:T(8,128)}) custom-call(s32[2]{0:T(128)S(1)} %copy-done.36, bf16[512,1536]{1,0:T(8,128)(2,1)} %get-tuple-element.153.branch_ref, bf16[4,4,192,384]{3,2,1,0:T(8,128)(2,1)} %get-tuple-element.137.own_output_ref, ...), custom_call_target="tpu_custom_call", output_to_operand_aliasing={{2}: (12, {})} | custom-call | flops 8999999488 | bytes 15000000 | tf_op jit(solution)/shard_map/cond/branch_1_fun/pallas_call | solution.py:297
  471.5 2.5 add_convert_fusion.4
  474.1 1.9 copy-done.9
  483.2 17.9 %branch_1_fun.14 = (bf16[4,192,1024]{2,1,0:T(8,128)(2,1)}, bf16[4,192,1024]{2,1,0:T(8,128)(2,1)}, f32[512,1536]{1,0:T(8,128)}) custom-call(s32[2]{0:T(128)S(1)} %copy-done.36, bf16[512,1536]{1,0:T(8,128)(2,1)} %get-tuple-element.153.branch_ref, bf16[4,4,192,384]{3,2,1,0:T(8,128)(2,1)} %get-tuple-element.137.own_output_ref, ...), custom_call_target="tpu_custom_call", output_to_operand_aliasing={{2}: (12, {})} | custom-call | flops 8999999488 | bytes 15000000 | tf_op jit(solution)/shard_map/cond/branch_1_fun/pallas_call | solution.py:297
  501.1 38.7 %collective-permute-done.8 = bf16[2,4,96,1024]{3,2,1,0:T(8,128)(2,1)} collective-permute-done((bf16[2,4,96,1024]{3,2,1,0:T(8,128)(2,1)}, bf16[2,4,96,1024]{3,2,1,0:T(8,128)(2,1)}, u32[]{:S(2)}, u32[]{:S(2)}) %collective-permute-start.8) | collective-permute-done | bytes 1572896 | tf_op jit(solution)/shard_map/cond/branch_1_fun/ppermute | solution.py:669
  539.8 2.6 fusion.3
  544.2 2.3 fusion
  549.2 2.7 add_convert_fusion.1
  551.9 23.8 %collective-permute-done.10 = bf16[4,96,1024]{2,1,0:T(8,128)(2,1)} collective-permute-done((bf16[4,96,1024]{2,1,0:T(8,128)(2,1)}, bf16[4,96,1024]{2,1,0:T(8,128)(2,1)}, u32[]{:S(2)}, u32[]{:S(2)}) %collective-permute-start.10) | collective-permute-done | bytes 786464 | tf_op jit(solution)/shard_map/cond/branch_1_fun/ppermute | solution.py:669
  575.7 7.0 collective-permute-done.12
  582.7 3.0 fusion.5
  585.8 4.4 collective-permute-start.15
  591.8 8.7 %collective-permute-done.15 = bf16[192,1024]{1,0:T(8,128)(2,1)S(1)} collective-permute-done((bf16[192,1024]{1,0:T(8,128)(2,1)S(1)}, bf16[192,1024]{1,0:T(8,128)(2,1)S(1)}, u32[]{:S(2)}, u32[]{:S(2)}) %collective-permute-start.15) | collective-permute-done | bytes 393248 | tf_op jit(solution)/shard_map/cond/branch_1_fun/ppermute | solution.py:603
  600.4 22.3 %collective-permute-done.14 = bf16[192,1024]{1,0:T(8,128)(2,1)S(1)} collective-permute-done((bf16[192,1024]{1,0:T(8,128)(2,1)S(1)}, bf16[192,1024]{1,0:T(8,128)(2,1)S(1)}, u32[]{:S(2)}, u32[]{:S(2)}) %collective-permute-start.14) | collective-permute-done | bytes 393248 | tf_op jit(solution)/shard_map/cond/branch_1_fun/ppermute | solution.py:603
  629.4 36.4 %collective-permute-done.21 = f32[18,1536]{1,0:T(8,128)} collective-permute-done((f32[18,1536]{1,0:T(8,128)}, f32[18,1536]{1,0:T(8,128)}, u32[]{:S(2)}, u32[]{:S(2)}) %collective-permute-start.21) | collective-permute-done | bytes 110624 | tf_op jit(solution)/shard_map/cond/branch_1_fun/ppermute | solution.py:1003
  666.8 2.0 collective-permute-start.22
  671.3 4.3 collective-permute-done.22
  675.8 5.2 collective-permute-done.23
  681.6 3.8 add_convert_fusion.2
  685.4 2.8 collective-permute-done.24
  689.5 5.8 branch_1_fun.15
  695.5 4.2 convert_reduce_fusion
  701.3 21.0 %convert_element_type.187 = f32[4,1536,1536]{2,1,0:T(8,128)} convert(bf16[4,1536,1536]{2,1,0:T(8,128)(2,1)} %all-reduce.6.cloned.1.call-done) | non-fusion elementwise | flops 9437184 | bytes 56623104 | tf_op jit(solution)/shard_map/convert_element_type | solution.py:922
  (223 shorter events, 69.1 us)
Async XLA Ops:
  7.2 9.3 %copy-start.23 = (bf16[384,1536]{1,0:T(8,128)(2,1)S(1)}, bf16[384,1536]{1,0:T(8,128)(2,1)}, u32[]{:S(2)}) copy-start(bf16[384,1536]{1,0:T(8,128)(2,1)} %param.15) | copy-start | bytes 3538948
  7.2 188.5 %all-gather.3.cloned.1.call-start = ((), (), s32[]{:S(2)}) async-start(), calls=%async_computation.3 | async-start | bytes 7864320 | tf_op jit(solution)/shard_map/all_gather | solution.py:840
  10.7 12.2 %collective-permute-start.27 = (bf16[192,640]{1,0:T(8,128)(2,1)S(1)}, bf16[192,640]{1,0:T(8,128)(2,1)}, u32[]{:S(2)}, u32[]{:S(2)}) collective-permute-start(bf16[192,640]{1,0:T(8,128)(2,1)S(1)} %get-tuple-element.408), channel_id=1, source_target_pairs={{0,3},{1,2},{2,1},{3,0},{4,7},{5,6},{6,5},{7,4},{8,11},{9,10},{10,... | collective-permute-start | bytes 737288 | tf_op jit(solution)/shard_map/ppermute | solution.py:603
  15.8 21.0 %collective-permute-start.26 = (bf16[192,640]{1,0:T(8,128)(2,1)S(1)}, bf16[192,640]{1,0:T(8,128)(2,1)}, u32[]{:S(2)}, u32[]{:S(2)}) collective-permute-start(bf16[192,640]{1,0:T(8,128)(2,1)S(1)} %get-tuple-element.408), channel_id=1, source_target_pairs={{0,2},{1,3},{2,0},{3,1},{4,6},{5,7},{6,4},{7,5},{8,10},{9,11},{10,... | collective-permute-start | bytes 737288 | tf_op jit(solution)/shard_map/ppermute | solution.py:603
  15.8 21.0 %collective-permute-start.25 = (bf16[192,640]{1,0:T(8,128)(2,1)S(1)}, bf16[192,640]{1,0:T(8,128)(2,1)}, u32[]{:S(2)}, u32[]{:S(2)}) collective-permute-start(bf16[192,640]{1,0:T(8,128)(2,1)S(1)} %get-tuple-element.408), channel_id=1, source_target_pairs={{0,1},{1,0},{2,3},{3,2},{4,5},{5,4},{6,7},{7,6},{8,9},{9,8},{10,11... | collective-permute-start | bytes 737288 | tf_op jit(solution)/shard_map/ppermute | solution.py:603
  17.7 21.4 %copy-start.28 = (s32[512,8]{0,1:T(8,128)S(1)}, s32[512,8]{0,1:T(8,128)}, u32[]{:S(2)}) copy-start(s32[512,8]{0,1:T(8,128)} %param.20) | copy-start | bytes 49156
  17.7 22.5 %copy-start.29 = (bf16[384,16]{0,1:T(8,128)(2,1)S(1)}, bf16[384,16]{0,1:T(8,128)(2,1)}, u32[]{:S(2)}) copy-start(bf16[384,16]{0,1:T(8,128)(2,1)} %param.18) | copy-start | bytes 36868
  36.8 4.9 copy-start.33
  43.5 40.5 %copy-start.35 = (s32[2]{0:T(128)}, s32[2]{0:T(128)S(1)}, u32[]{:S(2)}) copy-start(s32[2]{0:T(128)S(1)} %pad_add_fusion.1) | copy-start | bytes 28
  44.2 31.5 %copy-start.26 = (f32[512]{0:T(512)}, f32[512]{0:T(512)S(1)}, u32[]{:S(2)}) copy-start(f32[512]{0:T(512)S(1)} %fusion.17) | copy-start | bytes 6148
  45.2 11.5 %collective-permute-start.33 = (bf16[240,384]{1,0:T(8,128)(2,1)S(1)}, bf16[240,384]{1,0:T(8,128)(2,1)S(1)}, u32[]{:S(2)}, u32[]{:S(2)}) collective-permute-start(bf16[240,384]{1,0:T(8,128)(2,1)S(1)} %pad_maximum_fusion.10), channel_id=1, source_target_pairs={{0,3},{1,2},{2,1},{3,0},{4,7},{5,6},{6,5},{7,4},{8,11},{9,10},{10,... | collective-permute-start | bytes 552968 | tf_op jit(solution)/shard_map/ppermute | solution.py:603
  47.7 28.0 %collective-permute-start.32 = (bf16[240,384]{1,0:T(8,128)(2,1)S(1)}, bf16[240,384]{1,0:T(8,128)(2,1)S(1)}, u32[]{:S(2)}, u32[]{:S(2)}) collective-permute-start(bf16[240,384]{1,0:T(8,128)(2,1)S(1)} %pad_maximum_fusion.10), channel_id=1, source_target_pairs={{0,2},{1,3},{2,0},{3,1},{4,6},{5,7},{6,4},{7,5},{8,10},{9,11},{10,... | collective-permute-start | bytes 552968 | tf_op jit(solution)/shard_map/ppermute | solution.py:603
  47.7 28.0 %collective-permute-start.31 = (bf16[240,384]{1,0:T(8,128)(2,1)S(1)}, bf16[240,384]{1,0:T(8,128)(2,1)S(1)}, u32[]{:S(2)}, u32[]{:S(2)}) collective-permute-start(bf16[240,384]{1,0:T(8,128)(2,1)S(1)} %pad_maximum_fusion.10), channel_id=1, source_target_pairs={{0,1},{1,0},{2,3},{3,2},{4,5},{5,4},{6,7},{7,6},{8,9},{9,8},{10,11... | collective-permute-start | bytes 552968 | tf_op jit(solution)/shard_map/ppermute | solution.py:603
  49.7 31.8 %collective-permute-start.28 = (bf16[3,192,640]{2,1,0:T(8,128)(2,1)}, bf16[3,192,640]{2,1,0:T(8,128)(2,1)}, u32[]{:S(2)}, u32[]{:S(2)}) collective-permute-start(bf16[3,192,640]{2,1,0:T(8,128)(2,1)} %pad_maximum_fusion.6), channel_id=1, source_target_pairs={{0,8},{4,12},{8,0},{12,4},{16,24},{20,28},{24,16},{28,20},{1,9},{5... | collective-permute-start | bytes 2211848 | tf_op jit(solution)/shard_map/ppermute | solution.py:669
  51.1 32.5 %collective-permute-start.29 = (bf16[3,192,640]{2,1,0:T(8,128)(2,1)}, bf16[3,192,640]{2,1,0:T(8,128)(2,1)}, u32[]{:S(2)}, u32[]{:S(2)}) collective-permute-start(bf16[3,192,640]{2,1,0:T(8,128)(2,1)} %pad_maximum_fusion.6), channel_id=1, source_target_pairs={{0,16},{4,20},{8,24},{12,28},{16,0},{20,4},{24,8},{28,12},{1,17},{... | collective-permute-start | bytes 2211848 | tf_op jit(solution)/shard_map/ppermute | solution.py:669
  56.7 27.0 %collective-permute-start.30 = (bf16[3,192,640]{2,1,0:T(8,128)(2,1)}, bf16[3,192,640]{2,1,0:T(8,128)(2,1)}, u32[]{:S(2)}, u32[]{:S(2)}) collective-permute-start(bf16[3,192,640]{2,1,0:T(8,128)(2,1)} %pad_maximum_fusion.6), channel_id=1, source_target_pairs={{0,24},{4,28},{8,16},{12,20},{16,8},{20,12},{24,0},{28,4},{1,25},{... | collective-permute-start | bytes 2211848 | tf_op jit(solution)/shard_map/ppermute | solution.py:669
  88.8 7.1 collective-permute-start
  96.0 31.0 %collective-permute-start.3 = (bf16[3,192,384]{2,1,0:T(8,128)(2,1)S(1)}, bf16[3,192,384]{2,1,0:T(8,128)(2,1)S(1)}, u32[]{:S(2)}, u32[]{:S(2)}) collective-permute-start(bf16[3,192,384]{2,1,0:T(8,128)(2,1)S(1)} %get-tuple-element.106), channel_id=1, source_target_pairs={{0,24},{4,28},{8,16},{12,20},{16,8},{20,12},{24,0},{28,4},{1,25},{... | collective-permute-start | bytes 1327112 | tf_op jit(solution)/shard_map/cond/branch_1_fun/ppermute | solution.py:669
  97.5 29.5 %collective-permute-start.2 = (bf16[3,192,384]{2,1,0:T(8,128)(2,1)S(1)}, bf16[3,192,384]{2,1,0:T(8,128)(2,1)S(1)}, u32[]{:S(2)}, u32[]{:S(2)}) collective-permute-start(bf16[3,192,384]{2,1,0:T(8,128)(2,1)S(1)} %get-tuple-element.106), channel_id=1, source_target_pairs={{0,16},{4,20},{8,24},{12,28},{16,0},{20,4},{24,8},{28,12},{1,17},{... | collective-permute-start | bytes 1327112 | tf_op jit(solution)/shard_map/cond/branch_1_fun/ppermute | solution.py:669
  98.7 28.3 %collective-permute-start.1 = (bf16[3,192,384]{2,1,0:T(8,128)(2,1)S(1)}, bf16[3,192,384]{2,1,0:T(8,128)(2,1)S(1)}, u32[]{:S(2)}, u32[]{:S(2)}) collective-permute-start(bf16[3,192,384]{2,1,0:T(8,128)(2,1)S(1)} %get-tuple-element.106), channel_id=1, source_target_pairs={{0,8},{4,12},{8,0},{12,4},{16,24},{20,28},{24,16},{28,20},{1,9},{5... | collective-permute-start | bytes 1327112 | tf_op jit(solution)/shard_map/cond/branch_1_fun/ppermute | solution.py:669
  99.5 28.3 %copy-start.14 = (bf16[4,192,384]{2,1,0:T(8,128)(2,1)S(1)}, bf16[4,192,384]{2,1,0:T(8,128)(2,1)}, u32[]{:S(2)}) copy-start(bf16[4,192,384]{2,1,0:T(8,128)(2,1)} %get-tuple-element.104) | copy-start | bytes 1769476 | tf_op jit(solution)/shard_map/cond
  127.8 7.6 %copy-start.7 = (bf16[512,1536]{1,0:T(8,128)(2,1)S(1)}, bf16[512,1536]{1,0:T(8,128)(2,1)}, u32[]{:S(2)}) copy-start(bf16[512,1536]{1,0:T(8,128)(2,1)} %get-tuple-element.115.input_ref) | copy-start | bytes 4718596 | tf_op jit(solution)/shard_map/cond
  130.4 4.9 collective-permute-start.4
  145.6 50.1 %collective-permute-start.34 = (bf16[512,1536]{1,0:T(8,128)(2,1)}, bf16[512,1536]{1,0:T(8,128)(2,1)}, u32[]{:S(2)}, u32[]{:S(2)}) collective-permute-start(bf16[512,1536]{1,0:T(8,128)(2,1)} %get-tuple-element.238.inner_ref.outer_ref), channel_id=1, source_target_pairs={{0,1},{1,0},{2,3},{3,2},{4,5},{5,4},{6,7},{7,6},{8,9},{9,8},{10,11... | collective-permute-start | bytes 4718600 | tf_op jit(solution)/shard_map/ppermute | solution.py:603
  145.9 49.8 %collective-permute-start.35 = (bf16[512,1536]{1,0:T(8,128)(2,1)}, bf16[512,1536]{1,0:T(8,128)(2,1)}, u32[]{:S(2)}, u32[]{:S(2)}) collective-permute-start(bf16[512,1536]{1,0:T(8,128)(2,1)} %get-tuple-element.238.inner_ref.outer_ref), channel_id=1, source_target_pairs={{1,2},{2,1},{5,6},{6,5},{9,10},{10,9},{13,14},{14,13},{17,18},{18,... | collective-permute-start | bytes 4718600 | tf_op jit(solution)/shard_map/ppermute | solution.py:631
  195.7 41.6 %collective-permute-start.36 = (bf16[512,1536]{1,0:T(8,128)(2,1)}, bf16[512,1536]{1,0:T(8,128)(2,1)}, u32[]{:S(2)}, u32[]{:S(2)}) collective-permute-start(bf16[512,1536]{1,0:T(8,128)(2,1)} %collective-permute-done.34.outer_ref.inner_ref), channel_id=1, source_target_pairs={{1,2},{2,1},{5,6},{6,5},{9,10},{10,9},{13,14},{14,13},{17,18},{18,... | collective-permute-start | bytes 4718600 | tf_op jit(solution)/shard_map/ppermute | solution.py:635
  197.5 41.0 %collective-permute-start.38 = (bf16[512,1536]{1,0:T(8,128)(2,1)}, bf16[512,1536]{1,0:T(8,128)(2,1)S(1)}, u32[]{:S(2)}, u32[]{:S(2)}) collective-permute-start(bf16[512,1536]{1,0:T(8,128)(2,1)} %collective-permute-done.35.inner_ref), channel_id=1, source_target_pairs={{1,0},{2,3},{5,4},{6,7},{9,8},{10,11},{13,12},{14,15},{17,16},{18,... | collective-permute-start | bytes 4718600 | tf_op jit(solution)/shard_map/ppermute | solution.py:636
  230.6 78.3 %collective-permute-start.39 = (bf16[512,1536]{1,0:T(8,128)(2,1)}, bf16[512,1536]{1,0:T(8,128)(2,1)}, u32[]{:S(2)}, u32[]{:S(2)}) collective-permute-start(bf16[512,1536]{1,0:T(8,128)(2,1)} %get-tuple-element.263), channel_id=1, source_target_pairs={{0,1},{3,2},{4,5},{7,6},{8,9},{11,10},{12,13},{15,14},{16,17},{19,... | collective-permute-start | bytes 4718600 | tf_op jit(solution)/shard_map/ppermute | solution.py:658
  236.5 137.4 %collective-permute-start.40 = (bf16[512,1536]{1,0:T(8,128)(2,1)}, bf16[512,1536]{1,0:T(8,128)(2,1)S(1)}, u32[]{:S(2)}, u32[]{:S(2)}) collective-permute-start(bf16[512,1536]{1,0:T(8,128)(2,1)} %get-tuple-element.263), channel_id=1, source_target_pairs={{1,2},{2,1},{5,6},{6,5},{9,10},{10,9},{13,14},{14,13},{17,18},{18,... | collective-permute-start | bytes 4718600 | tf_op jit(solution)/shard_map/ppermute | solution.py:658
  237.3 41.7 %collective-permute-start.37 = (bf16[512,1536]{1,0:T(8,128)(2,1)}, bf16[512,1536]{1,0:T(8,128)(2,1)}, u32[]{:S(2)}, u32[]{:S(2)}) collective-permute-start(bf16[512,1536]{1,0:T(8,128)(2,1)} %collective-permute-done.36.inner_ref), channel_id=1, source_target_pairs={{1,0},{2,3},{5,4},{6,7},{9,8},{10,11},{13,12},{14,15},{17,16},{18,... | collective-permute-start | bytes 4718600 | tf_op jit(solution)/shard_map/ppermute | solution.py:639
  271.0 102.9 %collective-permute-start.41 = (bf16[512,1536]{1,0:T(8,128)(2,1)}, bf16[512,1536]{1,0:T(8,128)(2,1)S(1)}, u32[]{:S(2)}, u32[]{:S(2)}) collective-permute-start(bf16[512,1536]{1,0:T(8,128)(2,1)} %get-tuple-element.264), channel_id=1, source_target_pairs={{0,2},{3,1},{4,6},{7,5},{8,10},{11,9},{12,14},{15,13},{16,18},{19,... | collective-permute-start | bytes 4718600 | tf_op jit(solution)/shard_map/ppermute | solution.py:658
  277.5 106.5 %collective-permute-start.42 = (bf16[512,1536]{1,0:T(8,128)(2,1)}, bf16[512,1536]{1,0:T(8,128)(2,1)}, u32[]{:S(2)}, u32[]{:S(2)}) collective-permute-start(bf16[512,1536]{1,0:T(8,128)(2,1)} %get-tuple-element.264), channel_id=1, source_target_pairs={{1,0},{2,3},{5,4},{6,7},{9,8},{10,11},{13,12},{14,15},{17,16},{18,... | collective-permute-start | bytes 4718600 | tf_op jit(solution)/shard_map/ppermute | solution.py:658
  305.3 78.7 %collective-permute-start.43 = (bf16[512,1536]{1,0:T(8,128)(2,1)}, bf16[512,1536]{1,0:T(8,128)(2,1)}, u32[]{:S(2)}, u32[]{:S(2)}) collective-permute-start(bf16[512,1536]{1,0:T(8,128)(2,1)} %get-tuple-element.265), channel_id=1, source_target_pairs={{0,3},{3,0},{4,7},{7,4},{8,11},{11,8},{12,15},{15,12},{16,19},{19,... | collective-permute-start | bytes 4718600 | tf_op jit(solution)/shard_map/ppermute | solution.py:658
  308.9 75.1 %collective-permute-start.44 = (bf16[512,1536]{1,0:T(8,128)(2,1)}, bf16[512,1536]{1,0:T(8,128)(2,1)}, u32[]{:S(2)}, u32[]{:S(2)}) collective-permute-start(bf16[512,1536]{1,0:T(8,128)(2,1)} %get-tuple-element.265), channel_id=1, source_target_pairs={{1,3},{2,0},{5,7},{6,4},{9,11},{10,8},{13,15},{14,12},{17,19},{18,... | collective-permute-start | bytes 4718600 | tf_op jit(solution)/shard_map/ppermute | solution.py:658
  359.0 25.4 %all-to-all-start.1 = ((f32[4,16,512]{2,1,0:T(8,128)}), f32[4,16,512]{2,1,0:T(8,128)}, u32[]{:S(2)}, u32[]{:S(2)}) async-start(f32[4,16,512]{2,1,0:T(8,128)} %get-tuple-element.274), calls=%async_computation.1 | async-start | bytes 262144 | tf_op jit(solution)/shard_map/all_to_all | solution.py:933
  373.9 10.4 %copy-start.19 = (bf16[512,1536]{1,0:T(8,128)(2,1)}, bf16[512,1536]{1,0:T(8,128)(2,1)S(1)}, u32[]{:S(2)}) copy-start(bf16[512,1536]{1,0:T(8,128)(2,1)S(1)} %collective-permute-done.40) | copy-start | bytes 4718596
  373.9 10.4 %copy-start.20 = (bf16[512,1536]{1,0:T(8,128)(2,1)}, bf16[512,1536]{1,0:T(8,128)(2,1)S(1)}, u32[]{:S(2)}) copy-start(bf16[512,1536]{1,0:T(8,128)(2,1)S(1)} %collective-permute-done.41) | copy-start | bytes 4718596
  384.4 311.1 %all-to-all-start = ((bf16[4,512,1536]{2,1,0:T(8,128)(2,1)}), bf16[4,512,1536]{2,1,0:T(8,128)(2,1)}, u32[]{:S(2)}, u32[]{:S(2)}) async-start(bf16[4,512,1536]{2,1,0:T(8,128)(2,1)} %shard_map.157), calls=%async_computation | async-start | bytes 12582912 | tf_op jit(solution)/shard_map/all_to_all | solution.py:934
  389.6 311.7 %all-reduce.6.cloned.1.call-start = ((), (), s32[]{:S(2)}) async-start(), calls=%async_computation.2 | async-start | bytes 37748736 | tf_op jit(solution)/shard_map/psum | solution.py:922
  432.1 17.8 %collective-permute-start.6 = (bf16[4,192,1024]{2,1,0:T(8,128)(2,1)}, bf16[4,192,1024]{2,1,0:T(8,128)(2,1)}, u32[]{:S(2)}, u32[]{:S(2)}) collective-permute-start(bf16[4,192,1024]{2,1,0:T(8,128)(2,1)} %get-tuple-element.152), channel_id=1, source_target_pairs={{0,4},{4,0},{8,12},{12,8},{16,20},{20,16},{24,28},{28,24},{1,5},{5... | collective-permute-start | bytes 4718600 | tf_op jit(solution)/shard_map/cond/branch_1_fun/ppermute | solution.py:669
  449.2 22.3 %collective-permute-start.5 = (bf16[4,192,1024]{2,1,0:T(8,128)(2,1)}, bf16[4,192,1024]{2,1,0:T(8,128)(2,1)}, u32[]{:S(2)}, u32[]{:S(2)}) collective-permute-start(bf16[4,192,1024]{2,1,0:T(8,128)(2,1)} %get-tuple-element.149), channel_id=1, source_target_pairs={{0,4},{4,0},{8,12},{12,8},{16,20},{20,16},{24,28},{28,24},{1,5},{5... | collective-permute-start | bytes 4718600 | tf_op jit(solution)/shard_map/cond/branch_1_fun/ppermute | solution.py:669
  471.4 7.9 %collective-permute-start.9 = (bf16[4,192,1024]{2,1,0:T(8,128)(2,1)}, bf16[4,192,1024]{2,1,0:T(8,128)(2,1)S(1)}, u32[]{:S(2)}, u32[]{:S(2)}) collective-permute-start(bf16[4,192,1024]{2,1,0:T(8,128)(2,1)} %get-tuple-element.164), channel_id=1, source_target_pairs={{0,4},{4,0},{8,12},{12,8},{16,20},{20,16},{24,28},{28,24},{1,5},{5... | collective-permute-start | bytes 4718600 | tf_op jit(solution)/shard_map/cond/branch_1_fun/ppermute | solution.py:669
  477.6 62.3 %collective-permute-start.8 = (bf16[2,4,96,1024]{3,2,1,0:T(8,128)(2,1)}, bf16[2,4,96,1024]{3,2,1,0:T(8,128)(2,1)}, u32[]{:S(2)}, u32[]{:S(2)}) collective-permute-start(bf16[2,4,96,1024]{3,2,1,0:T(8,128)(2,1)} %pad_maximum_fusion), channel_id=1, source_target_pairs={{0,8},{4,12},{8,0},{12,4},{16,24},{20,28},{24,16},{28,20},{1,9},{5... | collective-permute-start | bytes 4718600 | tf_op jit(solution)/shard_map/cond/branch_1_fun/ppermute | solution.py:669
  481.7 62.5 %collective-permute-start.11 = (bf16[2,4,96,1024]{3,2,1,0:T(8,128)(2,1)}, bf16[2,4,96,1024]{3,2,1,0:T(8,128)(2,1)}, u32[]{:S(2)}, u32[]{:S(2)}) collective-permute-start(bf16[2,4,96,1024]{3,2,1,0:T(8,128)(2,1)} %pad_maximum_fusion.1), channel_id=1, source_target_pairs={{0,16},{4,20},{8,24},{12,28},{16,0},{20,4},{24,8},{28,12},{1,17},{... | collective-permute-start | bytes 4718600 | tf_op jit(solution)/shard_map/cond/branch_1_fun/ppermute | solution.py:669
  501.1 43.1 %copy-start.11 = (bf16[4,192,1024]{2,1,0:T(8,128)(2,1)S(1)}, bf16[4,192,1024]{2,1,0:T(8,128)(2,1)}, u32[]{:S(2)}) copy-start(bf16[4,192,1024]{2,1,0:T(8,128)(2,1)} %copy-done.10) | copy-start | bytes 4718596 | tf_op jit(solution)/shard_map/cond
  501.1 48.0 %collective-permute-start.7 = (bf16[4,192,1024]{2,1,0:T(8,128)(2,1)}, bf16[4,192,1024]{2,1,0:T(8,128)(2,1)}, u32[]{:S(2)}, u32[]{:S(2)}) collective-permute-start(bf16[4,192,1024]{2,1,0:T(8,128)(2,1)} %get-tuple-element.162), channel_id=1, source_target_pairs={{0,4},{4,0},{8,12},{12,8},{16,20},{20,16},{24,28},{28,24},{1,5},{5... | collective-permute-start | bytes 4718600 | tf_op jit(solution)/shard_map/cond/branch_1_fun/ppermute | solution.py:669
  542.5 33.3 %collective-permute-start.10 = (bf16[4,96,1024]{2,1,0:T(8,128)(2,1)}, bf16[4,96,1024]{2,1,0:T(8,128)(2,1)}, u32[]{:S(2)}, u32[]{:S(2)}) collective-permute-start(bf16[4,96,1024]{2,1,0:T(8,128)(2,1)} %fusion.3), channel_id=1, source_target_pairs={{0,16},{4,20},{8,24},{12,28},{16,0},{20,4},{24,8},{28,12},{1,17},{... | collective-permute-start | bytes 2359304 | tf_op jit(solution)/shard_map/cond/branch_1_fun/ppermute | solution.py:669
  546.5 36.2 %collective-permute-start.12 = (bf16[4,96,1024]{2,1,0:T(8,128)(2,1)}, bf16[4,96,1024]{2,1,0:T(8,128)(2,1)}, u32[]{:S(2)}, u32[]{:S(2)}) collective-permute-start(bf16[4,96,1024]{2,1,0:T(8,128)(2,1)} %fusion), channel_id=1, source_target_pairs={{0,8},{4,12},{8,0},{12,4},{16,24},{20,28},{24,16},{28,20},{1,9},{5... | collective-permute-start | bytes 2359304 | tf_op jit(solution)/shard_map/cond/branch_1_fun/ppermute | solution.py:669
  582.7 8.2 %copy-start.1 = (f32[512,1536]{1,0:T(8,128)S(1)}, f32[512,1536]{1,0:T(8,128)}, u32[]{:S(2)}) copy-start(f32[512,1536]{1,0:T(8,128)} %get-tuple-element.156) | copy-start | bytes 9437188 | tf_op jit(solution)/shard_map/cond
  585.8 14.6 %collective-permute-start.15 = (bf16[192,1024]{1,0:T(8,128)(2,1)S(1)}, bf16[192,1024]{1,0:T(8,128)(2,1)S(1)}, u32[]{:S(2)}, u32[]{:S(2)}) collective-permute-start(bf16[192,1024]{1,0:T(8,128)(2,1)S(1)} %get-tuple-element.383), channel_id=1, source_target_pairs={{0,3},{1,2},{2,1},{3,0},{4,7},{5,6},{6,5},{7,4},{8,11},{9,10},{10,... | collective-permute-start | bytes 1179656 | tf_op jit(solution)/shard_map/cond/branch_1_fun/ppermute | solution.py:603
  590.3 32.5 %collective-permute-start.14 = (bf16[192,1024]{1,0:T(8,128)(2,1)S(1)}, bf16[192,1024]{1,0:T(8,128)(2,1)S(1)}, u32[]{:S(2)}, u32[]{:S(2)}) collective-permute-start(bf16[192,1024]{1,0:T(8,128)(2,1)S(1)} %get-tuple-element.384), channel_id=1, source_target_pairs={{0,2},{1,3},{2,0},{3,1},{4,6},{5,7},{6,4},{7,5},{8,10},{9,11},{10,... | collective-permute-start | bytes 1179656 | tf_op jit(solution)/shard_map/cond/branch_1_fun/ppermute | solution.py:603
  590.3 32.5 %collective-permute-start.13 = (bf16[192,1024]{1,0:T(8,128)(2,1)S(1)}, bf16[192,1024]{1,0:T(8,128)(2,1)S(1)}, u32[]{:S(2)}, u32[]{:S(2)}) collective-permute-start(bf16[192,1024]{1,0:T(8,128)(2,1)S(1)} %get-tuple-element.382), channel_id=1, source_target_pairs={{0,1},{1,0},{2,3},{3,2},{4,5},{5,4},{6,7},{7,6},{8,9},{9,8},{10,11... | collective-permute-start | bytes 1179656 | tf_op jit(solution)/shard_map/cond/branch_1_fun/ppermute | solution.py:603
  591.7 34.9 %collective-permute-start.20 = (f32[18,1536]{1,0:T(8,128)S(1)}, f32[18,1536]{1,0:T(8,128)S(1)}, u32[]{:S(2)}, u32[]{:S(2)}) collective-permute-start(f32[18,1536]{1,0:T(8,128)S(1)} %pad_maximum_fusion.4), channel_id=1, source_target_pairs={{0,4},{4,0},{8,12},{12,8},{16,20},{20,16},{24,28},{28,24},{1,5},{5... | collective-permute-start | bytes 331784 | tf_op jit(solution)/shard_map/cond/branch_1_fun/ppermute | solution.py:1003
  623.0 45.8 %collective-permute-start.18 = (bf16[192,1024]{1,0:T(8,128)(2,1)S(1)}, bf16[192,1024]{1,0:T(8,128)(2,1)}, u32[]{:S(2)}, u32[]{:S(2)}) collective-permute-start(bf16[192,1024]{1,0:T(8,128)(2,1)S(1)} %fusion.8), channel_id=1, source_target_pairs={{0,24},{4,28},{8,16},{12,20},{16,8},{20,12},{24,0},{28,4},{1,25},{... | collective-permute-start | bytes 1179656 | tf_op jit(solution)/shard_map/cond/branch_1_fun/ppermute | solution.py:669
  624.6 44.2 %collective-permute-start.17 = (bf16[192,1024]{1,0:T(8,128)(2,1)S(1)}, bf16[192,1024]{1,0:T(8,128)(2,1)}, u32[]{:S(2)}, u32[]{:S(2)}) collective-permute-start(bf16[192,1024]{1,0:T(8,128)(2,1)S(1)} %fusion.8), channel_id=1, source_target_pairs={{0,16},{4,20},{8,24},{12,28},{16,0},{20,4},{24,8},{28,12},{1,17},{... | collective-permute-start | bytes 1179656 | tf_op jit(solution)/shard_map/cond/branch_1_fun/ppermute | solution.py:669
  626.1 42.7 %collective-permute-start.16 = (bf16[192,1024]{1,0:T(8,128)(2,1)S(1)}, bf16[192,1024]{1,0:T(8,128)(2,1)}, u32[]{:S(2)}, u32[]{:S(2)}) collective-permute-start(bf16[192,1024]{1,0:T(8,128)(2,1)S(1)} %fusion.8), channel_id=1, source_target_pairs={{0,8},{4,12},{8,0},{12,4},{16,24},{20,28},{24,16},{28,20},{1,9},{5... | collective-permute-start | bytes 1179656 | tf_op jit(solution)/shard_map/cond/branch_1_fun/ppermute | solution.py:669
  627.3 38.5 %collective-permute-start.21 = (f32[18,1536]{1,0:T(8,128)}, f32[18,1536]{1,0:T(8,128)}, u32[]{:S(2)}, u32[]{:S(2)}) collective-permute-start(f32[18,1536]{1,0:T(8,128)} %fusion.16), channel_id=1, source_target_pairs={{0,8},{4,12},{8,0},{12,4},{16,24},{20,28},{24,16},{28,20},{1,9},{5... | collective-permute-start | bytes 331784 | tf_op jit(solution)/shard_map/cond/branch_1_fun/ppermute | solution.py:1003
  666.8 8.8 %collective-permute-start.22 = (f32[18,1536]{1,0:T(8,128)S(1)}, f32[18,1536]{1,0:T(8,128)S(1)}, u32[]{:S(2)}, u32[]{:S(2)}) collective-permute-start(f32[18,1536]{1,0:T(8,128)S(1)} %add.186), channel_id=1, source_target_pairs={{0,16},{4,20},{8,24},{12,28},{16,0},{20,4},{24,8},{28,12},{1,17},{... | collective-permute-start | bytes 331784 | tf_op jit(solution)/shard_map/cond/branch_1_fun/ppermute | solution.py:1003
  668.8 12.8 %copy-start.2 = (f32[512,1536]{1,0:T(8,128)S(1)}, f32[512,1536]{1,0:T(8,128)}, u32[]{:S(2)}) copy-start(f32[512,1536]{1,0:T(8,128)} %get-tuple-element.156) | copy-start | bytes 9437188 | tf_op jit(solution)/shard_map/cond
  668.8 12.8 %copy-start.31 = (f32[512]{0:T(512)S(1)}, f32[512]{0:T(512)}, u32[]{:S(2)}) copy-start(f32[512]{0:T(512)} %add_rsqrt_fusion) | copy-start | bytes 6148 | tf_op jit(solution)/shard_map/cond
  670.5 14.9 %copy-start.8 = (bf16[4,192,1024]{2,1,0:T(8,128)(2,1)}, bf16[4,192,1024]{2,1,0:T(8,128)(2,1)S(1)}, u32[]{:S(2)}) copy-start(bf16[4,192,1024]{2,1,0:T(8,128)(2,1)S(1)} %pad_maximum_fusion.2.own_ref) | copy-start | bytes 4718596 | tf_op jit(solution)/shard_map/cond
  670.5 18.9 %collective-permute-start.19 = (bf16[4,192,1024]{2,1,0:T(8,128)(2,1)S(1)}, bf16[4,192,1024]{2,1,0:T(8,128)(2,1)}, u32[]{:S(2)}, u32[]{:S(2)}) collective-permute-start(bf16[4,192,1024]{2,1,0:T(8,128)(2,1)S(1)} %pad_maximum_fusion.2.own_ref), channel_id=1, source_target_pairs={{0,4},{4,0},{8,12},{12,8},{16,20},{20,16},{24,28},{28,24},{1,5},{5... | collective-permute-start | bytes 4718600 | tf_op jit(solution)/shard_map/cond/branch_1_fun/ppermute | solution.py:669
  675.7 5.3 collective-permute-start.23
  681.0 7.3 collective-permute-start.24
  (22 other events, 44.3 us)
Sparse Core Ops, SparseCore 0:
  39.1 134.7 all-gather.2
  394.8 302.6 all-reduce.5
